TPU v7x, 32 devices: a whole 2x2x4 slice. The times are simulated.
32 devices in a mesh: frame: 4 (over y, core), head: 4 (over z), fsdp: 2 (over x).
Axes of the slice: x: 2, y: 2, z: 4, core: 2. Of those that a mesh axis runs over, the one named last changes fastest.
Arguments:
- queries: bfloat16 [2, 8, 256, 5120], P('fsdp', 'frame', 'head'), may hold values from -6 to 6
- key_rows: bfloat16 [2, 8, 256, 5120], P('fsdp', 'frame', 'head'), may hold values from -6 to 6
- value_rows: bfloat16 [2, 8, 256, 5120], P('fsdp', 'frame', 'head'), may hold values from -6 to 6
- saved_out: bfloat16 [2, 8, 256, 5120], P('fsdp', 'frame', 'head'), may hold values from -6 to 6
- cotangent: bfloat16 [2, 8, 256, 5120], P('fsdp', 'frame', 'head'), may hold values from -192 to 192
- out_weight: bfloat16 [5120, 5120], P('head'), may hold values from -0.078125 to 0.078125
- gate_table: float32 [64, 5120], replicated, may hold values from 0.25 to 2.5
- levels: int32 [8], P('frame'), may hold values from 0 to 63, as said below
- reach_flags: int32 [8, 2], replicated, may hold values from 0 to 1
Outputs:
- d_queries: bfloat16 [2, 8, 256, 5120], P('fsdp', 'frame', None, 'head')
- d_keys: bfloat16 [2, 8, 256, 5120], P('fsdp', 'frame', None, 'head')
- d_values: bfloat16 [2, 8, 256, 5120], P('fsdp', 'frame', None, 'head')
- d_weight: float32 [5120, 5120], P('head', ('frame', 'fsdp'))
Inputs may be any that keep to these rules, and one draw needn't show every extreme that they name: `levels`: each frame's level is at least the level of the frame before it; the first frame has level 0 and the last frame level 63.
All inputs are finite; a program needn't handle non-finite values.
Results may differ from a plain program's by a relative error of at most 0.017.
Values may be sent and summed in bfloat16 or wider, within the bound.
No kernel may reach another device: no remote copies, remote signals or barrier semaphores. Data moves between devices by JAX's collectives and lax.ppermute only.
A program may use at most 128 MiB of HBM per device.

v0:
```python
from functools import partial

import jax
import jax.numpy as jnp
from jax import lax
from jax.experimental import pallas as pl
from jax.experimental.pallas import tpu as pltpu
from jax.sharding import PartitionSpec as P

HD = 128
NEG = -1e30
NT = (((1,), (1,)), ((), ()))
NN = (((1,), (0,)), ((), ()))
TN = (((0,), (0,)), ((), ()))


def dot(lhs, rhs, dims):
    return lax.dot_general(lhs, rhs, dims, preferred_element_type=jnp.float32)


def attention_kernel(
    limits, q_ref, k_ref, v_ref, o_ref, d_ref, kp_ref, kn_ref, vp_ref, vn_ref,
    dq_ref, dk_ref, dv_ref, dkp_ref, dkn_ref, dvp_ref, dvn_ref,
):
    frames = q_ref.shape[1]
    inv_root = HD ** (-0.5)

    def whole(ref, frame):
        return ref[:, frame].reshape(-1, HD)

    def side(ref):
        return ref[...].reshape(-1, HD)

    keys = [side(kp_ref)] + [whole(k_ref, f) for f in range(frames)] + [side(kn_ref)]
    vals = [side(vp_ref)] + [whole(v_ref, f) for f in range(frames)] + [side(vn_ref)]
    tokens = keys[0].shape[0]
    row = lax.broadcasted_iota(jnp.int32, (tokens, tokens), 0)
    key_grads = [None] * (frames + 2)
    value_grads = [None] * (frames + 2)

    def put(grads, slot, term):
        grads[slot] = term if grads[slot] is None else grads[slot] + term

    for f in range(frames):
        q, d = whole(q_ref, f), whole(d_ref, f)
        prod = d.astype(jnp.float32) * whole(o_ref, f).astype(jnp.float32)
        delta = lax.dot_general(
            jnp.ones((8, HD), jnp.float32), prod, NT,
            precision=lax.Precision.HIGHEST, preferred_element_type=jnp.float32,
        )[0:1]
        scores = []
        for w in range(3):
            s = dot(keys[f + w], q, NT) * inv_root
            if w != 1:
                s = jnp.where(row < limits[f, w // 2], s, NEG)
            scores.append(s)
        top = jnp.max(jnp.maximum(jnp.maximum(scores[0], scores[1]), scores[2]), axis=0, keepdims=True)
        exps = [jnp.exp(s - top) for s in scores]
        total = jnp.sum(exps[0] + exps[1] + exps[2], axis=0, keepdims=True)
        inv_total = 1.0 / total
        dq = None
        for w in range(3):
            prob = exps[w] * inv_total
            put(value_grads, f + w, dot(prob.astype(jnp.bfloat16), d, NN))
            d_prob = dot(vals[f + w], d, NT)
            d_score = (prob * (d_prob - delta)).astype(jnp.bfloat16)
            put(key_grads, f + w, dot(d_score, q, NN))
            term = dot(d_score, keys[f + w], TN)
            dq = term if dq is None else dq + term
        dq_ref[f] = (dq * inv_root).astype(jnp.bfloat16)
    for f in range(frames):
        dk_ref[f] = key_grads[f + 1] * inv_root
        dv_ref[f] = value_grads[f + 1]
    dkp_ref[...] = (key_grads[0] * inv_root).astype(jnp.bfloat16)
    dkn_ref[...] = (key_grads[frames + 1] * inv_root).astype(jnp.bfloat16)
    dvp_ref[...] = value_grads[0].astype(jnp.bfloat16)
    dvn_ref[...] = value_grads[frames + 1].astype(jnp.bfloat16)


def attention(limits, q, k, v, o, d, kp, kn, vp, vn):
    parts, frames, rows, width = q.shape
    tokens = parts * rows
    heads = width // HD
    whole = pl.BlockSpec((parts, frames, rows, HD), lambda h, lim: (0, 0, 0, h))
    side = pl.BlockSpec((parts, rows, HD), lambda h, lim: (0, 0, h))
    out = pl.BlockSpec((frames, tokens, HD), lambda h, lim: (0, 0, h))
    edge = pl.BlockSpec((tokens, HD), lambda h, lim: (0, h))
    full_shape, edge_shape = (frames, tokens, width), (tokens, width)
    return pl.pallas_call(
        attention_kernel,
        grid_spec=pltpu.PrefetchScalarGridSpec(
            num_scalar_prefetch=1,
            grid=(heads,),
            in_specs=[whole] * 5 + [side] * 4,
            out_specs=[out] * 3 + [edge] * 4,
        ),
        out_shape=[
            jax.ShapeDtypeStruct(full_shape, jnp.bfloat16),
            jax.ShapeDtypeStruct(full_shape, jnp.float32),
            jax.ShapeDtypeStruct(full_shape, jnp.float32),
        ]
        + [jax.ShapeDtypeStruct(edge_shape, jnp.bfloat16)] * 4,
        compiler_params=pltpu.CompilerParams(vmem_limit_bytes=48 * 2**20),
        cost_estimate=pl.CostEstimate(
            flops=heads * frames * 3 * tokens * tokens * HD * 10,
            bytes_accessed=heads * HD * tokens * frames * 2 * 16,
            transcendentals=heads * frames * 3 * tokens * tokens,
        ),
        name="attention_backward",
    )(limits, q, k, v, o, d, kp, kn, vp, vn)


def shifted(array, axis, step):
    count = lax.axis_size(axis)
    pairs = [(i, i + step) for i in range(count) if 0 <= i + step < count]
    return lax.ppermute(array, axis, pairs)


def per_device(
    queries, key_rows, value_rows, saved_out, cotangent, out_weight, gate_table, levels, reach_flags
):
    _, frames, rows, model = queries.shape
    parts = lax.axis_size("head")
    width = model // parts
    frames_all = frames * lax.axis_size("frame")
    tokens = rows * parts
    first_frame = lax.axis_index("frame") * frames
    tokens_all = lax.axis_size("fsdp") * frames_all * tokens

    gain = jnp.concatenate(
        [lax.dynamic_slice_in_dim(gate_table, levels[f], 1, axis=0) for f in range(frames)], axis=0
    )
    gated = (cotangent[0].astype(jnp.float32) * gain[:, None, :]).astype(jnp.bfloat16)
    gathered = lax.all_gather(gated, "head", axis=0, tiled=False)

    def exchange(array):
        split = jnp.stack([array[0, :, :, j * width : (j + 1) * width] for j in range(parts)])
        return lax.all_to_all(split, "head", split_axis=0, concat_axis=0, tiled=True)

    o, k, v, q = exchange(saved_out), exchange(key_rows), exchange(value_rows), exchange(queries)
    kp, kn = shifted(k[:, frames - 1], "frame", 1), shifted(k[:, 0], "frame", -1)
    vp, vn = shifted(v[:, frames - 1], "frame", 1), shifted(v[:, 0], "frame", -1)

    gated_rows = gathered.reshape(parts * frames * rows, model)
    d = dot(gated_rows, out_weight, NT).astype(jnp.bfloat16).reshape(parts, frames, rows, width)
    grad_t = dot(gated_rows, o.reshape(parts * frames * rows, width), TN)
    grad_t = (grad_t / tokens_all).astype(jnp.bfloat16)
    d_weight = lax.psum_scatter(
        grad_t, ("frame", "fsdp"), scatter_dimension=0, tiled=True
    ).T.astype(jnp.float32)

    ids = first_frame + jnp.arange(frames, dtype=jnp.int32)
    chosen = lax.dynamic_slice_in_dim(reach_flags, first_frame, frames, axis=0)
    inside = jnp.stack([ids > 0, ids < frames_all - 1], axis=1)
    limits = jnp.where(inside, jnp.where(chosen == 1, tokens, tokens // 2), 0).astype(jnp.int32)

    d_queries, dk, dv, dkp, dkn, dvp, dvn = attention(limits, q, k, v, o, d, kp, kn, vp, vn)

    def combine(own, to_prev, to_next):
        from_next = shifted(to_prev, "frame", -1)
        from_prev = shifted(to_next, "frame", 1)
        terms = [own[f] for f in range(frames)]
        terms[0] = terms[0] + from_prev.astype(jnp.float32)
        terms[frames - 1] = terms[frames - 1] + from_next.astype(jnp.float32)
        return jnp.stack(terms).astype(jnp.bfloat16)[None]

    return d_queries[None], combine(dk, dkp, dkn), combine(dv, dvp, dvn), d_weight


def solution(mesh):
    rows = P("fsdp", "frame", "head", None)
    heads = P("fsdp", "frame", None, "head")
    in_specs = (rows, rows, rows, rows, rows, P("head", None), P(), P("frame"), P())
    out_specs = (heads, heads, heads, P("head", ("frame", "fsdp")))
    return jax.shard_map(
        per_device, mesh=mesh, in_specs=in_specs, out_specs=out_specs, check_vma=False
    )
```

profile of v0, /device:TPU:11, one launch (start us, length us, event | category | flops | bytes accessed | tf_op | source)
XLA Modules:
  0.0 323.2 jit_solution(4865376110554907965)
XLA Ops:
  7.2 0.0 all-gather.2.cloned.1.call-start
  7.2 1.3 fusion.15
  12.4 1.0 constant_dynamic-slice_fusion.1
  13.5 2.6 multiply_convert_fusion
  16.1 0.0 reduce-scatter.2.cloned.1.call-start
  16.2 1.2 copy-done.5
  17.4 0.1 fusion.11
  17.5 0.2 pad_maximum_fusion.3
  17.7 61.6 %all_to_all.20.o_ref = bf16[4,2,64,1280]{3,2,1,0:T(8,128)(2,1)S(1)} all-to-all(bf16[4,2,64,1280]{3,2,1,0:T(8,128)(2,1)S(1)} %pad_maximum_fusion.3), channel_id=1, replica_groups=mesh['frame'=4,'head'=4,'fsdp'=2] {'head'}, dimensions={0} | all-to-all | bytes 2621440 | tf_op jit(solution)/shard_map/all_to_all | solution.py:138
  79.3 56.3 %all-gather.2.cloned.1.call-done = bf16[4,2,64,5120]{3,2,1,0:T(8,128)(2,1)} async-done(((bf16[1,2,64,5120]{3,2,1,0:T(8,128)(2,1)}), bf16[4,2,64,5120]{3,2,1,0:T(8,128)(2,1)}) %all-gather.2.cloned.1.call-update) | async-done | bytes 5242896 | tf_op jit(solution)/shard_map/all_gather | solution.py:134
  135.6 14.0 %fusion = bf16[5120,1280]{1,0:T(8,128)(2,1)} fusion(bf16[4,2,64,5120]{3,2,1,0:T(8,128)(2,1)} %all-gather.2.cloned.1.call-done, bf16[4,2,64,1280]{3,2,1,0:T(8,128)(2,1)S(1)} %all_to_all.20.o_ref), kind=kOutput, calls=%fused_computation.1 | convolution fusion | flops 6723993600 | bytes 19660800 | tf_op jit(solution)/shard_map/dot_general | solution.py:18
  149.6 1.3 copy-done.6
  150.9 0.1 fusion.12
  151.0 1.2 pad_maximum_fusion.2
  152.2 7.0 %all-to-all-start.2 = ((bf16[4,2,64,1280]{3,2,1,0:T(8,128)(2,1)}), bf16[4,2,64,1280]{3,2,1,0:T(8,128)(2,1)S(1)}, u32[]{:S(2)}, u32[]{:S(2)}) async-start(bf16[4,2,64,1280]{3,2,1,0:T(8,128)(2,1)} %pad_maximum_fusion.2), calls=%async_computation.2 | async-start | bytes 2621440 | tf_op jit(solution)/shard_map/all_to_all | solution.py:138
  159.2 0.1 fusion.13
  159.3 1.2 pad_maximum_fusion.1
  160.5 26.7 %all-to-all-done.2.v_ref = bf16[4,2,64,1280]{3,2,1,0:T(8,128)(2,1)S(1)} async-done(((bf16[4,2,64,1280]{3,2,1,0:T(8,128)(2,1)}), bf16[4,2,64,1280]{3,2,1,0:T(8,128)(2,1)S(1)}, u32[]{:S(2)}, u32[]{:S(2)}) %all-to-all-start.2) | async-done | bytes 1310752 | tf_op jit(solution)/shard_map/all_to_all | solution.py:138
  187.2 6.5 %all-to-all-start.1 = ((bf16[4,2,64,1280]{3,2,1,0:T(8,128)(2,1)}), bf16[4,2,64,1280]{3,2,1,0:T(8,128)(2,1)S(1)}, u32[]{:S(2)}, u32[]{:S(2)}) async-start(bf16[4,2,64,1280]{3,2,1,0:T(8,128)(2,1)} %pad_maximum_fusion.1), calls=%async_computation.1 | async-start | bytes 2621440 | tf_op jit(solution)/shard_map/all_to_all | solution.py:138
  193.7 0.1 constant_dynamic-slice_fusion.2
  193.8 0.1 copy.32
  193.9 0.1 add_select_fusion.limits
  194.0 1.4 fusion.14
  195.4 1.2 pad_maximum_fusion
  196.6 1.0 slice_bitcast_fusion
  197.5 3.5 %collective-permute-start.3 = (bf16[4,64,1280]{2,1,0:T(8,128)(2,1)}, bf16[4,64,1280]{2,1,0:T(8,128)(2,1)S(1)}, u32[]{:S(2)}, u32[]{:S(2)}) collective-permute-start(bf16[4,64,1280]{2,1,0:T(8,128)(2,1)} %get-tuple-element.30), channel_id=1, source_target_pairs={{8,0},{16,8},{24,16},{9,1},{17,9},{25,17},{10,2},{18,10},{26,18},{... | collective-permute-start | bytes 1966088 | tf_op jit(solution)/shard_map/ppermute | solution.py:116
  201.0 3.1 collective-permute-start.2
  204.1 16.7 %all-to-all-done.1.k_ref = bf16[4,2,64,1280]{3,2,1,0:T(8,128)(2,1)S(1)} async-done(((bf16[4,2,64,1280]{3,2,1,0:T(8,128)(2,1)}), bf16[4,2,64,1280]{3,2,1,0:T(8,128)(2,1)S(1)}, u32[]{:S(2)}, u32[]{:S(2)}) %all-to-all-start.1) | async-done | bytes 1310752 | tf_op jit(solution)/shard_map/all_to_all | solution.py:138
  220.8 8.0 %all-to-all-start = ((bf16[4,2,64,1280]{3,2,1,0:T(8,128)(2,1)}), bf16[4,2,64,1280]{3,2,1,0:T(8,128)(2,1)}, u32[]{:S(2)}, u32[]{:S(2)}) async-start(bf16[4,2,64,1280]{3,2,1,0:T(8,128)(2,1)} %pad_maximum_fusion), calls=%async_computation | async-start | bytes 2621440 | tf_op jit(solution)/shard_map/all_to_all | solution.py:138
  228.8 1.1 slice_bitcast_fusion.2
  230.0 3.6 %collective-permute-start.1 = (bf16[4,64,1280]{2,1,0:T(8,128)(2,1)}, bf16[4,64,1280]{2,1,0:T(8,128)(2,1)S(1)}, u32[]{:S(2)}, u32[]{:S(2)}) collective-permute-start(bf16[4,64,1280]{2,1,0:T(8,128)(2,1)} %get-tuple-element.32), channel_id=1, source_target_pairs={{8,0},{16,8},{24,16},{9,1},{17,9},{25,17},{10,2},{18,10},{26,18},{... | collective-permute-start | bytes 1966088 | tf_op jit(solution)/shard_map/ppermute | solution.py:116
  233.6 3.3 %collective-permute-start = (bf16[4,64,1280]{2,1,0:T(8,128)(2,1)}, bf16[4,64,1280]{2,1,0:T(8,128)(2,1)S(1)}, u32[]{:S(2)}, u32[]{:S(2)}) collective-permute-start(bf16[4,64,1280]{2,1,0:T(8,128)(2,1)} %get-tuple-element.33), channel_id=1, source_target_pairs={{0,8},{8,16},{16,24},{1,9},{9,17},{17,25},{2,10},{10,18},{18,26},{... | collective-permute-start | bytes 1966088 | tf_op jit(solution)/shard_map/ppermute | solution.py:116
  236.9 13.8 %convolution_convert_fusion = bf16[512,1280]{1,0:T(8,128)(2,1)} fusion(bf16[512,5120]{1,0:T(8,128)(2,1)} %bitcast.65, bf16[1280,5120]{1,0:T(8,128)(2,1)} %param.14), kind=kOutput, calls=%fused_computation.3 | convolution fusion | flops 6711541760 | bytes 19660800 | tf_op jit(solution)/shard_map/dot_general | solution.py:18
  250.7 5.1 %all-to-all-done.q_ref = bf16[4,2,64,1280]{3,2,1,0:T(8,128)(2,1)} async-done(((bf16[4,2,64,1280]{3,2,1,0:T(8,128)(2,1)}), bf16[4,2,64,1280]{3,2,1,0:T(8,128)(2,1)}, u32[]{:S(2)}, u32[]{:S(2)}) %all-to-all-start) | async-done | bytes 1310752 | tf_op jit(solution)/shard_map/all_to_all | solution.py:138
  255.8 1.8 collective-permute-done.1.kn_ref
  257.6 29.5 %attention_backward.1 = (bf16[2,256,1280]{2,1,0:T(8,128)(2,1)}, f32[2,256,1280]{2,1,0:T(8,128)}, f32[2,256,1280]{2,1,0:T(8,128)}, bf16[256,1280]{1,0:T(8,128)(2,...) custom-call(s32[2,2]{1,0:T(2,128)S(1)} %add_select_fusion.limits, ...), custom_call_target="tpu_custom_call" | custom-call | flops 5033164800 | bytes 20971520 | tf_op jit(solution)/shard_map/attention_backward/pallas_call | solution.py:89
  287.1 4.0 %collective-permute-start.4 = (bf16[256,1280]{1,0:T(8,128)(2,1)S(1)}, bf16[256,1280]{1,0:T(8,128)(2,1)S(1)}, u32[]{:S(2)}, u32[]{:S(2)}) collective-permute-start(bf16[256,1280]{1,0:T(8,128)(2,1)S(1)} %get-tuple-element.13), channel_id=1, source_target_pairs={{0,8},{8,16},{16,24},{1,9},{9,17},{17,25},{2,10},{10,18},{18,26},{... | collective-permute-start | bytes 1966088 | tf_op jit(solution)/shard_map/ppermute | solution.py:116
  291.2 1.9 collective-permute-start.5
  293.1 3.6 %collective-permute-start.6 = (bf16[256,1280]{1,0:T(8,128)(2,1)S(1)}, bf16[256,1280]{1,0:T(8,128)(2,1)S(1)}, u32[]{:S(2)}, u32[]{:S(2)}) collective-permute-start(bf16[256,1280]{1,0:T(8,128)(2,1)S(1)} %get-tuple-element.16), channel_id=1, source_target_pairs={{0,8},{8,16},{16,24},{1,9},{9,17},{17,25},{2,10},{10,18},{18,26},{... | collective-permute-start | bytes 1966088 | tf_op jit(solution)/shard_map/ppermute | solution.py:116
  296.7 1.9 collective-permute-start.7
  298.7 4.4 %collective-permute-done.5 = bf16[256,1280]{1,0:T(8,128)(2,1)S(1)} collective-permute-done((bf16[256,1280]{1,0:T(8,128)(2,1)S(1)}, bf16[256,1280]{1,0:T(8,128)(2,1)S(1)}, u32[]{:S(2)}, u32[]{:S(2)}) %collective-permute-start.5) | collective-permute-done | bytes 655392 | tf_op jit(solution)/shard_map/ppermute | solution.py:116
  303.1 2.0 fusion.5
  305.1 1.2 pad_maximum_fusion.4
  306.3 3.8 %collective-permute-done.7 = bf16[256,1280]{1,0:T(8,128)(2,1)S(1)} collective-permute-done((bf16[256,1280]{1,0:T(8,128)(2,1)S(1)}, bf16[256,1280]{1,0:T(8,128)(2,1)S(1)}, u32[]{:S(2)}, u32[]{:S(2)}) %collective-permute-start.7) | collective-permute-done | bytes 655392 | tf_op jit(solution)/shard_map/ppermute | solution.py:116
  310.1 0.3 fusion.7
  310.4 1.2 pad_maximum_fusion.5
  311.5 1.7 convert_bitcast_fusion
  313.2 3.1 copy.30
  (26 shorter events, 0.1 us)
Async XLA Ops:
  7.2 186.6 %copy-start = (s32[8,2]{0,1:T(2,128)S(1)}, s32[8,2]{0,1:T(2,128)}, u32[]{:S(2)}) copy-start(s32[8,2]{0,1:T(2,128)} %param.17) | copy-start | bytes 196
  7.2 128.4 %all-gather.2.cloned.1.call-start = ((), (), s32[]{:S(2)}) async-start(), calls=%async_computation.5 | async-start | bytes 6553600 | tf_op jit(solution)/shard_map/all_gather | solution.py:134
  16.1 1.3 copy-start.5
  16.1 295.4 %reduce-scatter.2.cloned.1.call-start = ((), (), s32[]{:S(2)}) async-start(), calls=%async_computation.6 | async-start | bytes 14745600 | tf_op jit(solution)/shard_map/reduce_scatter | solution.py:148
  79.3 70.3 %copy-start.8 = (bf16[4,2,64,1280]{3,2,1,0:T(8,128)(2,1)}, bf16[4,2,64,1280]{3,2,1,0:T(8,128)(2,1)S(1)}, u32[]{:S(2)}) copy-start(bf16[4,2,64,1280]{3,2,1,0:T(8,128)(2,1)S(1)} %all_to_all.20.o_ref) | copy-start | bytes 3932164
  149.6 1.3 copy-start.6
  152.2 7.0 %copy-start.7 = (bf16[1,2,64,5120]{3,2,1,0:T(8,128)(2,1)S(1)}, bf16[1,2,64,5120]{3,2,1,0:T(8,128)(2,1)}, u32[]{:S(2)}) copy-start(bf16[1,2,64,5120]{3,2,1,0:T(8,128)(2,1)} %param.10) | copy-start | bytes 3932164
  152.2 35.0 %all-to-all-start.2 = ((bf16[4,2,64,1280]{3,2,1,0:T(8,128)(2,1)}), bf16[4,2,64,1280]{3,2,1,0:T(8,128)(2,1)S(1)}, u32[]{:S(2)}, u32[]{:S(2)}) async-start(bf16[4,2,64,1280]{3,2,1,0:T(8,128)(2,1)} %pad_maximum_fusion.2), calls=%async_computation.2 | async-start | bytes 2621440 | tf_op jit(solution)/shard_map/all_to_all | solution.py:138
  187.2 9.4 %copy-start.2 = (bf16[4,2,64,1280]{3,2,1,0:T(8,128)(2,1)}, bf16[4,2,64,1280]{3,2,1,0:T(8,128)(2,1)S(1)}, u32[]{:S(2)}) copy-start(bf16[4,2,64,1280]{3,2,1,0:T(8,128)(2,1)S(1)} %all-to-all-done.2.v_ref) | copy-start | bytes 3932164
  187.2 33.6 %all-to-all-start.1 = ((bf16[4,2,64,1280]{3,2,1,0:T(8,128)(2,1)}), bf16[4,2,64,1280]{3,2,1,0:T(8,128)(2,1)S(1)}, u32[]{:S(2)}, u32[]{:S(2)}) async-start(bf16[4,2,64,1280]{3,2,1,0:T(8,128)(2,1)} %pad_maximum_fusion.1), calls=%async_computation.1 | async-start | bytes 2621440 | tf_op jit(solution)/shard_map/all_to_all | solution.py:138
  197.5 58.2 %collective-permute-start.3 = (bf16[4,64,1280]{2,1,0:T(8,128)(2,1)}, bf16[4,64,1280]{2,1,0:T(8,128)(2,1)S(1)}, u32[]{:S(2)}, u32[]{:S(2)}) collective-permute-start(bf16[4,64,1280]{2,1,0:T(8,128)(2,1)} %get-tuple-element.30), channel_id=1, source_target_pairs={{8,0},{16,8},{24,16},{9,1},{17,9},{25,17},{10,2},{18,10},{26,18},{... | collective-permute-start | bytes 1966088 | tf_op jit(solution)/shard_map/ppermute | solution.py:116
  201.0 54.8 %collective-permute-start.2 = (bf16[4,64,1280]{2,1,0:T(8,128)(2,1)S(1)}, bf16[4,64,1280]{2,1,0:T(8,128)(2,1)S(1)}, u32[]{:S(2)}, u32[]{:S(2)}) collective-permute-start(bf16[4,64,1280]{2,1,0:T(8,128)(2,1)S(1)} %get-tuple-element.31), channel_id=1, source_target_pairs={{0,8},{8,16},{16,24},{1,9},{9,17},{17,25},{2,10},{10,18},{18,26},{... | collective-permute-start | bytes 1966088 | tf_op jit(solution)/shard_map/ppermute | solution.py:116
  220.8 8.0 %copy-start.3 = (bf16[4,2,64,1280]{3,2,1,0:T(8,128)(2,1)}, bf16[4,2,64,1280]{3,2,1,0:T(8,128)(2,1)S(1)}, u32[]{:S(2)}) copy-start(bf16[4,2,64,1280]{3,2,1,0:T(8,128)(2,1)S(1)} %all-to-all-done.1.k_ref) | copy-start | bytes 3932164
  220.8 34.9 %all-to-all-start = ((bf16[4,2,64,1280]{3,2,1,0:T(8,128)(2,1)}), bf16[4,2,64,1280]{3,2,1,0:T(8,128)(2,1)}, u32[]{:S(2)}, u32[]{:S(2)}) async-start(bf16[4,2,64,1280]{3,2,1,0:T(8,128)(2,1)} %pad_maximum_fusion), calls=%async_computation | async-start | bytes 2621440 | tf_op jit(solution)/shard_map/all_to_all | solution.py:138
  230.0 27.7 %collective-permute-start.1 = (bf16[4,64,1280]{2,1,0:T(8,128)(2,1)}, bf16[4,64,1280]{2,1,0:T(8,128)(2,1)S(1)}, u32[]{:S(2)}, u32[]{:S(2)}) collective-permute-start(bf16[4,64,1280]{2,1,0:T(8,128)(2,1)} %get-tuple-element.32), channel_id=1, source_target_pairs={{8,0},{16,8},{24,16},{9,1},{17,9},{25,17},{10,2},{18,10},{26,18},{... | collective-permute-start | bytes 1966088 | tf_op jit(solution)/shard_map/ppermute | solution.py:116
  233.6 24.0 %collective-permute-start = (bf16[4,64,1280]{2,1,0:T(8,128)(2,1)}, bf16[4,64,1280]{2,1,0:T(8,128)(2,1)S(1)}, u32[]{:S(2)}, u32[]{:S(2)}) collective-permute-start(bf16[4,64,1280]{2,1,0:T(8,128)(2,1)} %get-tuple-element.33), channel_id=1, source_target_pairs={{0,8},{8,16},{16,24},{1,9},{9,17},{17,25},{2,10},{10,18},{18,26},{... | collective-permute-start | bytes 1966088 | tf_op jit(solution)/shard_map/ppermute | solution.py:116
  287.1 11.5 %collective-permute-start.4 = (bf16[256,1280]{1,0:T(8,128)(2,1)S(1)}, bf16[256,1280]{1,0:T(8,128)(2,1)S(1)}, u32[]{:S(2)}, u32[]{:S(2)}) collective-permute-start(bf16[256,1280]{1,0:T(8,128)(2,1)S(1)} %get-tuple-element.13), channel_id=1, source_target_pairs={{0,8},{8,16},{16,24},{1,9},{9,17},{17,25},{2,10},{10,18},{18,26},{... | collective-permute-start | bytes 1966088 | tf_op jit(solution)/shard_map/ppermute | solution.py:116
  291.2 11.9 %collective-permute-start.5 = (bf16[256,1280]{1,0:T(8,128)(2,1)S(1)}, bf16[256,1280]{1,0:T(8,128)(2,1)S(1)}, u32[]{:S(2)}, u32[]{:S(2)}) collective-permute-start(bf16[256,1280]{1,0:T(8,128)(2,1)S(1)} %get-tuple-element.14), channel_id=1, source_target_pairs={{8,0},{16,8},{24,16},{9,1},{17,9},{25,17},{10,2},{18,10},{26,18},{... | collective-permute-start | bytes 1966088 | tf_op jit(solution)/shard_map/ppermute | solution.py:116
  293.1 13.2 %collective-permute-start.6 = (bf16[256,1280]{1,0:T(8,128)(2,1)S(1)}, bf16[256,1280]{1,0:T(8,128)(2,1)S(1)}, u32[]{:S(2)}, u32[]{:S(2)}) collective-permute-start(bf16[256,1280]{1,0:T(8,128)(2,1)S(1)} %get-tuple-element.16), channel_id=1, source_target_pairs={{0,8},{8,16},{16,24},{1,9},{9,17},{17,25},{2,10},{10,18},{18,26},{... | collective-permute-start | bytes 1966088 | tf_op jit(solution)/shard_map/ppermute | solution.py:116
  296.7 13.3 %collective-permute-start.7 = (bf16[256,1280]{1,0:T(8,128)(2,1)S(1)}, bf16[256,1280]{1,0:T(8,128)(2,1)S(1)}, u32[]{:S(2)}, u32[]{:S(2)}) collective-permute-start(bf16[256,1280]{1,0:T(8,128)(2,1)S(1)} %get-tuple-element.17), channel_id=1, source_target_pairs={{8,0},{16,8},{24,16},{9,1},{17,9},{25,17},{10,2},{18,10},{26,18},{... | collective-permute-start | bytes 1966088 | tf_op jit(solution)/shard_map/ppermute | solution.py:116
  305.1 5.0 %copy-start.4 = (f32[2,256,1280]{2,1,0:T(8,128)S(1)}, f32[2,256,1280]{2,1,0:T(8,128)}, u32[]{:S(2)}) copy-start(f32[2,256,1280]{2,1,0:T(8,128)} %get-tuple-element.15) | copy-start | bytes 7864324
  313.2 3.1 copy-start.1
Sparse Core Ops, SparseCore 0:
  16.3 119.2 all-gather.1
  149.7 110.8 reduce-scatter.1
where the time goes:
time: 327 us; the launch traced here: 323 us
  waiting for transfers between devices  115 us (35%)
  blocking collectives  61.6 us (19%)
  starting transfers between devices  46.5 us (14%)
  Pallas kernels  29.5 us (9%)
  matrix products  27.8 us (9%)
  between operations  18.1 us (6%)
  other arithmetic  12.9 us (4%)
  local copies, waits for them, and re-layouts  11.9 us (4%)
    all_to_all x1, blocking collectives, exchange(): lax.all_to_all(split, 'head', split_axis=0, concat_axis=0, tiled=True)  61.6 us
    all_gather x1, waiting for transfers between devices, per_device(): gathered = lax.all_gather(gated, 'head', axis=0, tiled=False)  56.3 us
    all_to_all x3, waiting for transfers between devices, exchange(): lax.all_to_all(split, 'head', split_axis=0, concat_axis=0, tiled=True)  48.5 us
    pallas_call x1, Pallas kernels, attention(): pl.pallas_call(attention_kernel, grid_spec=pltpu.PrefetchScalarGridSpec(n...  29.5 us
    dot_general x2, matrix products, dot(): return lax.dot_general(lhs, rhs, dims, preferred_element_type=jnp.float32)  27.8 us
    ppermute x8, starting transfers between devices, shifted(): return lax.ppermute(array, axis, pairs)  25 us
    all_to_all x3, starting transfers between devices, exchange(): lax.all_to_all(split, 'head', split_axis=0, concat_axis=0, tiled=True)  21.5 us
    ppermute x8, waiting for transfers between devices, shifted(): return lax.ppermute(array, axis, pairs)  10 us
  transfers between devices with their start and end apart: 13, of which 7 were waited for; matrix products, arithmetic and copies ran while one was open for 8% of the time, Pallas kernels for 9%

commit v1 on v0

v1 whole, which is shorter than its diff:
```python
from functools import partial

import jax
import jax.numpy as jnp
from jax import lax
from jax.experimental import pallas as pl
from jax.experimental.pallas import tpu as pltpu
from jax.sharding import PartitionSpec as P

HD = 128
NEG = -1e30
NT = (((1,), (1,)), ((), ()))
NN = (((1,), (0,)), ((), ()))
TN = (((0,), (0,)), ((), ()))


def dot(lhs, rhs, dims):
    return lax.dot_general(lhs, rhs, dims, preferred_element_type=jnp.float32)


def attention_kernel(parts, scal, *refs):
    own_q, own_k, own_v, own_o = refs[:4]
    packs = refs[4 : 4 + parts - 1]
    o_refs = refs[3 + parts : 2 + 2 * parts]
    d_ref, prev_ref, next_ref = refs[2 + 2 * parts : 5 + 2 * parts]
    dq_ref, dk_ref, dv_ref, to_prev_ref, to_next_ref = refs[5 + 2 * parts : 10 + 2 * parts]
    q_all, k_all, v_all, o_all, d_all = refs[10 + 2 * parts :]
    _, frames, rows, _ = own_q.shape
    me = scal[0]
    inv_root = HD ** (-0.5)
    for s in range(parts):
        source = lax.rem(me + parts - s, parts)
        at = pl.ds(pl.multiple_of(source * rows, rows), rows)
        for f in range(frames):
            q_all[f, at] = own_q[0, f] if s == 0 else packs[s - 1][2, f]
            k_all[f + 1, at] = own_k[0, f] if s == 0 else packs[s - 1][0, f]
            v_all[f + 1, at] = own_v[0, f] if s == 0 else packs[s - 1][1, f]
            o_all[f, at] = own_o[0, f] if s == 0 else o_refs[s - 1][f]
            d_all[f, at] = d_ref[s, f]
        k_all[0, at] = prev_ref[0, s]
        v_all[0, at] = prev_ref[1, s]
        k_all[frames + 1, at] = next_ref[0, s]
        v_all[frames + 1, at] = next_ref[1, s]
    tokens = rows * parts
    row = lax.broadcasted_iota(jnp.int32, (tokens, tokens), 0)
    key_grads = [None] * (frames + 2)
    value_grads = [None] * (frames + 2)

    def put(grads, slot, term):
        grads[slot] = term if grads[slot] is None else grads[slot] + term

    for f in range(frames):
        q, d = q_all[f], d_all[f]
        prod = d.astype(jnp.float32) * o_all[f].astype(jnp.float32)
        delta = lax.dot_general(
            jnp.ones((8, HD), jnp.float32), prod, NT,
            precision=lax.Precision.HIGHEST, preferred_element_type=jnp.float32,
        )[0:1]
        scores = []
        for w in range(3):
            s = dot(k_all[f + w], q, NT) * inv_root
            if w != 1:
                s = jnp.where(row < scal[2 + 2 * f + w // 2], s, NEG)
            scores.append(s)
        top = jnp.max(jnp.maximum(jnp.maximum(scores[0], scores[1]), scores[2]), axis=0, keepdims=True)
        exps = [jnp.exp(s - top) for s in scores]
        total = jnp.sum(exps[0] + exps[1] + exps[2], axis=0, keepdims=True)
        inv_total = 1.0 / total
        dq = None
        for w in range(3):
            prob = exps[w] * inv_total
            put(value_grads, f + w, dot(prob.astype(jnp.bfloat16), d, NN))
            d_prob = dot(v_all[f + w], d, NT)
            d_score = (prob * (d_prob - delta)).astype(jnp.bfloat16)
            put(key_grads, f + w, dot(d_score, q, NN))
            term = dot(d_score, k_all[f + w], TN)
            dq = term if dq is None else dq + term
        dq_ref[f] = (dq * inv_root).astype(jnp.bfloat16)
    for f in range(frames):
        dk_ref[f] = key_grads[f + 1] * inv_root
        dv_ref[f] = value_grads[f + 1]
    to_prev_ref[0] = (key_grads[0] * inv_root).astype(jnp.bfloat16)
    to_prev_ref[1] = value_grads[0].astype(jnp.bfloat16)
    to_next_ref[0] = (key_grads[frames + 1] * inv_root).astype(jnp.bfloat16)
    to_next_ref[1] = value_grads[frames + 1].astype(jnp.bfloat16)


def attention(scal, head0, heads, local, packs, o_pieces, d, from_prev, from_next):
    parts = len(packs) + 1
    _, frames, rows, _ = local[0].shape
    tokens, width = parts * rows, heads * HD
    own = pl.BlockSpec((1, frames, rows, HD), lambda h, sc: (0, 0, 0, sc[1] + head0 + h))
    pack = pl.BlockSpec((3, frames, rows, HD), lambda h, sc: (0, 0, 0, h))
    piece = pl.BlockSpec((frames, rows, HD), lambda h, sc: (0, 0, head0 + h))
    dsp = pl.BlockSpec((parts, frames, rows, HD), lambda h, sc: (0, 0, 0, head0 + h))
    halo = pl.BlockSpec((2, parts, rows, HD), lambda h, sc: (0, 0, 0, h))
    out = pl.BlockSpec((frames, tokens, HD), lambda h, sc: (0, 0, h))
    edge = pl.BlockSpec((2, tokens, HD), lambda h, sc: (0, 0, h))
    full_shape, edge_shape = (frames, tokens, width), (2, tokens, width)
    pads = pltpu.VMEM((frames + 2, tokens, HD), jnp.bfloat16)
    flats = pltpu.VMEM((frames, tokens, HD), jnp.bfloat16)
    return pl.pallas_call(
        partial(attention_kernel, parts),
        grid_spec=pltpu.PrefetchScalarGridSpec(
            num_scalar_prefetch=1,
            grid=(heads,),
            in_specs=[own] * 4 + [pack] * (parts - 1) + [piece] * (parts - 1) + [dsp, halo, halo],
            out_specs=[out] * 3 + [edge] * 2,
            scratch_shapes=[flats, pads, pads, flats, flats],
        ),
        out_shape=[
            jax.ShapeDtypeStruct(full_shape, jnp.bfloat16),
            jax.ShapeDtypeStruct(full_shape, jnp.float32),
            jax.ShapeDtypeStruct(full_shape, jnp.float32),
            jax.ShapeDtypeStruct(edge_shape, jnp.bfloat16),
            jax.ShapeDtypeStruct(edge_shape, jnp.bfloat16),
        ],
        compiler_params=pltpu.CompilerParams(vmem_limit_bytes=40 * 2**20),
        cost_estimate=pl.CostEstimate(
            flops=heads * frames * 3 * tokens * tokens * HD * 10,
            bytes_accessed=heads * HD * tokens * frames * 2 * 16,
            transcendentals=heads * frames * 3 * tokens * tokens,
        ),
        name="attention_backward",
    )(scal, *local, *packs, *o_pieces, d, from_prev, from_next)


def shifted(array, axis, step):
    count = lax.axis_size(axis)
    pairs = [(i, i + step) for i in range(count) if 0 <= i + step < count]
    return lax.ppermute(array, axis, pairs)


def rotated(array, axis, step):
    count = lax.axis_size(axis)
    return lax.ppermute(array, axis, [(i, (i + step) % count) for i in range(count)])


def after(array, event):
    return lax.optimization_barrier((array, event))


def line_step(right, left, axis, step):
    count = lax.axis_size(axis)
    right = lax.ppermute(right, axis, [(i, i + 1) for i in range(step - 1, count - 1)])
    left = lax.ppermute(left, axis, [(i, i - 1) for i in range(1, count - step + 1)])
    return right, left


def line_pieces(own, rights, lefts, axis):
    count, me = lax.axis_size(axis), lax.axis_index(axis)
    return [own] + [
        jnp.where(me >= r, rights[r - 1], lefts[count - r - 1]) for r in range(1, count)
    ]


def per_device(
    queries, key_rows, value_rows, saved_out, cotangent, out_weight, gate_table, levels, reach_flags
):
    _, frames, rows, model = queries.shape
    parts = lax.axis_size("head")
    me = lax.axis_index("head")
    width = model // parts
    heads = width // HD
    frames_all = frames * lax.axis_size("frame")
    tokens = rows * parts
    first_frame = lax.axis_index("frame") * frames
    tokens_all = lax.axis_size("fsdp") * frames_all * tokens
    blocks = lax.axis_size("frame") * lax.axis_size("fsdp")
    block = model // blocks
    cut = (block // 2) // 128 * 128 or block // 2

    def columns_for(array, step, start, size):
        target = lax.rem(me + step, parts)
        return lax.dynamic_slice_in_dim(array[0], target * width + start, size, axis=2)

    o_pieces = [
        rotated(columns_for(saved_out, s, 0, width), "head", s) for s in range(1, parts)
    ]

    gain = jnp.concatenate(
        [lax.dynamic_slice_in_dim(gate_table, levels[f], 1, axis=0) for f in range(frames)], axis=0
    )
    gated = (cotangent[0].astype(jnp.float32) * gain[:, None, :]).astype(jnp.bfloat16)
    gated = gated.reshape(frames * rows, model)
    rest = block - cut
    chunk0 = jnp.concatenate([gated[:, b * block :][:, :cut] for b in range(blocks)], axis=1)
    chunk1 = jnp.concatenate([gated[:, b * block + cut :][:, :rest] for b in range(blocks)], axis=1)

    rights, lefts = [[], []], [[], []]
    right, left = chunk0, chunk0
    for step in range(1, parts):
        right, left = line_step(right, left, "head", step)
        if step == 1:
            chunk1, right = after(chunk1, right)
        rights[0].append(right)
        lefts[0].append(left)
    right, left = chunk1, chunk1
    for step in range(1, parts):
        right, left = line_step(right, left, "head", step)
        rights[1].append(right)
        lefts[1].append(left)

    def weight_chunk(pieces, o_rows):
        rows_c = jnp.concatenate(pieces, axis=0)
        grad = dot(rows_c, o_rows, TN)
        grad = (grad / tokens_all).astype(jnp.bfloat16)
        return rows_c, lax.psum_scatter(grad, ("frame", "fsdp"), scatter_dimension=0, tiled=True)

    own_o = columns_for(saved_out, 0, 0, width)
    o_rows = jnp.concatenate(
        [piece.reshape(frames * rows, width) for piece in [own_o] + o_pieces], axis=0
    )
    rows0, grad0 = weight_chunk(line_pieces(chunk0, rights[0], lefts[0], "head"), o_rows)
    rows1, grad1 = weight_chunk(line_pieces(chunk1, rights[1], lefts[1], "head"), o_rows)
    d_weight = jnp.concatenate([grad0, grad1], axis=0).T.astype(jnp.float32)

    columns = []
    for b in range(blocks):
        columns += [rows0[:, b * cut : (b + 1) * cut], rows1[:, b * rest : (b + 1) * rest]]
    gated_rows = jnp.concatenate(columns, axis=1)
    d = dot(gated_rows, out_weight, NT).astype(jnp.bfloat16).reshape(parts, frames, rows, width)

    ids = first_frame + jnp.arange(frames, dtype=jnp.int32)
    chosen = lax.dynamic_slice_in_dim(reach_flags, first_frame, frames, axis=0)
    inside = jnp.stack([ids > 0, ids < frames_all - 1], axis=1)
    limits = jnp.where(inside, jnp.where(chosen == 1, tokens, tokens // 2), 0).astype(jnp.int32)
    scal = jnp.concatenate([jnp.stack([me, me * heads]).astype(jnp.int32), limits.reshape(-1)])

    first = (heads + 1) // 2
    groups = [(0, first), (first, heads - first)]
    results = []
    for g, (head0, count) in enumerate(groups):
        start, size = head0 * HD, count * HD

        def packed(step):
            return jnp.stack(
                [columns_for(a, step, start, size) for a in (key_rows, value_rows, queries)]
            )

        packs = [packed(s) for s in range(1, parts)]
        event = rights[g][parts - 2]
        packs, event = after(packs, event)
        rights[g][parts - 2] = event
        packs = [rotated(p, "head", s) for s, p in zip(range(1, parts), packs)]
        own = [columns_for(a, 0, start, size) for a in (key_rows, value_rows)]

        def boundary(frame):
            return jnp.stack(
                [jnp.stack([own[t][frame]] + [p[t, frame] for p in packs]) for t in range(2)]
            )

        from_prev = shifted(boundary(frames - 1), "frame", 1)
        from_next = shifted(boundary(0), "frame", -1)
        local = (queries, key_rows, value_rows, saved_out)
        dq, dk, dv, to_prev, to_next = attention(
            scal, head0, count, local, packs, o_pieces, d, from_prev, from_next
        )
        grad_next = shifted(to_prev, "frame", -1)
        grad_prev = shifted(to_next, "frame", 1)

        def combine(own_grad, t):
            terms = [own_grad[f] for f in range(frames)]
            terms[0] = terms[0] + grad_prev[t].astype(jnp.float32)
            terms[frames - 1] = terms[frames - 1] + grad_next[t].astype(jnp.float32)
            return jnp.stack(terms).astype(jnp.bfloat16)

        results.append((dq, combine(dk, 0), combine(dv, 1)))

    d_queries, d_keys, d_values = (
        jnp.concatenate([r[i] for r in results], axis=2)[None] for i in range(3)
    )
    return d_queries, d_keys, d_values, d_weight


def solution(mesh):
    rows = P("fsdp", "frame", "head", None)
    heads = P("fsdp", "frame", None, "head")
    in_specs = (rows, rows, rows, rows, rows, P("head", None), P(), P("frame"), P())
    out_specs = (heads, heads, heads, P("head", ("frame", "fsdp")))
    return jax.shard_map(
        per_device, mesh=mesh, in_specs=in_specs, out_specs=out_specs, check_vma=False
    )
```

time: 327 us -> 345 us (1.055)
  blocking collectives: 61.6 us -> 0 us
  waiting for transfers between devices: 115 us -> 149 us
  starting transfers between devices: 46.5 us -> 65.5 us
  other arithmetic: 12.9 us -> 30.8 us
  local copies, waits for them, and re-layouts: 11.9 us -> 21 us
    ppermute x0 -> x21, waiting for transfers between devices: none -> 140 us  [the longest x9 89.7 us: rotated(): lax.ppermute(array, axis, [(i, (i + step) % count) for i in range(count)])]
    all_to_all x1 -> x0, blocking collectives: 61.6 us -> none  [exchange(): lax.all_to_all(split, 'head', split_axis=0, concat_axis=0, tiled=True)]
    all_gather x1 -> x0, waiting for transfers between devices: 56.3 us -> none  [per_device(): gathered = lax.all_gather(gated, 'head', axis=0, tiled=False)]
    all_to_all x3 -> x0, waiting for transfers between devices: 48.5 us -> none  [exchange(): lax.all_to_all(split, 'head', split_axis=0, concat_axis=0, tiled=True)]
    ppermute x0 -> x21, starting transfers between devices: none -> 43.3 us  [the longest x6 17.7 us: line_step(): lax.ppermute(right, axis, [(i, i + 1) for i in range(step - 1, count - 1)])]
    all_to_all x3 -> x0, starting transfers between devices: 21.5 us -> none  [exchange(): lax.all_to_all(split, 'head', split_axis=0, concat_axis=0, tiled=True)]
    unnamed x20 -> x106, local copies, waits for them, and re-layouts: 5.8 us -> 14.3 us
    select_n x0 -> x6, other arithmetic: none -> 7.48 us  [line_pieces(): jnp.where(me >= r, rights[r - 1], lefts[count - r - 1])]
  transfers between devices with their start and end apart: 13 -> 31, of which waited for: 7 -> 16; matrix products, arithmetic and copies ran while one was open for 8% -> 17% of each run, Pallas kernels for 9% -> 9%
where the time goes in v1:
time: 345 us; the launch traced here: 344 us
  waiting for transfers between devices  149 us (43%)
  starting transfers between devices  65.5 us (19%)
  Pallas kernels  32.2 us (9%)
  other arithmetic  30.8 us (9%)
  matrix products  26.9 us (8%)
  local copies, waits for them, and re-layouts  21 us (6%)
  between operations  18.9 us (5%)
    ppermute x9, waiting for transfers between devices, rotated(): lax.ppermute(array, axis, [(i, (i + step) % count) for i in range(count)])  89.7 us
    ppermute x6, waiting for transfers between devices, line_step(): lax.ppermute(left, axis, [(i, i - 1) for i in range(1, count - step + 1)])  50.5 us
    pallas_call x2, Pallas kernels, attention(): pl.pallas_call(partial(attention_kernel, parts), grid_spec=pltpu.Prefetch...  32.2 us
    dot_general x3, matrix products, dot(): return lax.dot_general(lhs, rhs, dims, preferred_element_type=jnp.float32)  26.9 us
    ppermute x8, starting transfers between devices, shifted(): return lax.ppermute(array, axis, pairs)  22.1 us
    ppermute x6, starting transfers between devices, line_step(): lax.ppermute(right, axis, [(i, i + 1) for i in range(step - 1, count - 1)])  17.7 us
    ppermute x6, starting transfers between devices, line_step(): lax.ppermute(left, axis, [(i, i - 1) for i in range(1, count - step + 1)])  17.1 us
    unnamed x106, local copies, waits for them, and re-layouts  14.3 us
  transfers between devices with their start and end apart: 31, of which 16 were waited for; matrix products, arithmetic and copies ran while one was open for 17% of the time, Pallas kernels for 9%

profile of v1, /device:TPU:11, one launch (start us, length us, event | category | flops | bytes accessed | tf_op | source)
XLA Modules:
  0.0 344.0 jit_solution(705995797186674990)
XLA Ops:
  13.5 1.7 fusion
  15.3 3.2 collective-permute-start
  18.6 2.9 collective-permute-start.9
  25.3 7.6 %collective-permute-done.9 = bf16[128,2048]{1,0:T(8,128)(2,1)S(1)} collective-permute-done((bf16[128,2048]{1,0:T(8,128)(2,1)S(1)}, bf16[128,2048]{1,0:T(8,128)(2,1)S(1)}, u32[]{:S(2)}, u32[]{:S(2)}) %collective-permute-start.9) | collective-permute-done | bytes 524320 | tf_op jit(solution)/shard_map/ppermute | solution.py:146
  32.9 2.9 collective-permute-start.10
  37.1 4.0 %collective-permute-start.1 = (bf16[128,2048]{1,0:T(8,128)(2,1)}, bf16[128,2048]{1,0:T(8,128)(2,1)}, u32[]{:S(2)}, u32[]{:S(2)}) collective-permute-start(bf16[128,2048]{1,0:T(8,128)(2,1)} %collective-permute-done), channel_id=1, source_target_pairs={{2,4},{4,6},{3,5},{5,7},{10,12},{12,14},{11,13},{13,15},{18,20},{2... | collective-permute-start | bytes 1572872 | tf_op jit(solution)/shard_map/ppermute | solution.py:145
  41.1 5.4 %collective-permute-done.10 = bf16[128,2048]{1,0:T(8,128)(2,1)} collective-permute-done((bf16[128,2048]{1,0:T(8,128)(2,1)S(1)}, bf16[128,2048]{1,0:T(8,128)(2,1)}, u32[]{:S(2)}, u32[]{:S(2)}) %collective-permute-start.10) | collective-permute-done | bytes 524320 | tf_op jit(solution)/shard_map/ppermute | solution.py:146
  46.5 3.7 %collective-permute-start.11 = (bf16[128,2048]{1,0:T(8,128)(2,1)}, bf16[128,2048]{1,0:T(8,128)(2,1)}, u32[]{:S(2)}, u32[]{:S(2)}) collective-permute-start(bf16[128,2048]{1,0:T(8,128)(2,1)} %collective-permute-done.10), channel_id=1, source_target_pairs={{2,0},{3,1},{10,8},{11,9},{18,16},{19,17},{26,24},{27,25}} | collective-permute-start | bytes 1572872 | tf_op jit(solution)/shard_map/ppermute | solution.py:146
  54.7 13.4 %collective-permute-done.11 = bf16[128,2048]{1,0:T(8,128)(2,1)} collective-permute-done((bf16[128,2048]{1,0:T(8,128)(2,1)}, bf16[128,2048]{1,0:T(8,128)(2,1)}, u32[]{:S(2)}, u32[]{:S(2)}) %collective-permute-start.11) | collective-permute-done | bytes 524320 | tf_op jit(solution)/shard_map/ppermute | solution.py:146
  70.6 6.8 %collective-permute-done.7.refs_8_ = bf16[2,64,1280]{2,1,0:T(8,128)(2,1)S(1)} collective-permute-done((bf16[2,64,1280]{2,1,0:T(8,128)(2,1)}, bf16[2,64,1280]{2,1,0:T(8,128)(2,1)S(1)}, u32[]{:S(2)}, u32[]{:S(2)}) %collective-permute-start.7) | collective-permute-done | bytes 327712 | tf_op jit(solution)/shard_map/ppermute | solution.py:136
  77.4 4.1 %collective-permute-done.8.refs_9_ = bf16[2,64,1280]{2,1,0:T(8,128)(2,1)S(1)} collective-permute-done((bf16[2,64,1280]{2,1,0:T(8,128)(2,1)}, bf16[2,64,1280]{2,1,0:T(8,128)(2,1)S(1)}, u32[]{:S(2)}, u32[]{:S(2)}) %collective-permute-start.8) | collective-permute-done | bytes 327712 | tf_op jit(solution)/shard_map/ppermute | solution.py:136
  81.5 4.8 %multiply_convert_fusion.1 = bf16[2048,1280]{1,0:T(8,128)(2,1)} fusion(bf16[128,1280]{1,0:T(8,128)(2,1)S(1)} %bitcast.114, bf16[128,1280]{1,0:T(8,128)(2,1)S(1)} %bitcast.112, bf16[128,1280]{1,0:T(8,128)(2,1)S(1)} %bitcast.110, bf16[128,1280]{1,0:T(8,128)(2,1)S(1)} %bitcast.118, bf16[128,2048]{1,0:T(8,128)(2,1)S(1)} %broadcast_select_fusion.3, ...), kind=kOutput, calls=%fused_computation.1 | convolution fusion | flops 2703228928 | bytes 8650752 | tf_op jit(solution)/shard_map/dot_general | solution.py:18
  86.4 2.6 collective-permute-start.13
  89.0 3.8 %collective-permute-start.12 = (bf16[128,3072]{1,0:T(8,128)(2,1)}, bf16[128,3072]{1,0:T(8,128)(2,1)}, u32[]{:S(2)}, u32[]{:S(2)}) collective-permute-start(bf16[128,3072]{1,0:T(8,128)(2,1)} %slice_dynamic-update-slice_fusion.16), channel_id=1, source_target_pairs={{0,2},{2,4},{4,6},{1,3},{3,5},{5,7},{8,10},{10,12},{12,14},{9,11},... | collective-permute-start | bytes 2359304 | tf_op jit(solution)/shard_map/ppermute | solution.py:145
  95.6 11.1 %collective-permute-done.13 = bf16[128,3072]{1,0:T(8,128)(2,1)} collective-permute-done((bf16[128,3072]{1,0:T(8,128)(2,1)}, bf16[128,3072]{1,0:T(8,128)(2,1)}, u32[]{:S(2)}, u32[]{:S(2)}) %collective-permute-start.13) | collective-permute-done | bytes 786464 | tf_op jit(solution)/shard_map/ppermute | solution.py:146
  106.7 1.9 collective-permute-start.14
  109.5 5.2 %collective-permute-start.16 = (bf16[128,3072]{1,0:T(8,128)(2,1)}, bf16[128,3072]{1,0:T(8,128)(2,1)}, u32[]{:S(2)}, u32[]{:S(2)}) collective-permute-start(bf16[128,3072]{1,0:T(8,128)(2,1)} %collective-permute-done.12), channel_id=1, source_target_pairs={{2,4},{4,6},{3,5},{5,7},{10,12},{12,14},{11,13},{13,15},{18,20},{2... | collective-permute-start | bytes 2359304 | tf_op jit(solution)/shard_map/ppermute | solution.py:145
  114.8 2.0 pad_maximum_fusion.8
  116.8 1.9 pad_maximum_fusion.9
  118.7 1.9 pad_maximum_fusion.12
  122.4 2.6 collective-permute-done.14
  125.0 3.1 collective-permute-start.15
  130.3 10.4 %collective-permute-done.15 = bf16[128,3072]{1,0:T(8,128)(2,1)} collective-permute-done((bf16[128,3072]{1,0:T(8,128)(2,1)}, bf16[128,3072]{1,0:T(8,128)(2,1)}, u32[]{:S(2)}, u32[]{:S(2)}) %collective-permute-start.15) | collective-permute-done | bytes 786464 | tf_op jit(solution)/shard_map/ppermute | solution.py:146
  144.4 8.6 %multiply_convert_fusion = bf16[3072,1280]{1,0:T(8,128)(2,1)} fusion(bf16[128,1280]{1,0:T(8,128)(2,1)S(1)} %bitcast.115, bf16[128,1280]{1,0:T(8,128)(2,1)S(1)} %bitcast.113, bf16[128,1280]{1,0:T(8,128)(2,1)S(1)} %bitcast.111, bf16[128,1280]{1,0:T(8,128)(2,1)S(1)} %bitcast.119, bf16[128,3072]{1,0:T(8,128)(2,1)S(1)} %broadcast_select_fusion, ...), kind=kOutput, calls=%fused_computation | convolution fusion | flops 4052221952 | bytes 12320768 | tf_op jit(solution)/shard_map/dot_general | solution.py:18
  154.1 2.2 collective-permute-start.3
  156.3 2.1 collective-permute-start.4
  158.4 1.8 pad_maximum_fusion.1
  160.4 2.9 collective-permute-done.3.refs_4_
  163.4 30.0 %collective-permute-done.4.refs_5_ = bf16[3,2,64,640]{3,2,1,0:T(8,128)(2,1)S(1)} collective-permute-done((bf16[3,2,64,640]{3,2,1,0:T(8,128)(2,1)}, bf16[3,2,64,640]{3,2,1,0:T(8,128)(2,1)S(1)}, u32[]{:S(2)}, u32[]{:S(2)}) %collective-permute-start.4) | collective-permute-done | bytes 491552 | tf_op jit(solution)/shard_map/ppermute | solution.py:136
  193.4 7.0 %collective-permute-done.5.refs_6_ = bf16[3,2,64,640]{3,2,1,0:T(8,128)(2,1)S(1)} collective-permute-done((bf16[3,2,64,640]{3,2,1,0:T(8,128)(2,1)S(1)}, bf16[3,2,64,640]{3,2,1,0:T(8,128)(2,1)S(1)}, u32[]{:S(2)}, u32[]{:S(2)}) %collective-permute-start.5) | collective-permute-done | bytes 491552 | tf_op jit(solution)/shard_map/ppermute | solution.py:136
  201.5 3.0 collective-permute-start.19
  205.6 3.0 collective-permute-start.18
  214.1 7.3 %collective-permute-done.20.refs_4_ = bf16[3,2,64,640]{3,2,1,0:T(8,128)(2,1)S(1)} collective-permute-done((bf16[3,2,64,640]{3,2,1,0:T(8,128)(2,1)S(1)}, bf16[3,2,64,640]{3,2,1,0:T(8,128)(2,1)S(1)}, u32[]{:S(2)}, u32[]{:S(2)}) %collective-permute-start.20) | collective-permute-done | bytes 491552 | tf_op jit(solution)/shard_map/ppermute | solution.py:136
  221.4 29.6 %collective-permute-done.21.refs_5_ = bf16[3,2,64,640]{3,2,1,0:T(8,128)(2,1)S(1)} collective-permute-done((bf16[3,2,64,640]{3,2,1,0:T(8,128)(2,1)S(1)}, bf16[3,2,64,640]{3,2,1,0:T(8,128)(2,1)S(1)}, u32[]{:S(2)}, u32[]{:S(2)}) %collective-permute-start.21) | collective-permute-done | bytes 491552 | tf_op jit(solution)/shard_map/ppermute | solution.py:136
  251.0 2.0 collective-permute-done.22.refs_6_
  254.9 2.6 collective-permute-start.23
  258.5 3.0 collective-permute-start.24
  261.5 13.6 %convolution_convert_fusion = bf16[512,1280]{1,0:T(8,128)(2,1)} fusion(bf16[512,5120]{1,0:T(8,128)(2,1)} %copy-done.36, bf16[1280,5120]{1,0:T(8,128)(2,1)} %param.14), kind=kOutput, calls=%fused_computation.4 | convolution fusion | flops 6711541760 | bytes 19660800 | tf_op jit(solution)/shard_map/dot_general | solution.py:18
  277.0 16.1 %attention_backward.2 = (bf16[2,256,640]{2,1,0:T(8,128)(2,1)S(1)}, f32[2,256,640]{2,1,0:T(8,128)S(1)}, f32[2,256,640]{2,1,0:T(8,128)S(1)}, bf16[2,256,640]{2,1,0:T(8,128)(2,1)S(1)}, bf16[2,256,640]{2,1,0:T(8,128)(2,1)S(1)}) custom-call(s32[6]{0:T(128)S(1)} %pad_add_fusion.scal, bf16[1,2,64,5120]{3,2,1,0:T(8,128)(2,1)S(1)} %copy-done.5, ...), custom_call_target="tpu_custom_call" | custom-call | flops 2516582400 | bytes 10485760 | tf_op jit(solution)/shard_map/attention_backward/pallas_call | solution.py:102
  293.1 3.0 collective-permute-start.25
  296.1 1.9 collective-permute-start.26
  298.1 16.1 %attention_backward.3 = (bf16[2,256,640]{2,1,0:T(8,128)(2,1)S(1)}, f32[2,256,640]{2,1,0:T(8,128)S(1)}, f32[2,256,640]{2,1,0:T(8,128)S(1)}, bf16[2,256,640]{2,1,0:T(8,128)(2,1)S(1)}, bf16[2,256,640]{2,1,0:T(8,128)(2,1)S(1)}) custom-call(s32[6]{0:T(128)S(1)} %pad_add_fusion.scal, bf16[1,2,64,5120]{3,2,1,0:T(8,128)(2,1)S(1)} %copy-done.5, ...), custom_call_target="tpu_custom_call" | custom-call | flops 2516582400 | bytes 10485760 | tf_op jit(solution)/shard_map/attention_backward/pallas_call | solution.py:102
  314.2 3.6 %collective-permute-start.27 = (bf16[2,256,640]{2,1,0:T(8,128)(2,1)S(1)}, bf16[2,256,640]{2,1,0:T(8,128)(2,1)S(1)}, u32[]{:S(2)}, u32[]{:S(2)}) collective-permute-start(bf16[2,256,640]{2,1,0:T(8,128)(2,1)S(1)} %get-tuple-element.36), channel_id=1, source_target_pairs={{0,8},{8,16},{16,24},{1,9},{9,17},{17,25},{2,10},{10,18},{18,26},{... | collective-permute-start | bytes 1966088 | tf_op jit(solution)/shard_map/ppermute | solution.py:131
  317.9 1.9 collective-permute-start.28
  321.4 4.0 %collective-permute-done.27 = bf16[2,256,640]{2,1,0:T(8,128)(2,1)S(1)} collective-permute-done((bf16[2,256,640]{2,1,0:T(8,128)(2,1)S(1)}, bf16[2,256,640]{2,1,0:T(8,128)(2,1)S(1)}, u32[]{:S(2)}, u32[]{:S(2)}) %collective-permute-start.27) | collective-permute-done | bytes 655392 | tf_op jit(solution)/shard_map/ppermute | solution.py:131
  325.4 4.4 %collective-permute-done.28 = bf16[2,256,640]{2,1,0:T(8,128)(2,1)S(1)} collective-permute-done((bf16[2,256,640]{2,1,0:T(8,128)(2,1)S(1)}, bf16[2,256,640]{2,1,0:T(8,128)(2,1)S(1)}, u32[]{:S(2)}, u32[]{:S(2)}) %collective-permute-start.28) | collective-permute-done | bytes 655392 | tf_op jit(solution)/shard_map/ppermute | solution.py:131
  332.4 1.6 convert_bitcast_fusion
  334.0 3.1 copy.14
  (181 shorter events, 43.7 us)
Async XLA Ops:
  7.2 325.2 %reduce-scatter.3.cloned.1.call-start = ((), (), s32[]{:S(2)}) async-start(), calls=%async_computation.2 | async-start | bytes 5898240 | tf_op jit(solution)/shard_map/reduce_scatter | solution.py:208
  13.5 36.7 %copy-start.2 = (bf16[1,2,64,5120]{3,2,1,0:T(8,128)(2,1)S(1)}, bf16[1,2,64,5120]{3,2,1,0:T(8,128)(2,1)}, u32[]{:S(2)}) copy-start(bf16[1,2,64,5120]{3,2,1,0:T(8,128)(2,1)} %refs_3_.3) | copy-start | bytes 3932164
  15.3 66.1 %copy-start.22 = (bf16[128,2048]{1,0:T(8,128)(2,1)}, bf16[128,2048]{1,0:T(8,128)(2,1)S(1)}, u32[]{:S(2)}) copy-start(bf16[128,2048]{1,0:T(8,128)(2,1)S(1)} %constant_dynamic-update-slice_fusion) | copy-start | bytes 1572868
  15.3 21.8 %collective-permute-start = (bf16[128,2048]{1,0:T(8,128)(2,1)S(1)}, bf16[128,2048]{1,0:T(8,128)(2,1)}, u32[]{:S(2)}, u32[]{:S(2)}) collective-permute-start(bf16[128,2048]{1,0:T(8,128)(2,1)S(1)} %constant_dynamic-update-slice_fusion), channel_id=1, source_target_pairs={{0,2},{2,4},{4,6},{1,3},{3,5},{5,7},{8,10},{10,12},{12,14},{9,11},... | collective-permute-start | bytes 1572872 | tf_op jit(solution)/shard_map/ppermute | solution.py:145
  18.6 14.4 %collective-permute-start.9 = (bf16[128,2048]{1,0:T(8,128)(2,1)S(1)}, bf16[128,2048]{1,0:T(8,128)(2,1)S(1)}, u32[]{:S(2)}, u32[]{:S(2)}) collective-permute-start(bf16[128,2048]{1,0:T(8,128)(2,1)S(1)} %constant_dynamic-update-slice_fusion), channel_id=1, source_target_pairs={{2,0},{4,2},{6,4},{3,1},{5,3},{7,5},{10,8},{12,10},{14,12},{11,9},... | collective-permute-start | bytes 1572872 | tf_op jit(solution)/shard_map/ppermute | solution.py:146
  32.9 21.7 %copy-start.28 = (bf16[128,2048]{1,0:T(8,128)(2,1)}, bf16[128,2048]{1,0:T(8,128)(2,1)S(1)}, u32[]{:S(2)}) copy-start(bf16[128,2048]{1,0:T(8,128)(2,1)S(1)} %collective-permute-done.9) | copy-start | bytes 1572868
  32.9 13.5 %collective-permute-start.10 = (bf16[128,2048]{1,0:T(8,128)(2,1)S(1)}, bf16[128,2048]{1,0:T(8,128)(2,1)}, u32[]{:S(2)}, u32[]{:S(2)}) collective-permute-start(bf16[128,2048]{1,0:T(8,128)(2,1)S(1)} %collective-permute-done.9), channel_id=1, source_target_pairs={{2,0},{4,2},{3,1},{5,3},{10,8},{12,10},{11,9},{13,11},{18,16},{20,... | collective-permute-start | bytes 1572872 | tf_op jit(solution)/shard_map/ppermute | solution.py:146
  37.1 15.6 %collective-permute-start.1 = (bf16[128,2048]{1,0:T(8,128)(2,1)}, bf16[128,2048]{1,0:T(8,128)(2,1)}, u32[]{:S(2)}, u32[]{:S(2)}) collective-permute-start(bf16[128,2048]{1,0:T(8,128)(2,1)} %collective-permute-done), channel_id=1, source_target_pairs={{2,4},{4,6},{3,5},{5,7},{10,12},{12,14},{11,13},{13,15},{18,20},{2... | collective-permute-start | bytes 1572872 | tf_op jit(solution)/shard_map/ppermute | solution.py:145
  46.5 21.7 %collective-permute-start.11 = (bf16[128,2048]{1,0:T(8,128)(2,1)}, bf16[128,2048]{1,0:T(8,128)(2,1)}, u32[]{:S(2)}, u32[]{:S(2)}) collective-permute-start(bf16[128,2048]{1,0:T(8,128)(2,1)} %collective-permute-done.10), channel_id=1, source_target_pairs={{2,0},{3,1},{10,8},{11,9},{18,16},{19,17},{26,24},{27,25}} | collective-permute-start | bytes 1572872 | tf_op jit(solution)/shard_map/ppermute | solution.py:146
  51.2 19.3 %collective-permute-start.6 = (bf16[2,64,1280]{2,1,0:T(8,128)(2,1)}, bf16[2,64,1280]{2,1,0:T(8,128)(2,1)S(1)}, u32[]{:S(2)}, u32[]{:S(2)}) collective-permute-start(bf16[2,64,1280]{2,1,0:T(8,128)(2,1)} %get-tuple-element.47), channel_id=1, source_target_pairs={{0,2},{2,4},{4,6},{6,0},{1,3},{3,5},{5,7},{7,1},{8,10},{10,12},{12... | collective-permute-start | bytes 983048 | tf_op jit(solution)/shard_map/ppermute | solution.py:136
  51.2 26.1 %collective-permute-start.7 = (bf16[2,64,1280]{2,1,0:T(8,128)(2,1)}, bf16[2,64,1280]{2,1,0:T(8,128)(2,1)S(1)}, u32[]{:S(2)}, u32[]{:S(2)}) collective-permute-start(bf16[2,64,1280]{2,1,0:T(8,128)(2,1)} %get-tuple-element.46), channel_id=1, source_target_pairs={{0,4},{2,6},{4,0},{6,2},{1,5},{3,7},{5,1},{7,3},{8,12},{10,14},{12... | collective-permute-start | bytes 983048 | tf_op jit(solution)/shard_map/ppermute | solution.py:136
  51.9 29.5 %collective-permute-start.8 = (bf16[2,64,1280]{2,1,0:T(8,128)(2,1)}, bf16[2,64,1280]{2,1,0:T(8,128)(2,1)S(1)}, u32[]{:S(2)}, u32[]{:S(2)}) collective-permute-start(bf16[2,64,1280]{2,1,0:T(8,128)(2,1)} %get-tuple-element.45), channel_id=1, source_target_pairs={{0,6},{2,0},{4,2},{6,4},{1,7},{3,1},{5,3},{7,5},{8,14},{10,8},{12,... | collective-permute-start | bytes 983048 | tf_op jit(solution)/shard_map/ppermute | solution.py:136
  52.7 28.8 %copy-start.34 = (bf16[1,2,64,1280]{3,2,1,0:T(8,128)(2,1)S(1)}, bf16[1,2,64,1280]{3,2,1,0:T(8,128)(2,1)}, u32[]{:S(2)}) copy-start(bf16[1,2,64,1280]{3,2,1,0:T(8,128)(2,1)} %get-tuple-element.44) | copy-start | bytes 983044
  52.7 16.5 %collective-permute-start.2 = (bf16[128,2048]{1,0:T(8,128)(2,1)}, bf16[128,2048]{1,0:T(8,128)(2,1)S(1)}, u32[]{:S(2)}, u32[]{:S(2)}) collective-permute-start(bf16[128,2048]{1,0:T(8,128)(2,1)} %collective-permute-done.1), channel_id=1, source_target_pairs={{4,6},{5,7},{12,14},{13,15},{20,22},{21,23},{28,30},{29,31}} | collective-permute-start | bytes 1572872 | tf_op jit(solution)/shard_map/ppermute | solution.py:145
  54.7 31.6 %copy-start.19 = (bf16[128,2048]{1,0:T(8,128)(2,1)}, bf16[128,2048]{1,0:T(8,128)(2,1)S(1)}, u32[]{:S(2)}) copy-start(bf16[128,2048]{1,0:T(8,128)(2,1)S(1)} %broadcast_select_fusion.4) | copy-start | bytes 1572868
  69.2 17.0 %copy-start.20 = (bf16[128,2048]{1,0:T(8,128)(2,1)}, bf16[128,2048]{1,0:T(8,128)(2,1)S(1)}, u32[]{:S(2)}) copy-start(bf16[128,2048]{1,0:T(8,128)(2,1)S(1)} %broadcast_select_fusion.5) | copy-start | bytes 1572868
  70.5 15.7 %copy-start.21 = (bf16[128,2048]{1,0:T(8,128)(2,1)}, bf16[128,2048]{1,0:T(8,128)(2,1)S(1)}, u32[]{:S(2)}) copy-start(bf16[128,2048]{1,0:T(8,128)(2,1)S(1)} %broadcast_select_fusion.3) | copy-start | bytes 1572868
  77.4 66.1 %copy-start.8 = (bf16[2,64,1280]{2,1,0:T(8,128)(2,1)}, bf16[2,64,1280]{2,1,0:T(8,128)(2,1)S(1)}, u32[]{:S(2)}) copy-start(bf16[2,64,1280]{2,1,0:T(8,128)(2,1)S(1)} %collective-permute-done.7.refs_8_) | copy-start | bytes 983044
  86.3 246.1 %reduce-scatter.5.cloned.1.call-start = ((), (), s32[]{:S(2)}) async-start(), calls=%async_computation.3 | async-start | bytes 8847360 | tf_op jit(solution)/shard_map/reduce_scatter | solution.py:208
  86.4 20.4 %collective-permute-start.13 = (bf16[128,3072]{1,0:T(8,128)(2,1)}, bf16[128,3072]{1,0:T(8,128)(2,1)}, u32[]{:S(2)}, u32[]{:S(2)}) collective-permute-start(bf16[128,3072]{1,0:T(8,128)(2,1)} %slice_dynamic-update-slice_fusion.16), channel_id=1, source_target_pairs={{2,0},{4,2},{6,4},{3,1},{5,3},{7,5},{10,8},{12,10},{14,12},{11,9},... | collective-permute-start | bytes 2359304 | tf_op jit(solution)/shard_map/ppermute | solution.py:146
  89.0 20.5 %collective-permute-start.12 = (bf16[128,3072]{1,0:T(8,128)(2,1)}, bf16[128,3072]{1,0:T(8,128)(2,1)}, u32[]{:S(2)}, u32[]{:S(2)}) collective-permute-start(bf16[128,3072]{1,0:T(8,128)(2,1)} %slice_dynamic-update-slice_fusion.16), channel_id=1, source_target_pairs={{0,2},{2,4},{4,6},{1,3},{3,5},{5,7},{8,10},{10,12},{12,14},{9,11},... | collective-permute-start | bytes 2359304 | tf_op jit(solution)/shard_map/ppermute | solution.py:145
  106.7 18.3 %collective-permute-start.14 = (bf16[128,3072]{1,0:T(8,128)(2,1)}, bf16[128,3072]{1,0:T(8,128)(2,1)}, u32[]{:S(2)}, u32[]{:S(2)}) collective-permute-start(bf16[128,3072]{1,0:T(8,128)(2,1)} %collective-permute-done.13), channel_id=1, source_target_pairs={{2,0},{4,2},{3,1},{5,3},{10,8},{12,10},{11,9},{13,11},{18,16},{20,... | collective-permute-start | bytes 2359304 | tf_op jit(solution)/shard_map/ppermute | solution.py:146
  109.5 18.6 %copy-start.37 = (s32[8,2]{0,1:T(2,128)S(1)}, s32[8,2]{0,1:T(2,128)}, u32[]{:S(2)}) copy-start(s32[8,2]{0,1:T(2,128)} %param.17) | copy-start | bytes 196
  109.5 18.9 %collective-permute-start.16 = (bf16[128,3072]{1,0:T(8,128)(2,1)}, bf16[128,3072]{1,0:T(8,128)(2,1)}, u32[]{:S(2)}, u32[]{:S(2)}) collective-permute-start(bf16[128,3072]{1,0:T(8,128)(2,1)} %collective-permute-done.12), channel_id=1, source_target_pairs={{2,4},{4,6},{3,5},{5,7},{10,12},{12,14},{11,13},{13,15},{18,20},{2... | collective-permute-start | bytes 2359304 | tf_op jit(solution)/shard_map/ppermute | solution.py:145
  125.0 15.7 %collective-permute-start.15 = (bf16[128,3072]{1,0:T(8,128)(2,1)}, bf16[128,3072]{1,0:T(8,128)(2,1)}, u32[]{:S(2)}, u32[]{:S(2)}) collective-permute-start(bf16[128,3072]{1,0:T(8,128)(2,1)} %collective-permute-done.14), channel_id=1, source_target_pairs={{2,0},{3,1},{10,8},{11,9},{18,16},{19,17},{26,24},{27,25}} | collective-permute-start | bytes 2359304 | tf_op jit(solution)/shard_map/ppermute | solution.py:146
  128.4 13.6 %collective-permute-start.17 = (bf16[128,3072]{1,0:T(8,128)(2,1)}, bf16[128,3072]{1,0:T(8,128)(2,1)S(1)}, u32[]{:S(2)}, u32[]{:S(2)}) collective-permute-start(bf16[128,3072]{1,0:T(8,128)(2,1)} %collective-permute-done.16), channel_id=1, source_target_pairs={{4,6},{5,7},{12,14},{13,15},{20,22},{21,23},{28,30},{29,31}} | collective-permute-start | bytes 2359304 | tf_op jit(solution)/shard_map/ppermute | solution.py:145
  130.3 13.2 %copy-start.13 = (bf16[128,3072]{1,0:T(8,128)(2,1)}, bf16[128,3072]{1,0:T(8,128)(2,1)S(1)}, u32[]{:S(2)}) copy-start(bf16[128,3072]{1,0:T(8,128)(2,1)S(1)} %broadcast_select_fusion.1) | copy-start | bytes 2359300
  130.3 14.1 %copy-start.11 = (bf16[2,64,1280]{2,1,0:T(8,128)(2,1)S(1)}, bf16[2,64,1280]{2,1,0:T(8,128)(2,1)}, u32[]{:S(2)}) copy-start(bf16[2,64,1280]{2,1,0:T(8,128)(2,1)} %copy-done.10) | copy-start | bytes 983044
  130.3 14.1 %copy-start.35 = (bf16[1,2,64,1280]{3,2,1,0:T(8,128)(2,1)S(1)}, bf16[1,2,64,1280]{3,2,1,0:T(8,128)(2,1)}, u32[]{:S(2)}) copy-start(bf16[1,2,64,1280]{3,2,1,0:T(8,128)(2,1)} %get-tuple-element.44) | copy-start | bytes 983044
  154.1 9.2 %collective-permute-start.3 = (bf16[3,2,64,640]{3,2,1,0:T(8,128)(2,1)S(1)}, bf16[3,2,64,640]{3,2,1,0:T(8,128)(2,1)S(1)}, u32[]{:S(2)}, u32[]{:S(2)}) collective-permute-start(bf16[3,2,64,640]{3,2,1,0:T(8,128)(2,1)S(1)} %copy-done.32), channel_id=1, source_target_pairs={{0,2},{2,4},{4,6},{6,0},{1,3},{3,5},{5,7},{7,1},{8,10},{10,12},{12... | collective-permute-start | bytes 1474568 | tf_op jit(solution)/shard_map/ppermute | solution.py:136
  156.3 37.1 %collective-permute-start.4 = (bf16[3,2,64,640]{3,2,1,0:T(8,128)(2,1)}, bf16[3,2,64,640]{3,2,1,0:T(8,128)(2,1)S(1)}, u32[]{:S(2)}, u32[]{:S(2)}) collective-permute-start(bf16[3,2,64,640]{3,2,1,0:T(8,128)(2,1)} %pad_maximum_fusion.8), channel_id=1, source_target_pairs={{0,4},{2,6},{4,0},{6,2},{1,5},{3,7},{5,1},{7,3},{8,12},{10,14},{12... | collective-permute-start | bytes 1474568 | tf_op jit(solution)/shard_map/ppermute | solution.py:136
  160.1 40.2 %collective-permute-start.5 = (bf16[3,2,64,640]{3,2,1,0:T(8,128)(2,1)S(1)}, bf16[3,2,64,640]{3,2,1,0:T(8,128)(2,1)S(1)}, u32[]{:S(2)}, u32[]{:S(2)}) collective-permute-start(bf16[3,2,64,640]{3,2,1,0:T(8,128)(2,1)S(1)} %copy-done.33), channel_id=1, source_target_pairs={{0,6},{2,0},{4,2},{6,4},{1,7},{3,1},{5,3},{7,5},{8,14},{10,8},{12,... | collective-permute-start | bytes 1474568 | tf_op jit(solution)/shard_map/ppermute | solution.py:136
  200.4 8.3 %copy-start.14 = (bf16[128,3072]{1,0:T(8,128)(2,1)S(1)}, bf16[128,3072]{1,0:T(8,128)(2,1)}, u32[]{:S(2)}) copy-start(bf16[128,3072]{1,0:T(8,128)(2,1)} %copy-done.13) | copy-start | bytes 2359300
  201.5 73.6 %collective-permute-start.19 = (bf16[2,4,64,640]{3,2,1,0:T(8,128)(2,1)}, bf16[2,4,64,640]{3,2,1,0:T(8,128)(2,1)}, u32[]{:S(2)}, u32[]{:S(2)}) collective-permute-start(bf16[2,4,64,640]{3,2,1,0:T(8,128)(2,1)} %pad_maximum_fusion.4), channel_id=1, source_target_pairs={{8,0},{16,8},{24,16},{9,1},{17,9},{25,17},{10,2},{18,10},{26,18},{... | collective-permute-start | bytes 1966088 | tf_op jit(solution)/shard_map/ppermute | solution.py:131
  205.6 69.5 %collective-permute-start.18 = (bf16[2,4,64,640]{3,2,1,0:T(8,128)(2,1)}, bf16[2,4,64,640]{3,2,1,0:T(8,128)(2,1)}, u32[]{:S(2)}, u32[]{:S(2)}) collective-permute-start(bf16[2,4,64,640]{3,2,1,0:T(8,128)(2,1)} %pad_maximum_fusion.3), channel_id=1, source_target_pairs={{0,8},{8,16},{16,24},{1,9},{9,17},{17,25},{2,10},{10,18},{18,26},{... | collective-permute-start | bytes 1966088 | tf_op jit(solution)/shard_map/ppermute | solution.py:131
  208.6 12.8 %collective-permute-start.20 = (bf16[3,2,64,640]{3,2,1,0:T(8,128)(2,1)S(1)}, bf16[3,2,64,640]{3,2,1,0:T(8,128)(2,1)S(1)}, u32[]{:S(2)}, u32[]{:S(2)}) collective-permute-start(bf16[3,2,64,640]{3,2,1,0:T(8,128)(2,1)S(1)} %copy-done.31), channel_id=1, source_target_pairs={{0,2},{2,4},{4,6},{6,0},{1,3},{3,5},{5,7},{7,1},{8,10},{10,12},{12... | collective-permute-start | bytes 1474568 | tf_op jit(solution)/shard_map/ppermute | solution.py:136
  211.4 39.6 %collective-permute-start.21 = (bf16[3,2,64,640]{3,2,1,0:T(8,128)(2,1)S(1)}, bf16[3,2,64,640]{3,2,1,0:T(8,128)(2,1)S(1)}, u32[]{:S(2)}, u32[]{:S(2)}) collective-permute-start(bf16[3,2,64,640]{3,2,1,0:T(8,128)(2,1)S(1)} %copy-done.30), channel_id=1, source_target_pairs={{0,4},{2,6},{4,0},{6,2},{1,5},{3,7},{5,1},{7,3},{8,12},{10,14},{12... | collective-permute-start | bytes 1474568 | tf_op jit(solution)/shard_map/ppermute | solution.py:136
  212.5 40.5 %collective-permute-start.22 = (bf16[3,2,64,640]{3,2,1,0:T(8,128)(2,1)S(1)}, bf16[3,2,64,640]{3,2,1,0:T(8,128)(2,1)S(1)}, u32[]{:S(2)}, u32[]{:S(2)}) collective-permute-start(bf16[3,2,64,640]{3,2,1,0:T(8,128)(2,1)S(1)} %copy-done.29), channel_id=1, source_target_pairs={{0,6},{2,0},{4,2},{6,4},{1,7},{3,1},{5,3},{7,5},{8,14},{10,8},{12,... | collective-permute-start | bytes 1474568 | tf_op jit(solution)/shard_map/ppermute | solution.py:136
  214.1 44.5 %copy-start.36 = (bf16[512,5120]{1,0:T(8,128)(2,1)}, bf16[512,5120]{1,0:T(8,128)(2,1)S(1)}, u32[]{:S(2)}) copy-start(bf16[512,5120]{1,0:T(8,128)(2,1)S(1)} %slice_dynamic-update-slice_fusion) | copy-start | bytes 15728644
  254.9 43.2 %collective-permute-start.23 = (bf16[2,4,64,640]{3,2,1,0:T(8,128)(2,1)}, bf16[2,4,64,640]{3,2,1,0:T(8,128)(2,1)}, u32[]{:S(2)}, u32[]{:S(2)}) collective-permute-start(bf16[2,4,64,640]{3,2,1,0:T(8,128)(2,1)} %pad_maximum_fusion.5), channel_id=1, source_target_pairs={{0,8},{8,16},{16,24},{1,9},{9,17},{17,25},{2,10},{10,18},{18,26},{... | collective-permute-start | bytes 1966088 | tf_op jit(solution)/shard_map/ppermute | solution.py:131
  258.5 16.6 %copy-start.3 = (bf16[1,2,64,5120]{3,2,1,0:T(8,128)(2,1)S(1)}, bf16[1,2,64,5120]{3,2,1,0:T(8,128)(2,1)}, u32[]{:S(2)}) copy-start(bf16[1,2,64,5120]{3,2,1,0:T(8,128)(2,1)} %refs_3_.3) | copy-start | bytes 3932164
  258.5 16.6 %copy-start.5 = (bf16[1,2,64,5120]{3,2,1,0:T(8,128)(2,1)S(1)}, bf16[1,2,64,5120]{3,2,1,0:T(8,128)(2,1)}, u32[]{:S(2)}) copy-start(bf16[1,2,64,5120]{3,2,1,0:T(8,128)(2,1)} %refs_0_.3) | copy-start | bytes 3932164
  258.5 39.5 %collective-permute-start.24 = (bf16[2,4,64,640]{3,2,1,0:T(8,128)(2,1)}, bf16[2,4,64,640]{3,2,1,0:T(8,128)(2,1)}, u32[]{:S(2)}, u32[]{:S(2)}) collective-permute-start(bf16[2,4,64,640]{3,2,1,0:T(8,128)(2,1)} %pad_maximum_fusion.6), channel_id=1, source_target_pairs={{8,0},{16,8},{24,16},{9,1},{17,9},{25,17},{10,2},{18,10},{26,18},{... | collective-permute-start | bytes 1966088 | tf_op jit(solution)/shard_map/ppermute | solution.py:131
  277.0 21.0 %copy-start.7 = (bf16[3,2,64,640]{3,2,1,0:T(8,128)(2,1)S(1)}, bf16[3,2,64,640]{3,2,1,0:T(8,128)(2,1)}, u32[]{:S(2)}) copy-start(bf16[3,2,64,640]{3,2,1,0:T(8,128)(2,1)} %copy-done.6) | copy-start | bytes 1474564
  293.1 26.7 %collective-permute-start.25 = (bf16[2,256,640]{2,1,0:T(8,128)(2,1)S(1)}, bf16[2,256,640]{2,1,0:T(8,128)(2,1)S(1)}, u32[]{:S(2)}, u32[]{:S(2)}) collective-permute-start(bf16[2,256,640]{2,1,0:T(8,128)(2,1)S(1)} %get-tuple-element.33), channel_id=1, source_target_pairs={{0,8},{8,16},{16,24},{1,9},{9,17},{17,25},{2,10},{10,18},{18,26},{... | collective-permute-start | bytes 1966088 | tf_op jit(solution)/shard_map/ppermute | solution.py:131
  296.1 23.7 %collective-permute-start.26 = (bf16[2,256,640]{2,1,0:T(8,128)(2,1)S(1)}, bf16[2,256,640]{2,1,0:T(8,128)(2,1)S(1)}, u32[]{:S(2)}, u32[]{:S(2)}) collective-permute-start(bf16[2,256,640]{2,1,0:T(8,128)(2,1)S(1)} %get-tuple-element.34), channel_id=1, source_target_pairs={{8,0},{16,8},{24,16},{9,1},{17,9},{25,17},{10,2},{18,10},{26,18},{... | collective-permute-start | bytes 1966088 | tf_op jit(solution)/shard_map/ppermute | solution.py:131
  314.2 11.2 %collective-permute-start.27 = (bf16[2,256,640]{2,1,0:T(8,128)(2,1)S(1)}, bf16[2,256,640]{2,1,0:T(8,128)(2,1)S(1)}, u32[]{:S(2)}, u32[]{:S(2)}) collective-permute-start(bf16[2,256,640]{2,1,0:T(8,128)(2,1)S(1)} %get-tuple-element.36), channel_id=1, source_target_pairs={{0,8},{8,16},{16,24},{1,9},{9,17},{17,25},{2,10},{10,18},{18,26},{... | collective-permute-start | bytes 1966088 | tf_op jit(solution)/shard_map/ppermute | solution.py:131
  317.9 11.9 %collective-permute-start.28 = (bf16[2,256,640]{2,1,0:T(8,128)(2,1)S(1)}, bf16[2,256,640]{2,1,0:T(8,128)(2,1)S(1)}, u32[]{:S(2)}, u32[]{:S(2)}) collective-permute-start(bf16[2,256,640]{2,1,0:T(8,128)(2,1)S(1)} %get-tuple-element.37), channel_id=1, source_target_pairs={{8,0},{16,8},{24,16},{9,1},{17,9},{25,17},{10,2},{18,10},{26,18},{... | collective-permute-start | bytes 1966088 | tf_op jit(solution)/shard_map/ppermute | solution.py:131
  (21 other events, 92.8 us)
Sparse Core Ops, SparseCore 0:
  86.4 60.1 reduce-scatter.2
  153.2 77.1 reduce-scatter.4

commit v2 on v1

--- a/solution.py
+++ b/solution.py
@@ -20,11 +20,12 @@
 
 def attention_kernel(parts, scal, *refs):
     own_q, own_k, own_v, own_o = refs[:4]
-    packs = refs[4 : 4 + parts - 1]
-    o_refs = refs[3 + parts : 2 + 2 * parts]
-    d_ref, prev_ref, next_ref = refs[2 + 2 * parts : 5 + 2 * parts]
-    dq_ref, dk_ref, dv_ref, to_prev_ref, to_next_ref = refs[5 + 2 * parts : 10 + 2 * parts]
-    q_all, k_all, v_all, o_all, d_all = refs[10 + 2 * parts :]
+    others, refs = parts - 1, refs[4:]
+    kv_refs, q_refs, o_refs = refs[:others], refs[others : 2 * others], refs[2 * others : 3 * others]
+    d_ref, prev_ref, next_ref, dq_ref, dk_ref, dv_ref, to_prev_ref, to_next_ref = refs[
+        3 * others : 3 * others + 8
+    ]
+    q_all, k_all, v_all, o_all, d_all = refs[3 * others + 8 :]
     _, frames, rows, _ = own_q.shape
     me = scal[0]
     inv_root = HD ** (-0.5)
@@ -32,9 +33,9 @@
         source = lax.rem(me + parts - s, parts)
         at = pl.ds(pl.multiple_of(source * rows, rows), rows)
         for f in range(frames):
-            q_all[f, at] = own_q[0, f] if s == 0 else packs[s - 1][2, f]
-            k_all[f + 1, at] = own_k[0, f] if s == 0 else packs[s - 1][0, f]
-            v_all[f + 1, at] = own_v[0, f] if s == 0 else packs[s - 1][1, f]
+            q_all[f, at] = own_q[0, f] if s == 0 else q_refs[s - 1][f]
+            k_all[f + 1, at] = own_k[0, f] if s == 0 else kv_refs[s - 1][0, f]
+            v_all[f + 1, at] = own_v[0, f] if s == 0 else kv_refs[s - 1][1, f]
             o_all[f, at] = own_o[0, f] if s == 0 else o_refs[s - 1][f]
             d_all[f, at] = d_ref[s, f]
         k_all[0, at] = prev_ref[0, s]
@@ -85,15 +86,16 @@
     to_next_ref[1] = value_grads[frames + 1].astype(jnp.bfloat16)
 
 
-def attention(scal, head0, heads, local, packs, o_pieces, d, from_prev, from_next):
-    parts = len(packs) + 1
+def attention(scal, head0, heads, local, kv, q_pieces, o_pieces, d, from_prev, from_next):
+    parts = len(kv) + 1
     _, frames, rows, _ = local[0].shape
     tokens, width = parts * rows, heads * HD
     own = pl.BlockSpec((1, frames, rows, HD), lambda h, sc: (0, 0, 0, sc[1] + head0 + h))
-    pack = pl.BlockSpec((3, frames, rows, HD), lambda h, sc: (0, 0, 0, h))
+    pack = pl.BlockSpec((2, frames, rows, HD), lambda h, sc: (0, 0, 0, head0 + h))
+    q_spec = pl.BlockSpec((frames, rows, HD), lambda h, sc: (0, 0, h))
     piece = pl.BlockSpec((frames, rows, HD), lambda h, sc: (0, 0, head0 + h))
     dsp = pl.BlockSpec((parts, frames, rows, HD), lambda h, sc: (0, 0, 0, head0 + h))
-    halo = pl.BlockSpec((2, parts, rows, HD), lambda h, sc: (0, 0, 0, h))
+    halo = pl.BlockSpec((2, parts, rows, HD), lambda h, sc: (0, 0, 0, head0 + h))
     out = pl.BlockSpec((frames, tokens, HD), lambda h, sc: (0, 0, h))
     edge = pl.BlockSpec((2, tokens, HD), lambda h, sc: (0, 0, h))
     full_shape, edge_shape = (frames, tokens, width), (2, tokens, width)
@@ -104,7 +106,11 @@
         grid_spec=pltpu.PrefetchScalarGridSpec(
             num_scalar_prefetch=1,
             grid=(heads,),
-            in_specs=[own] * 4 + [pack] * (parts - 1) + [piece] * (parts - 1) + [dsp, halo, halo],
+            in_specs=[own] * 4
+            + [pack] * (parts - 1)
+            + [q_spec] * (parts - 1)
+            + [piece] * (parts - 1)
+            + [dsp, halo, halo],
             out_specs=[out] * 3 + [edge] * 2,
             scratch_shapes=[flats, pads, pads, flats, flats],
         ),
@@ -122,7 +128,7 @@
             transcendentals=heads * frames * 3 * tokens * tokens,
         ),
         name="attention_backward",
-    )(scal, *local, *packs, *o_pieces, d, from_prev, from_next)
+    )(scal, *local, *kv, *q_pieces, *o_pieces, d, from_prev, from_next)
 
 
 def shifted(array, axis, step):
@@ -174,9 +180,8 @@
         target = lax.rem(me + step, parts)
         return lax.dynamic_slice_in_dim(array[0], target * width + start, size, axis=2)
 
-    o_pieces = [
-        rotated(columns_for(saved_out, s, 0, width), "head", s) for s in range(1, parts)
-    ]
+    shifts = range(1, parts)
+    o_pieces = [rotated(columns_for(saved_out, s, 0, width), "head", s) for s in shifts]
 
     gain = jnp.concatenate(
         [lax.dynamic_slice_in_dim(gate_table, levels[f], 1, axis=0) for f in range(frames)], axis=0
@@ -187,32 +192,48 @@
     chunk0 = jnp.concatenate([gated[:, b * block :][:, :cut] for b in range(blocks)], axis=1)
     chunk1 = jnp.concatenate([gated[:, b * block + cut :][:, :rest] for b in range(blocks)], axis=1)
 
-    rights, lefts = [[], []], [[], []]
-    right, left = chunk0, chunk0
-    for step in range(1, parts):
-        right, left = line_step(right, left, "head", step)
-        if step == 1:
-            chunk1, right = after(chunk1, right)
-        rights[0].append(right)
-        lefts[0].append(left)
-    right, left = chunk1, chunk1
-    for step in range(1, parts):
-        right, left = line_step(right, left, "head", step)
-        rights[1].append(right)
-        lefts[1].append(left)
-
-    def weight_chunk(pieces, o_rows):
-        rows_c = jnp.concatenate(pieces, axis=0)
+    ways = [[(chunk0, chunk0)], [(chunk1, chunk1)]]
+    for step in shifts:
+        if step == 2:
+            o_pieces, ways[1][-1] = after(o_pieces, ways[1][-1])
+        if step == parts - 1:
+            ways[0][-1], ways[1][1] = after(ways[0][-1], ways[1][1])
+        ways[0].append(line_step(*ways[0][-1], "head", step))
+        if step < parts - 1:
+            ways[1].append(line_step(*ways[1][-1], "head", step))
+    kv_send = [
+        jnp.stack([columns_for(a, s, 0, width) for a in (key_rows, value_rows)]) for s in shifts
+    ]
+    ways[0][-1], ways[1][-1] = after(ways[0][-1], ways[1][-1])
+    kv_send, ways[0][-1] = after(kv_send, ways[0][-1])
+    kv = [rotated(a, "head", s) for s, a in zip(shifts, kv_send)]
+    ways[1].append(line_step(*ways[1][-1], "head", parts - 1))
+
+    first = (heads + 1) // 2
+    groups = [(0, first), (first, heads - first)]
+    q_send = [
+        [columns_for(queries, s, head0 * HD, count * HD) for s in shifts]
+        for head0, count in groups
+    ]
+    q_send, ways[1][-1] = after(q_send, ways[1][-1])
+    q_pieces = [[rotated(a, "head", s) for s, a in zip(shifts, sends)] for sends in q_send]
+
+    def pieces(own, way):
+        return line_pieces(own, [w[0] for w in way[1:]], [w[1] for w in way[1:]], "head")
+
+    def weight_chunk(rows_c, o_rows):
         grad = dot(rows_c, o_rows, TN)
         grad = (grad / tokens_all).astype(jnp.bfloat16)
-        return rows_c, lax.psum_scatter(grad, ("frame", "fsdp"), scatter_dimension=0, tiled=True)
+        return lax.psum_scatter(grad, ("frame", "fsdp"), scatter_dimension=0, tiled=True)
 
     own_o = columns_for(saved_out, 0, 0, width)
     o_rows = jnp.concatenate(
         [piece.reshape(frames * rows, width) for piece in [own_o] + o_pieces], axis=0
     )
-    rows0, grad0 = weight_chunk(line_pieces(chunk0, rights[0], lefts[0], "head"), o_rows)
-    rows1, grad1 = weight_chunk(line_pieces(chunk1, rights[1], lefts[1], "head"), o_rows)
+    rows0 = jnp.concatenate(pieces(chunk0, ways[0]), axis=0)
+    rows1 = jnp.concatenate(pieces(chunk1, ways[1]), axis=0)
+    grad0 = weight_chunk(rows0, o_rows)
+    grad1 = weight_chunk(rows1, o_rows)
     d_weight = jnp.concatenate([grad0, grad1], axis=0).T.astype(jnp.float32)
 
     columns = []
@@ -227,49 +248,37 @@
     limits = jnp.where(inside, jnp.where(chosen == 1, tokens, tokens // 2), 0).astype(jnp.int32)
     scal = jnp.concatenate([jnp.stack([me, me * heads]).astype(jnp.int32), limits.reshape(-1)])
 
-    first = (heads + 1) // 2
-    groups = [(0, first), (first, heads - first)]
+    kv, d = after(kv, d)
+    own = [columns_for(a, 0, 0, width) for a in (key_rows, value_rows)]
+
+    def boundary(frame):
+        return jnp.stack(
+            [jnp.stack([own[t][frame]] + [p[t, frame] for p in kv]) for t in range(2)]
+        )
+
+    from_prev = shifted(boundary(frames - 1), "frame", 1)
+    from_next = shifted(boundary(0), "frame", -1)
+    local = (queries, key_rows, value_rows, saved_out)
     results = []
-    for g, (head0, count) in enumerate(groups):
-        start, size = head0 * HD, count * HD
-
-        def packed(step):
-            return jnp.stack(
-                [columns_for(a, step, start, size) for a in (key_rows, value_rows, queries)]
-            )
-
-        packs = [packed(s) for s in range(1, parts)]
-        event = rights[g][parts - 2]
-        packs, event = after(packs, event)
-        rights[g][parts - 2] = event
-        packs = [rotated(p, "head", s) for s, p in zip(range(1, parts), packs)]
-        own = [columns_for(a, 0, start, size) for a in (key_rows, value_rows)]
-
-        def boundary(frame):
-            return jnp.stack(
-                [jnp.stack([own[t][frame]] + [p[t, frame] for p in packs]) for t in range(2)]
-            )
-
-        from_prev = shifted(boundary(frames - 1), "frame", 1)
-        from_next = shifted(boundary(0), "frame", -1)
-        local = (queries, key_rows, value_rows, saved_out)
+    for (head0, count), q_group in zip(groups, q_pieces):
+        if results:
+            q_group, results[-1][0] = after(q_group, results[-1][0])
         dq, dk, dv, to_prev, to_next = attention(
-            scal, head0, count, local, packs, o_pieces, d, from_prev, from_next
+            scal, head0, count, local, kv, q_group, o_pieces, d, from_prev, from_next
         )
         grad_next = shifted(to_prev, "frame", -1)
         grad_prev = shifted(to_next, "frame", 1)
-
-        def combine(own_grad, t):
-            terms = [own_grad[f] for f in range(frames)]
-            terms[0] = terms[0] + grad_prev[t].astype(jnp.float32)
-            terms[frames - 1] = terms[frames - 1] + grad_next[t].astype(jnp.float32)
-            return jnp.stack(terms).astype(jnp.bfloat16)
-
-        results.append((dq, combine(dk, 0), combine(dv, 1)))
-
-    d_queries, d_keys, d_values = (
-        jnp.concatenate([r[i] for r in results], axis=2)[None] for i in range(3)
-    )
+        results.append([dq, dk, dv, grad_prev, grad_next])
+
+    def combine(own_grad, t, grad_prev, grad_next):
+        terms = [own_grad[f] for f in range(frames)]
+        terms[0] = terms[0] + grad_prev[t].astype(jnp.float32)
+        terms[frames - 1] = terms[frames - 1] + grad_next[t].astype(jnp.float32)
+        return jnp.stack(terms).astype(jnp.bfloat16)
+
+    d_queries = jnp.concatenate([r[0] for r in results], axis=2)[None]
+    d_keys = jnp.concatenate([combine(r[1], 0, r[3], r[4]) for r in results], axis=2)[None]
+    d_values = jnp.concatenate([combine(r[2], 1, r[3], r[4]) for r in results], axis=2)[None]
     return d_queries, d_keys, d_values, d_weight
 
 

time: 345 us -> 337 us (0.977)
  waiting for transfers between devices: 149 us -> 97.8 us
  local copies, waits for them, and re-layouts: 21 us -> 48.7 us
  starting transfers between devices: 65.5 us -> 85.4 us
  other arithmetic: 30.8 us -> 24.7 us
    ppermute x9 -> x12, waiting for transfers between devices: 89.7 us -> 42.7 us  [rotated(): lax.ppermute(array, axis, [(i, (i + step) % count) for i in range(count)])]
    unnamed x106 -> x92, local copies, waits for them, and re-layouts: 14.3 us -> 35.4 us
    ppermute x8 -> x6, starting transfers between devices: 22.1 us -> 37.7 us  [shifted(): return lax.ppermute(array, axis, pairs)]
    ppermute x9 -> x12, starting transfers between devices: 8.53 us -> 15.9 us  [rotated(): lax.ppermute(array, axis, [(i, (i + step) % count) for i in range(count)])]
    ppermute x6, waiting for transfers between devices: 50.5 us -> 43.3 us  [line_step(): lax.ppermute(left, axis, [(i, i - 1) for i in range(1, count - step + 1)])]
    another operation x20 -> x11, other arithmetic: 13.3 us -> 6.21 us  [the longest x3 2.79 us: per_device(): jnp.stack([columns_for(a, s, 0, width) for a in (key_rows, value_rows)])]
    ppermute x6, starting transfers between devices: 17.7 us -> 11.9 us  [line_step(): lax.ppermute(right, axis, [(i, i + 1) for i in range(step - 1, count - 1)])]
    select_n x6 -> x5, other arithmetic: 7.48 us -> 6.47 us  [line_pieces(): jnp.where(me >= r, rights[r - 1], lefts[count - r - 1])]
  transfers between devices with their start and end apart: 31 -> 32, of which waited for: 16 -> 13; matrix products, arithmetic and copies ran while one was open for 17% -> 20% of each run, Pallas kernels for 9% -> 10%
where the time goes in v2:
time: 337 us; the launch traced here: 335 us
  waiting for transfers between devices  97.8 us (29%)
  starting transfers between devices  85.4 us (25%)
  local copies, waits for them, and re-layouts  48.7 us (14%)
  Pallas kernels  32.1 us (10%)
  matrix products  27.5 us (8%)
  other arithmetic  24.7 us (7%)
  between operations  18.6 us (6%)
    ppermute x6, waiting for transfers between devices, line_step(): lax.ppermute(left, axis, [(i, i - 1) for i in range(1, count - step + 1)])  43.3 us
    ppermute x12, waiting for transfers between devices, rotated(): lax.ppermute(array, axis, [(i, (i + step) % count) for i in range(count)])  42.7 us
    ppermute x6, starting transfers between devices, shifted(): return lax.ppermute(array, axis, pairs)  37.7 us
    unnamed x92, local copies, waits for them, and re-layouts  35.4 us
    pallas_call x2, Pallas kernels, attention(): pl.pallas_call(partial(attention_kernel, parts), grid_spec=pltpu.Prefetch...  32.1 us
    dot_general x3, matrix products, dot(): return lax.dot_general(lhs, rhs, dims, preferred_element_type=jnp.float32)  27.5 us
    ppermute x6, starting transfers between devices, line_step(): lax.ppermute(left, axis, [(i, i - 1) for i in range(1, count - step + 1)])  19.9 us
    ppermute x12, starting transfers between devices, rotated(): lax.ppermute(array, axis, [(i, (i + step) % count) for i in range(count)])  15.9 us
  transfers between devices with their start and end apart: 32, of which 13 were waited for; matrix products, arithmetic and copies ran while one was open for 20% of the time, Pallas kernels for 10%

profile of v2, /device:TPU:11, one launch (start us, length us, event | category | flops | bytes accessed | tf_op | source)
XLA Modules:
  0.0 334.8 jit_solution(6054487985534753771)
XLA Ops:
  13.5 1.6 fusion
  20.2 3.2 collective-permute-start
  23.4 2.9 collective-permute-start.2
  26.3 2.1 constant_dynamic-slice_fusion
  29.0 1.8 collective-permute-start.5
  38.1 2.3 collective-permute-start.7
  40.4 1.9 collective-permute-done.4.refs_10_
  42.3 6.9 %collective-permute-start.8 = (bf16[128,3072]{1,0:T(8,128)(2,1)S(1)}, bf16[128,3072]{1,0:T(8,128)(2,1)}, u32[]{:S(2)}, u32[]{:S(2)}) collective-permute-start(bf16[128,3072]{1,0:T(8,128)(2,1)S(1)} %slice_dynamic-update-slice_fusion.16), channel_id=1, source_target_pairs={{2,0},{4,2},{6,4},{3,1},{5,3},{7,5},{10,8},{12,10},{14,12},{11,9},... | collective-permute-start | bytes 2359304 | tf_op jit(solution)/shard_map/ppermute | solution.py:152
  49.2 6.1 %collective-permute-done.5.refs_11_ = bf16[2,64,1280]{2,1,0:T(8,128)(2,1)S(1)} collective-permute-done((bf16[2,64,1280]{2,1,0:T(8,128)(2,1)S(1)}, bf16[2,64,1280]{2,1,0:T(8,128)(2,1)S(1)}, u32[]{:S(2)}, u32[]{:S(2)}) %collective-permute-start.5) | collective-permute-done | bytes 327712 | tf_op jit(solution)/shard_map/ppermute | solution.py:142
  55.3 5.0 %collective-permute-start.6 = (bf16[2,64,1280]{2,1,0:T(8,128)(2,1)S(1)}, bf16[2,64,1280]{2,1,0:T(8,128)(2,1)}, u32[]{:S(2)}, u32[]{:S(2)}) collective-permute-start(bf16[2,64,1280]{2,1,0:T(8,128)(2,1)S(1)} %get-tuple-element.97), channel_id=1, source_target_pairs={{0,6},{2,0},{4,2},{6,4},{1,7},{3,1},{5,3},{7,5},{8,14},{10,8},{12,... | collective-permute-start | bytes 983048 | tf_op jit(solution)/shard_map/ppermute | solution.py:142
  60.3 2.1 collective-permute-start.1
  62.4 1.9 collective-permute-start.3
  65.5 17.6 %collective-permute-done.6.refs_12_ = bf16[2,64,1280]{2,1,0:T(8,128)(2,1)} collective-permute-done((bf16[2,64,1280]{2,1,0:T(8,128)(2,1)S(1)}, bf16[2,64,1280]{2,1,0:T(8,128)(2,1)}, u32[]{:S(2)}, u32[]{:S(2)}) %collective-permute-start.6) | collective-permute-done | bytes 327712 | tf_op jit(solution)/shard_map/ppermute | solution.py:142
  83.1 2.2 collective-permute-start.11
  85.3 1.9 collective-permute-start.12
  88.1 2.4 collective-permute-done.1
  90.5 3.8 %collective-permute-done.3 = bf16[128,2048]{1,0:T(8,128)(2,1)} collective-permute-done((bf16[128,2048]{1,0:T(8,128)(2,1)}, bf16[128,2048]{1,0:T(8,128)(2,1)}, u32[]{:S(2)}, u32[]{:S(2)}) %collective-permute-start.3) | collective-permute-done | bytes 524320 | tf_op jit(solution)/shard_map/ppermute | solution.py:152
  94.3 2.1 collective-permute-start.10
  96.4 1.4 collective-permute-start.9
  100.0 16.2 %collective-permute-done.10 = bf16[128,2048]{1,0:T(8,128)(2,1)} collective-permute-done((bf16[128,2048]{1,0:T(8,128)(2,1)}, bf16[128,2048]{1,0:T(8,128)(2,1)}, u32[]{:S(2)}, u32[]{:S(2)}) %collective-permute-start.10) | collective-permute-done | bytes 524320 | tf_op jit(solution)/shard_map/ppermute | solution.py:152
  119.4 6.5 %multiply_convert_fusion.1 = bf16[2048,1280]{1,0:T(8,128)(2,1)} fusion(bf16[128,1280]{1,0:T(8,128)(2,1)} %bitcast.42, bf16[128,1280]{1,0:T(8,128)(2,1)S(1)} %bitcast.86, bf16[128,1280]{1,0:T(8,128)(2,1)S(1)} %bitcast.84, bf16[128,1280]{1,0:T(8,128)(2,1)S(1)} %bitcast.88, bf16[128,2048]{1,0:T(8,128)(2,1)S(1)} %broadcast_select_fusion.3, ...), kind=kOutput, calls=%fused_computation.1 | convolution fusion | flops 2703228928 | bytes 8650752 | tf_op jit(solution)/shard_map/dot_general | solution.py:18
  126.0 2.4 dynamic-slice_bitcast_fusion.7
  129.9 4.2 %collective-permute-start.14 = (bf16[128,3072]{1,0:T(8,128)(2,1)}, bf16[128,3072]{1,0:T(8,128)(2,1)S(1)}, u32[]{:S(2)}, u32[]{:S(2)}) collective-permute-start(bf16[128,3072]{1,0:T(8,128)(2,1)} %collective-permute-done.12), channel_id=1, source_target_pairs={{2,0},{3,1},{10,8},{11,9},{18,16},{19,17},{26,24},{27,25}} | collective-permute-start | bytes 2359304 | tf_op jit(solution)/shard_map/ppermute | solution.py:152
  136.3 1.4 collective-permute-start.19
  139.1 23.3 %collective-permute-done.14 = bf16[128,3072]{1,0:T(8,128)(2,1)S(1)} collective-permute-done((bf16[128,3072]{1,0:T(8,128)(2,1)}, bf16[128,3072]{1,0:T(8,128)(2,1)S(1)}, u32[]{:S(2)}, u32[]{:S(2)}) %collective-permute-start.14) | collective-permute-done | bytes 786464 | tf_op jit(solution)/shard_map/ppermute | solution.py:152
  162.4 1.6 broadcast_select_fusion
  165.2 7.5 %multiply_convert_fusion = bf16[3072,1280]{1,0:T(8,128)(2,1)} fusion(bf16[128,1280]{1,0:T(8,128)(2,1)} %bitcast.42, bf16[128,1280]{1,0:T(8,128)(2,1)S(1)} %bitcast.87, bf16[128,1280]{1,0:T(8,128)(2,1)S(1)} %bitcast.85, bf16[128,1280]{1,0:T(8,128)(2,1)S(1)} %bitcast.89, bf16[128,3072]{1,0:T(8,128)(2,1)S(1)} %get-tuple-element.151, ...), kind=kOutput, calls=%fused_computation | convolution fusion | flops 4052221952 | bytes 12320768 | tf_op jit(solution)/shard_map/dot_general | solution.py:18
  172.8 2.2 pad_maximum_fusion
  187.0 13.5 %convolution_convert_fusion = bf16[512,1280]{1,0:T(8,128)(2,1)} fusion(bf16[512,5120]{1,0:T(8,128)(2,1)} %slice_dynamic-update-slice_fusion, bf16[1280,5120]{1,0:T(8,128)(2,1)} %param.14), kind=kOutput, calls=%fused_computation.4 | convolution fusion | flops 6711541760 | bytes 19660800 | tf_op jit(solution)/shard_map/dot_general | solution.py:18
  200.6 1.4 slice_bitcast_fusion.4
  202.0 1.4 slice_bitcast_fusion.3
  204.8 23.3 %collective-permute-start.25 = (bf16[2,4,64,1280]{3,2,1,0:T(8,128)(2,1)}, bf16[2,4,64,1280]{3,2,1,0:T(8,128)(2,1)}, u32[]{:S(2)}, u32[]{:S(2)}) collective-permute-start(bf16[2,4,64,1280]{3,2,1,0:T(8,128)(2,1)} %pad_maximum_fusion.3), channel_id=1, source_target_pairs={{8,0},{16,8},{24,16},{9,1},{17,9},{25,17},{10,2},{18,10},{26,18},{... | collective-permute-start | bytes 3932168 | tf_op jit(solution)/shard_map/ppermute | solution.py:137
  229.5 3.0 collective-permute-start.24
  232.7 3.5 %collective-permute-start.22 = (bf16[2,64,640]{2,1,0:T(8,128)(2,1)}, bf16[2,64,640]{2,1,0:T(8,128)(2,1)}, u32[]{:S(2)}, u32[]{:S(2)}) collective-permute-start(bf16[2,64,640]{2,1,0:T(8,128)(2,1)} %get-tuple-element.72), channel_id=1, source_target_pairs={{0,4},{2,6},{4,0},{6,2},{1,5},{3,7},{5,1},{7,3},{8,12},{10,14},{12... | collective-permute-start | bytes 491528 | tf_op jit(solution)/shard_map/ppermute | solution.py:142
  236.5 1.9 collective-permute-done.21.refs_7_
  238.7 8.0 %collective-permute-done.22.refs_8_ = bf16[2,64,640]{2,1,0:T(8,128)(2,1)} collective-permute-done((bf16[2,64,640]{2,1,0:T(8,128)(2,1)}, bf16[2,64,640]{2,1,0:T(8,128)(2,1)}, u32[]{:S(2)}, u32[]{:S(2)}) %collective-permute-start.22) | collective-permute-done | bytes 163872 | tf_op jit(solution)/shard_map/ppermute | solution.py:142
  246.7 3.2 collective-permute-start.16
  249.9 7.2 %collective-permute-done.23.refs_9_ = bf16[2,64,640]{2,1,0:T(8,128)(2,1)} collective-permute-done((bf16[2,64,640]{2,1,0:T(8,128)(2,1)}, bf16[2,64,640]{2,1,0:T(8,128)(2,1)}, u32[]{:S(2)}, u32[]{:S(2)}) %collective-permute-start.23) | collective-permute-done | bytes 163872 | tf_op jit(solution)/shard_map/ppermute | solution.py:142
  263.9 16.0 %attention_backward.2 = (bf16[2,256,640]{2,1,0:T(8,128)(2,1)S(1)}, f32[2,256,640]{2,1,0:T(8,128)S(1)}, f32[2,256,640]{2,1,0:T(8,128)S(1)}, bf16[2,256,640]{2,1,0:T(8,128)(2,1)S(1)}, bf16[2,256,640]{2,1,0:T(8,128)(2,1)S(1)}) custom-call(s32[6]{0:T(128)S(1)} %pad_add_fusion.scal, bf16[1,2,64,5120]{3,2,1,0:T(8,128)(2,1)S(1)} %copy-done.3, ...), custom_call_target="tpu_custom_call" | custom-call | flops 2516582400 | bytes 10485760 | tf_op jit(solution)/shard_map/attention_backward/pallas_call | solution.py:104
  280.0 3.7 %collective-permute-start.26 = (bf16[2,256,640]{2,1,0:T(8,128)(2,1)S(1)}, bf16[2,256,640]{2,1,0:T(8,128)(2,1)S(1)}, u32[]{:S(2)}, u32[]{:S(2)}) collective-permute-start(bf16[2,256,640]{2,1,0:T(8,128)(2,1)S(1)} %get-tuple-element.85), channel_id=1, source_target_pairs={{0,8},{8,16},{16,24},{1,9},{9,17},{17,25},{2,10},{10,18},{18,26},{... | collective-permute-start | bytes 1966088 | tf_op jit(solution)/shard_map/ppermute | solution.py:137
  283.6 2.1 collective-permute-start.27
  285.8 16.1 %attention_backward.3 = (bf16[2,256,640]{2,1,0:T(8,128)(2,1)S(1)}, f32[2,256,640]{2,1,0:T(8,128)S(1)}, f32[2,256,640]{2,1,0:T(8,128)S(1)}, bf16[2,256,640]{2,1,0:T(8,128)(2,1)S(1)}, bf16[2,256,640]{2,1,0:T(8,128)(2,1)S(1)}) custom-call(s32[6]{0:T(128)S(1)} %pad_add_fusion.scal, bf16[1,2,64,5120]{3,2,1,0:T(8,128)(2,1)S(1)} %copy-done.3, ...), custom_call_target="tpu_custom_call" | custom-call | flops 2516582400 | bytes 10485760 | tf_op jit(solution)/shard_map/attention_backward/pallas_call | solution.py:104
  301.9 3.6 %collective-permute-start.28 = (bf16[2,256,640]{2,1,0:T(8,128)(2,1)S(1)}, bf16[2,256,640]{2,1,0:T(8,128)(2,1)S(1)}, u32[]{:S(2)}, u32[]{:S(2)}) collective-permute-start(bf16[2,256,640]{2,1,0:T(8,128)(2,1)S(1)} %get-tuple-element.88), channel_id=1, source_target_pairs={{0,8},{8,16},{16,24},{1,9},{9,17},{17,25},{2,10},{10,18},{18,26},{... | collective-permute-start | bytes 1966088 | tf_op jit(solution)/shard_map/ppermute | solution.py:137
  305.5 1.9 collective-permute-start.29
  309.0 4.1 %collective-permute-done.28 = bf16[2,256,640]{2,1,0:T(8,128)(2,1)S(1)} collective-permute-done((bf16[2,256,640]{2,1,0:T(8,128)(2,1)S(1)}, bf16[2,256,640]{2,1,0:T(8,128)(2,1)S(1)}, u32[]{:S(2)}, u32[]{:S(2)}) %collective-permute-start.28) | collective-permute-done | bytes 655392 | tf_op jit(solution)/shard_map/ppermute | solution.py:137
  313.0 4.4 %collective-permute-done.29 = bf16[2,256,640]{2,1,0:T(8,128)(2,1)S(1)} collective-permute-done((bf16[2,256,640]{2,1,0:T(8,128)(2,1)S(1)}, bf16[2,256,640]{2,1,0:T(8,128)(2,1)S(1)}, u32[]{:S(2)}, u32[]{:S(2)}) %collective-permute-start.29) | collective-permute-done | bytes 655392 | tf_op jit(solution)/shard_map/ppermute | solution.py:137
  320.1 3.3 convert_bitcast_fusion
  323.4 4.6 %copy.14 = f32[1280,640]{1,0:T(8,128)} copy(f32[1280,640]{0,1:T(8,128)} %convert_bitcast_fusion) | data formatting | bytes 6553600
  (156 shorter events, 55.6 us)
Async XLA Ops:
  7.2 313.0 %reduce-scatter.3.cloned.1.call-start = ((), (), s32[]{:S(2)}) async-start(), calls=%async_computation.2 | async-start | bytes 5898240 | tf_op jit(solution)/shard_map/reduce_scatter | solution.py:227
  15.8 48.6 %copy-start = (bf16[1,2,64,5120]{3,2,1,0:T(8,128)(2,1)S(1)}, bf16[1,2,64,5120]{3,2,1,0:T(8,128)(2,1)}, u32[]{:S(2)}) copy-start(bf16[1,2,64,5120]{3,2,1,0:T(8,128)(2,1)} %refs_1_.3) | copy-start | bytes 3932164
  15.8 48.6 %copy-start.1 = (bf16[1,2,64,5120]{3,2,1,0:T(8,128)(2,1)S(1)}, bf16[1,2,64,5120]{3,2,1,0:T(8,128)(2,1)}, u32[]{:S(2)}) copy-start(bf16[1,2,64,5120]{3,2,1,0:T(8,128)(2,1)} %refs_2_.3) | copy-start | bytes 3932164
  20.2 40.1 %collective-permute-start = (bf16[128,2048]{1,0:T(8,128)(2,1)}, bf16[128,2048]{1,0:T(8,128)(2,1)}, u32[]{:S(2)}, u32[]{:S(2)}) collective-permute-start(bf16[128,2048]{1,0:T(8,128)(2,1)} %constant_dynamic-update-slice_fusion), channel_id=1, source_target_pairs={{0,2},{2,4},{4,6},{1,3},{3,5},{5,7},{8,10},{10,12},{12,14},{9,11},... | collective-permute-start | bytes 1572872 | tf_op jit(solution)/shard_map/ppermute | solution.py:151
  23.4 39.0 %collective-permute-start.2 = (bf16[128,2048]{1,0:T(8,128)(2,1)}, bf16[128,2048]{1,0:T(8,128)(2,1)}, u32[]{:S(2)}, u32[]{:S(2)}) collective-permute-start(bf16[128,2048]{1,0:T(8,128)(2,1)} %constant_dynamic-update-slice_fusion), channel_id=1, source_target_pairs={{2,0},{4,2},{6,4},{3,1},{5,3},{7,5},{10,8},{12,10},{14,12},{11,9},... | collective-permute-start | bytes 1572872 | tf_op jit(solution)/shard_map/ppermute | solution.py:152
  28.5 13.8 %collective-permute-start.4 = (bf16[2,64,1280]{2,1,0:T(8,128)(2,1)S(1)}, bf16[2,64,1280]{2,1,0:T(8,128)(2,1)S(1)}, u32[]{:S(2)}, u32[]{:S(2)}) collective-permute-start(bf16[2,64,1280]{2,1,0:T(8,128)(2,1)S(1)} %get-tuple-element.99), channel_id=1, source_target_pairs={{0,2},{2,4},{4,6},{6,0},{1,3},{3,5},{5,7},{7,1},{8,10},{10,12},{12... | collective-permute-start | bytes 983048 | tf_op jit(solution)/shard_map/ppermute | solution.py:142
  29.0 26.4 %collective-permute-start.5 = (bf16[2,64,1280]{2,1,0:T(8,128)(2,1)S(1)}, bf16[2,64,1280]{2,1,0:T(8,128)(2,1)S(1)}, u32[]{:S(2)}, u32[]{:S(2)}) collective-permute-start(bf16[2,64,1280]{2,1,0:T(8,128)(2,1)S(1)} %get-tuple-element.98), channel_id=1, source_target_pairs={{0,4},{2,6},{4,0},{6,2},{1,5},{3,7},{5,1},{7,3},{8,12},{10,14},{12... | collective-permute-start | bytes 983048 | tf_op jit(solution)/shard_map/ppermute | solution.py:142
  38.1 27.4 %copy-start.23 = (bf16[128,3072]{1,0:T(8,128)(2,1)}, bf16[128,3072]{1,0:T(8,128)(2,1)S(1)}, u32[]{:S(2)}) copy-start(bf16[128,3072]{1,0:T(8,128)(2,1)S(1)} %slice_dynamic-update-slice_fusion.16) | copy-start | bytes 2359300
  38.1 45.0 %collective-permute-start.7 = (bf16[128,3072]{1,0:T(8,128)(2,1)S(1)}, bf16[128,3072]{1,0:T(8,128)(2,1)}, u32[]{:S(2)}, u32[]{:S(2)}) collective-permute-start(bf16[128,3072]{1,0:T(8,128)(2,1)S(1)} %slice_dynamic-update-slice_fusion.16), channel_id=1, source_target_pairs={{0,2},{2,4},{4,6},{1,3},{3,5},{5,7},{8,10},{10,12},{12,14},{9,11},... | collective-permute-start | bytes 2359304 | tf_op jit(solution)/shard_map/ppermute | solution.py:151
  42.2 76.4 %copy-start.5 = (bf16[2,64,1280]{2,1,0:T(8,128)(2,1)}, bf16[2,64,1280]{2,1,0:T(8,128)(2,1)S(1)}, u32[]{:S(2)}) copy-start(bf16[2,64,1280]{2,1,0:T(8,128)(2,1)S(1)} %collective-permute-done.4.refs_10_) | copy-start | bytes 983044
  42.3 40.9 %collective-permute-start.8 = (bf16[128,3072]{1,0:T(8,128)(2,1)S(1)}, bf16[128,3072]{1,0:T(8,128)(2,1)}, u32[]{:S(2)}, u32[]{:S(2)}) collective-permute-start(bf16[128,3072]{1,0:T(8,128)(2,1)S(1)} %slice_dynamic-update-slice_fusion.16), channel_id=1, source_target_pairs={{2,0},{4,2},{6,4},{3,1},{5,3},{7,5},{10,8},{12,10},{14,12},{11,9},... | collective-permute-start | bytes 2359304 | tf_op jit(solution)/shard_map/ppermute | solution.py:152
  55.3 63.3 %copy-start.8 = (bf16[2,64,1280]{2,1,0:T(8,128)(2,1)}, bf16[2,64,1280]{2,1,0:T(8,128)(2,1)S(1)}, u32[]{:S(2)}) copy-start(bf16[2,64,1280]{2,1,0:T(8,128)(2,1)S(1)} %collective-permute-done.5.refs_11_) | copy-start | bytes 983044
  55.3 27.8 %collective-permute-start.6 = (bf16[2,64,1280]{2,1,0:T(8,128)(2,1)S(1)}, bf16[2,64,1280]{2,1,0:T(8,128)(2,1)}, u32[]{:S(2)}, u32[]{:S(2)}) collective-permute-start(bf16[2,64,1280]{2,1,0:T(8,128)(2,1)S(1)} %get-tuple-element.97), channel_id=1, source_target_pairs={{0,6},{2,0},{4,2},{6,4},{1,7},{3,1},{5,3},{7,5},{8,14},{10,8},{12,... | collective-permute-start | bytes 983048 | tf_op jit(solution)/shard_map/ppermute | solution.py:142
  60.3 30.2 %collective-permute-start.1 = (bf16[128,2048]{1,0:T(8,128)(2,1)}, bf16[128,2048]{1,0:T(8,128)(2,1)}, u32[]{:S(2)}, u32[]{:S(2)}) collective-permute-start(bf16[128,2048]{1,0:T(8,128)(2,1)} %collective-permute-done), channel_id=1, source_target_pairs={{2,4},{4,6},{3,5},{5,7},{10,12},{12,14},{11,13},{13,15},{18,20},{2... | collective-permute-start | bytes 1572872 | tf_op jit(solution)/shard_map/ppermute | solution.py:151
  62.4 31.9 %collective-permute-start.3 = (bf16[128,2048]{1,0:T(8,128)(2,1)}, bf16[128,2048]{1,0:T(8,128)(2,1)}, u32[]{:S(2)}, u32[]{:S(2)}) collective-permute-start(bf16[128,2048]{1,0:T(8,128)(2,1)} %collective-permute-done.2), channel_id=1, source_target_pairs={{2,0},{4,2},{3,1},{5,3},{10,8},{12,10},{11,9},{13,11},{18,16},{20,... | collective-permute-start | bytes 1572872 | tf_op jit(solution)/shard_map/ppermute | solution.py:152
  83.1 33.1 %collective-permute-start.11 = (bf16[128,3072]{1,0:T(8,128)(2,1)}, bf16[128,3072]{1,0:T(8,128)(2,1)}, u32[]{:S(2)}, u32[]{:S(2)}) collective-permute-start(bf16[128,3072]{1,0:T(8,128)(2,1)} %collective-permute-done.7), channel_id=1, source_target_pairs={{2,4},{4,6},{3,5},{5,7},{10,12},{12,14},{11,13},{13,15},{18,20},{2... | collective-permute-start | bytes 2359304 | tf_op jit(solution)/shard_map/ppermute | solution.py:151
  85.3 30.9 %collective-permute-start.12 = (bf16[128,3072]{1,0:T(8,128)(2,1)}, bf16[128,3072]{1,0:T(8,128)(2,1)}, u32[]{:S(2)}, u32[]{:S(2)}) collective-permute-start(bf16[128,3072]{1,0:T(8,128)(2,1)} %collective-permute-done.8), channel_id=1, source_target_pairs={{2,0},{4,2},{3,1},{5,3},{10,8},{12,10},{11,9},{13,11},{18,16},{20,... | collective-permute-start | bytes 2359304 | tf_op jit(solution)/shard_map/ppermute | solution.py:152
  94.3 21.8 %collective-permute-start.10 = (bf16[128,2048]{1,0:T(8,128)(2,1)}, bf16[128,2048]{1,0:T(8,128)(2,1)}, u32[]{:S(2)}, u32[]{:S(2)}) collective-permute-start(bf16[128,2048]{1,0:T(8,128)(2,1)} %collective-permute-done.3), channel_id=1, source_target_pairs={{2,0},{3,1},{10,8},{11,9},{18,16},{19,17},{26,24},{27,25}} | collective-permute-start | bytes 1572872 | tf_op jit(solution)/shard_map/ppermute | solution.py:152
  96.4 19.7 %collective-permute-start.9 = (bf16[128,2048]{1,0:T(8,128)(2,1)}, bf16[128,2048]{1,0:T(8,128)(2,1)}, u32[]{:S(2)}, u32[]{:S(2)}) collective-permute-start(bf16[128,2048]{1,0:T(8,128)(2,1)} %collective-permute-done.1), channel_id=1, source_target_pairs={{4,6},{5,7},{12,14},{13,15},{20,22},{21,23},{28,30},{29,31}} | collective-permute-start | bytes 1572872 | tf_op jit(solution)/shard_map/ppermute | solution.py:151
  98.8 20.6 %copy-start.28 = (bf16[1,2,64,1280]{3,2,1,0:T(8,128)(2,1)S(1)}, bf16[1,2,64,1280]{3,2,1,0:T(8,128)(2,1)}, u32[]{:S(2)}) copy-start(bf16[1,2,64,1280]{3,2,1,0:T(8,128)(2,1)} %get-tuple-element.96) | copy-start | bytes 983044
  100.0 18.7 %copy-start.17 = (bf16[128,2048]{1,0:T(8,128)(2,1)}, bf16[128,2048]{1,0:T(8,128)(2,1)S(1)}, u32[]{:S(2)}) copy-start(bf16[128,2048]{1,0:T(8,128)(2,1)S(1)} %broadcast_select_fusion.4) | copy-start | bytes 1572868
  125.9 8.2 %copy-start.18 = (bf16[128,2048]{1,0:T(8,128)(2,1)S(1)}, bf16[128,2048]{1,0:T(8,128)(2,1)}, u32[]{:S(2)}) copy-start(bf16[128,2048]{1,0:T(8,128)(2,1)} %copy-done.17) | copy-start | bytes 1572868
  125.9 194.2 %reduce-scatter.5.cloned.1.call-start = ((), (), s32[]{:S(2)}) async-start(), calls=%async_computation.3 | async-start | bytes 8847360 | tf_op jit(solution)/shard_map/reduce_scatter | solution.py:227
  126.0 8.1 %copy-start.20 = (bf16[128,2048]{1,0:T(8,128)(2,1)S(1)}, bf16[128,2048]{1,0:T(8,128)(2,1)}, u32[]{:S(2)}) copy-start(bf16[128,2048]{1,0:T(8,128)(2,1)} %copy-done.19) | copy-start | bytes 1572868
  129.2 9.9 %collective-permute-start.13 = (bf16[128,3072]{1,0:T(8,128)(2,1)}, bf16[128,3072]{1,0:T(8,128)(2,1)S(1)}, u32[]{:S(2)}, u32[]{:S(2)}) collective-permute-start(bf16[128,3072]{1,0:T(8,128)(2,1)} %collective-permute-done.11), channel_id=1, source_target_pairs={{4,6},{5,7},{12,14},{13,15},{20,22},{21,23},{28,30},{29,31}} | collective-permute-start | bytes 2359304 | tf_op jit(solution)/shard_map/ppermute | solution.py:151
  129.9 32.5 %collective-permute-start.14 = (bf16[128,3072]{1,0:T(8,128)(2,1)}, bf16[128,3072]{1,0:T(8,128)(2,1)S(1)}, u32[]{:S(2)}, u32[]{:S(2)}) collective-permute-start(bf16[128,3072]{1,0:T(8,128)(2,1)} %collective-permute-done.12), channel_id=1, source_target_pairs={{2,0},{3,1},{10,8},{11,9},{18,16},{19,17},{26,24},{27,25}} | collective-permute-start | bytes 2359304 | tf_op jit(solution)/shard_map/ppermute | solution.py:152
  135.4 28.6 %copy-start.11 = (bf16[512,2048]{1,0:T(8,128)(2,1)}, bf16[512,2048]{1,0:T(8,128)(2,1)S(1)}, u32[]{:S(2)}) copy-start(bf16[512,2048]{1,0:T(8,128)(2,1)S(1)} %pad_maximum_fusion.1) | copy-start | bytes 6291460
  136.3 64.2 %collective-permute-start.18 = (bf16[2,2,64,1280]{3,2,1,0:T(8,128)(2,1)}, bf16[2,2,64,1280]{3,2,1,0:T(8,128)(2,1)S(1)}, u32[]{:S(2)}, u32[]{:S(2)}) collective-permute-start(bf16[2,2,64,1280]{3,2,1,0:T(8,128)(2,1)} %pad_maximum_fusion.5), channel_id=1, source_target_pairs={{0,2},{2,4},{4,6},{6,0},{1,3},{3,5},{5,7},{7,1},{8,10},{10,12},{12... | collective-permute-start | bytes 1966088 | tf_op jit(solution)/shard_map/ppermute | solution.py:142
  136.3 64.2 %collective-permute-start.19 = (bf16[2,2,64,1280]{3,2,1,0:T(8,128)(2,1)}, bf16[2,2,64,1280]{3,2,1,0:T(8,128)(2,1)}, u32[]{:S(2)}, u32[]{:S(2)}) collective-permute-start(bf16[2,2,64,1280]{3,2,1,0:T(8,128)(2,1)} %pad_maximum_fusion.6), channel_id=1, source_target_pairs={{0,4},{2,6},{4,0},{6,2},{1,5},{3,7},{5,1},{7,3},{8,12},{10,14},{12... | collective-permute-start | bytes 1966088 | tf_op jit(solution)/shard_map/ppermute | solution.py:142
  137.7 62.9 %collective-permute-start.20 = (bf16[2,2,64,1280]{3,2,1,0:T(8,128)(2,1)}, bf16[2,2,64,1280]{3,2,1,0:T(8,128)(2,1)}, u32[]{:S(2)}, u32[]{:S(2)}) collective-permute-start(bf16[2,2,64,1280]{3,2,1,0:T(8,128)(2,1)} %pad_maximum_fusion.7), channel_id=1, source_target_pairs={{0,6},{2,0},{4,2},{6,4},{1,7},{3,1},{5,3},{7,5},{8,14},{10,8},{12,... | collective-permute-start | bytes 1966088 | tf_op jit(solution)/shard_map/ppermute | solution.py:142
  139.1 25.0 %copy-start.14 = (bf16[128,3072]{1,0:T(8,128)(2,1)}, bf16[128,3072]{1,0:T(8,128)(2,1)S(1)}, u32[]{:S(2)}) copy-start(bf16[128,3072]{1,0:T(8,128)(2,1)S(1)} %broadcast_select_fusion.1) | copy-start | bytes 2359300
  139.1 26.1 %copy-start.6 = (bf16[2,64,1280]{2,1,0:T(8,128)(2,1)S(1)}, bf16[2,64,1280]{2,1,0:T(8,128)(2,1)}, u32[]{:S(2)}) copy-start(bf16[2,64,1280]{2,1,0:T(8,128)(2,1)} %copy-done.5) | copy-start | bytes 983044
  139.1 26.1 %copy-start.9 = (bf16[2,64,1280]{2,1,0:T(8,128)(2,1)S(1)}, bf16[2,64,1280]{2,1,0:T(8,128)(2,1)}, u32[]{:S(2)}) copy-start(bf16[2,64,1280]{2,1,0:T(8,128)(2,1)} %copy-done.8) | copy-start | bytes 983044
  139.1 26.1 %copy-start.24 = (bf16[128,3072]{1,0:T(8,128)(2,1)S(1)}, bf16[128,3072]{1,0:T(8,128)(2,1)}, u32[]{:S(2)}) copy-start(bf16[128,3072]{1,0:T(8,128)(2,1)} %copy-done.23) | copy-start | bytes 2359300
  139.1 26.1 %copy-start.29 = (bf16[1,2,64,1280]{3,2,1,0:T(8,128)(2,1)S(1)}, bf16[1,2,64,1280]{3,2,1,0:T(8,128)(2,1)}, u32[]{:S(2)}) copy-start(bf16[1,2,64,1280]{3,2,1,0:T(8,128)(2,1)} %get-tuple-element.96) | copy-start | bytes 983044
  203.5 24.7 %copy-start.25 = (bf16[1,64,1280]{2,1,0:T(8,128)(2,1)S(1)}, bf16[1,64,1280]{2,1,0:T(8,128)(2,1)}, u32[]{:S(2)}) copy-start(bf16[1,64,1280]{2,1,0:T(8,128)(2,1)} %get-tuple-element.149) | copy-start | bytes 491524
  204.8 53.2 %collective-permute-start.25 = (bf16[2,4,64,1280]{3,2,1,0:T(8,128)(2,1)}, bf16[2,4,64,1280]{3,2,1,0:T(8,128)(2,1)}, u32[]{:S(2)}, u32[]{:S(2)}) collective-permute-start(bf16[2,4,64,1280]{3,2,1,0:T(8,128)(2,1)} %pad_maximum_fusion.3), channel_id=1, source_target_pairs={{8,0},{16,8},{24,16},{9,1},{17,9},{25,17},{10,2},{18,10},{26,18},{... | collective-permute-start | bytes 3932168 | tf_op jit(solution)/shard_map/ppermute | solution.py:137
  229.5 28.5 %collective-permute-start.24 = (bf16[2,4,64,1280]{3,2,1,0:T(8,128)(2,1)}, bf16[2,4,64,1280]{3,2,1,0:T(8,128)(2,1)}, u32[]{:S(2)}, u32[]{:S(2)}) collective-permute-start(bf16[2,4,64,1280]{3,2,1,0:T(8,128)(2,1)} %pad_maximum_fusion.2), channel_id=1, source_target_pairs={{0,8},{8,16},{16,24},{1,9},{9,17},{17,25},{2,10},{10,18},{18,26},{... | collective-permute-start | bytes 3932168 | tf_op jit(solution)/shard_map/ppermute | solution.py:137
  232.6 5.8 %collective-permute-start.21 = (bf16[2,64,640]{2,1,0:T(8,128)(2,1)}, bf16[2,64,640]{2,1,0:T(8,128)(2,1)S(1)}, u32[]{:S(2)}, u32[]{:S(2)}) collective-permute-start(bf16[2,64,640]{2,1,0:T(8,128)(2,1)} %get-tuple-element.71), channel_id=1, source_target_pairs={{0,2},{2,4},{4,6},{6,0},{1,3},{3,5},{5,7},{7,1},{8,10},{10,12},{12... | collective-permute-start | bytes 491528 | tf_op jit(solution)/shard_map/ppermute | solution.py:142
  232.7 14.0 %collective-permute-start.22 = (bf16[2,64,640]{2,1,0:T(8,128)(2,1)}, bf16[2,64,640]{2,1,0:T(8,128)(2,1)}, u32[]{:S(2)}, u32[]{:S(2)}) collective-permute-start(bf16[2,64,640]{2,1,0:T(8,128)(2,1)} %get-tuple-element.72), channel_id=1, source_target_pairs={{0,4},{2,6},{4,0},{6,2},{1,5},{3,7},{5,1},{7,3},{8,12},{10,14},{12... | collective-permute-start | bytes 491528 | tf_op jit(solution)/shard_map/ppermute | solution.py:142
  236.2 20.9 %collective-permute-start.23 = (bf16[2,64,640]{2,1,0:T(8,128)(2,1)}, bf16[2,64,640]{2,1,0:T(8,128)(2,1)}, u32[]{:S(2)}, u32[]{:S(2)}) collective-permute-start(bf16[2,64,640]{2,1,0:T(8,128)(2,1)} %get-tuple-element.73), channel_id=1, source_target_pairs={{0,6},{2,0},{4,2},{6,4},{1,7},{3,1},{5,3},{7,5},{8,14},{10,8},{12,... | collective-permute-start | bytes 491528 | tf_op jit(solution)/shard_map/ppermute | solution.py:142
  238.4 47.4 %collective-permute-start.15 = (bf16[2,64,640]{2,1,0:T(8,128)(2,1)}, bf16[2,64,640]{2,1,0:T(8,128)(2,1)S(1)}, u32[]{:S(2)}, u32[]{:S(2)}) collective-permute-start(bf16[2,64,640]{2,1,0:T(8,128)(2,1)} %get-tuple-element.54), channel_id=1, source_target_pairs={{0,2},{2,4},{4,6},{6,0},{1,3},{3,5},{5,7},{7,1},{8,10},{10,12},{12... | collective-permute-start | bytes 491528 | tf_op jit(solution)/shard_map/ppermute | solution.py:142
  246.7 39.1 %collective-permute-start.16 = (bf16[2,64,640]{2,1,0:T(8,128)(2,1)}, bf16[2,64,640]{2,1,0:T(8,128)(2,1)S(1)}, u32[]{:S(2)}, u32[]{:S(2)}) collective-permute-start(bf16[2,64,640]{2,1,0:T(8,128)(2,1)} %get-tuple-element.55), channel_id=1, source_target_pairs={{0,4},{2,6},{4,0},{6,2},{1,5},{3,7},{5,1},{7,3},{8,12},{10,14},{12... | collective-permute-start | bytes 491528 | tf_op jit(solution)/shard_map/ppermute | solution.py:142
  257.1 28.7 %collective-permute-start.17 = (bf16[2,64,640]{2,1,0:T(8,128)(2,1)}, bf16[2,64,640]{2,1,0:T(8,128)(2,1)S(1)}, u32[]{:S(2)}, u32[]{:S(2)}) collective-permute-start(bf16[2,64,640]{2,1,0:T(8,128)(2,1)} %get-tuple-element.56), channel_id=1, source_target_pairs={{0,6},{2,0},{4,2},{6,4},{1,7},{3,1},{5,3},{7,5},{8,14},{10,8},{12,... | collective-permute-start | bytes 491528 | tf_op jit(solution)/shard_map/ppermute | solution.py:142
  280.0 28.7 %collective-permute-start.26 = (bf16[2,256,640]{2,1,0:T(8,128)(2,1)S(1)}, bf16[2,256,640]{2,1,0:T(8,128)(2,1)S(1)}, u32[]{:S(2)}, u32[]{:S(2)}) collective-permute-start(bf16[2,256,640]{2,1,0:T(8,128)(2,1)S(1)} %get-tuple-element.85), channel_id=1, source_target_pairs={{0,8},{8,16},{16,24},{1,9},{9,17},{17,25},{2,10},{10,18},{18,26},{... | collective-permute-start | bytes 1966088 | tf_op jit(solution)/shard_map/ppermute | solution.py:137
  283.6 25.0 %collective-permute-start.27 = (bf16[2,256,640]{2,1,0:T(8,128)(2,1)S(1)}, bf16[2,256,640]{2,1,0:T(8,128)(2,1)S(1)}, u32[]{:S(2)}, u32[]{:S(2)}) collective-permute-start(bf16[2,256,640]{2,1,0:T(8,128)(2,1)S(1)} %get-tuple-element.86), channel_id=1, source_target_pairs={{8,0},{16,8},{24,16},{9,1},{17,9},{25,17},{10,2},{18,10},{26,18},{... | collective-permute-start | bytes 1966088 | tf_op jit(solution)/shard_map/ppermute | solution.py:137
  301.9 11.2 %collective-permute-start.28 = (bf16[2,256,640]{2,1,0:T(8,128)(2,1)S(1)}, bf16[2,256,640]{2,1,0:T(8,128)(2,1)S(1)}, u32[]{:S(2)}, u32[]{:S(2)}) collective-permute-start(bf16[2,256,640]{2,1,0:T(8,128)(2,1)S(1)} %get-tuple-element.88), channel_id=1, source_target_pairs={{0,8},{8,16},{16,24},{1,9},{9,17},{17,25},{2,10},{10,18},{18,26},{... | collective-permute-start | bytes 1966088 | tf_op jit(solution)/shard_map/ppermute | solution.py:137
  305.5 11.9 %collective-permute-start.29 = (bf16[2,256,640]{2,1,0:T(8,128)(2,1)S(1)}, bf16[2,256,640]{2,1,0:T(8,128)(2,1)S(1)}, u32[]{:S(2)}, u32[]{:S(2)}) collective-permute-start(bf16[2,256,640]{2,1,0:T(8,128)(2,1)S(1)} %get-tuple-element.89), channel_id=1, source_target_pairs={{8,0},{16,8},{24,16},{9,1},{17,9},{25,17},{10,2},{18,10},{26,18},{... | collective-permute-start | bytes 1966088 | tf_op jit(solution)/shard_map/ppermute | solution.py:137
  (15 other events, 39.7 us)
Sparse Core Ops, SparseCore 0:
  126.0 58.8 reduce-scatter.2
  188.8 80.8 reduce-scatter.4

commit v3 on v2

--- a/solution.py
+++ b/solution.py
@@ -19,13 +19,11 @@
 
 
 def attention_kernel(parts, scal, *refs):
-    own_q, own_k, own_v, own_o = refs[:4]
-    others, refs = parts - 1, refs[4:]
-    kv_refs, q_refs, o_refs = refs[:others], refs[others : 2 * others], refs[2 * others : 3 * others]
-    d_ref, prev_ref, next_ref, dq_ref, dk_ref, dv_ref, to_prev_ref, to_next_ref = refs[
-        3 * others : 3 * others + 8
-    ]
-    q_all, k_all, v_all, o_all, d_all = refs[3 * others + 8 :]
+    own_q, own_k, own_v = refs[:3]
+    others, refs = parts - 1, refs[3:]
+    kv_refs, q_refs, refs = refs[:others], refs[others : 2 * others], refs[2 * others :]
+    o_ref, d_ref, prev_ref, next_ref, dq_ref, dk_ref, dv_ref, to_prev_ref, to_next_ref = refs[:9]
+    q_all, k_all, v_all = refs[9:]
     _, frames, rows, _ = own_q.shape
     me = scal[0]
     inv_root = HD ** (-0.5)
@@ -36,8 +34,6 @@
             q_all[f, at] = own_q[0, f] if s == 0 else q_refs[s - 1][f]
             k_all[f + 1, at] = own_k[0, f] if s == 0 else kv_refs[s - 1][0, f]
             v_all[f + 1, at] = own_v[0, f] if s == 0 else kv_refs[s - 1][1, f]
-            o_all[f, at] = own_o[0, f] if s == 0 else o_refs[s - 1][f]
-            d_all[f, at] = d_ref[s, f]
         k_all[0, at] = prev_ref[0, s]
         v_all[0, at] = prev_ref[1, s]
         k_all[frames + 1, at] = next_ref[0, s]
@@ -51,8 +47,8 @@
         grads[slot] = term if grads[slot] is None else grads[slot] + term
 
     for f in range(frames):
-        q, d = q_all[f], d_all[f]
-        prod = d.astype(jnp.float32) * o_all[f].astype(jnp.float32)
+        q, d = q_all[f], d_ref[:, f].reshape(tokens, HD)
+        prod = d.astype(jnp.float32) * o_ref[:, f].reshape(tokens, HD).astype(jnp.float32)
         delta = lax.dot_general(
             jnp.ones((8, HD), jnp.float32), prod, NT,
             precision=lax.Precision.HIGHEST, preferred_element_type=jnp.float32,
@@ -86,14 +82,13 @@
     to_next_ref[1] = value_grads[frames + 1].astype(jnp.bfloat16)
 
 
-def attention(scal, head0, heads, local, kv, q_pieces, o_pieces, d, from_prev, from_next):
+def attention(scal, head0, heads, local, kv, q_pieces, o, d, from_prev, from_next):
     parts = len(kv) + 1
     _, frames, rows, _ = local[0].shape
     tokens, width = parts * rows, heads * HD
     own = pl.BlockSpec((1, frames, rows, HD), lambda h, sc: (0, 0, 0, sc[1] + head0 + h))
     pack = pl.BlockSpec((2, frames, rows, HD), lambda h, sc: (0, 0, 0, head0 + h))
     q_spec = pl.BlockSpec((frames, rows, HD), lambda h, sc: (0, 0, h))
-    piece = pl.BlockSpec((frames, rows, HD), lambda h, sc: (0, 0, head0 + h))
     dsp = pl.BlockSpec((parts, frames, rows, HD), lambda h, sc: (0, 0, 0, head0 + h))
     halo = pl.BlockSpec((2, parts, rows, HD), lambda h, sc: (0, 0, 0, head0 + h))
     out = pl.BlockSpec((frames, tokens, HD), lambda h, sc: (0, 0, h))
@@ -106,13 +101,12 @@
         grid_spec=pltpu.PrefetchScalarGridSpec(
             num_scalar_prefetch=1,
             grid=(heads,),
-            in_specs=[own] * 4
+            in_specs=[own] * 3
             + [pack] * (parts - 1)
             + [q_spec] * (parts - 1)
-            + [piece] * (parts - 1)
-            + [dsp, halo, halo],
+            + [dsp, dsp, halo, halo],
             out_specs=[out] * 3 + [edge] * 2,
-            scratch_shapes=[flats, pads, pads, flats, flats],
+            scratch_shapes=[flats, pads, pads],
         ),
         out_shape=[
             jax.ShapeDtypeStruct(full_shape, jnp.bfloat16),
@@ -128,7 +122,7 @@
             transcendentals=heads * frames * 3 * tokens * tokens,
         ),
         name="attention_backward",
-    )(scal, *local, *kv, *q_pieces, *o_pieces, d, from_prev, from_next)
+    )(scal, *local, *kv, *q_pieces, o, d, from_prev, from_next)
 
 
 def shifted(array, axis, step):
@@ -146,18 +140,47 @@
     return lax.optimization_barrier((array, event))
 
 
-def line_step(right, left, axis, step):
-    count = lax.axis_size(axis)
-    right = lax.ppermute(right, axis, [(i, i + 1) for i in range(step - 1, count - 1)])
-    left = lax.ppermute(left, axis, [(i, i - 1) for i in range(1, count - step + 1)])
-    return right, left
-
-
-def line_pieces(own, rights, lefts, axis):
-    count, me = lax.axis_size(axis), lax.axis_index(axis)
-    return [own] + [
-        jnp.where(me >= r, rights[r - 1], lefts[count - r - 1]) for r in range(1, count)
-    ]
+def flipped(array, axis, bit):
+    return lax.ppermute(array, axis, [(i, i ^ bit) for i in range(lax.axis_size(axis))])
+
+
+def weight_kernel(scale, table, near_ref, far_ref, g_near, g_far, out_ref):
+    step = pl.program_id(0)
+
+    @pl.when(step == 0)
+    def _():
+        out_ref[...] = jnp.zeros_like(out_ref)
+
+    total = dot(near_ref[0], g_near[0], TN) + dot(far_ref[0], g_far[0], TN)
+    out_ref[...] += total * scale
+
+
+def weight_grad(table, near, far, gated, scale):
+    count, rows, width = near.shape
+    columns = gated.shape[2]
+    side = pl.BlockSpec((1, rows, width), lambda j, tab: (j, 0, 0))
+    return pl.pallas_call(
+        partial(weight_kernel, scale),
+        grid_spec=pltpu.PrefetchScalarGridSpec(
+            num_scalar_prefetch=1,
+            grid=(count,),
+            in_specs=[
+                side,
+                side,
+                pl.BlockSpec((1, rows, columns), lambda j, tab: (tab[0, j], 0, 0)),
+                pl.BlockSpec((1, rows, columns), lambda j, tab: (tab[1, j], 0, 0)),
+            ],
+            out_specs=pl.BlockSpec((width, columns), lambda j, tab: (0, 0)),
+        ),
+        out_shape=jax.ShapeDtypeStruct((width, columns), jnp.float32),
+        compiler_params=pltpu.CompilerParams(vmem_limit_bytes=40 * 2**20),
+        cost_estimate=pl.CostEstimate(
+            flops=4 * count * rows * width * columns,
+            bytes_accessed=4 * count * rows * (width + columns) + 4 * width * columns,
+            transcendentals=0,
+        ),
+        name="weight_gradient",
+    )(table, near, far, gated, gated)
 
 
 def per_device(
@@ -174,12 +197,11 @@
     tokens_all = lax.axis_size("fsdp") * frames_all * tokens
     blocks = lax.axis_size("frame") * lax.axis_size("fsdp")
     block = model // blocks
-    cut = (block // 2) // 128 * 128 or block // 2
-
     def columns_for(array, step, start, size):
         target = lax.rem(me + step, parts)
         return lax.dynamic_slice_in_dim(array[0], target * width + start, size, axis=2)
 
+    shifts = range(1, parts)
     shifts = range(1, parts)
     o_pieces = [rotated(columns_for(saved_out, s, 0, width), "head", s) for s in shifts]
 
@@ -187,27 +209,41 @@
         [lax.dynamic_slice_in_dim(gate_table, levels[f], 1, axis=0) for f in range(frames)], axis=0
     )
     gated = (cotangent[0].astype(jnp.float32) * gain[:, None, :]).astype(jnp.bfloat16)
-    gated = gated.reshape(frames * rows, model)
-    rest = block - cut
-    chunk0 = jnp.concatenate([gated[:, b * block :][:, :cut] for b in range(blocks)], axis=1)
-    chunk1 = jnp.concatenate([gated[:, b * block + cut :][:, :rest] for b in range(blocks)], axis=1)
-
-    ways = [[(chunk0, chunk0)], [(chunk1, chunk1)]]
-    for step in shifts:
-        if step == 2:
-            o_pieces, ways[1][-1] = after(o_pieces, ways[1][-1])
-        if step == parts - 1:
-            ways[0][-1], ways[1][1] = after(ways[0][-1], ways[1][1])
-        ways[0].append(line_step(*ways[0][-1], "head", step))
-        if step < parts - 1:
-            ways[1].append(line_step(*ways[1][-1], "head", step))
+    gathered = lax.all_gather(gated, "head", axis=0, tiled=False).reshape(-1, model)
+
     kv_send = [
         jnp.stack([columns_for(a, s, 0, width) for a in (key_rows, value_rows)]) for s in shifts
     ]
-    ways[0][-1], ways[1][-1] = after(ways[0][-1], ways[1][-1])
-    kv_send, ways[0][-1] = after(kv_send, ways[0][-1])
+    kv_send, o_pieces = after(kv_send, o_pieces)
     kv = [rotated(a, "head", s) for s, a in zip(shifts, kv_send)]
-    ways[1].append(line_step(*ways[1][-1], "head", parts - 1))
+
+    o = jnp.zeros((parts, frames, rows, width), jnp.bfloat16)
+    for s, piece in enumerate([columns_for(saved_out, 0, 0, width)] + o_pieces):
+        o = lax.dynamic_update_slice_in_dim(o, piece[None], lax.rem(me + parts - s, parts), axis=0)
+
+    levels_xy = [("fsdp", 1 << i) for i in range(lax.axis_size("fsdp").bit_length() - 1)]
+    levels_xy += [("frame", 1 << i) for i in range(lax.axis_size("frame").bit_length() - 2, 0, -1)]
+    near = o.reshape(1, parts * frames * rows, width)
+    flips = [(0, 0)]
+    for axis, bit in levels_xy:
+        near = jnp.concatenate([near, flipped(near, axis, bit)], axis=0)
+        flips += [(a ^ bit, b) if axis == "frame" else (a, b ^ bit) for a, b in flips]
+    far = flipped(near, "frame", 1)
+    my_frame, my_video = lax.axis_index("frame"), lax.axis_index("fsdp")
+    videos = lax.axis_size("fsdp")
+    table = jnp.stack(
+        [
+            jnp.stack([(my_frame ^ (a ^ c)) * videos + (my_video ^ b) for a, b in flips])
+            for c in range(2)
+        ]
+    ).astype(jnp.int32)
+
+    gated_out = jnp.stack([gathered[:, b * block : (b + 1) * block] for b in range(blocks)])
+    gated_in = lax.all_to_all(
+        gated_out, ("frame", "fsdp"), split_axis=0, concat_axis=0, tiled=True
+    )
+    d_weight = weight_grad(table, near, far, gated_in, 1.0 / tokens_all)
+    d = dot(gathered, out_weight, NT).astype(jnp.bfloat16).reshape(parts, frames, rows, width)
 
     first = (heads + 1) // 2
     groups = [(0, first), (first, heads - first)]
@@ -215,32 +251,8 @@
         [columns_for(queries, s, head0 * HD, count * HD) for s in shifts]
         for head0, count in groups
     ]
-    q_send, ways[1][-1] = after(q_send, ways[1][-1])
+    q_send, kv = after(q_send, kv)
     q_pieces = [[rotated(a, "head", s) for s, a in zip(shifts, sends)] for sends in q_send]
-
-    def pieces(own, way):
-        return line_pieces(own, [w[0] for w in way[1:]], [w[1] for w in way[1:]], "head")
-
-    def weight_chunk(rows_c, o_rows):
-        grad = dot(rows_c, o_rows, TN)
-        grad = (grad / tokens_all).astype(jnp.bfloat16)
-        return lax.psum_scatter(grad, ("frame", "fsdp"), scatter_dimension=0, tiled=True)
-
-    own_o = columns_for(saved_out, 0, 0, width)
-    o_rows = jnp.concatenate(
-        [piece.reshape(frames * rows, width) for piece in [own_o] + o_pieces], axis=0
-    )
-    rows0 = jnp.concatenate(pieces(chunk0, ways[0]), axis=0)
-    rows1 = jnp.concatenate(pieces(chunk1, ways[1]), axis=0)
-    grad0 = weight_chunk(rows0, o_rows)
-    grad1 = weight_chunk(rows1, o_rows)
-    d_weight = jnp.concatenate([grad0, grad1], axis=0).T.astype(jnp.float32)
-
-    columns = []
-    for b in range(blocks):
-        columns += [rows0[:, b * cut : (b + 1) * cut], rows1[:, b * rest : (b + 1) * rest]]
-    gated_rows = jnp.concatenate(columns, axis=1)
-    d = dot(gated_rows, out_weight, NT).astype(jnp.bfloat16).reshape(parts, frames, rows, width)
 
     ids = first_frame + jnp.arange(frames, dtype=jnp.int32)
     chosen = lax.dynamic_slice_in_dim(reach_flags, first_frame, frames, axis=0)
@@ -248,7 +260,6 @@
     limits = jnp.where(inside, jnp.where(chosen == 1, tokens, tokens // 2), 0).astype(jnp.int32)
     scal = jnp.concatenate([jnp.stack([me, me * heads]).astype(jnp.int32), limits.reshape(-1)])
 
-    kv, d = after(kv, d)
     own = [columns_for(a, 0, 0, width) for a in (key_rows, value_rows)]
 
     def boundary(frame):
@@ -258,13 +269,13 @@
 
     from_prev = shifted(boundary(frames - 1), "frame", 1)
     from_next = shifted(boundary(0), "frame", -1)
-    local = (queries, key_rows, value_rows, saved_out)
+    local = (queries, key_rows, value_rows)
     results = []
     for (head0, count), q_group in zip(groups, q_pieces):
         if results:
             q_group, results[-1][0] = after(q_group, results[-1][0])
         dq, dk, dv, to_prev, to_next = attention(
-            scal, head0, count, local, kv, q_group, o_pieces, d, from_prev, from_next
+            scal, head0, count, local, kv, q_group, o, d, from_prev, from_next
         )
         grad_next = shifted(to_prev, "frame", -1)
         grad_prev = shifted(to_next, "frame", 1)

time: 337 us -> 390 us (1.16)
  waiting for transfers between devices: 97.8 us -> 207 us
  starting transfers between devices: 85.4 us -> 38.8 us
  matrix products: 27.5 us -> 12.7 us
  Pallas kernels: 32.1 us -> 46 us
  local copies, waits for them, and re-layouts: 48.7 us -> 39.9 us
    ppermute x12, waiting for transfers between devices: 42.7 us -> 134 us  [rotated(): lax.ppermute(array, axis, [(i, (i + step) % count) for i in range(count)])]
    ppermute x6, waiting for transfers between devices: 9.38 us -> 59.3 us  [shifted(): return lax.ppermute(array, axis, pairs)]
    ppermute x12 -> x3, waiting for transfers between devices: 45.7 us -> 13.6 us  [flipped(): lax.ppermute(array, axis, [(i, i ^ bit) for i in range(lax.axis_size(axis...]
    ppermute x12 -> x3, starting transfers between devices: 31.8 us -> 1.42 us  [flipped(): lax.ppermute(array, axis, [(i, i ^ bit) for i in range(lax.axis_size(axis...]
    ppermute x6, starting transfers between devices: 37.7 us -> 21.8 us  [shifted(): return lax.ppermute(array, axis, pairs)]
    dot_general x3 -> x1, matrix products: 27.5 us -> 12.7 us  [dot(): return lax.dot_general(lhs, rhs, dims, preferred_element_type=jnp.float32)]
    unnamed x92 -> x49, local copies, waits for them, and re-layouts: 35.4 us -> 21.1 us
    pallas_call x0 -> x1, Pallas kernels: none -> 13.7 us  [weight_grad(): pl.pallas_call(partial(weight_kernel, scale), grid_spec=pltpu.PrefetchSca...]
  transfers between devices with their start and end apart: 32 -> 23, of which waited for: 13 -> 11; matrix products, arithmetic and copies ran while one was open for 20% -> 16% of each run, Pallas kernels for 10% -> 8%
where the time goes in v3:
time: 390 us; the launch traced here: 389 us
  waiting for transfers between devices  207 us (53%)
  Pallas kernels  46 us (12%)
  local copies, waits for them, and re-layouts  39.9 us (10%)
  starting transfers between devices  38.8 us (10%)
  other arithmetic  26 us (7%)
  between operations  18.2 us (5%)
  matrix products  12.7 us (3%)
    ppermute x12, waiting for transfers between devices, rotated(): lax.ppermute(array, axis, [(i, (i + step) % count) for i in range(count)])  134 us
    ppermute x6, waiting for transfers between devices, shifted(): return lax.ppermute(array, axis, pairs)  59.3 us
    pallas_call x2, Pallas kernels, attention(): pl.pallas_call(partial(attention_kernel, parts), grid_spec=pltpu.Prefetch...  32.4 us
    ppermute x6, starting transfers between devices, shifted(): return lax.ppermute(array, axis, pairs)  21.8 us
    unnamed x49, local copies, waits for them, and re-layouts  21.1 us
    pallas_call x1, Pallas kernels, weight_grad(): pl.pallas_call(partial(weight_kernel, scale), grid_spec=pltpu.PrefetchSca...  13.7 us
    ppermute x3, waiting for transfers between devices, flipped(): lax.ppermute(array, axis, [(i, i ^ bit) for i in range(lax.axis_size(axis...  13.6 us
    dot_general x1, matrix products, dot(): return lax.dot_general(lhs, rhs, dims, preferred_element_type=jnp.float32)  12.7 us
  transfers between devices with their start and end apart: 23, of which 11 were waited for; matrix products, arithmetic and copies ran while one was open for 16% of the time, Pallas kernels for 8%

profile of v3, /device:TPU:11, one launch (start us, length us, event | category | flops | bytes accessed | tf_op | source)
XLA Modules:
  0.0 388.6 jit_solution(6291278022399878047)
XLA Ops:
  7.2 1.3 fusion.10
  13.5 2.6 multiply_convert_fusion
  16.3 2.3 dynamic-slice_dynamic-update-slice_fusion
  18.6 2.3 collective-permute-start.1
  20.9 1.5 collective-permute-start.2
  22.4 1.3 constant_dynamic-slice_fusion.3
  26.4 27.0 %collective-permute-done.1 = bf16[2,64,1280]{2,1,0:T(8,128)(2,1)} collective-permute-done((bf16[2,64,1280]{2,1,0:T(8,128)(2,1)}, bf16[2,64,1280]{2,1,0:T(8,128)(2,1)}, u32[]{:S(2)}, u32[]{:S(2)}) %collective-permute-start.1) | collective-permute-done | bytes 327712 | tf_op jit(solution)/shard_map/ppermute | solution.py:136
  53.5 31.1 %collective-permute-done = bf16[2,64,1280]{2,1,0:T(8,128)(2,1)} collective-permute-done((bf16[2,64,1280]{2,1,0:T(8,128)(2,1)}, bf16[2,64,1280]{2,1,0:T(8,128)(2,1)}, u32[]{:S(2)}, u32[]{:S(2)}) %collective-permute-start) | collective-permute-done | bytes 327712 | tf_op jit(solution)/shard_map/ppermute | solution.py:136
  84.5 3.1 collective-permute-done.2
  91.0 1.8 dynamic-slice_bitcast_fusion.3
  92.9 1.5 collective-permute-start.5
  94.6 13.5 %collective-permute-done.18 = bf16[1,512,1280]{2,1,0:T(8,128)(2,1)} collective-permute-done((bf16[1,512,1280]{2,1,0:T(8,128)(2,1)S(1)}, bf16[1,512,1280]{2,1,0:T(8,128)(2,1)}, u32[]{:S(2)}, u32[]{:S(2)}) %collective-permute-start.18) | collective-permute-done | bytes 1310752 | tf_op jit(solution)/shard_map/ppermute | solution.py:144
  108.2 3.1 pad_maximum_fusion.1
  112.4 2.3 dynamic-slice_bitcast_fusion.7
  114.7 30.2 %collective-permute-done.3.refs_3_ = bf16[2,2,64,1280]{3,2,1,0:T(8,128)(2,1)S(1)} collective-permute-done((bf16[2,2,64,1280]{3,2,1,0:T(8,128)(2,1)}, bf16[2,2,64,1280]{3,2,1,0:T(8,128)(2,1)S(1)}, u32[]{:S(2)}, u32[]{:S(2)}) %collective-permute-start.3) | collective-permute-done | bytes 655392 | tf_op jit(solution)/shard_map/ppermute | solution.py:136
  144.9 42.0 %collective-permute-done.4.refs_4_ = bf16[2,2,64,1280]{3,2,1,0:T(8,128)(2,1)} collective-permute-done((bf16[2,2,64,1280]{3,2,1,0:T(8,128)(2,1)}, bf16[2,2,64,1280]{3,2,1,0:T(8,128)(2,1)}, u32[]{:S(2)}, u32[]{:S(2)}) %collective-permute-start.4) | collective-permute-done | bytes 655392 | tf_op jit(solution)/shard_map/ppermute | solution.py:136
  187.5 2.5 collective-permute-start.10
  190.1 1.4 collective-permute-start.11
  192.2 1.9 slice_bitcast_fusion.12
  194.0 1.8 slice_bitcast_fusion.11
  196.1 1.2 pad_maximum_fusion.2
  197.3 9.6 %collective-permute-start.12 = (bf16[2,4,64,1280]{3,2,1,0:T(8,128)(2,1)}, bf16[2,4,64,1280]{3,2,1,0:T(8,128)(2,1)}, u32[]{:S(2)}, u32[]{:S(2)}) collective-permute-start(bf16[2,4,64,1280]{3,2,1,0:T(8,128)(2,1)} %pad_maximum_fusion.2), channel_id=1, source_target_pairs={{0,8},{8,16},{16,24},{1,9},{9,17},{17,25},{2,10},{10,18},{18,26},{... | collective-permute-start | bytes 3932168 | tf_op jit(solution)/shard_map/ppermute | solution.py:131
  207.8 5.0 %pad_maximum_fusion.near_ref = bf16[4,512,1280]{2,1,0:T(8,128)(2,1)} fusion(bf16[2,512,1280]{2,1,0:T(8,128)(2,1)} %collective-permute-done.19, bf16[1,512,1280]{2,1,0:T(8,128)(2,1)} %collective-permute-done.18, bf16[1,512,1280]{2,1,0:T(8,128)(2,1)S(1)} %bitcast.125), kind=kLoop, calls=%fused_computation | loop fusion | flops 5242880 | bytes 10485760 | tf_op jit(solution)/shard_map/concatenate | solution.py:229
  212.7 2.1 fusion.7
  214.9 2.0 fusion.6
  216.9 2.0 fusion.5
  218.8 2.0 fusion.4
  224.6 4.6 %all-to-all-start = ((bf16[8,512,640]{2,1,0:T(8,128)(2,1)}), bf16[8,512,640]{2,1,0:T(8,128)(2,1)}, u32[]{:S(2)}, u32[]{:S(2)}) async-start(bf16[8,512,640]{2,1,0:T(8,128)(2,1)} %fusion), calls=%async_computation | async-start | bytes 10485760 | tf_op jit(solution)/shard_map/all_to_all | solution.py:242
  229.2 1.2 maximum_bitcast_fusion.6
  230.4 2.3 pad_maximum_fusion.3
  232.7 2.6 collective-permute-start.13
  235.2 12.7 %convolution_convert_fusion = bf16[512,1280]{1,0:T(8,128)(2,1)S(1)} fusion(bf16[512,5120]{1,0:T(8,128)(2,1)} %bitcast.132, bf16[1280,5120]{1,0:T(8,128)(2,1)} %param.14), kind=kOutput, calls=%fused_computation.1 | convolution fusion | flops 6711541760 | bytes 19660800 | tf_op jit(solution)/shard_map/dot_general | solution.py:18
  248.1 1.8 collective-permute-start.7
  249.8 51.7 %collective-permute-done.13.refs_12_ = bf16[2,4,64,1280]{3,2,1,0:T(8,128)(2,1)S(1)} collective-permute-done((bf16[2,4,64,1280]{3,2,1,0:T(8,128)(2,1)}, bf16[2,4,64,1280]{3,2,1,0:T(8,128)(2,1)S(1)}, u32[]{:S(2)}, u32[]{:S(2)}) %collective-permute-start.13) | collective-permute-done | bytes 1310752 | tf_op jit(solution)/shard_map/ppermute | solution.py:131
  302.6 1.3 copy-done.2
  303.9 15.9 %attention_backward.2 = (bf16[2,256,640]{2,1,0:T(8,128)(2,1)S(1)}, f32[2,256,640]{2,1,0:T(8,128)S(1)}, f32[2,256,640]{2,1,0:T(8,128)S(1)}, bf16[2,256,640]{2,1,0:T(8,128)(2,1)S(1)}, bf16[2,256,640]{2,1,0:T(8,128)(2,1)S(1)}) custom-call(s32[6]{0:T(128)S(1)} %pad_add_fusion.1.scal, bf16[1,2,64,5120]{3,2,1,0:T(8,128)(2,1)S(1)} %copy-done.2, ...), custom_call_target="tpu_custom_call" | custom-call | flops 2516582400 | bytes 10485760 | tf_op jit(solution)/shard_map/attention_backward/pallas_call | solution.py:99
  324.7 16.5 %attention_backward.3 = (bf16[2,256,640]{2,1,0:T(8,128)(2,1)S(1)}, f32[2,256,640]{2,1,0:T(8,128)S(1)}, f32[2,256,640]{2,1,0:T(8,128)S(1)}, bf16[2,256,640]{2,1,0:T(8,128)(2,1)}, bf16[2,256,640]{2,1,0:T(8,128)(2,1)}) custom-call(s32[6]{0:T(128)S(1)} %pad_add_fusion.1.scal, bf16[1,2,64,5120]{3,2,1,0:T(8,128)(2,1)S(1)} %copy-done.2, ...), custom_call_target="tpu_custom_call" | custom-call | flops 2516582400 | bytes 10485760 | tf_op jit(solution)/shard_map/attention_backward/pallas_call | solution.py:99
  344.1 2.2 collective-permute-start.16
  346.3 2.4 collective-permute-start.17
  348.9 3.1 collective-permute-start.14
  352.0 1.9 collective-permute-start.15
  353.9 2.4 maximum_bitcast_fusion
  356.4 2.2 collective-permute-done.17
  358.5 1.5 add_convert_fusion.5
  361.2 4.3 %collective-permute-done.15 = bf16[2,256,640]{2,1,0:T(8,128)(2,1)S(1)} collective-permute-done((bf16[2,256,640]{2,1,0:T(8,128)(2,1)}, bf16[2,256,640]{2,1,0:T(8,128)(2,1)S(1)}, u32[]{:S(2)}, u32[]{:S(2)}) %collective-permute-start.15) | collective-permute-done | bytes 655392 | tf_op jit(solution)/shard_map/ppermute | solution.py:131
  365.8 1.2 maximum_bitcast_fusion.1
  366.9 1.2 maximum_bitcast_fusion.2
  368.1 13.7 %weight_gradient.1 = f32[1280,640]{1,0:T(8,128)} custom-call(s32[2,4]{1,0:T(2,128)S(1)} %pad_add_fusion.table, bf16[4,512,1280]{2,1,0:T(8,128)(2,1)} %pad_maximum_fusion.near_ref, bf16[4,512,1280]{2,1,0:T(8,128)(2,1)} %collective-permute-done.20.far_ref, bf16[8,512,640]{2,1,0:T(8,128)(2,1)} %all-to-all-done.g_near.g_far, ...), custom_call_target="tpu_custom_call" | custom-call | flops 6710886400 | bytes 19005440 | tf_op jit(solution)/shard_map/weight_gradient/pallas_call | solution.py:162
  (91 shorter events, 25.3 us)
Async XLA Ops:
  7.2 205.6 %all-gather.2.cloned.1.call-start = ((), (), s32[]{:S(2)}) async-start(), calls=%async_computation.1 | async-start | bytes 6553600 | tf_op jit(solution)/shard_map/all_gather | solution.py:212
  16.1 6.3 %copy-start = (bf16[1,2,64,5120]{3,2,1,0:T(8,128)(2,1)S(1)}, bf16[1,2,64,5120]{3,2,1,0:T(8,128)(2,1)}, u32[]{:S(2)}) copy-start(bf16[1,2,64,5120]{3,2,1,0:T(8,128)(2,1)} %refs_1_.3) | copy-start | bytes 3932164
  18.6 34.8 %collective-permute-start.1 = (bf16[2,64,1280]{2,1,0:T(8,128)(2,1)}, bf16[2,64,1280]{2,1,0:T(8,128)(2,1)}, u32[]{:S(2)}, u32[]{:S(2)}) collective-permute-start(bf16[2,64,1280]{2,1,0:T(8,128)(2,1)} %get-tuple-element.81), channel_id=1, source_target_pairs={{0,4},{2,6},{4,0},{6,2},{1,5},{3,7},{5,1},{7,3},{8,12},{10,14},{12... | collective-permute-start | bytes 983048 | tf_op jit(solution)/shard_map/ppermute | solution.py:136
  20.9 63.6 %collective-permute-start = (bf16[2,64,1280]{2,1,0:T(8,128)(2,1)}, bf16[2,64,1280]{2,1,0:T(8,128)(2,1)}, u32[]{:S(2)}, u32[]{:S(2)}) collective-permute-start(bf16[2,64,1280]{2,1,0:T(8,128)(2,1)} %get-tuple-element.82), channel_id=1, source_target_pairs={{0,2},{2,4},{4,6},{6,0},{1,3},{3,5},{5,7},{7,1},{8,10},{10,12},{12... | collective-permute-start | bytes 983048 | tf_op jit(solution)/shard_map/ppermute | solution.py:136
  20.9 66.8 %collective-permute-start.2 = (bf16[2,64,1280]{2,1,0:T(8,128)(2,1)}, bf16[2,64,1280]{2,1,0:T(8,128)(2,1)}, u32[]{:S(2)}, u32[]{:S(2)}) collective-permute-start(bf16[2,64,1280]{2,1,0:T(8,128)(2,1)} %get-tuple-element.83), channel_id=1, source_target_pairs={{0,6},{2,0},{4,2},{6,4},{1,7},{3,1},{5,3},{7,5},{8,14},{10,8},{12,... | collective-permute-start | bytes 983048 | tf_op jit(solution)/shard_map/ppermute | solution.py:136
  25.5 68.8 %copy-start.20 = (s32[8,2]{0,1:T(2,128)S(1)}, s32[8,2]{0,1:T(2,128)}, u32[]{:S(2)}) copy-start(s32[8,2]{0,1:T(2,128)} %param.17) | copy-start | bytes 196
  90.7 17.5 %collective-permute-start.18 = (bf16[1,512,1280]{2,1,0:T(8,128)(2,1)S(1)}, bf16[1,512,1280]{2,1,0:T(8,128)(2,1)}, u32[]{:S(2)}, u32[]{:S(2)}) collective-permute-start(bf16[1,512,1280]{2,1,0:T(8,128)(2,1)S(1)} %bitcast.123), channel_id=1, source_target_pairs={{0,1},{1,0},{2,3},{3,2},{4,5},{5,4},{6,7},{7,6},{8,9},{9,8},{10,11... | collective-permute-start | bytes 3932168 | tf_op jit(solution)/shard_map/ppermute | solution.py:144
  92.9 52.0 %collective-permute-start.3 = (bf16[2,2,64,1280]{3,2,1,0:T(8,128)(2,1)}, bf16[2,2,64,1280]{3,2,1,0:T(8,128)(2,1)S(1)}, u32[]{:S(2)}, u32[]{:S(2)}) collective-permute-start(bf16[2,2,64,1280]{3,2,1,0:T(8,128)(2,1)} %pad_maximum_fusion.4), channel_id=1, source_target_pairs={{0,2},{2,4},{4,6},{6,0},{1,3},{3,5},{5,7},{7,1},{8,10},{10,12},{12... | collective-permute-start | bytes 1966088 | tf_op jit(solution)/shard_map/ppermute | solution.py:136
  92.9 94.0 %collective-permute-start.4 = (bf16[2,2,64,1280]{3,2,1,0:T(8,128)(2,1)}, bf16[2,2,64,1280]{3,2,1,0:T(8,128)(2,1)}, u32[]{:S(2)}, u32[]{:S(2)}) collective-permute-start(bf16[2,2,64,1280]{3,2,1,0:T(8,128)(2,1)} %pad_maximum_fusion.5), channel_id=1, source_target_pairs={{0,4},{2,6},{4,0},{6,2},{1,5},{3,7},{5,1},{7,3},{8,12},{10,14},{12... | collective-permute-start | bytes 1966088 | tf_op jit(solution)/shard_map/ppermute | solution.py:136
  92.9 94.6 %collective-permute-start.5 = (bf16[2,2,64,1280]{3,2,1,0:T(8,128)(2,1)}, bf16[2,2,64,1280]{3,2,1,0:T(8,128)(2,1)}, u32[]{:S(2)}, u32[]{:S(2)}) collective-permute-start(bf16[2,2,64,1280]{3,2,1,0:T(8,128)(2,1)} %pad_maximum_fusion.6), channel_id=1, source_target_pairs={{0,6},{2,0},{4,2},{6,4},{1,7},{3,1},{5,3},{7,5},{8,14},{10,8},{12,... | collective-permute-start | bytes 1966088 | tf_op jit(solution)/shard_map/ppermute | solution.py:136
  111.2 96.5 %collective-permute-start.19 = (bf16[2,512,1280]{2,1,0:T(8,128)(2,1)}, bf16[2,512,1280]{2,1,0:T(8,128)(2,1)}, u32[]{:S(2)}, u32[]{:S(2)}) collective-permute-start(bf16[2,512,1280]{2,1,0:T(8,128)(2,1)} %pad_maximum_fusion.1), channel_id=1, source_target_pairs={{0,16},{8,24},{16,0},{24,8},{1,17},{9,25},{17,1},{25,9},{2,18},{10... | collective-permute-start | bytes 7864328 | tf_op jit(solution)/shard_map/ppermute | solution.py:144
  112.4 83.5 %copy-start.19 = (bf16[1,64,1280]{2,1,0:T(8,128)(2,1)S(1)}, bf16[1,64,1280]{2,1,0:T(8,128)(2,1)}, u32[]{:S(2)}) copy-start(bf16[1,64,1280]{2,1,0:T(8,128)(2,1)} %get-tuple-element.77) | copy-start | bytes 491524
  187.5 8.5 %copy-start.18 = (bf16[1,64,1280]{2,1,0:T(8,128)(2,1)S(1)}, bf16[1,64,1280]{2,1,0:T(8,128)(2,1)}, u32[]{:S(2)}) copy-start(bf16[1,64,1280]{2,1,0:T(8,128)(2,1)} %get-tuple-element.117) | copy-start | bytes 491524
  187.5 45.1 %collective-permute-start.9 = (bf16[2,64,640]{2,1,0:T(8,128)(2,1)}, bf16[2,64,640]{2,1,0:T(8,128)(2,1)S(1)}, u32[]{:S(2)}, u32[]{:S(2)}) collective-permute-start(bf16[2,64,640]{2,1,0:T(8,128)(2,1)} %get-tuple-element.42), channel_id=1, source_target_pairs={{0,2},{2,4},{4,6},{6,0},{1,3},{3,5},{5,7},{7,1},{8,10},{10,12},{12... | collective-permute-start | bytes 491528 | tf_op jit(solution)/shard_map/ppermute | solution.py:136
  187.5 60.4 %collective-permute-start.10 = (bf16[2,64,640]{2,1,0:T(8,128)(2,1)}, bf16[2,64,640]{2,1,0:T(8,128)(2,1)}, u32[]{:S(2)}, u32[]{:S(2)}) collective-permute-start(bf16[2,64,640]{2,1,0:T(8,128)(2,1)} %get-tuple-element.43), channel_id=1, source_target_pairs={{0,4},{2,6},{4,0},{6,2},{1,5},{3,7},{5,1},{7,3},{8,12},{10,14},{12... | collective-permute-start | bytes 491528 | tf_op jit(solution)/shard_map/ppermute | solution.py:136
  190.1 58.0 %collective-permute-start.11 = (bf16[2,64,640]{2,1,0:T(8,128)(2,1)}, bf16[2,64,640]{2,1,0:T(8,128)(2,1)}, u32[]{:S(2)}, u32[]{:S(2)}) collective-permute-start(bf16[2,64,640]{2,1,0:T(8,128)(2,1)} %get-tuple-element.44), channel_id=1, source_target_pairs={{0,6},{2,0},{4,2},{6,4},{1,7},{3,1},{5,3},{7,5},{8,14},{10,8},{12,... | collective-permute-start | bytes 491528 | tf_op jit(solution)/shard_map/ppermute | solution.py:136
  195.9 10.9 %copy-start.17 = (bf16[1,64,1280]{2,1,0:T(8,128)(2,1)S(1)}, bf16[1,64,1280]{2,1,0:T(8,128)(2,1)}, u32[]{:S(2)}) copy-start(bf16[1,64,1280]{2,1,0:T(8,128)(2,1)} %get-tuple-element.118) | copy-start | bytes 491524
  197.3 52.6 %collective-permute-start.12 = (bf16[2,4,64,1280]{3,2,1,0:T(8,128)(2,1)}, bf16[2,4,64,1280]{3,2,1,0:T(8,128)(2,1)}, u32[]{:S(2)}, u32[]{:S(2)}) collective-permute-start(bf16[2,4,64,1280]{3,2,1,0:T(8,128)(2,1)} %pad_maximum_fusion.2), channel_id=1, source_target_pairs={{0,8},{8,16},{16,24},{1,9},{9,17},{17,25},{2,10},{10,18},{18,26},{... | collective-permute-start | bytes 3932168 | tf_op jit(solution)/shard_map/ppermute | solution.py:131
  212.7 155.4 %collective-permute-start.20 = (bf16[4,512,1280]{2,1,0:T(8,128)(2,1)}, bf16[4,512,1280]{2,1,0:T(8,128)(2,1)}, u32[]{:S(2)}, u32[]{:S(2)}) collective-permute-start(bf16[4,512,1280]{2,1,0:T(8,128)(2,1)} %pad_maximum_fusion.near_ref), channel_id=1, source_target_pairs={{0,8},{8,0},{16,24},{24,16},{1,9},{9,1},{17,25},{25,17},{2,10},{10... | collective-permute-start | bytes 15728648 | tf_op jit(solution)/shard_map/ppermute | solution.py:144
  212.7 8.1 %copy-start.16 = (bf16[4,2,64,5120]{3,2,1,0:T(8,128)(2,1)S(1)}, bf16[4,2,64,5120]{3,2,1,0:T(8,128)(2,1)}, u32[]{:S(2)}) copy-start(bf16[4,2,64,5120]{3,2,1,0:T(8,128)(2,1)} %all-gather.2.cloned.1.call-done) | copy-start | bytes 15728644
  224.6 143.5 %all-to-all-start = ((bf16[8,512,640]{2,1,0:T(8,128)(2,1)}), bf16[8,512,640]{2,1,0:T(8,128)(2,1)}, u32[]{:S(2)}, u32[]{:S(2)}) async-start(bf16[8,512,640]{2,1,0:T(8,128)(2,1)} %fusion), calls=%async_computation | async-start | bytes 10485760 | tf_op jit(solution)/shard_map/all_to_all | solution.py:242
  232.7 70.0 %copy-start.1 = (bf16[1,2,64,5120]{3,2,1,0:T(8,128)(2,1)S(1)}, bf16[1,2,64,5120]{3,2,1,0:T(8,128)(2,1)}, u32[]{:S(2)}) copy-start(bf16[1,2,64,5120]{3,2,1,0:T(8,128)(2,1)} %refs_2_.3) | copy-start | bytes 3932164
  232.7 68.9 %collective-permute-start.13 = (bf16[2,4,64,1280]{3,2,1,0:T(8,128)(2,1)}, bf16[2,4,64,1280]{3,2,1,0:T(8,128)(2,1)S(1)}, u32[]{:S(2)}, u32[]{:S(2)}) collective-permute-start(bf16[2,4,64,1280]{3,2,1,0:T(8,128)(2,1)} %pad_maximum_fusion.3), channel_id=1, source_target_pairs={{8,0},{16,8},{24,16},{9,1},{17,9},{25,17},{10,2},{18,10},{26,18},{... | collective-permute-start | bytes 3932168 | tf_op jit(solution)/shard_map/ppermute | solution.py:131
  248.0 76.7 %collective-permute-start.6 = (bf16[2,64,640]{2,1,0:T(8,128)(2,1)}, bf16[2,64,640]{2,1,0:T(8,128)(2,1)S(1)}, u32[]{:S(2)}, u32[]{:S(2)}) collective-permute-start(bf16[2,64,640]{2,1,0:T(8,128)(2,1)} %get-tuple-element.36), channel_id=1, source_target_pairs={{0,2},{2,4},{4,6},{6,0},{1,3},{3,5},{5,7},{7,1},{8,10},{10,12},{12... | collective-permute-start | bytes 491528 | tf_op jit(solution)/shard_map/ppermute | solution.py:136
  248.1 76.6 %collective-permute-start.7 = (bf16[2,64,640]{2,1,0:T(8,128)(2,1)}, bf16[2,64,640]{2,1,0:T(8,128)(2,1)S(1)}, u32[]{:S(2)}, u32[]{:S(2)}) collective-permute-start(bf16[2,64,640]{2,1,0:T(8,128)(2,1)} %get-tuple-element.37), channel_id=1, source_target_pairs={{0,4},{2,6},{4,0},{6,2},{1,5},{3,7},{5,1},{7,3},{8,12},{10,14},{12... | collective-permute-start | bytes 491528 | tf_op jit(solution)/shard_map/ppermute | solution.py:136
  249.8 74.8 %collective-permute-start.8 = (bf16[2,64,640]{2,1,0:T(8,128)(2,1)}, bf16[2,64,640]{2,1,0:T(8,128)(2,1)S(1)}, u32[]{:S(2)}, u32[]{:S(2)}) collective-permute-start(bf16[2,64,640]{2,1,0:T(8,128)(2,1)} %get-tuple-element.38), channel_id=1, source_target_pairs={{0,6},{2,0},{4,2},{6,4},{1,7},{3,1},{5,3},{7,5},{8,14},{10,8},{12,... | collective-permute-start | bytes 491528 | tf_op jit(solution)/shard_map/ppermute | solution.py:136
  301.6 1.1 copy-start.15
  302.6 1.3 copy-start.2
  319.8 1.1 copy-start.3
  320.9 1.1 copy-start.5
  322.0 0.9 copy-start.11
  322.9 0.9 copy-start.13
  323.7 0.9 copy-start.14
  341.1 1.1 copy-start.7
  342.2 1.1 copy-start.9
  343.3 0.9 copy-start.12
  344.1 14.4 %copy-start.8 = (f32[2,256,640]{2,1,0:T(8,128)S(1)}, f32[2,256,640]{2,1,0:T(8,128)}, u32[]{:S(2)}) copy-start(f32[2,256,640]{2,1,0:T(8,128)} %copy-done.7) | copy-start | bytes 3932164
  344.1 14.4 %copy-start.10 = (f32[2,256,640]{2,1,0:T(8,128)S(1)}, f32[2,256,640]{2,1,0:T(8,128)}, u32[]{:S(2)}) copy-start(f32[2,256,640]{2,1,0:T(8,128)} %copy-done.9) | copy-start | bytes 3932164
  344.1 12.2 %collective-permute-start.16 = (bf16[2,256,640]{2,1,0:T(8,128)(2,1)}, bf16[2,256,640]{2,1,0:T(8,128)(2,1)S(1)}, u32[]{:S(2)}, u32[]{:S(2)}) collective-permute-start(bf16[2,256,640]{2,1,0:T(8,128)(2,1)} %get-tuple-element.58), channel_id=1, source_target_pairs={{0,8},{8,16},{16,24},{1,9},{9,17},{17,25},{2,10},{10,18},{18,26},{... | collective-permute-start | bytes 1966088 | tf_op jit(solution)/shard_map/ppermute | solution.py:131
  346.3 12.2 %collective-permute-start.17 = (bf16[2,256,640]{2,1,0:T(8,128)(2,1)}, bf16[2,256,640]{2,1,0:T(8,128)(2,1)}, u32[]{:S(2)}, u32[]{:S(2)}) collective-permute-start(bf16[2,256,640]{2,1,0:T(8,128)(2,1)} %get-tuple-element.59), channel_id=1, source_target_pairs={{8,0},{16,8},{24,16},{9,1},{17,9},{25,17},{10,2},{18,10},{26,18},{... | collective-permute-start | bytes 1966088 | tf_op jit(solution)/shard_map/ppermute | solution.py:131
  348.9 12.3 %collective-permute-start.14 = (bf16[2,256,640]{2,1,0:T(8,128)(2,1)}, bf16[2,256,640]{2,1,0:T(8,128)(2,1)S(1)}, u32[]{:S(2)}, u32[]{:S(2)}) collective-permute-start(bf16[2,256,640]{2,1,0:T(8,128)(2,1)} %copy-done.14), channel_id=1, source_target_pairs={{0,8},{8,16},{16,24},{1,9},{9,17},{17,25},{2,10},{10,18},{18,26},{... | collective-permute-start | bytes 1966088 | tf_op jit(solution)/shard_map/ppermute | solution.py:131
  352.0 13.5 %collective-permute-start.15 = (bf16[2,256,640]{2,1,0:T(8,128)(2,1)}, bf16[2,256,640]{2,1,0:T(8,128)(2,1)S(1)}, u32[]{:S(2)}, u32[]{:S(2)}) collective-permute-start(bf16[2,256,640]{2,1,0:T(8,128)(2,1)} %copy-done.13), channel_id=1, source_target_pairs={{8,0},{16,8},{24,16},{9,1},{17,9},{25,17},{10,2},{18,10},{26,18},{... | collective-permute-start | bytes 1966088 | tf_op jit(solution)/shard_map/ppermute | solution.py:131
  358.5 6.9 %copy-start.4 = (f32[2,256,640]{2,1,0:T(8,128)S(1)}, f32[2,256,640]{2,1,0:T(8,128)}, u32[]{:S(2)}) copy-start(f32[2,256,640]{2,1,0:T(8,128)} %copy-done.3) | copy-start | bytes 3932164
  358.5 6.9 %copy-start.6 = (f32[2,256,640]{2,1,0:T(8,128)S(1)}, f32[2,256,640]{2,1,0:T(8,128)}, u32[]{:S(2)}) copy-start(f32[2,256,640]{2,1,0:T(8,128)} %copy-done.5) | copy-start | bytes 3932164
Sparse Core Ops, SparseCore 0:
  16.3 166.8 all-gather.1

commit v4 on v3

--- a/solution.py
+++ b/solution.py
@@ -183,6 +183,49 @@
     )(table, near, far, gated, gated)
 
 
+def project_kernel(g_ref, w_ref, out_ref, acc_ref):
+    step = pl.program_id(0)
+    term = dot(g_ref[0], w_ref[...], NT)
+
+    @pl.when(step == 0)
+    def _():
+        acc_ref[...] = term
+
+    @pl.when(step > 0)
+    def _():
+        acc_ref[...] += term
+
+    @pl.when(step == pl.num_programs(0) - 1)
+    def _():
+        out_ref[...] = acc_ref[...].astype(out_ref.dtype)
+
+
+def project(gated, weight):
+    blocks, rows, columns = gated.shape
+    width = weight.shape[0]
+    if columns % 128:
+        whole = gated.transpose(1, 0, 2).reshape(rows, blocks * columns)
+        return dot(whole, weight, NT).astype(jnp.bfloat16)
+    return pl.pallas_call(
+        project_kernel,
+        grid=(blocks,),
+        in_specs=[
+            pl.BlockSpec((1, rows, columns), lambda b: (b, 0, 0)),
+            pl.BlockSpec((width, columns), lambda b: (0, b)),
+        ],
+        out_specs=pl.BlockSpec((rows, width), lambda b: (0, 0)),
+        out_shape=jax.ShapeDtypeStruct((rows, width), jnp.bfloat16),
+        scratch_shapes=[pltpu.VMEM((rows, width), jnp.float32)],
+        compiler_params=pltpu.CompilerParams(vmem_limit_bytes=40 * 2**20),
+        cost_estimate=pl.CostEstimate(
+            flops=2 * rows * width * blocks * columns,
+            bytes_accessed=2 * (rows + width) * blocks * columns + 2 * rows * width,
+            transcendentals=0,
+        ),
+        name="project_gated",
+    )(gated, weight)
+
+
 def per_device(
     queries, key_rows, value_rows, saved_out, cotangent, out_weight, gate_table, levels, reach_flags
 ):
@@ -209,12 +252,14 @@
         [lax.dynamic_slice_in_dim(gate_table, levels[f], 1, axis=0) for f in range(frames)], axis=0
     )
     gated = (cotangent[0].astype(jnp.float32) * gain[:, None, :]).astype(jnp.bfloat16)
-    gathered = lax.all_gather(gated, "head", axis=0, tiled=False).reshape(-1, model)
+    gated = gated.reshape(frames * rows, model)
+    gated = jnp.stack([gated[:, b * block : (b + 1) * block] for b in range(blocks)])
+    gathered = lax.all_gather(gated, "head", axis=1, tiled=True)
 
     kv_send = [
         jnp.stack([columns_for(a, s, 0, width) for a in (key_rows, value_rows)]) for s in shifts
     ]
-    kv_send, o_pieces = after(kv_send, o_pieces)
+    kv_send, gathered = after(kv_send, gathered)
     kv = [rotated(a, "head", s) for s, a in zip(shifts, kv_send)]
 
     o = jnp.zeros((parts, frames, rows, width), jnp.bfloat16)
@@ -238,12 +283,11 @@
         ]
     ).astype(jnp.int32)
 
-    gated_out = jnp.stack([gathered[:, b * block : (b + 1) * block] for b in range(blocks)])
     gated_in = lax.all_to_all(
-        gated_out, ("frame", "fsdp"), split_axis=0, concat_axis=0, tiled=True
+        gathered, ("frame", "fsdp"), split_axis=0, concat_axis=0, tiled=True
     )
     d_weight = weight_grad(table, near, far, gated_in, 1.0 / tokens_all)
-    d = dot(gathered, out_weight, NT).astype(jnp.bfloat16).reshape(parts, frames, rows, width)
+    d = project(gathered, out_weight)
 
     first = (heads + 1) // 2
     groups = [(0, first), (first, heads - first)]
@@ -251,7 +295,9 @@
         [columns_for(queries, s, head0 * HD, count * HD) for s in shifts]
         for head0, count in groups
     ]
-    q_send, kv = after(q_send, kv)
+    q_send, d = after(q_send, d)
+    kv, d = after(kv, d)
+    d = d.reshape(parts, frames, rows, width)
     q_pieces = [[rotated(a, "head", s) for s, a in zip(shifts, sends)] for sends in q_send]
 
     ids = first_frame + jnp.arange(frames, dtype=jnp.int32)
@@ -270,6 +316,7 @@
     from_prev = shifted(boundary(frames - 1), "frame", 1)
     from_next = shifted(boundary(0), "frame", -1)
     local = (queries, key_rows, value_rows)
+    scal, d_weight = after(scal, d_weight)
     results = []
     for (head0, count), q_group in zip(groups, q_pieces):
         if results:

time: 390 us -> 345 us (0.88)
  waiting for transfers between devices: 207 us -> 165 us
  starting transfers between devices: 38.8 us -> 70.6 us
  local copies, waits for them, and re-layouts: 39.9 us -> 12.6 us
  Pallas kernels: 46 us -> 59.4 us
  matrix products: 12.7 us -> 0 us
  other arithmetic: 26 us -> 15.6 us
    ppermute x3, waiting for transfers between devices: 13.6 us -> 70.5 us  [flipped(): lax.ppermute(array, axis, [(i, i ^ bit) for i in range(lax.axis_size(axis...]
    ppermute x6, waiting for transfers between devices: 59.3 us -> 9.97 us  [shifted(): return lax.ppermute(array, axis, pairs)]
    ppermute x12, waiting for transfers between devices: 134 us -> 84.8 us  [rotated(): lax.ppermute(array, axis, [(i, (i + step) % count) for i in range(count)])]
    ppermute x12, starting transfers between devices: 11 us -> 36.5 us  [rotated(): lax.ppermute(array, axis, [(i, (i + step) % count) for i in range(count)])]
    unnamed x49 -> x43, local copies, waits for them, and re-layouts: 21.1 us -> 5.74 us
    pallas_call x0 -> x1, Pallas kernels: none -> 13.3 us  [project(): pl.pallas_call(project_kernel, grid=(blocks,), in_specs=[pl.BlockSpec((1,...]
    dot_general x1 -> x0, matrix products: 12.7 us -> none  [dot(): return lax.dot_general(lhs, rhs, dims, preferred_element_type=jnp.float32)]
    ppermute x3, starting transfers between devices: 1.42 us -> 10.9 us  [flipped(): lax.ppermute(array, axis, [(i, i ^ bit) for i in range(lax.axis_size(axis...]
  transfers between devices with their start and end apart: 23 -> 23, of which waited for: 11 -> 9; matrix products, arithmetic and copies ran while one was open for 16% -> 5% of each run, Pallas kernels for 8% -> 13%
where the time goes in v4:
time: 345 us; the launch traced here: 342 us
  waiting for transfers between devices  165 us (48%)
  starting transfers between devices  70.6 us (20%)
  Pallas kernels  59.4 us (17%)
  between operations  18.5 us (5%)
  other arithmetic  15.6 us (5%)
  local copies, waits for them, and re-layouts  12.6 us (4%)
    ppermute x12, waiting for transfers between devices, rotated(): lax.ppermute(array, axis, [(i, (i + step) % count) for i in range(count)])  84.8 us
    ppermute x3, waiting for transfers between devices, flipped(): lax.ppermute(array, axis, [(i, i ^ bit) for i in range(lax.axis_size(axis...  70.5 us
    ppermute x12, starting transfers between devices, rotated(): lax.ppermute(array, axis, [(i, (i + step) % count) for i in range(count)])  36.5 us
    pallas_call x2, Pallas kernels, attention(): pl.pallas_call(partial(attention_kernel, parts), grid_spec=pltpu.Prefetch...  32 us
    ppermute x6, starting transfers between devices, shifted(): return lax.ppermute(array, axis, pairs)  18.5 us
    pallas_call x1, Pallas kernels, weight_grad(): pl.pallas_call(partial(weight_kernel, scale), grid_spec=pltpu.PrefetchSca...  14 us
    pallas_call x1, Pallas kernels, project(): pl.pallas_call(project_kernel, grid=(blocks,), in_specs=[pl.BlockSpec((1,...  13.3 us
    ppermute x3, starting transfers between devices, flipped(): lax.ppermute(array, axis, [(i, i ^ bit) for i in range(lax.axis_size(axis...  10.9 us
  transfers between devices with their start and end apart: 23, of which 9 were waited for; matrix products, arithmetic and copies ran while one was open for 5% of the time, Pallas kernels for 13%

profile of v4, /device:TPU:11, one launch (start us, length us, event | category | flops | bytes accessed | tf_op | source)
XLA Modules:
  0.0 342.0 jit_solution(12537117310115047064)
XLA Ops:
  7.2 1.3 fusion.11
  12.4 1.0 constant_dynamic-slice_fusion.2
  13.5 1.6 fusion
  15.3 1.0 copy-done.12
  16.6 1.2 copy-done.13
  17.7 0.8 dynamic-slice_bitcast_fusion
  18.6 1.3 collective-permute-start.3
  20.0 2.3 collective-permute-start.4
  22.3 5.0 %collective-permute-done.3 = bf16[2,64,1280]{2,1,0:T(8,128)(2,1)S(1)} collective-permute-done((bf16[2,64,1280]{2,1,0:T(8,128)(2,1)}, bf16[2,64,1280]{2,1,0:T(8,128)(2,1)S(1)}, u32[]{:S(2)}, u32[]{:S(2)}) %collective-permute-start.3) | collective-permute-done | bytes 327712 | tf_op jit(solution)/shard_map/ppermute | solution.py:136
  27.4 40.6 %collective-permute-done.4 = bf16[2,64,1280]{2,1,0:T(8,128)(2,1)S(1)} collective-permute-done((bf16[2,64,1280]{2,1,0:T(8,128)(2,1)S(1)}, bf16[2,64,1280]{2,1,0:T(8,128)(2,1)S(1)}, u32[]{:S(2)}, u32[]{:S(2)}) %collective-permute-start.4) | collective-permute-done | bytes 327712 | tf_op jit(solution)/shard_map/ppermute | solution.py:136
  68.4 22.7 %collective-permute-done.6 = bf16[1,512,1280]{2,1,0:T(8,128)(2,1)S(1)} collective-permute-done((bf16[1,512,1280]{2,1,0:T(8,128)(2,1)S(1)}, bf16[1,512,1280]{2,1,0:T(8,128)(2,1)S(1)}, u32[]{:S(2)}, u32[]{:S(2)}) %collective-permute-start.6) | collective-permute-done | bytes 1310752 | tf_op jit(solution)/shard_map/ppermute | solution.py:144
  91.3 1.3 collective-permute-start.7
  92.7 1.0 constant_dynamic-slice_fusion.3
  93.7 47.8 %collective-permute-done.7 = bf16[2,512,1280]{2,1,0:T(8,128)(2,1)S(1)} collective-permute-done((bf16[2,512,1280]{2,1,0:T(8,128)(2,1)S(1)}, bf16[2,512,1280]{2,1,0:T(8,128)(2,1)S(1)}, u32[]{:S(2)}, u32[]{:S(2)}) %collective-permute-start.7) | collective-permute-done | bytes 2621472 | tf_op jit(solution)/shard_map/ppermute | solution.py:144
  141.5 2.9 pad_maximum_fusion.near_ref
  144.4 9.1 %collective-permute-start.8 = (bf16[4,512,1280]{2,1,0:T(8,128)(2,1)}, bf16[4,512,1280]{2,1,0:T(8,128)(2,1)}, u32[]{:S(2)}, u32[]{:S(2)}) collective-permute-start(bf16[4,512,1280]{2,1,0:T(8,128)(2,1)} %pad_maximum_fusion.near_ref), channel_id=1, source_target_pairs={{0,8},{8,0},{16,24},{24,16},{1,9},{9,1},{17,25},{25,17},{2,10},{10... | collective-permute-start | bytes 15728648 | tf_op jit(solution)/shard_map/ppermute | solution.py:144
  153.6 0.9 pad_maximum_fusion.6
  154.5 2.0 pad_maximum_fusion.5
  156.4 0.9 pad_maximum_fusion.4
  157.3 4.8 %all-to-all-start = ((bf16[8,512,640]{2,1,0:T(8,128)(2,1)}), bf16[8,512,640]{2,1,0:T(8,128)(2,1)}, u32[]{:S(2)}, u32[]{:S(2)}) async-start(bf16[8,512,640]{2,1,0:T(8,128)(2,1)} %all-gather.2.cloned.1.call-done.g_ref), calls=%async_computation | async-start | bytes 10485760 | tf_op jit(solution)/shard_map/all_to_all | solution.py:286
  162.1 1.2 dynamic-slice_bitcast_fusion.3
  163.2 22.8 %collective-permute-start.9 = (bf16[2,2,64,1280]{3,2,1,0:T(8,128)(2,1)}, bf16[2,2,64,1280]{3,2,1,0:T(8,128)(2,1)S(1)}, u32[]{:S(2)}, u32[]{:S(2)}) collective-permute-start(bf16[2,2,64,1280]{3,2,1,0:T(8,128)(2,1)} %pad_maximum_fusion.4), channel_id=1, source_target_pairs={{0,2},{2,4},{4,6},{6,0},{1,3},{3,5},{5,7},{7,1},{8,10},{10,12},{12... | collective-permute-start | bytes 1966088 | tf_op jit(solution)/shard_map/ppermute | solution.py:136
  186.0 4.2 %collective-permute-start.10 = (bf16[2,2,64,1280]{3,2,1,0:T(8,128)(2,1)}, bf16[2,2,64,1280]{3,2,1,0:T(8,128)(2,1)S(1)}, u32[]{:S(2)}, u32[]{:S(2)}) collective-permute-start(bf16[2,2,64,1280]{3,2,1,0:T(8,128)(2,1)} %pad_maximum_fusion.5), channel_id=1, source_target_pairs={{0,4},{2,6},{4,0},{6,2},{1,5},{3,7},{5,1},{7,3},{8,12},{10,14},{12... | collective-permute-start | bytes 1966088 | tf_op jit(solution)/shard_map/ppermute | solution.py:136
  190.2 1.0 dynamic-slice_bitcast_fusion.7
  191.2 2.5 copy-done.11
  193.7 13.3 %project_gated.1 = bf16[512,1280]{1,0:T(8,128)(2,1)S(1)} custom-call(bf16[8,512,640]{2,1,0:T(8,128)(2,1)S(1)} %copy-done.11, bf16[1280,5120]{1,0:T(8,128)(2,1)} %w_ref.1), custom_call_target="tpu_custom_call" | custom-call | flops 6710886400 | bytes 19660800 | tf_op jit(solution)/shard_map/project_gated/pallas_call | solution.py:209
  207.0 35.2 %collective-permute-done.10.refs_4_ = bf16[2,2,64,1280]{3,2,1,0:T(8,128)(2,1)S(1)} collective-permute-done((bf16[2,2,64,1280]{3,2,1,0:T(8,128)(2,1)}, bf16[2,2,64,1280]{3,2,1,0:T(8,128)(2,1)S(1)}, u32[]{:S(2)}, u32[]{:S(2)}) %collective-permute-start.10) | collective-permute-done | bytes 655392 | tf_op jit(solution)/shard_map/ppermute | solution.py:136
  242.2 4.0 %collective-permute-done.11.refs_5_ = bf16[2,2,64,1280]{3,2,1,0:T(8,128)(2,1)S(1)} collective-permute-done((bf16[2,2,64,1280]{3,2,1,0:T(8,128)(2,1)}, bf16[2,2,64,1280]{3,2,1,0:T(8,128)(2,1)S(1)}, u32[]{:S(2)}, u32[]{:S(2)}) %collective-permute-start.11) | collective-permute-done | bytes 655392 | tf_op jit(solution)/shard_map/ppermute | solution.py:136
  247.4 1.2 pad_maximum_fusion.2
  248.6 4.2 %collective-permute-start.15 = (bf16[2,4,64,1280]{3,2,1,0:T(8,128)(2,1)}, bf16[2,4,64,1280]{3,2,1,0:T(8,128)(2,1)}, u32[]{:S(2)}, u32[]{:S(2)}) collective-permute-start(bf16[2,4,64,1280]{3,2,1,0:T(8,128)(2,1)} %pad_maximum_fusion.2), channel_id=1, source_target_pairs={{0,8},{8,16},{16,24},{1,9},{9,17},{17,25},{2,10},{10,18},{18,26},{... | collective-permute-start | bytes 3932168 | tf_op jit(solution)/shard_map/ppermute | solution.py:131
  253.0 1.2 pad_maximum_fusion.3
  254.1 1.9 collective-permute-start.16
  256.7 1.4 collective-permute-start.14
  258.1 14.0 %weight_gradient.1 = f32[1280,640]{1,0:T(8,128)} custom-call(s32[2,4]{1,0:T(2,128)S(1)} %pad_add_fusion.table, bf16[4,512,1280]{2,1,0:T(8,128)(2,1)} %pad_maximum_fusion.near_ref, bf16[4,512,1280]{2,1,0:T(8,128)(2,1)} %collective-permute-done.8.far_ref, bf16[8,512,640]{2,1,0:T(8,128)(2,1)} %all-to-all-done.g_near.g_far, ...), custom_call_target="tpu_custom_call" | custom-call | flops 6710886400 | bytes 19005440 | tf_op jit(solution)/shard_map/weight_gradient/pallas_call | solution.py:162
  272.2 1.3 collective-permute-start
  273.4 3.0 collective-permute-start.1
  276.5 16.0 %attention_backward.2 = (bf16[2,256,640]{2,1,0:T(8,128)(2,1)S(1)}, f32[2,256,640]{2,1,0:T(8,128)S(1)}, f32[2,256,640]{2,1,0:T(8,128)S(1)}, bf16[2,256,640]{2,1,0:T(8,128)(2,1)S(1)}, bf16[2,256,640]{2,1,0:T(8,128)(2,1)S(1)}) custom-call(s32[6]{0:T(128)S(1)} %pad_add_fusion.1.scal, bf16[1,2,64,5120]{3,2,1,0:T(8,128)(2,1)S(1)} %copy-done.4, ...), custom_call_target="tpu_custom_call" | custom-call | flops 2516582400 | bytes 10485760 | tf_op jit(solution)/shard_map/attention_backward/pallas_call | solution.py:99
  292.6 16.1 %attention_backward.3 = (bf16[2,256,640]{2,1,0:T(8,128)(2,1)S(1)}, f32[2,256,640]{2,1,0:T(8,128)S(1)}, f32[2,256,640]{2,1,0:T(8,128)S(1)}, bf16[2,256,640]{2,1,0:T(8,128)(2,1)S(1)}, bf16[2,256,640]{2,1,0:T(8,128)(2,1)S(1)}) custom-call(s32[6]{0:T(128)S(1)} %pad_add_fusion.1.scal, bf16[1,2,64,5120]{3,2,1,0:T(8,128)(2,1)S(1)} %copy-done.4, ...), custom_call_target="tpu_custom_call" | custom-call | flops 2516582400 | bytes 10485760 | tf_op jit(solution)/shard_map/attention_backward/pallas_call | solution.py:99
  308.6 4.9 %collective-permute-start.19 = (bf16[2,256,640]{2,1,0:T(8,128)(2,1)S(1)}, bf16[2,256,640]{2,1,0:T(8,128)(2,1)S(1)}, u32[]{:S(2)}, u32[]{:S(2)}) collective-permute-start(bf16[2,256,640]{2,1,0:T(8,128)(2,1)S(1)} %get-tuple-element.61), channel_id=1, source_target_pairs={{0,8},{8,16},{16,24},{1,9},{9,17},{17,25},{2,10},{10,18},{18,26},{... | collective-permute-start | bytes 1966088 | tf_op jit(solution)/shard_map/ppermute | solution.py:131
  313.5 1.9 collective-permute-start.20
  315.4 3.6 %collective-permute-start.17 = (bf16[2,256,640]{2,1,0:T(8,128)(2,1)S(1)}, bf16[2,256,640]{2,1,0:T(8,128)(2,1)S(1)}, u32[]{:S(2)}, u32[]{:S(2)}) collective-permute-start(bf16[2,256,640]{2,1,0:T(8,128)(2,1)S(1)} %get-tuple-element.58), channel_id=1, source_target_pairs={{0,8},{8,16},{16,24},{1,9},{9,17},{17,25},{2,10},{10,18},{18,26},{... | collective-permute-start | bytes 1966088 | tf_op jit(solution)/shard_map/ppermute | solution.py:131
  319.1 1.9 collective-permute-start.18
  321.0 1.2 maximum_bitcast_fusion
  322.2 3.2 collective-permute-done.20
  325.7 2.3 collective-permute-done.17
  328.0 4.4 %collective-permute-done.18 = bf16[2,256,640]{2,1,0:T(8,128)(2,1)S(1)} collective-permute-done((bf16[2,256,640]{2,1,0:T(8,128)(2,1)S(1)}, bf16[2,256,640]{2,1,0:T(8,128)(2,1)S(1)}, u32[]{:S(2)}, u32[]{:S(2)}) %collective-permute-start.18) | collective-permute-done | bytes 655392 | tf_op jit(solution)/shard_map/ppermute | solution.py:131
  332.8 1.2 maximum_bitcast_fusion.1
  334.0 1.2 maximum_bitcast_fusion.2
  (85 shorter events, 3.9 us)
Async XLA Ops:
  7.2 150.2 %all-gather.2.cloned.1.call-start = ((), (), s32[]{:S(2)}) async-start(), calls=%async_computation.1 | async-start | bytes 6553600 | tf_op jit(solution)/shard_map/all_gather | solution.py:257
  15.3 1.1 copy-start.12
  16.4 1.3 copy-start.13
  18.6 8.8 %collective-permute-start.3 = (bf16[2,64,1280]{2,1,0:T(8,128)(2,1)}, bf16[2,64,1280]{2,1,0:T(8,128)(2,1)S(1)}, u32[]{:S(2)}, u32[]{:S(2)}) collective-permute-start(bf16[2,64,1280]{2,1,0:T(8,128)(2,1)} %get-tuple-element.97), channel_id=1, source_target_pairs={{0,2},{2,4},{4,6},{6,0},{1,3},{3,5},{5,7},{7,1},{8,10},{10,12},{12... | collective-permute-start | bytes 983048 | tf_op jit(solution)/shard_map/ppermute | solution.py:136
  19.9 48.1 %collective-permute-start.5 = (bf16[2,64,1280]{2,1,0:T(8,128)(2,1)S(1)}, bf16[2,64,1280]{2,1,0:T(8,128)(2,1)S(1)}, u32[]{:S(2)}, u32[]{:S(2)}) collective-permute-start(bf16[2,64,1280]{2,1,0:T(8,128)(2,1)S(1)} %get-tuple-element.96), channel_id=1, source_target_pairs={{0,6},{2,0},{4,2},{6,4},{1,7},{3,1},{5,3},{7,5},{8,14},{10,8},{12,... | collective-permute-start | bytes 983048 | tf_op jit(solution)/shard_map/ppermute | solution.py:136
  20.0 47.9 %collective-permute-start.4 = (bf16[2,64,1280]{2,1,0:T(8,128)(2,1)S(1)}, bf16[2,64,1280]{2,1,0:T(8,128)(2,1)S(1)}, u32[]{:S(2)}, u32[]{:S(2)}) collective-permute-start(bf16[2,64,1280]{2,1,0:T(8,128)(2,1)S(1)} %get-tuple-element.99), channel_id=1, source_target_pairs={{0,4},{2,6},{4,0},{6,2},{1,5},{3,7},{5,1},{7,3},{8,12},{10,14},{12... | collective-permute-start | bytes 983048 | tf_op jit(solution)/shard_map/ppermute | solution.py:136
  68.0 24.7 %copy-start = (bf16[1,2,64,5120]{3,2,1,0:T(8,128)(2,1)S(1)}, bf16[1,2,64,5120]{3,2,1,0:T(8,128)(2,1)}, u32[]{:S(2)}) copy-start(bf16[1,2,64,5120]{3,2,1,0:T(8,128)(2,1)} %refs_1_.3) | copy-start | bytes 3932164
  68.0 24.6 %copy-start.1 = (bf16[1,2,64,5120]{3,2,1,0:T(8,128)(2,1)S(1)}, bf16[1,2,64,5120]{3,2,1,0:T(8,128)(2,1)}, u32[]{:S(2)}) copy-start(bf16[1,2,64,5120]{3,2,1,0:T(8,128)(2,1)} %refs_2_.3) | copy-start | bytes 3932164
  68.0 23.0 %collective-permute-start.6 = (bf16[1,512,1280]{2,1,0:T(8,128)(2,1)S(1)}, bf16[1,512,1280]{2,1,0:T(8,128)(2,1)S(1)}, u32[]{:S(2)}, u32[]{:S(2)}) collective-permute-start(bf16[1,512,1280]{2,1,0:T(8,128)(2,1)S(1)} %bitcast.125), channel_id=1, source_target_pairs={{0,1},{1,0},{2,3},{3,2},{4,5},{5,4},{6,7},{7,6},{8,9},{9,8},{10,11... | collective-permute-start | bytes 3932168 | tf_op jit(solution)/shard_map/ppermute | solution.py:144
  91.3 50.2 %collective-permute-start.7 = (bf16[2,512,1280]{2,1,0:T(8,128)(2,1)S(1)}, bf16[2,512,1280]{2,1,0:T(8,128)(2,1)S(1)}, u32[]{:S(2)}, u32[]{:S(2)}) collective-permute-start(bf16[2,512,1280]{2,1,0:T(8,128)(2,1)S(1)} %pad_maximum_fusion.1), channel_id=1, source_target_pairs={{0,16},{8,24},{16,0},{24,8},{1,17},{9,25},{17,1},{25,9},{2,18},{10... | collective-permute-start | bytes 7864328 | tf_op jit(solution)/shard_map/ppermute | solution.py:144
  144.4 112.2 %collective-permute-start.8 = (bf16[4,512,1280]{2,1,0:T(8,128)(2,1)}, bf16[4,512,1280]{2,1,0:T(8,128)(2,1)}, u32[]{:S(2)}, u32[]{:S(2)}) collective-permute-start(bf16[4,512,1280]{2,1,0:T(8,128)(2,1)} %pad_maximum_fusion.near_ref), channel_id=1, source_target_pairs={{0,8},{8,0},{16,24},{24,16},{1,9},{9,1},{17,25},{25,17},{2,10},{10... | collective-permute-start | bytes 15728648 | tf_op jit(solution)/shard_map/ppermute | solution.py:144
  157.3 100.7 %all-to-all-start = ((bf16[8,512,640]{2,1,0:T(8,128)(2,1)}), bf16[8,512,640]{2,1,0:T(8,128)(2,1)}, u32[]{:S(2)}, u32[]{:S(2)}) async-start(bf16[8,512,640]{2,1,0:T(8,128)(2,1)} %all-gather.2.cloned.1.call-done.g_ref), calls=%async_computation | async-start | bytes 10485760 | tf_op jit(solution)/shard_map/all_to_all | solution.py:286
  162.1 28.1 %copy-start.3 = (bf16[1,2,64,5120]{3,2,1,0:T(8,128)(2,1)S(1)}, bf16[1,2,64,5120]{3,2,1,0:T(8,128)(2,1)}, u32[]{:S(2)}) copy-start(bf16[1,2,64,5120]{3,2,1,0:T(8,128)(2,1)} %refs_0_.3) | copy-start | bytes 3932164
  163.2 43.7 %collective-permute-start.9 = (bf16[2,2,64,1280]{3,2,1,0:T(8,128)(2,1)}, bf16[2,2,64,1280]{3,2,1,0:T(8,128)(2,1)S(1)}, u32[]{:S(2)}, u32[]{:S(2)}) collective-permute-start(bf16[2,2,64,1280]{3,2,1,0:T(8,128)(2,1)} %pad_maximum_fusion.4), channel_id=1, source_target_pairs={{0,2},{2,4},{4,6},{6,0},{1,3},{3,5},{5,7},{7,1},{8,10},{10,12},{12... | collective-permute-start | bytes 1966088 | tf_op jit(solution)/shard_map/ppermute | solution.py:136
  186.0 56.2 %collective-permute-start.10 = (bf16[2,2,64,1280]{3,2,1,0:T(8,128)(2,1)}, bf16[2,2,64,1280]{3,2,1,0:T(8,128)(2,1)S(1)}, u32[]{:S(2)}, u32[]{:S(2)}) collective-permute-start(bf16[2,2,64,1280]{3,2,1,0:T(8,128)(2,1)} %pad_maximum_fusion.5), channel_id=1, source_target_pairs={{0,4},{2,6},{4,0},{6,2},{1,5},{3,7},{5,1},{7,3},{8,12},{10,14},{12... | collective-permute-start | bytes 1966088 | tf_op jit(solution)/shard_map/ppermute | solution.py:136
  190.2 56.1 %collective-permute-start.11 = (bf16[2,2,64,1280]{3,2,1,0:T(8,128)(2,1)}, bf16[2,2,64,1280]{3,2,1,0:T(8,128)(2,1)S(1)}, u32[]{:S(2)}, u32[]{:S(2)}) collective-permute-start(bf16[2,2,64,1280]{3,2,1,0:T(8,128)(2,1)} %pad_maximum_fusion.6), channel_id=1, source_target_pairs={{0,6},{2,0},{4,2},{6,4},{1,7},{3,1},{5,3},{7,5},{8,14},{10,8},{12,... | collective-permute-start | bytes 1966088 | tf_op jit(solution)/shard_map/ppermute | solution.py:136
  191.2 2.5 copy-start.11
  207.0 39.4 %copy-start.9 = (bf16[512,1280]{1,0:T(8,128)(2,1)}, bf16[512,1280]{1,0:T(8,128)(2,1)S(1)}, u32[]{:S(2)}) copy-start(bf16[512,1280]{1,0:T(8,128)(2,1)S(1)} %project_gated.1) | copy-start | bytes 3932164
  242.2 4.1 %copy-start.5 = (bf16[2,2,64,1280]{3,2,1,0:T(8,128)(2,1)}, bf16[2,2,64,1280]{3,2,1,0:T(8,128)(2,1)S(1)}, u32[]{:S(2)}) copy-start(bf16[2,2,64,1280]{3,2,1,0:T(8,128)(2,1)S(1)} %collective-permute-done.10.refs_4_) | copy-start | bytes 1966084
  246.2 0.9 copy-start.7
  248.6 27.9 %collective-permute-start.15 = (bf16[2,4,64,1280]{3,2,1,0:T(8,128)(2,1)}, bf16[2,4,64,1280]{3,2,1,0:T(8,128)(2,1)}, u32[]{:S(2)}, u32[]{:S(2)}) collective-permute-start(bf16[2,4,64,1280]{3,2,1,0:T(8,128)(2,1)} %pad_maximum_fusion.2), channel_id=1, source_target_pairs={{0,8},{8,16},{16,24},{1,9},{9,17},{17,25},{2,10},{10,18},{18,26},{... | collective-permute-start | bytes 3932168 | tf_op jit(solution)/shard_map/ppermute | solution.py:131
  252.9 3.1 copy-start.17
  254.1 22.4 %collective-permute-start.16 = (bf16[2,4,64,1280]{3,2,1,0:T(8,128)(2,1)}, bf16[2,4,64,1280]{3,2,1,0:T(8,128)(2,1)}, u32[]{:S(2)}, u32[]{:S(2)}) collective-permute-start(bf16[2,4,64,1280]{3,2,1,0:T(8,128)(2,1)} %pad_maximum_fusion.3), channel_id=1, source_target_pairs={{8,0},{16,8},{24,16},{9,1},{17,9},{25,17},{10,2},{18,10},{26,18},{... | collective-permute-start | bytes 3932168 | tf_op jit(solution)/shard_map/ppermute | solution.py:131
  256.5 15.6 %collective-permute-start.12 = (bf16[2,64,640]{2,1,0:T(8,128)(2,1)}, bf16[2,64,640]{2,1,0:T(8,128)(2,1)S(1)}, u32[]{:S(2)}, u32[]{:S(2)}) collective-permute-start(bf16[2,64,640]{2,1,0:T(8,128)(2,1)} %get-tuple-element.47), channel_id=1, source_target_pairs={{0,2},{2,4},{4,6},{6,0},{1,3},{3,5},{5,7},{7,1},{8,10},{10,12},{12... | collective-permute-start | bytes 491528 | tf_op jit(solution)/shard_map/ppermute | solution.py:136
  256.6 16.9 %collective-permute-start.13 = (bf16[2,64,640]{2,1,0:T(8,128)(2,1)}, bf16[2,64,640]{2,1,0:T(8,128)(2,1)}, u32[]{:S(2)}, u32[]{:S(2)}) collective-permute-start(bf16[2,64,640]{2,1,0:T(8,128)(2,1)} %get-tuple-element.48), channel_id=1, source_target_pairs={{0,4},{2,6},{4,0},{6,2},{1,5},{3,7},{5,1},{7,3},{8,12},{10,14},{12... | collective-permute-start | bytes 491528 | tf_op jit(solution)/shard_map/ppermute | solution.py:136
  256.7 19.8 %collective-permute-start.14 = (bf16[2,64,640]{2,1,0:T(8,128)(2,1)}, bf16[2,64,640]{2,1,0:T(8,128)(2,1)}, u32[]{:S(2)}, u32[]{:S(2)}) collective-permute-start(bf16[2,64,640]{2,1,0:T(8,128)(2,1)} %get-tuple-element.49), channel_id=1, source_target_pairs={{0,6},{2,0},{4,2},{6,4},{1,7},{3,1},{5,3},{7,5},{8,14},{10,8},{12,... | collective-permute-start | bytes 491528 | tf_op jit(solution)/shard_map/ppermute | solution.py:136
  258.0 14.1 %copy-start.16 = (bf16[2,64,640]{2,1,0:T(8,128)(2,1)S(1)}, bf16[2,64,640]{2,1,0:T(8,128)(2,1)}, u32[]{:S(2)}) copy-start(bf16[2,64,640]{2,1,0:T(8,128)(2,1)} %get-tuple-element.36) | copy-start | bytes 491524
  258.0 15.4 %copy-start.15 = (bf16[2,64,640]{2,1,0:T(8,128)(2,1)S(1)}, bf16[2,64,640]{2,1,0:T(8,128)(2,1)}, u32[]{:S(2)}) copy-start(bf16[2,64,640]{2,1,0:T(8,128)(2,1)} %get-tuple-element.37) | copy-start | bytes 491524
  258.0 18.4 %copy-start.14 = (bf16[2,64,640]{2,1,0:T(8,128)(2,1)S(1)}, bf16[2,64,640]{2,1,0:T(8,128)(2,1)}, u32[]{:S(2)}) copy-start(bf16[2,64,640]{2,1,0:T(8,128)(2,1)} %get-tuple-element.38) | copy-start | bytes 491524
  258.0 18.4 %copy-start.2 = (bf16[1,2,64,5120]{3,2,1,0:T(8,128)(2,1)S(1)}, bf16[1,2,64,5120]{3,2,1,0:T(8,128)(2,1)}, u32[]{:S(2)}) copy-start(bf16[1,2,64,5120]{3,2,1,0:T(8,128)(2,1)} %refs_2_.3) | copy-start | bytes 3932164
  258.1 18.4 %copy-start.4 = (bf16[1,2,64,5120]{3,2,1,0:T(8,128)(2,1)S(1)}, bf16[1,2,64,5120]{3,2,1,0:T(8,128)(2,1)}, u32[]{:S(2)}) copy-start(bf16[1,2,64,5120]{3,2,1,0:T(8,128)(2,1)} %refs_0_.3) | copy-start | bytes 3932164
  258.1 18.4 %copy-start.6 = (bf16[2,2,64,1280]{3,2,1,0:T(8,128)(2,1)S(1)}, bf16[2,2,64,1280]{3,2,1,0:T(8,128)(2,1)}, u32[]{:S(2)}) copy-start(bf16[2,2,64,1280]{3,2,1,0:T(8,128)(2,1)} %copy-done.5) | copy-start | bytes 1966084
  258.1 18.4 %copy-start.8 = (bf16[2,2,64,1280]{3,2,1,0:T(8,128)(2,1)S(1)}, bf16[2,2,64,1280]{3,2,1,0:T(8,128)(2,1)}, u32[]{:S(2)}) copy-start(bf16[2,2,64,1280]{3,2,1,0:T(8,128)(2,1)} %copy-done.7) | copy-start | bytes 1966084
  258.1 18.4 %copy-start.10 = (bf16[512,1280]{1,0:T(8,128)(2,1)S(1)}, bf16[512,1280]{1,0:T(8,128)(2,1)}, u32[]{:S(2)}) copy-start(bf16[512,1280]{1,0:T(8,128)(2,1)} %copy-done.9) | copy-start | bytes 3932164
  272.2 20.4 %collective-permute-start = (bf16[2,64,640]{2,1,0:T(8,128)(2,1)S(1)}, bf16[2,64,640]{2,1,0:T(8,128)(2,1)S(1)}, u32[]{:S(2)}, u32[]{:S(2)}) collective-permute-start(bf16[2,64,640]{2,1,0:T(8,128)(2,1)S(1)} %copy-done.16), channel_id=1, source_target_pairs={{0,2},{2,4},{4,6},{6,0},{1,3},{3,5},{5,7},{7,1},{8,10},{10,12},{12... | collective-permute-start | bytes 491528 | tf_op jit(solution)/shard_map/ppermute | solution.py:136
  273.4 19.1 %collective-permute-start.1 = (bf16[2,64,640]{2,1,0:T(8,128)(2,1)S(1)}, bf16[2,64,640]{2,1,0:T(8,128)(2,1)S(1)}, u32[]{:S(2)}, u32[]{:S(2)}) collective-permute-start(bf16[2,64,640]{2,1,0:T(8,128)(2,1)S(1)} %copy-done.15), channel_id=1, source_target_pairs={{0,4},{2,6},{4,0},{6,2},{1,5},{3,7},{5,1},{7,3},{8,12},{10,14},{12... | collective-permute-start | bytes 491528 | tf_op jit(solution)/shard_map/ppermute | solution.py:136
  276.5 16.1 %collective-permute-start.2 = (bf16[2,64,640]{2,1,0:T(8,128)(2,1)S(1)}, bf16[2,64,640]{2,1,0:T(8,128)(2,1)S(1)}, u32[]{:S(2)}, u32[]{:S(2)}) collective-permute-start(bf16[2,64,640]{2,1,0:T(8,128)(2,1)S(1)} %copy-done.14), channel_id=1, source_target_pairs={{0,6},{2,0},{4,2},{6,4},{1,7},{3,1},{5,3},{7,5},{8,14},{10,8},{12,... | collective-permute-start | bytes 491528 | tf_op jit(solution)/shard_map/ppermute | solution.py:136
  308.6 13.6 %collective-permute-start.19 = (bf16[2,256,640]{2,1,0:T(8,128)(2,1)S(1)}, bf16[2,256,640]{2,1,0:T(8,128)(2,1)S(1)}, u32[]{:S(2)}, u32[]{:S(2)}) collective-permute-start(bf16[2,256,640]{2,1,0:T(8,128)(2,1)S(1)} %get-tuple-element.61), channel_id=1, source_target_pairs={{0,8},{8,16},{16,24},{1,9},{9,17},{17,25},{2,10},{10,18},{18,26},{... | collective-permute-start | bytes 1966088 | tf_op jit(solution)/shard_map/ppermute | solution.py:131
  313.5 11.9 %collective-permute-start.20 = (bf16[2,256,640]{2,1,0:T(8,128)(2,1)S(1)}, bf16[2,256,640]{2,1,0:T(8,128)(2,1)S(1)}, u32[]{:S(2)}, u32[]{:S(2)}) collective-permute-start(bf16[2,256,640]{2,1,0:T(8,128)(2,1)S(1)} %get-tuple-element.62), channel_id=1, source_target_pairs={{8,0},{16,8},{24,16},{9,1},{17,9},{25,17},{10,2},{18,10},{26,18},{... | collective-permute-start | bytes 1966088 | tf_op jit(solution)/shard_map/ppermute | solution.py:131
  315.4 12.6 %collective-permute-start.17 = (bf16[2,256,640]{2,1,0:T(8,128)(2,1)S(1)}, bf16[2,256,640]{2,1,0:T(8,128)(2,1)S(1)}, u32[]{:S(2)}, u32[]{:S(2)}) collective-permute-start(bf16[2,256,640]{2,1,0:T(8,128)(2,1)S(1)} %get-tuple-element.58), channel_id=1, source_target_pairs={{0,8},{8,16},{16,24},{1,9},{9,17},{17,25},{2,10},{10,18},{18,26},{... | collective-permute-start | bytes 1966088 | tf_op jit(solution)/shard_map/ppermute | solution.py:131
  319.1 13.3 %collective-permute-start.18 = (bf16[2,256,640]{2,1,0:T(8,128)(2,1)S(1)}, bf16[2,256,640]{2,1,0:T(8,128)(2,1)S(1)}, u32[]{:S(2)}, u32[]{:S(2)}) collective-permute-start(bf16[2,256,640]{2,1,0:T(8,128)(2,1)S(1)} %get-tuple-element.59), channel_id=1, source_target_pairs={{8,0},{16,8},{24,16},{9,1},{17,9},{25,17},{10,2},{18,10},{26,18},{... | collective-permute-start | bytes 1966088 | tf_op jit(solution)/shard_map/ppermute | solution.py:131
Sparse Core Ops, SparseCore 0:
  16.5 116.7 all-gather.1

commit v5 on v4

--- a/solution.py
+++ b/solution.py
@@ -254,13 +254,24 @@
     gated = (cotangent[0].astype(jnp.float32) * gain[:, None, :]).astype(jnp.bfloat16)
     gated = gated.reshape(frames * rows, model)
     gated = jnp.stack([gated[:, b * block : (b + 1) * block] for b in range(blocks)])
-    gathered = lax.all_gather(gated, "head", axis=1, tiled=True)
 
     kv_send = [
         jnp.stack([columns_for(a, s, 0, width) for a in (key_rows, value_rows)]) for s in shifts
     ]
-    kv_send, gathered = after(kv_send, gathered)
     kv = [rotated(a, "head", s) for s, a in zip(shifts, kv_send)]
+    gated, o_pieces, kv = lax.optimization_barrier((gated, o_pieces, kv))
+    gathered = lax.all_gather(gated, "head", axis=1, tiled=True)
+
+    own = [columns_for(a, 0, 0, width) for a in (key_rows, value_rows)]
+
+    def boundary(frame):
+        return jnp.stack(
+            [jnp.stack([own[t][frame]] + [p[t, frame] for p in kv]) for t in range(2)]
+        )
+
+    from_prev = shifted(boundary(frames - 1), "frame", 1)
+    from_next = shifted(boundary(0), "frame", -1)
+    halos = (from_prev, from_next)
 
     o = jnp.zeros((parts, frames, rows, width), jnp.bfloat16)
     for s, piece in enumerate([columns_for(saved_out, 0, 0, width)] + o_pieces):
@@ -271,6 +282,8 @@
     near = o.reshape(1, parts * frames * rows, width)
     flips = [(0, 0)]
     for axis, bit in levels_xy:
+        if (axis, bit) == levels_xy[-1]:
+            near, halos = after(near, halos)
         near = jnp.concatenate([near, flipped(near, axis, bit)], axis=0)
         flips += [(a ^ bit, b) if axis == "frame" else (a, b ^ bit) for a, b in flips]
     far = flipped(near, "frame", 1)
@@ -295,8 +308,7 @@
         [columns_for(queries, s, head0 * HD, count * HD) for s in shifts]
         for head0, count in groups
     ]
-    q_send, d = after(q_send, d)
-    kv, d = after(kv, d)
+    q_send, gathered = after(q_send, gathered)
     d = d.reshape(parts, frames, rows, width)
     q_pieces = [[rotated(a, "head", s) for s, a in zip(shifts, sends)] for sends in q_send]
 
@@ -306,27 +318,20 @@
     limits = jnp.where(inside, jnp.where(chosen == 1, tokens, tokens // 2), 0).astype(jnp.int32)
     scal = jnp.concatenate([jnp.stack([me, me * heads]).astype(jnp.int32), limits.reshape(-1)])
 
-    own = [columns_for(a, 0, 0, width) for a in (key_rows, value_rows)]
-
-    def boundary(frame):
-        return jnp.stack(
-            [jnp.stack([own[t][frame]] + [p[t, frame] for p in kv]) for t in range(2)]
-        )
-
-    from_prev = shifted(boundary(frames - 1), "frame", 1)
-    from_next = shifted(boundary(0), "frame", -1)
     local = (queries, key_rows, value_rows)
-    scal, d_weight = after(scal, d_weight)
     results = []
     for (head0, count), q_group in zip(groups, q_pieces):
         if results:
             q_group, results[-1][0] = after(q_group, results[-1][0])
         dq, dk, dv, to_prev, to_next = attention(
-            scal, head0, count, local, kv, q_group, o, d, from_prev, from_next
+            scal, head0, count, local, kv, q_group, o, d, *halos
         )
         grad_next = shifted(to_prev, "frame", -1)
         grad_prev = shifted(to_next, "frame", 1)
         results.append([dq, dk, dv, grad_prev, grad_next])
+
+    edges, d_weight = after([r[3:] for r in results], d_weight)
+    results = [r[:3] + e for r, e in zip(results, edges)]
 
     def combine(own_grad, t, grad_prev, grad_next):
         terms = [own_grad[f] for f in range(frames)]

time: 345 us -> 306 us (0.89)
  waiting for transfers between devices: 165 us -> 117 us
  local copies, waits for them, and re-layouts: 12.6 us -> 27.6 us
  other arithmetic: 15.6 us -> 11.9 us
    ppermute x12, waiting for transfers between devices: 84.8 us -> 32.6 us  [rotated(): lax.ppermute(array, axis, [(i, (i + step) % count) for i in range(count)])]
    ppermute x3, waiting for transfers between devices: 70.5 us -> 84.2 us  [flipped(): lax.ppermute(array, axis, [(i, i ^ bit) for i in range(lax.axis_size(axis...]
    ppermute x6, waiting for transfers between devices: 9.97 us -> 0.02 us  [shifted(): return lax.ppermute(array, axis, pairs)]
    ppermute x3, starting transfers between devices: 10.9 us -> 0.99 us  [flipped(): lax.ppermute(array, axis, [(i, i ^ bit) for i in range(lax.axis_size(axis...]
    ppermute x12, starting transfers between devices: 36.5 us -> 44.7 us  [rotated(): lax.ppermute(array, axis, [(i, (i + step) % count) for i in range(count)])]
    unnamed x43 -> x50, local copies, waits for them, and re-layouts: 5.74 us -> 13.3 us
    dynamic_update_slice x3 -> x4, local copies, waits for them, and re-layouts: 0.08 us -> 4.05 us  [per_device(): lax.dynamic_update_slice_in_dim(o, piece[None], lax.rem(me + parts - s, p...]
  transfers between devices with their start and end apart: 23 -> 23, of which waited for: 9 -> 4; matrix products, arithmetic and copies ran while one was open for 5% -> 9% of each run, Pallas kernels for 13% -> 20%
where the time goes in v5:
time: 306 us; the launch traced here: 303 us
  waiting for transfers between devices  117 us (38%)
  starting transfers between devices  68.4 us (22%)
  Pallas kernels  60.2 us (20%)
  local copies, waits for them, and re-layouts  27.6 us (9%)
  between operations  18.3 us (6%)
  other arithmetic  11.9 us (4%)
    ppermute x3, waiting for transfers between devices, flipped(): lax.ppermute(array, axis, [(i, i ^ bit) for i in range(lax.axis_size(axis...  84.2 us
    ppermute x12, starting transfers between devices, rotated(): lax.ppermute(array, axis, [(i, (i + step) % count) for i in range(count)])  44.7 us
    pallas_call x2, Pallas kernels, attention(): pl.pallas_call(partial(attention_kernel, parts), grid_spec=pltpu.Prefetch...  33 us
    ppermute x12, waiting for transfers between devices, rotated(): lax.ppermute(array, axis, [(i, (i + step) % count) for i in range(count)])  32.6 us
    ppermute x6, starting transfers between devices, shifted(): return lax.ppermute(array, axis, pairs)  17.8 us
    pallas_call x1, Pallas kernels, weight_grad(): pl.pallas_call(partial(weight_kernel, scale), grid_spec=pltpu.PrefetchSca...  13.8 us
    pallas_call x1, Pallas kernels, project(): pl.pallas_call(project_kernel, grid=(blocks,), in_specs=[pl.BlockSpec((1,...  13.4 us
    unnamed x50, local copies, waits for them, and re-layouts  13.3 us
  transfers between devices with their start and end apart: 23, of which 4 were waited for; matrix products, arithmetic and copies ran while one was open for 9% of the time, Pallas kernels for 20%

profile of v5, /device:TPU:11, one launch (start us, length us, event | category | flops | bytes accessed | tf_op | source)
XLA Modules:
  0.0 303.3 jit_solution(4150480224060079160)
XLA Ops:
  7.4 1.2 copy-done.15
  8.6 1.0 dynamic-slice_dynamic-update-slice_fusion
  9.6 2.3 collective-permute-start.1
  12.1 0.9 pad_maximum_fusion.3
  13.4 0.9 pad_maximum_fusion.4
  14.3 3.2 %collective-permute-start.4 = (bf16[2,2,64,1280]{3,2,1,0:T(8,128)(2,1)}, bf16[2,2,64,1280]{3,2,1,0:T(8,128)(2,1)}, u32[]{:S(2)}, u32[]{:S(2)}) collective-permute-start(bf16[2,2,64,1280]{3,2,1,0:T(8,128)(2,1)} %pad_maximum_fusion.4), channel_id=1, source_target_pairs={{0,4},{2,6},{4,0},{6,2},{1,5},{3,7},{5,1},{7,3},{8,12},{10,14},{12... | collective-permute-start | bytes 1966088 | tf_op jit(solution)/shard_map/ppermute | solution.py:136
  17.5 0.9 pad_maximum_fusion.5
  23.0 1.0 constant_dynamic-slice_fusion.8
  24.1 1.6 fusion
  25.6 0.7 fusion.8
  29.1 0.7 fusion.3
  30.4 31.3 %collective-permute-start.2 = (bf16[2,64,1280]{2,1,0:T(8,128)(2,1)}, bf16[2,64,1280]{2,1,0:T(8,128)(2,1)}, u32[]{:S(2)}, u32[]{:S(2)}) collective-permute-start(bf16[2,64,1280]{2,1,0:T(8,128)(2,1)} %get-tuple-element.93), channel_id=1, source_target_pairs={{0,6},{2,0},{4,2},{6,4},{1,7},{3,1},{5,3},{7,5},{8,14},{10,8},{12,... | collective-permute-start | bytes 983048 | tf_op jit(solution)/shard_map/ppermute | solution.py:136
  62.4 1.8 dynamic-slice_bitcast_fusion.3
  64.2 31.5 %collective-permute-done.2 = bf16[2,64,1280]{2,1,0:T(8,128)(2,1)} collective-permute-done((bf16[2,64,1280]{2,1,0:T(8,128)(2,1)}, bf16[2,64,1280]{2,1,0:T(8,128)(2,1)}, u32[]{:S(2)}, u32[]{:S(2)}) %collective-permute-start.2) | collective-permute-done | bytes 327712 | tf_op jit(solution)/shard_map/ppermute | solution.py:136
  95.7 1.1 collective-permute-done.4.refs_4_
  96.9 1.2 slice_bitcast_fusion.12
  98.2 1.2 slice_bitcast_fusion.11
  99.7 3.7 %collective-permute-start.13 = (bf16[2,4,64,1280]{3,2,1,0:T(8,128)(2,1)S(1)}, bf16[2,4,64,1280]{3,2,1,0:T(8,128)(2,1)S(1)}, u32[]{:S(2)}, u32[]{:S(2)}) collective-permute-start(bf16[2,4,64,1280]{3,2,1,0:T(8,128)(2,1)S(1)} %pad_maximum_fusion.1), channel_id=1, source_target_pairs={{0,8},{8,16},{16,24},{1,9},{9,17},{17,25},{2,10},{10,18},{18,26},{... | collective-permute-start | bytes 3932168 | tf_op jit(solution)/shard_map/ppermute | solution.py:131
  103.4 1.0 bitcast_dynamic-update-slice_fusion.2
  104.4 1.0 bitcast_dynamic-update-slice_fusion.1
  105.4 1.0 bitcast_dynamic-update-slice_fusion.refs_9_
  107.1 1.9 collective-permute-start.14
  109.0 27.8 %collective-permute-done.12 = bf16[1,512,1280]{2,1,0:T(8,128)(2,1)S(1)} collective-permute-done((bf16[1,512,1280]{2,1,0:T(8,128)(2,1)S(1)}, bf16[1,512,1280]{2,1,0:T(8,128)(2,1)S(1)}, u32[]{:S(2)}, u32[]{:S(2)}) %collective-permute-start.12) | collective-permute-done | bytes 1310752 | tf_op jit(solution)/shard_map/ppermute | solution.py:144
  137.2 1.8 constant_dynamic-update-slice_fusion.1
  139.4 56.4 %collective-permute-done.19 = bf16[2,512,1280]{2,1,0:T(8,128)(2,1)S(1)} collective-permute-done((bf16[2,512,1280]{2,1,0:T(8,128)(2,1)S(1)}, bf16[2,512,1280]{2,1,0:T(8,128)(2,1)S(1)}, u32[]{:S(2)}, u32[]{:S(2)}) %collective-permute-start.19) | collective-permute-done | bytes 2621472 | tf_op jit(solution)/shard_map/ppermute | solution.py:144
  195.9 1.7 constant_dynamic-update-slice_fusion.near_ref
  198.2 4.8 %all-to-all-start = ((bf16[8,512,640]{2,1,0:T(8,128)(2,1)}), bf16[8,512,640]{2,1,0:T(8,128)(2,1)}, u32[]{:S(2)}, u32[]{:S(2)}) async-start(bf16[8,512,640]{2,1,0:T(8,128)(2,1)} %all-gather.2.cloned.1.call-done.g_ref), calls=%async_computation | async-start | bytes 10485760 | tf_op jit(solution)/shard_map/all_to_all | solution.py:299
  203.4 1.4 dynamic-slice_bitcast_fusion.7
  204.9 3.4 %collective-permute-start.9 = (bf16[2,64,640]{2,1,0:T(8,128)(2,1)S(1)}, bf16[2,64,640]{2,1,0:T(8,128)(2,1)S(1)}, u32[]{:S(2)}, u32[]{:S(2)}) collective-permute-start(bf16[2,64,640]{2,1,0:T(8,128)(2,1)S(1)} %get-tuple-element.46), channel_id=1, source_target_pairs={{0,2},{2,4},{4,6},{6,0},{1,3},{3,5},{5,7},{7,1},{8,10},{10,12},{12... | collective-permute-start | bytes 491528 | tf_op jit(solution)/shard_map/ppermute | solution.py:136
  208.5 1.1 collective-permute-start.11
  209.6 2.5 copy-done.4
  212.1 13.4 %project_gated.1 = bf16[512,1280]{1,0:T(8,128)(2,1)S(1)} custom-call(bf16[8,512,640]{2,1,0:T(8,128)(2,1)S(1)} %copy-done.4, bf16[1280,5120]{1,0:T(8,128)(2,1)} %w_ref.1), custom_call_target="tpu_custom_call" | custom-call | flops 6710886400 | bytes 19660800 | tf_op jit(solution)/shard_map/project_gated/pallas_call | solution.py:209
  225.4 1.2 collective-permute-start.7
  226.6 1.4 collective-permute-start.8
  228.1 16.5 %attention_backward.2 = (bf16[2,256,640]{2,1,0:T(8,128)(2,1)S(1)}, f32[2,256,640]{2,1,0:T(8,128)S(1)}, f32[2,256,640]{2,1,0:T(8,128)S(1)}, bf16[2,256,640]{2,1,0:T(8,128)(2,1)}, bf16[2,256,640]{2,1,0:T(8,128)(2,1)}) custom-call(s32[6]{0:T(128)S(1)} %pad_add_fusion.1.scal, bf16[1,2,64,5120]{3,2,1,0:T(8,128)(2,1)S(1)} %copy-done.3, ...), custom_call_target="tpu_custom_call" | custom-call | flops 2516582400 | bytes 10485760 | tf_op jit(solution)/shard_map/attention_backward/pallas_call | solution.py:99
  244.6 1.1 copy-done.5
  245.7 1.1 copy-done.7
  246.7 16.5 %attention_backward.3 = (bf16[2,256,640]{2,1,0:T(8,128)(2,1)S(1)}, f32[2,256,640]{2,1,0:T(8,128)S(1)}, f32[2,256,640]{2,1,0:T(8,128)S(1)}, bf16[2,256,640]{2,1,0:T(8,128)(2,1)}, bf16[2,256,640]{2,1,0:T(8,128)(2,1)}) custom-call(s32[6]{0:T(128)S(1)} %pad_add_fusion.1.scal, bf16[1,2,64,5120]{3,2,1,0:T(8,128)(2,1)S(1)} %copy-done.3, ...), custom_call_target="tpu_custom_call" | custom-call | flops 2516582400 | bytes 10485760 | tf_op jit(solution)/shard_map/attention_backward/pallas_call | solution.py:99
  263.2 4.8 %collective-permute-start.17 = (bf16[2,256,640]{2,1,0:T(8,128)(2,1)}, bf16[2,256,640]{2,1,0:T(8,128)(2,1)}, u32[]{:S(2)}, u32[]{:S(2)}) collective-permute-start(bf16[2,256,640]{2,1,0:T(8,128)(2,1)} %get-tuple-element.63), channel_id=1, source_target_pairs={{0,8},{8,16},{16,24},{1,9},{9,17},{17,25},{2,10},{10,18},{18,26},{... | collective-permute-start | bytes 1966088 | tf_op jit(solution)/shard_map/ppermute | solution.py:131
  268.0 1.9 collective-permute-start.18
  269.9 3.6 %collective-permute-start.15 = (bf16[2,256,640]{2,1,0:T(8,128)(2,1)}, bf16[2,256,640]{2,1,0:T(8,128)(2,1)S(1)}, u32[]{:S(2)}, u32[]{:S(2)}) collective-permute-start(bf16[2,256,640]{2,1,0:T(8,128)(2,1)} %get-tuple-element.61), channel_id=1, source_target_pairs={{0,8},{8,16},{16,24},{1,9},{9,17},{17,25},{2,10},{10,18},{18,26},{... | collective-permute-start | bytes 1966088 | tf_op jit(solution)/shard_map/ppermute | solution.py:131
  273.6 1.9 collective-permute-start.16
  275.5 1.2 maximum_bitcast_fusion
  276.7 13.8 %weight_gradient.1 = f32[1280,640]{1,0:T(8,128)} custom-call(s32[2,4]{1,0:T(2,128)S(1)} %pad_add_fusion.table, bf16[4,512,1280]{2,1,0:T(8,128)(2,1)} %constant_dynamic-update-slice_fusion.near_ref, bf16[4,512,1280]{2,1,0:T(8,128)(2,1)} %collective-permute-done.20.far_ref, bf16[8,512,640]{2,1,0:T(8,128)(2,1)} %all-to-all-done.g_near.g_far, ...), custom_call_target="tpu_custom_call" | custom-call | flops 6710886400 | bytes 19005440 | tf_op jit(solution)/shard_map/weight_gradient/pallas_call | solution.py:162
  290.6 1.7 add_convert_fusion.5
  292.7 1.4 add_convert_fusion.7
  294.1 1.2 maximum_bitcast_fusion.1
  295.3 1.2 maximum_bitcast_fusion.2
  (92 shorter events, 9.0 us)
Async XLA Ops:
  7.2 191.0 %all-gather.2.cloned.1.call-start = ((), (), s32[]{:S(2)}) async-start(), calls=%async_computation.1 | async-start | bytes 6553600 | tf_op jit(solution)/shard_map/all_gather | solution.py:263
  7.3 1.3 copy-start.15
  8.6 3.3 %copy-start = (bf16[1,2,64,5120]{3,2,1,0:T(8,128)(2,1)S(1)}, bf16[1,2,64,5120]{3,2,1,0:T(8,128)(2,1)}, u32[]{:S(2)}) copy-start(bf16[1,2,64,5120]{3,2,1,0:T(8,128)(2,1)} %refs_1_.3) | copy-start | bytes 3932164
  8.6 3.3 %copy-start.1 = (bf16[1,2,64,5120]{3,2,1,0:T(8,128)(2,1)S(1)}, bf16[1,2,64,5120]{3,2,1,0:T(8,128)(2,1)}, u32[]{:S(2)}) copy-start(bf16[1,2,64,5120]{3,2,1,0:T(8,128)(2,1)} %refs_2_.3) | copy-start | bytes 3932164
  9.6 20.8 %collective-permute-start.1 = (bf16[2,64,1280]{2,1,0:T(8,128)(2,1)}, bf16[2,64,1280]{2,1,0:T(8,128)(2,1)}, u32[]{:S(2)}, u32[]{:S(2)}) collective-permute-start(bf16[2,64,1280]{2,1,0:T(8,128)(2,1)} %get-tuple-element.91), channel_id=1, source_target_pairs={{0,4},{2,6},{4,0},{6,2},{1,5},{3,7},{5,1},{7,3},{8,12},{10,14},{12... | collective-permute-start | bytes 983048 | tf_op jit(solution)/shard_map/ppermute | solution.py:136
  11.9 52.3 %collective-permute-start = (bf16[2,64,1280]{2,1,0:T(8,128)(2,1)}, bf16[2,64,1280]{2,1,0:T(8,128)(2,1)}, u32[]{:S(2)}, u32[]{:S(2)}) collective-permute-start(bf16[2,64,1280]{2,1,0:T(8,128)(2,1)} %get-tuple-element.92), channel_id=1, source_target_pairs={{0,2},{2,4},{4,6},{6,0},{1,3},{3,5},{5,7},{7,1},{8,10},{10,12},{12... | collective-permute-start | bytes 983048 | tf_op jit(solution)/shard_map/ppermute | solution.py:136
  13.0 82.7 %collective-permute-start.3 = (bf16[2,2,64,1280]{3,2,1,0:T(8,128)(2,1)}, bf16[2,2,64,1280]{3,2,1,0:T(8,128)(2,1)S(1)}, u32[]{:S(2)}, u32[]{:S(2)}) collective-permute-start(bf16[2,2,64,1280]{3,2,1,0:T(8,128)(2,1)} %pad_maximum_fusion.3), channel_id=1, source_target_pairs={{0,2},{2,4},{4,6},{6,0},{1,3},{3,5},{5,7},{7,1},{8,10},{10,12},{12... | collective-permute-start | bytes 1966088 | tf_op jit(solution)/shard_map/ppermute | solution.py:136
  13.4 5.2 %copy-start.19 = (s32[2]{0:T(128)S(1)}, s32[2]{0:T(128)}, u32[]{:S(2)}) copy-start(s32[2]{0:T(128)} %param.16) | copy-start | bytes 28
  14.3 82.6 %collective-permute-start.4 = (bf16[2,2,64,1280]{3,2,1,0:T(8,128)(2,1)}, bf16[2,2,64,1280]{3,2,1,0:T(8,128)(2,1)}, u32[]{:S(2)}, u32[]{:S(2)}) collective-permute-start(bf16[2,2,64,1280]{3,2,1,0:T(8,128)(2,1)} %pad_maximum_fusion.4), channel_id=1, source_target_pairs={{0,4},{2,6},{4,0},{6,2},{1,5},{3,7},{5,1},{7,3},{8,12},{10,14},{12... | collective-permute-start | bytes 1966088 | tf_op jit(solution)/shard_map/ppermute | solution.py:136
  18.4 78.5 %collective-permute-start.5 = (bf16[2,2,64,1280]{3,2,1,0:T(8,128)(2,1)}, bf16[2,2,64,1280]{3,2,1,0:T(8,128)(2,1)}, u32[]{:S(2)}, u32[]{:S(2)}) collective-permute-start(bf16[2,2,64,1280]{3,2,1,0:T(8,128)(2,1)} %pad_maximum_fusion.5), channel_id=1, source_target_pairs={{0,6},{2,0},{4,2},{6,4},{1,7},{3,1},{5,3},{7,5},{8,14},{10,8},{12,... | collective-permute-start | bytes 1966088 | tf_op jit(solution)/shard_map/ppermute | solution.py:136
  30.4 65.3 %collective-permute-start.2 = (bf16[2,64,1280]{2,1,0:T(8,128)(2,1)}, bf16[2,64,1280]{2,1,0:T(8,128)(2,1)}, u32[]{:S(2)}, u32[]{:S(2)}) collective-permute-start(bf16[2,64,1280]{2,1,0:T(8,128)(2,1)} %get-tuple-element.93), channel_id=1, source_target_pairs={{0,6},{2,0},{4,2},{6,4},{1,7},{3,1},{5,3},{7,5},{8,14},{10,8},{12,... | collective-permute-start | bytes 983048 | tf_op jit(solution)/shard_map/ppermute | solution.py:136
  96.9 2.5 copy-start.18
  98.2 1.4 copy-start.17
  99.7 7.0 %copy-start.16 = (bf16[1,64,1280]{2,1,0:T(8,128)(2,1)S(1)}, bf16[1,64,1280]{2,1,0:T(8,128)(2,1)}, u32[]{:S(2)}) copy-start(bf16[1,64,1280]{2,1,0:T(8,128)(2,1)} %get-tuple-element.127) | copy-start | bytes 491524
  99.7 37.3 %collective-permute-start.13 = (bf16[2,4,64,1280]{3,2,1,0:T(8,128)(2,1)S(1)}, bf16[2,4,64,1280]{3,2,1,0:T(8,128)(2,1)S(1)}, u32[]{:S(2)}, u32[]{:S(2)}) collective-permute-start(bf16[2,4,64,1280]{3,2,1,0:T(8,128)(2,1)S(1)} %pad_maximum_fusion.1), channel_id=1, source_target_pairs={{0,8},{8,16},{16,24},{1,9},{9,17},{17,25},{2,10},{10,18},{18,26},{... | collective-permute-start | bytes 3932168 | tf_op jit(solution)/shard_map/ppermute | solution.py:131
  106.5 30.4 %collective-permute-start.12 = (bf16[1,512,1280]{2,1,0:T(8,128)(2,1)S(1)}, bf16[1,512,1280]{2,1,0:T(8,128)(2,1)S(1)}, u32[]{:S(2)}, u32[]{:S(2)}) collective-permute-start(bf16[1,512,1280]{2,1,0:T(8,128)(2,1)S(1)} %bitcast.125), channel_id=1, source_target_pairs={{0,1},{1,0},{2,3},{3,2},{4,5},{5,4},{6,7},{7,6},{8,9},{9,8},{10,11... | collective-permute-start | bytes 3932168 | tf_op jit(solution)/shard_map/ppermute | solution.py:144
  107.1 30.0 %collective-permute-start.14 = (bf16[2,4,64,1280]{3,2,1,0:T(8,128)(2,1)S(1)}, bf16[2,4,64,1280]{3,2,1,0:T(8,128)(2,1)S(1)}, u32[]{:S(2)}, u32[]{:S(2)}) collective-permute-start(bf16[2,4,64,1280]{3,2,1,0:T(8,128)(2,1)S(1)} %pad_maximum_fusion.2), channel_id=1, source_target_pairs={{8,0},{16,8},{24,16},{9,1},{17,9},{25,17},{10,2},{18,10},{26,18},{... | collective-permute-start | bytes 3932168 | tf_op jit(solution)/shard_map/ppermute | solution.py:131
  137.1 1.9 copy-start.13
  137.1 2.3 copy-start.14
  137.1 58.7 %collective-permute-start.19 = (bf16[2,512,1280]{2,1,0:T(8,128)(2,1)S(1)}, bf16[2,512,1280]{2,1,0:T(8,128)(2,1)S(1)}, u32[]{:S(2)}, u32[]{:S(2)}) collective-permute-start(bf16[2,512,1280]{2,1,0:T(8,128)(2,1)S(1)} %pad_maximum_fusion), channel_id=1, source_target_pairs={{0,16},{8,24},{16,0},{24,8},{1,17},{9,25},{17,1},{25,9},{2,18},{10... | collective-permute-start | bytes 7864328 | tf_op jit(solution)/shard_map/ppermute | solution.py:144
  197.6 5.5 %copy-start.20 = (s32[8,2]{0,1:T(2,128)S(1)}, s32[8,2]{0,1:T(2,128)}, u32[]{:S(2)}) copy-start(s32[8,2]{0,1:T(2,128)} %param.17) | copy-start | bytes 196
  197.6 79.1 %collective-permute-start.20 = (bf16[4,512,1280]{2,1,0:T(8,128)(2,1)}, bf16[4,512,1280]{2,1,0:T(8,128)(2,1)}, u32[]{:S(2)}, u32[]{:S(2)}) collective-permute-start(bf16[4,512,1280]{2,1,0:T(8,128)(2,1)} %constant_dynamic-update-slice_fusion.near_ref), channel_id=1, source_target_pairs={{0,8},{8,0},{16,24},{24,16},{1,9},{9,1},{17,25},{25,17},{2,10},{10... | collective-permute-start | bytes 15728648 | tf_op jit(solution)/shard_map/ppermute | solution.py:144
  198.2 78.6 %all-to-all-start = ((bf16[8,512,640]{2,1,0:T(8,128)(2,1)}), bf16[8,512,640]{2,1,0:T(8,128)(2,1)}, u32[]{:S(2)}, u32[]{:S(2)}) async-start(bf16[8,512,640]{2,1,0:T(8,128)(2,1)} %all-gather.2.cloned.1.call-done.g_ref), calls=%async_computation | async-start | bytes 10485760 | tf_op jit(solution)/shard_map/all_to_all | solution.py:299
  204.8 23.2 %copy-start.2 = (bf16[1,2,64,5120]{3,2,1,0:T(8,128)(2,1)S(1)}, bf16[1,2,64,5120]{3,2,1,0:T(8,128)(2,1)}, u32[]{:S(2)}) copy-start(bf16[1,2,64,5120]{3,2,1,0:T(8,128)(2,1)} %refs_2_.3) | copy-start | bytes 3932164
  204.9 23.2 %copy-start.3 = (bf16[1,2,64,5120]{3,2,1,0:T(8,128)(2,1)S(1)}, bf16[1,2,64,5120]{3,2,1,0:T(8,128)(2,1)}, u32[]{:S(2)}) copy-start(bf16[1,2,64,5120]{3,2,1,0:T(8,128)(2,1)} %refs_0_.3) | copy-start | bytes 3932164
  204.9 41.9 %collective-permute-start.6 = (bf16[2,64,640]{2,1,0:T(8,128)(2,1)S(1)}, bf16[2,64,640]{2,1,0:T(8,128)(2,1)S(1)}, u32[]{:S(2)}, u32[]{:S(2)}) collective-permute-start(bf16[2,64,640]{2,1,0:T(8,128)(2,1)S(1)} %get-tuple-element.40), channel_id=1, source_target_pairs={{0,2},{2,4},{4,6},{6,0},{1,3},{3,5},{5,7},{7,1},{8,10},{10,12},{12... | collective-permute-start | bytes 491528 | tf_op jit(solution)/shard_map/ppermute | solution.py:136
  204.9 20.5 %collective-permute-start.9 = (bf16[2,64,640]{2,1,0:T(8,128)(2,1)S(1)}, bf16[2,64,640]{2,1,0:T(8,128)(2,1)S(1)}, u32[]{:S(2)}, u32[]{:S(2)}) collective-permute-start(bf16[2,64,640]{2,1,0:T(8,128)(2,1)S(1)} %get-tuple-element.46), channel_id=1, source_target_pairs={{0,2},{2,4},{4,6},{6,0},{1,3},{3,5},{5,7},{7,1},{8,10},{10,12},{12... | collective-permute-start | bytes 491528 | tf_op jit(solution)/shard_map/ppermute | solution.py:136
  208.3 18.3 %collective-permute-start.10 = (bf16[2,64,640]{2,1,0:T(8,128)(2,1)S(1)}, bf16[2,64,640]{2,1,0:T(8,128)(2,1)S(1)}, u32[]{:S(2)}, u32[]{:S(2)}) collective-permute-start(bf16[2,64,640]{2,1,0:T(8,128)(2,1)S(1)} %get-tuple-element.47), channel_id=1, source_target_pairs={{0,4},{2,6},{4,0},{6,2},{1,5},{3,7},{5,1},{7,3},{8,12},{10,14},{12... | collective-permute-start | bytes 491528 | tf_op jit(solution)/shard_map/ppermute | solution.py:136
  208.5 19.6 %collective-permute-start.11 = (bf16[2,64,640]{2,1,0:T(8,128)(2,1)S(1)}, bf16[2,64,640]{2,1,0:T(8,128)(2,1)S(1)}, u32[]{:S(2)}, u32[]{:S(2)}) collective-permute-start(bf16[2,64,640]{2,1,0:T(8,128)(2,1)S(1)} %get-tuple-element.48), channel_id=1, source_target_pairs={{0,6},{2,0},{4,2},{6,4},{1,7},{3,1},{5,3},{7,5},{8,14},{10,8},{12,... | collective-permute-start | bytes 491528 | tf_op jit(solution)/shard_map/ppermute | solution.py:136
  209.6 2.5 copy-start.4
  225.4 21.3 %collective-permute-start.7 = (bf16[2,64,640]{2,1,0:T(8,128)(2,1)S(1)}, bf16[2,64,640]{2,1,0:T(8,128)(2,1)S(1)}, u32[]{:S(2)}, u32[]{:S(2)}) collective-permute-start(bf16[2,64,640]{2,1,0:T(8,128)(2,1)S(1)} %get-tuple-element.41), channel_id=1, source_target_pairs={{0,4},{2,6},{4,0},{6,2},{1,5},{3,7},{5,1},{7,3},{8,12},{10,14},{12... | collective-permute-start | bytes 491528 | tf_op jit(solution)/shard_map/ppermute | solution.py:136
  226.6 20.1 %collective-permute-start.8 = (bf16[2,64,640]{2,1,0:T(8,128)(2,1)S(1)}, bf16[2,64,640]{2,1,0:T(8,128)(2,1)S(1)}, u32[]{:S(2)}, u32[]{:S(2)}) collective-permute-start(bf16[2,64,640]{2,1,0:T(8,128)(2,1)S(1)} %get-tuple-element.42), channel_id=1, source_target_pairs={{0,6},{2,0},{4,2},{6,4},{1,7},{3,1},{5,3},{7,5},{8,14},{10,8},{12,... | collective-permute-start | bytes 491528 | tf_op jit(solution)/shard_map/ppermute | solution.py:136
  244.6 1.1 copy-start.5
  245.7 1.1 copy-start.7
  263.2 13.4 %copy-start.9 = (f32[2,256,640]{2,1,0:T(8,128)}, f32[2,256,640]{2,1,0:T(8,128)S(1)}, u32[]{:S(2)}) copy-start(f32[2,256,640]{2,1,0:T(8,128)S(1)} %get-tuple-element.68) | copy-start | bytes 3932164
  263.2 13.4 %copy-start.11 = (f32[2,256,640]{2,1,0:T(8,128)}, f32[2,256,640]{2,1,0:T(8,128)S(1)}, u32[]{:S(2)}) copy-start(f32[2,256,640]{2,1,0:T(8,128)S(1)} %get-tuple-element.72) | copy-start | bytes 3932164
  263.2 27.3 %collective-permute-start.17 = (bf16[2,256,640]{2,1,0:T(8,128)(2,1)}, bf16[2,256,640]{2,1,0:T(8,128)(2,1)}, u32[]{:S(2)}, u32[]{:S(2)}) collective-permute-start(bf16[2,256,640]{2,1,0:T(8,128)(2,1)} %get-tuple-element.63), channel_id=1, source_target_pairs={{0,8},{8,16},{16,24},{1,9},{9,17},{17,25},{2,10},{10,18},{18,26},{... | collective-permute-start | bytes 1966088 | tf_op jit(solution)/shard_map/ppermute | solution.py:131
  268.0 22.6 %collective-permute-start.18 = (bf16[2,256,640]{2,1,0:T(8,128)(2,1)}, bf16[2,256,640]{2,1,0:T(8,128)(2,1)}, u32[]{:S(2)}, u32[]{:S(2)}) collective-permute-start(bf16[2,256,640]{2,1,0:T(8,128)(2,1)} %get-tuple-element.64), channel_id=1, source_target_pairs={{8,0},{16,8},{24,16},{9,1},{17,9},{25,17},{10,2},{18,10},{26,18},{... | collective-permute-start | bytes 1966088 | tf_op jit(solution)/shard_map/ppermute | solution.py:131
  269.9 20.6 %collective-permute-start.15 = (bf16[2,256,640]{2,1,0:T(8,128)(2,1)}, bf16[2,256,640]{2,1,0:T(8,128)(2,1)S(1)}, u32[]{:S(2)}, u32[]{:S(2)}) collective-permute-start(bf16[2,256,640]{2,1,0:T(8,128)(2,1)} %get-tuple-element.61), channel_id=1, source_target_pairs={{0,8},{8,16},{16,24},{1,9},{9,17},{17,25},{2,10},{10,18},{18,26},{... | collective-permute-start | bytes 1966088 | tf_op jit(solution)/shard_map/ppermute | solution.py:131
  273.6 17.0 %collective-permute-start.16 = (bf16[2,256,640]{2,1,0:T(8,128)(2,1)}, bf16[2,256,640]{2,1,0:T(8,128)(2,1)}, u32[]{:S(2)}, u32[]{:S(2)}) collective-permute-start(bf16[2,256,640]{2,1,0:T(8,128)(2,1)} %get-tuple-element.62), channel_id=1, source_target_pairs={{8,0},{16,8},{24,16},{9,1},{17,9},{25,17},{10,2},{18,10},{26,18},{... | collective-permute-start | bytes 1966088 | tf_op jit(solution)/shard_map/ppermute | solution.py:131
  276.7 13.9 %copy-start.10 = (f32[2,256,640]{2,1,0:T(8,128)S(1)}, f32[2,256,640]{2,1,0:T(8,128)}, u32[]{:S(2)}) copy-start(f32[2,256,640]{2,1,0:T(8,128)} %copy-done.9) | copy-start | bytes 3932164
  276.7 13.9 %copy-start.12 = (f32[2,256,640]{2,1,0:T(8,128)S(1)}, f32[2,256,640]{2,1,0:T(8,128)}, u32[]{:S(2)}) copy-start(f32[2,256,640]{2,1,0:T(8,128)} %copy-done.11) | copy-start | bytes 3932164
  290.6 1.7 copy-start.6
  290.6 2.1 copy-start.8
Sparse Core Ops, SparseCore 0:
  97.0 97.1 all-gather.1

commit v6 on v5

v6 whole, which is shorter than its diff:
```python
from functools import partial

import jax
import jax.numpy as jnp
from jax import lax
from jax.experimental import pallas as pl
from jax.experimental.pallas import tpu as pltpu
from jax.sharding import PartitionSpec as P

HD = 128
NEG = -1e30
NT = (((1,), (1,)), ((), ()))
NN = (((1,), (0,)), ((), ()))
TN = (((0,), (0,)), ((), ()))


def dot(lhs, rhs, dims):
    return lax.dot_general(lhs, rhs, dims, preferred_element_type=jnp.float32)


def attention_kernel(parts, f, adds, scal, *refs):
    own_q, own_k, own_v = refs[:3]
    others, refs = parts - 1, refs[3:]
    kv_refs, q_refs, refs = refs[:others], refs[others : 2 * others], refs[2 * others :]
    o_ref, d_ref, prev_ref, next_ref = refs[:4]
    refs = refs[4:]
    add_refs = []
    for count in adds:
        add_refs.append(refs[:count])
        refs = refs[count:]
    dq_ref, slot_refs, (q_all, k_all, v_all) = refs[0], refs[1:4], refs[4:]
    _, frames, rows, _ = own_k.shape
    tokens = rows * parts
    me = scal[0]
    inv_root = HD ** (-0.5)
    for s in range(parts):
        source = lax.rem(me + parts - s, parts)
        at = pl.ds(pl.multiple_of(source * rows, rows), rows)
        q_all[at] = own_q[0, 0] if s == 0 else q_refs[s - 1][...]
        for w in range(3):
            frame = f + w - 1
            if frame < 0 or frame == frames:
                side = prev_ref if frame < 0 else next_ref
                k_all[w, at] = side[0, s]
                v_all[w, at] = side[1, s]
            else:
                k_all[w, at] = own_k[0, frame] if s == 0 else kv_refs[s - 1][0, frame]
                v_all[w, at] = own_v[0, frame] if s == 0 else kv_refs[s - 1][1, frame]
    row = lax.broadcasted_iota(jnp.int32, (tokens, tokens), 0)
    q, d = q_all[...], d_ref[...]
    prod = d.astype(jnp.float32) * o_ref[0].reshape(tokens, HD).astype(jnp.float32)
    delta = lax.dot_general(
        jnp.ones((8, HD), jnp.float32), prod, NT,
        precision=lax.Precision.HIGHEST, preferred_element_type=jnp.float32,
    )[0:1]
    scores = []
    for w in range(3):
        s = dot(k_all[w], q, NT) * inv_root
        if w != 1:
            s = jnp.where(row < scal[2 + 2 * f + w // 2], s, NEG)
        scores.append(s)
    top = jnp.max(jnp.maximum(jnp.maximum(scores[0], scores[1]), scores[2]), axis=0, keepdims=True)
    exps = [jnp.exp(s - top) for s in scores]
    total = jnp.sum(exps[0] + exps[1] + exps[2], axis=0, keepdims=True)
    inv_total = 1.0 / total
    dq = None
    for w in range(3):
        prob = exps[w] * inv_total
        d_value = dot(prob.astype(jnp.bfloat16), d, NN)
        d_prob = dot(v_all[w], d, NT)
        d_score = (prob * (d_prob - delta)).astype(jnp.bfloat16)
        d_key = dot(d_score, q, NN) * inv_root
        term = dot(d_score, k_all[w], TN)
        dq = term if dq is None else dq + term
        for ref in add_refs[w]:
            d_key += ref[0].astype(jnp.float32)
            d_value += ref[1].astype(jnp.float32)
        slot_refs[w][0] = d_key.astype(slot_refs[w].dtype)
        slot_refs[w][1] = d_value.astype(slot_refs[w].dtype)
    dq_ref[...] = (dq * inv_root).astype(jnp.bfloat16)


def attention(scal, f, local, kv, q_pieces, o, d, halos, adds, dtypes):
    parts = len(kv) + 1
    _, frames, rows, _ = local[0].shape
    tokens, width = d.shape
    heads = width // HD
    own_q = pl.BlockSpec((1, 1, rows, HD), lambda h, sc: (0, f, 0, sc[1] + h))
    own = pl.BlockSpec((1, frames, rows, HD), lambda h, sc: (0, 0, 0, sc[1] + h))
    pack = pl.BlockSpec((2, frames, rows, HD), lambda h, sc: (0, 0, 0, h))
    q_spec = pl.BlockSpec((rows, HD), lambda h, sc: (0, h))
    o_spec = pl.BlockSpec((1, parts, rows, HD), lambda h, sc: (f, 0, 0, h))
    flat = pl.BlockSpec((tokens, HD), lambda h, sc: (0, h))
    halo = pl.BlockSpec((2, parts, rows, HD), lambda h, sc: (0, 0, 0, h))
    pair = pl.BlockSpec((2, tokens, HD), lambda h, sc: (0, 0, h))
    flat_adds = [a for group in adds for a in group]
    pads = pltpu.VMEM((3, tokens, HD), jnp.bfloat16)
    return pl.pallas_call(
        partial(attention_kernel, parts, f, [len(group) for group in adds]),
        grid_spec=pltpu.PrefetchScalarGridSpec(
            num_scalar_prefetch=1,
            grid=(heads,),
            in_specs=[own_q, own, own]
            + [pack] * (parts - 1)
            + [q_spec] * (parts - 1)
            + [o_spec, flat, halo, halo]
            + [pair] * len(flat_adds),
            out_specs=[flat] + [pair] * 3,
            scratch_shapes=[pltpu.VMEM((tokens, HD), jnp.bfloat16), pads, pads],
        ),
        out_shape=[jax.ShapeDtypeStruct((tokens, width), jnp.bfloat16)]
        + [jax.ShapeDtypeStruct((2, tokens, width), t) for t in dtypes],
        compiler_params=pltpu.CompilerParams(vmem_limit_bytes=40 * 2**20),
        cost_estimate=pl.CostEstimate(
            flops=heads * 3 * tokens * tokens * HD * 10,
            bytes_accessed=heads * HD * tokens * 40,
            transcendentals=heads * 3 * tokens * tokens,
        ),
        name="attention_backward",
    )(scal, *local, *kv, *q_pieces, o, d, *halos, *flat_adds)


def shifted(array, axis, step):
    count = lax.axis_size(axis)
    pairs = [(i, i + step) for i in range(count) if 0 <= i + step < count]
    return lax.ppermute(array, axis, pairs)


def rotated(array, axis, step):
    count = lax.axis_size(axis)
    return lax.ppermute(array, axis, [(i, (i + step) % count) for i in range(count)])


def after(array, event):
    return lax.optimization_barrier((array, event))


def flipped(array, axis, bit):
    return lax.ppermute(array, axis, [(i, i ^ bit) for i in range(lax.axis_size(axis))])


def weight_kernel(scale, table, near_ref, far_ref, g_near, g_far, *refs):
    out_ref = refs[-1]

    @pl.when(pl.program_id(0) == 0)
    def _():
        out_ref[...] = refs[0][...] if len(refs) > 1 else jnp.zeros_like(out_ref)

    total = dot(near_ref[0], g_near[0], TN) + dot(far_ref[0], g_far[0], TN)
    out_ref[...] += total * scale


def weight_grad(table, f, near, far, gated, scale, before):
    count, _, width = near.shape
    _, rows, columns = gated.shape
    side = pl.BlockSpec((1, rows, width), lambda j, tab: (j, f, 0))
    whole = pl.BlockSpec((width, columns), lambda j, tab: (0, 0))
    return pl.pallas_call(
        partial(weight_kernel, scale),
        grid_spec=pltpu.PrefetchScalarGridSpec(
            num_scalar_prefetch=1,
            grid=(count,),
            in_specs=[
                side,
                side,
                pl.BlockSpec((1, rows, columns), lambda j, tab: (tab[0, j], 0, 0)),
                pl.BlockSpec((1, rows, columns), lambda j, tab: (tab[1, j], 0, 0)),
            ]
            + [whole] * len(before),
            out_specs=whole,
        ),
        out_shape=jax.ShapeDtypeStruct((width, columns), jnp.float32),
        compiler_params=pltpu.CompilerParams(vmem_limit_bytes=40 * 2**20),
        cost_estimate=pl.CostEstimate(
            flops=4 * count * rows * width * columns,
            bytes_accessed=4 * count * rows * (width + columns) + 4 * width * columns,
            transcendentals=0,
        ),
        name="weight_gradient",
    )(table, near, far, gated, gated, *before)


def project_kernel(g_ref, w_ref, out_ref, acc_ref):
    step = pl.program_id(0)
    term = dot(g_ref[0], w_ref[...], NT)

    @pl.when(step == 0)
    def _():
        acc_ref[...] = term

    @pl.when(step > 0)
    def _():
        acc_ref[...] += term

    @pl.when(step == pl.num_programs(0) - 1)
    def _():
        out_ref[...] = acc_ref[...].astype(out_ref.dtype)


def project(gated, weight):
    blocks, rows, columns = gated.shape
    width = weight.shape[0]
    if columns % 128:
        whole = gated.transpose(1, 0, 2).reshape(rows, blocks * columns)
        return dot(whole, weight, NT).astype(jnp.bfloat16)
    return pl.pallas_call(
        project_kernel,
        grid=(blocks,),
        in_specs=[
            pl.BlockSpec((1, rows, columns), lambda b: (b, 0, 0)),
            pl.BlockSpec((width, columns), lambda b: (0, b)),
        ],
        out_specs=pl.BlockSpec((rows, width), lambda b: (0, 0)),
        out_shape=jax.ShapeDtypeStruct((rows, width), jnp.bfloat16),
        scratch_shapes=[pltpu.VMEM((rows, width), jnp.float32)],
        compiler_params=pltpu.CompilerParams(vmem_limit_bytes=40 * 2**20),
        cost_estimate=pl.CostEstimate(
            flops=2 * rows * width * blocks * columns,
            bytes_accessed=2 * (rows + width) * blocks * columns + 2 * rows * width,
            transcendentals=0,
        ),
        name="project_gated",
    )(gated, weight)


def per_device(
    queries, key_rows, value_rows, saved_out, cotangent, out_weight, gate_table, levels, reach_flags
):
    _, frames, rows, model = queries.shape
    parts = lax.axis_size("head")
    me = lax.axis_index("head")
    width = model // parts
    heads = width // HD
    frames_all = frames * lax.axis_size("frame")
    tokens = rows * parts
    first_frame = lax.axis_index("frame") * frames
    tokens_all = lax.axis_size("fsdp") * frames_all * tokens
    blocks = lax.axis_size("frame") * lax.axis_size("fsdp")
    block = model // blocks
    def columns_for(array, step, start, size):
        target = lax.rem(me + step, parts)
        return lax.dynamic_slice_in_dim(array[0], target * width + start, size, axis=2)

    shifts = range(1, parts)
    o_pieces = [rotated(columns_for(saved_out, s, 0, width), "head", s) for s in shifts]

    gain = jnp.concatenate(
        [lax.dynamic_slice_in_dim(gate_table, levels[f], 1, axis=0) for f in range(frames)], axis=0
    )
    gated = (cotangent[0].astype(jnp.float32) * gain[:, None, :]).astype(jnp.bfloat16)
    gated = [
        jnp.stack([gated[f, :, b * block : (b + 1) * block] for b in range(blocks)])
        for f in range(frames)
    ]

    kv_send = [
        jnp.stack([columns_for(a, s, 0, width) for a in (key_rows, value_rows)]) for s in shifts
    ]
    q_send = [[columns_for(queries, s, 0, width)[f] for s in shifts] for f in range(frames)]
    kv_send, q_send[0], o_pieces = lax.optimization_barrier((kv_send, q_send[0], o_pieces))
    kv = [rotated(a, "head", s) for s, a in zip(shifts, kv_send)]
    q_pieces = [[rotated(a, "head", s) for s, a in zip(shifts, q_send[0])]]

    own = [columns_for(a, 0, 0, width) for a in (key_rows, value_rows)]

    def boundary(frame):
        return jnp.stack(
            [jnp.stack([own[t][frame]] + [p[t, frame] for p in kv]) for t in range(2)]
        )

    gated[0], q_pieces[0], kv = lax.optimization_barrier((gated[0], q_pieces[0], kv))
    halos = (
        shifted(boundary(frames - 1), "frame", 1),
        shifted(boundary(0), "frame", -1),
    )

    gathered = [lax.all_gather(gated[0], "head", axis=1, tiled=True)]
    for f in range(1, frames):
        gated[f], gathered[-1], halos = lax.optimization_barrier((gated[f], gathered[-1], halos))
        gathered.append(lax.all_gather(gated[f], "head", axis=1, tiled=True))
        q_send[f], gathered[f] = after(q_send[f], gathered[f])
        q_pieces.append([rotated(a, "head", s) for s, a in zip(shifts, q_send[f])])

    o = jnp.zeros((frames, parts, rows, width), jnp.bfloat16)
    for s, piece in enumerate([columns_for(saved_out, 0, 0, width)] + o_pieces):
        source = lax.rem(me + parts - s, parts)
        o = lax.dynamic_update_slice_in_dim(o, piece[:, None], source, axis=1)

    levels_xy = [("fsdp", 1 << i) for i in range(lax.axis_size("fsdp").bit_length() - 1)]
    levels_xy += [("frame", 1 << i) for i in range(lax.axis_size("frame").bit_length() - 2, 0, -1)]
    near = o.reshape(1, frames * parts * rows, width)
    flips = [(0, 0)]
    for axis, bit in levels_xy:
        near = jnp.concatenate([near, flipped(near, axis, bit)], axis=0)
        flips += [(a ^ bit, b) if axis == "frame" else (a, b ^ bit) for a, b in flips]
    far = flipped(near, "frame", 1)
    my_frame, my_video = lax.axis_index("frame"), lax.axis_index("fsdp")
    videos = lax.axis_size("fsdp")
    table = jnp.stack(
        [
            jnp.stack([(my_frame ^ (a ^ c)) * videos + (my_video ^ b) for a, b in flips])
            for c in range(2)
        ]
    ).astype(jnp.int32)

    ids = first_frame + jnp.arange(frames, dtype=jnp.int32)
    chosen = lax.dynamic_slice_in_dim(reach_flags, first_frame, frames, axis=0)
    inside = jnp.stack([ids > 0, ids < frames_all - 1], axis=1)
    limits = jnp.where(inside, jnp.where(chosen == 1, tokens, tokens // 2), 0).astype(jnp.int32)
    scal = jnp.concatenate([jnp.stack([me, me * heads]).astype(jnp.int32), limits.reshape(-1)])

    local = (queries, key_rows, value_rows)
    d_queries, done, before = [], [None] * frames, []
    own_part, next_part, from_next = None, None, None
    last = frames - 1
    for f in range(frames):
        columns = lax.all_to_all(
            gathered[f], ("frame", "fsdp"), split_axis=0, concat_axis=0, tiled=True
        )
        d = project(gathered[f], out_weight)
        d, before = after(d, before)
        adds = [[], [], []]
        if f > 0:
            adds = [[own_part], [next_part], []]
        if f > 0 and f == last:
            adds[1].append(from_next)
        exact, low = jnp.float32, jnp.bfloat16
        dtypes = [
            exact if f == 1 else low,
            low if f == last and f > 0 else exact,
            low if f == last else exact,
        ]
        dq, to_prev, own_part, next_part = attention(
            scal, f, local, kv, q_pieces[f], o, d, halos, adds, dtypes
        )
        d_queries.append(dq)
        if f == 0:
            from_next = shifted(to_prev, "frame", -1)
        else:
            done[f - 1] = to_prev
        before = [weight_grad(table, f, near, far, columns, 1.0 / tokens_all, before)]
    done[last] = own_part
    from_prev = shifted(next_part, "frame", 1)
    d_weight, from_prev = after(before[0], from_prev)
    done[0] = done[0].astype(jnp.float32) + from_prev.astype(jnp.float32)
    if last == 0:
        done[0] = done[0] + from_next.astype(jnp.float32)
    done = [pair.astype(jnp.bfloat16) for pair in done]
    d_keys, d_values = (jnp.stack([pair[t] for pair in done])[None] for t in range(2))
    return jnp.stack(d_queries)[None], d_keys, d_values, d_weight


def solution(mesh):
    rows = P("fsdp", "frame", "head", None)
    heads = P("fsdp", "frame", None, "head")
    in_specs = (rows, rows, rows, rows, rows, P("head", None), P(), P("frame"), P())
    out_specs = (heads, heads, heads, P("head", ("frame", "fsdp")))
    return jax.shard_map(
        per_device, mesh=mesh, in_specs=in_specs, out_specs=out_specs, check_vma=False
    )
```

time: 306 us -> 335 us (1.095)
  waiting for transfers between devices: 117 us -> 139 us
  starting transfers between devices: 68.4 us -> 46.7 us
  Pallas kernels: 60.2 us -> 75.6 us
  local copies, waits for them, and re-layouts: 27.6 us -> 35.5 us
  other arithmetic: 11.9 us -> 16.2 us
    ppermute x3, waiting for transfers between devices: 84.2 us -> 46.9 us  [flipped(): lax.ppermute(array, axis, [(i, i ^ bit) for i in range(lax.axis_size(axis...]
    ppermute x12, waiting for transfers between devices: 32.6 us -> 67.4 us  [rotated(): lax.ppermute(array, axis, [(i, (i + step) % count) for i in range(count)])]
    ppermute x12, starting transfers between devices: 44.7 us -> 19.3 us  [rotated(): lax.ppermute(array, axis, [(i, (i + step) % count) for i in range(count)])]
    all_gather x1 -> x2, waiting for transfers between devices: 0.01 us -> 14.5 us  [the longest x1 14.5 us: per_device(): gathered.append(lax.all_gather(gated[f], 'head', axis=1, tiled=True))]
    ppermute x6 -> x4, waiting for transfers between devices: 0.02 us -> 10.2 us  [shifted(): return lax.ppermute(array, axis, pairs)]
    pallas_call x1 -> x2, Pallas kernels: 13.4 us -> 21.6 us  [project(): pl.pallas_call(project_kernel, grid=(blocks,), in_specs=[pl.BlockSpec((1,...]
    unnamed x50 -> x81, local copies, waits for them, and re-layouts: 13.3 us -> 19.8 us
    ppermute x6 -> x4, starting transfers between devices: 17.8 us -> 11.9 us  [shifted(): return lax.ppermute(array, axis, pairs)]
  transfers between devices with their start and end apart: 23 -> 23, of which waited for: 4 -> 7; matrix products, arithmetic and copies ran while one was open for 9% -> 9% of each run, Pallas kernels for 20% -> 23%
where the time goes in v6:
time: 335 us; the launch traced here: 332 us
  waiting for transfers between devices  139 us (41%)
  Pallas kernels  75.6 us (23%)
  starting transfers between devices  46.7 us (14%)
  local copies, waits for them, and re-layouts  35.5 us (11%)
  between operations  18.5 us (6%)
  other arithmetic  16.2 us (5%)
    ppermute x12, waiting for transfers between devices, rotated(): lax.ppermute(array, axis, [(i, (i + step) % count) for i in range(count)])  67.4 us
    ppermute x3, waiting for transfers between devices, flipped(): lax.ppermute(array, axis, [(i, i ^ bit) for i in range(lax.axis_size(axis...  46.9 us
    pallas_call x2, Pallas kernels, attention(): pl.pallas_call(partial(attention_kernel, parts, f, [len(group) for group...  36.6 us
    pallas_call x2, Pallas kernels, project(): pl.pallas_call(project_kernel, grid=(blocks,), in_specs=[pl.BlockSpec((1,...  21.6 us
    unnamed x81, local copies, waits for them, and re-layouts  19.8 us
    ppermute x12, starting transfers between devices, rotated(): lax.ppermute(array, axis, [(i, (i + step) % count) for i in range(count)])  19.3 us
    pallas_call x2, Pallas kernels, weight_grad(): pl.pallas_call(partial(weight_kernel, scale), grid_spec=pltpu.PrefetchSca...  17.4 us
    all_gather x1, waiting for transfers between devices, per_device(): gathered.append(lax.all_gather(gated[f], 'head', axis=1, tiled=True))  14.5 us
  transfers between devices with their start and end apart: 23, of which 7 were waited for; matrix products, arithmetic and copies ran while one was open for 9% of the time, Pallas kernels for 23%

profile of v6, /device:TPU:11, one launch (start us, length us, event | category | flops | bytes accessed | tf_op | source)
XLA Modules:
  0.0 331.5 jit_solution(8655011563333744637)
XLA Ops:
  7.2 2.2 dynamic-slice_bitcast_fusion
  9.6 2.3 collective-permute-start.1
  11.9 2.2 collective-permute-start
  19.7 1.7 fusion
  25.3 1.6 slice_dynamic-update-slice_fusion.6
  26.9 1.6 slice_dynamic-update-slice_fusion.5
  31.1 1.6 slice_dynamic-update-slice_fusion.4
  32.7 2.2 dynamic-slice_bitcast_fusion.3
  34.9 5.1 %collective-permute-done = bf16[2,64,1280]{2,1,0:T(8,128)(2,1)} collective-permute-done((bf16[2,64,1280]{2,1,0:T(8,128)(2,1)}, bf16[2,64,1280]{2,1,0:T(8,128)(2,1)}, u32[]{:S(2)}, u32[]{:S(2)}) %collective-permute-start) | collective-permute-done | bytes 327712 | tf_op jit(solution)/shard_map/ppermute | solution.py:131
  44.8 2.2 collective-permute-start.3
  47.0 1.3 collective-permute-start.7
  49.6 1.9 collective-permute-start.4
  52.2 59.9 %collective-permute-done.4.refs_7_ = bf16[64,1280]{1,0:T(8,128)(2,1)S(1)} collective-permute-done((bf16[64,1280]{1,0:T(8,128)(2,1)S(1)}, bf16[64,1280]{1,0:T(8,128)(2,1)S(1)}, u32[]{:S(2)}, u32[]{:S(2)}) %collective-permute-start.4) | collective-permute-done | bytes 163872 | tf_op jit(solution)/shard_map/ppermute | solution.py:131
  112.1 4.4 %collective-permute-start.5 = (bf16[64,1280]{1,0:T(8,128)(2,1)S(1)}, bf16[64,1280]{1,0:T(8,128)(2,1)S(1)}, u32[]{:S(2)}, u32[]{:S(2)}) collective-permute-start(bf16[64,1280]{1,0:T(8,128)(2,1)S(1)} %get-tuple-element.42), channel_id=1, source_target_pairs={{0,6},{2,0},{4,2},{6,4},{1,7},{3,1},{5,3},{7,5},{8,14},{10,8},{12,... | collective-permute-start | bytes 491528 | tf_op jit(solution)/shard_map/ppermute | solution.py:131
  117.2 2.4 collective-permute-done.5.refs_8_
  120.5 1.6 pad_maximum_fusion.1
  122.0 1.3 collective-permute-start.15
  123.3 1.2 slice_bitcast_fusion.4
  124.5 1.2 slice_bitcast_fusion.3
  126.1 3.8 %collective-permute-start.9 = (bf16[2,4,64,1280]{3,2,1,0:T(8,128)(2,1)S(1)}, bf16[2,4,64,1280]{3,2,1,0:T(8,128)(2,1)S(1)}, u32[]{:S(2)}, u32[]{:S(2)}) collective-permute-start(bf16[2,4,64,1280]{3,2,1,0:T(8,128)(2,1)S(1)} %pad_maximum_fusion.2), channel_id=1, source_target_pairs={{0,8},{8,16},{16,24},{1,9},{9,17},{17,25},{2,10},{10,18},{18,26},{... | collective-permute-start | bytes 3932168 | tf_op jit(solution)/shard_map/ppermute | solution.py:126
  130.2 1.9 collective-permute-start.10
  132.2 46.9 %collective-permute-done.15 = bf16[2,512,1280]{2,1,0:T(8,128)(2,1)S(1)} collective-permute-done((bf16[2,512,1280]{2,1,0:T(8,128)(2,1)S(1)}, bf16[2,512,1280]{2,1,0:T(8,128)(2,1)S(1)}, u32[]{:S(2)}, u32[]{:S(2)}) %collective-permute-start.15) | collective-permute-done | bytes 2621472 | tf_op jit(solution)/shard_map/ppermute | solution.py:139
  179.1 4.2 %pad_maximum_fusion.near_ref = bf16[4,512,1280]{2,1,0:T(8,128)(2,1)} fusion(bf16[2,512,1280]{2,1,0:T(8,128)(2,1)S(1)} %collective-permute-done.15, bf16[1,512,1280]{2,1,0:T(8,128)(2,1)} %collective-permute-done.14, bf16[1,512,1280]{2,1,0:T(8,128)(2,1)S(1)} %bitcast.96), kind=kLoop, calls=%fused_computation | loop fusion | flops 5242880 | bytes 10485760 | tf_op jit(solution)/shard_map/concatenate | solution.py:294
  183.3 3.2 collective-permute-start.16
  186.4 7.6 %collective-permute-done.9.refs_11_ = bf16[2,4,64,1280]{3,2,1,0:T(8,128)(2,1)S(1)} collective-permute-done((bf16[2,4,64,1280]{3,2,1,0:T(8,128)(2,1)S(1)}, bf16[2,4,64,1280]{3,2,1,0:T(8,128)(2,1)S(1)}, u32[]{:S(2)}, u32[]{:S(2)}) %collective-permute-start.9) | collective-permute-done | bytes 1310752 | tf_op jit(solution)/shard_map/ppermute | solution.py:126
  195.1 1.1 copy-done.13
  196.2 5.3 %all-to-all-start = ((bf16[8,256,640]{2,1,0:T(8,128)(2,1)}), bf16[8,256,640]{2,1,0:T(8,128)(2,1)}, u32[]{:S(2)}, u32[]{:S(2)}) async-start(bf16[8,256,640]{2,1,0:T(8,128)(2,1)} %all-gather.3.cloned.1.call-done.g_ref), calls=%async_computation | async-start | bytes 5242880 | tf_op jit(solution)/shard_map/all_to_all | solution.py:317
  201.9 1.7 copy-done.7
  203.6 11.3 %project_gated.2.refs_10_ = bf16[256,1280]{1,0:T(8,128)(2,1)S(1)} custom-call(bf16[8,256,640]{2,1,0:T(8,128)(2,1)S(1)} %copy-done.7, bf16[1280,5120]{1,0:T(8,128)(2,1)} %w_ref.3), custom_call_target="tpu_custom_call" | custom-call | flops 3355443200 | bytes 16384000 | tf_op jit(solution)/shard_map/project_gated/pallas_call | solution.py:206
  215.0 17.8 %attention_backward.2 = (bf16[256,1280]{1,0:T(8,128)(2,1)S(1)}, bf16[2,256,1280]{2,1,0:T(8,128)(2,1)}, f32[2,256,1280]{2,1,0:T(8,128)}, f32[2,256,1280]{2,1,0:T(8,128)}) custom-call(s32[6]{0:T(128)S(1)} %pad_add_fusion.1.scal, bf16[1,2,64,5120]{3,2,1,0:T(8,128)(2,1)S(1)} %copy-done.8, bf16[1,2,64,5120]{3,2,1,0:T(8,128)(2,1)S(1)} %copy-done.2, ...), custom_call_target="tpu_custom_call" | custom-call | flops 2516582400 | bytes 13107200 | tf_op jit(solution)/shard_map/attention_backward/pallas_call | solution.py:98
  233.7 2.3 collective-permute-start.17
  235.9 14.5 %all-gather.5.cloned.1.call-done.g_ref = bf16[8,256,640]{2,1,0:T(8,128)(2,1)} async-done(((bf16[8,64,640]{2,1,0:T(8,128)(2,1)}), bf16[8,256,640]{2,1,0:T(8,128)(2,1)}) %all-gather.5.cloned.1.call-update) | async-done | bytes 2621456 | tf_op jit(solution)/shard_map/all_gather | solution.py:280
  250.4 5.3 %all-to-all-start.1 = ((bf16[8,256,640]{2,1,0:T(8,128)(2,1)}), bf16[8,256,640]{2,1,0:T(8,128)(2,1)}, u32[]{:S(2)}, u32[]{:S(2)}) async-start(bf16[8,256,640]{2,1,0:T(8,128)(2,1)} %all-gather.5.cloned.1.call-done.g_ref), calls=%async_computation.1 | async-start | bytes 5242880 | tf_op jit(solution)/shard_map/all_to_all | solution.py:317
  255.8 1.9 collective-permute-start.11
  257.7 2.3 collective-permute-start.12
  260.0 1.7 copy-done.6
  261.8 10.3 %project_gated.3.refs_10_ = bf16[256,1280]{1,0:T(8,128)(2,1)S(1)} custom-call(bf16[8,256,640]{2,1,0:T(8,128)(2,1)S(1)} %copy-done.6, bf16[1280,5120]{1,0:T(8,128)(2,1)} %w_ref.3), custom_call_target="tpu_custom_call" | custom-call | flops 3355443200 | bytes 16384000 | tf_op jit(solution)/shard_map/project_gated/pallas_call | solution.py:206
  272.2 8.0 %weight_gradient.2.refs_0_ = f32[1280,640]{1,0:T(8,128)S(1)} custom-call(s32[2,4]{1,0:T(2,128)S(1)} %pad_add_fusion.table, bf16[4,512,1280]{2,1,0:T(8,128)(2,1)} %pad_maximum_fusion.near_ref, bf16[4,512,1280]{2,1,0:T(8,128)(2,1)} %collective-permute-done.16.far_ref, bf16[8,256,640]{2,1,0:T(8,128)(2,1)} %all-to-all-done.g_near.g_far, ...), custom_call_target="tpu_custom_call" | custom-call | flops 3355443200 | bytes 11141120 | tf_op jit(solution)/shard_map/weight_gradient/pallas_call | solution.py:158
  280.1 1.7 copy-done
  281.9 18.8 %attention_backward.3 = (bf16[256,1280]{1,0:T(8,128)(2,1)S(1)}, f32[2,256,1280]{2,1,0:T(8,128)}, bf16[2,256,1280]{2,1,0:T(8,128)(2,1)S(1)}, bf16[2,256,1280]{2,1,0:T(8,128)(2,1)}) custom-call(s32[6]{0:T(128)S(1)} %pad_add_fusion.1.scal, bf16[1,2,64,5120]{3,2,1,0:T(8,128)(2,1)S(1)} %copy-done.9, bf16[1,2,64,5120]{3,2,1,0:T(8,128)(2,1)S(1)} %copy-done.2, ...), custom_call_target="tpu_custom_call" | custom-call | flops 2516582400 | bytes 13107200 | tf_op jit(solution)/shard_map/attention_backward/pallas_call | solution.py:98
  300.7 3.9 %collective-permute-start.18 = (bf16[2,256,1280]{2,1,0:T(8,128)(2,1)}, bf16[2,256,1280]{2,1,0:T(8,128)(2,1)}, u32[]{:S(2)}, u32[]{:S(2)}) collective-permute-start(bf16[2,256,1280]{2,1,0:T(8,128)(2,1)} %get-tuple-element.72), channel_id=1, source_target_pairs={{0,8},{8,16},{16,24},{1,9},{9,17},{17,25},{2,10},{10,18},{18,26},{... | collective-permute-start | bytes 3932168 | tf_op jit(solution)/shard_map/ppermute | solution.py:126
  304.7 1.2 maximum_bitcast_fusion
  305.8 1.2 fusion.4
  307.5 9.4 %weight_gradient.3 = f32[1280,640]{1,0:T(8,128)} custom-call(s32[2,4]{1,0:T(2,128)S(1)} %pad_add_fusion.table, bf16[4,512,1280]{2,1,0:T(8,128)(2,1)} %pad_maximum_fusion.near_ref, bf16[4,512,1280]{2,1,0:T(8,128)(2,1)} %collective-permute-done.16.far_ref, bf16[8,256,640]{2,1,0:T(8,128)(2,1)} %all-to-all-done.1.g_near.g_far, ...), custom_call_target="tpu_custom_call" | custom-call | flops 3355443200 | bytes 11141120 | tf_op jit(solution)/shard_map/weight_gradient/pallas_call | solution.py:158
  316.9 2.6 collective-permute-done.18
  319.5 1.7 add_convert_fusion
  322.2 1.2 maximum_bitcast_fusion.2
  323.5 1.2 maximum_bitcast_fusion.1
  (128 shorter events, 21.4 us)
Async XLA Ops:
  7.2 6.9 %copy-start.35 = (s32[2]{0:T(128)S(1)}, s32[2]{0:T(128)}, u32[]{:S(2)}) copy-start(s32[2]{0:T(128)} %param.16) | copy-start | bytes 28
  7.2 189.0 %all-gather.3.cloned.1.call-start = ((), (), s32[]{:S(2)}) async-start(), calls=%async_computation.2 | async-start | bytes 3276800 | tf_op jit(solution)/shard_map/all_gather | solution.py:277
  9.4 25.5 %collective-permute-start.2 = (bf16[2,64,1280]{2,1,0:T(8,128)(2,1)}, bf16[2,64,1280]{2,1,0:T(8,128)(2,1)}, u32[]{:S(2)}, u32[]{:S(2)}) collective-permute-start(bf16[2,64,1280]{2,1,0:T(8,128)(2,1)} %get-tuple-element.106), channel_id=1, source_target_pairs={{0,6},{2,0},{4,2},{6,4},{1,7},{3,1},{5,3},{7,5},{8,14},{10,8},{12,... | collective-permute-start | bytes 983048 | tf_op jit(solution)/shard_map/ppermute | solution.py:131
  9.6 25.3 %collective-permute-start.1 = (bf16[2,64,1280]{2,1,0:T(8,128)(2,1)}, bf16[2,64,1280]{2,1,0:T(8,128)(2,1)}, u32[]{:S(2)}, u32[]{:S(2)}) collective-permute-start(bf16[2,64,1280]{2,1,0:T(8,128)(2,1)} %get-tuple-element.107), channel_id=1, source_target_pairs={{0,4},{2,6},{4,0},{6,2},{1,5},{3,7},{5,1},{7,3},{8,12},{10,14},{12... | collective-permute-start | bytes 983048 | tf_op jit(solution)/shard_map/ppermute | solution.py:131
  11.9 28.1 %collective-permute-start = (bf16[2,64,1280]{2,1,0:T(8,128)(2,1)}, bf16[2,64,1280]{2,1,0:T(8,128)(2,1)}, u32[]{:S(2)}, u32[]{:S(2)}) collective-permute-start(bf16[2,64,1280]{2,1,0:T(8,128)(2,1)} %get-tuple-element.108), channel_id=1, source_target_pairs={{0,2},{2,4},{4,6},{6,0},{1,3},{3,5},{5,7},{7,1},{8,10},{10,12},{12... | collective-permute-start | bytes 983048 | tf_op jit(solution)/shard_map/ppermute | solution.py:131
  19.7 3.4 %copy-start.2 = (bf16[1,2,64,5120]{3,2,1,0:T(8,128)(2,1)S(1)}, bf16[1,2,64,5120]{3,2,1,0:T(8,128)(2,1)}, u32[]{:S(2)}) copy-start(bf16[1,2,64,5120]{3,2,1,0:T(8,128)(2,1)} %refs_1_.3) | copy-start | bytes 3932164
  19.7 3.4 %copy-start.3 = (bf16[1,2,64,5120]{3,2,1,0:T(8,128)(2,1)S(1)}, bf16[1,2,64,5120]{3,2,1,0:T(8,128)(2,1)}, u32[]{:S(2)}) copy-start(bf16[1,2,64,5120]{3,2,1,0:T(8,128)(2,1)} %refs_2_.3) | copy-start | bytes 3932164
  32.7 14.3 %copy-start.34 = (bf16[2,2,64,1280]{3,2,1,0:T(8,128)(2,1)S(1)}, bf16[2,2,64,1280]{3,2,1,0:T(8,128)(2,1)}, u32[]{:S(2)}) copy-start(bf16[2,2,64,1280]{3,2,1,0:T(8,128)(2,1)} %pad_maximum_fusion.4) | copy-start | bytes 1966084
  32.7 14.3 %copy-start.33 = (bf16[2,2,64,1280]{3,2,1,0:T(8,128)(2,1)S(1)}, bf16[2,2,64,1280]{3,2,1,0:T(8,128)(2,1)}, u32[]{:S(2)}) copy-start(bf16[2,2,64,1280]{3,2,1,0:T(8,128)(2,1)} %pad_maximum_fusion.5) | copy-start | bytes 1966084
  34.9 8.4 %copy-start.23 = (bf16[2,64,5120]{2,1,0:T(8,128)(2,1)S(1)}, bf16[2,64,5120]{2,1,0:T(8,128)(2,1)}, u32[]{:S(2)}) copy-start(bf16[2,64,5120]{2,1,0:T(8,128)(2,1)} %copy-done.22) | copy-start | bytes 3932164
  34.9 13.4 %copy-start.32 = (bf16[2,2,64,1280]{3,2,1,0:T(8,128)(2,1)S(1)}, bf16[2,2,64,1280]{3,2,1,0:T(8,128)(2,1)}, u32[]{:S(2)}) copy-start(bf16[2,2,64,1280]{3,2,1,0:T(8,128)(2,1)} %pad_maximum_fusion.6) | copy-start | bytes 1966084
  43.0 77.5 %collective-permute-start.14 = (bf16[1,512,1280]{2,1,0:T(8,128)(2,1)S(1)}, bf16[1,512,1280]{2,1,0:T(8,128)(2,1)}, u32[]{:S(2)}, u32[]{:S(2)}) collective-permute-start(bf16[1,512,1280]{2,1,0:T(8,128)(2,1)S(1)} %bitcast.94), channel_id=1, source_target_pairs={{0,1},{1,0},{2,3},{3,2},{4,5},{5,4},{6,7},{7,6},{8,9},{9,8},{10,11... | collective-permute-start | bytes 3932168 | tf_op jit(solution)/shard_map/ppermute | solution.py:139
  44.8 4.8 %collective-permute-start.3 = (bf16[64,1280]{1,0:T(8,128)(2,1)S(1)}, bf16[64,1280]{1,0:T(8,128)(2,1)S(1)}, u32[]{:S(2)}, u32[]{:S(2)}) collective-permute-start(bf16[64,1280]{1,0:T(8,128)(2,1)S(1)} %get-tuple-element.40), channel_id=1, source_target_pairs={{0,2},{2,4},{4,6},{6,0},{1,3},{3,5},{5,7},{7,1},{8,10},{10,12},{12... | collective-permute-start | bytes 491528 | tf_op jit(solution)/shard_map/ppermute | solution.py:131
  47.0 73.3 %collective-permute-start.6 = (bf16[2,2,64,1280]{3,2,1,0:T(8,128)(2,1)S(1)}, bf16[2,2,64,1280]{3,2,1,0:T(8,128)(2,1)S(1)}, u32[]{:S(2)}, u32[]{:S(2)}) collective-permute-start(bf16[2,2,64,1280]{3,2,1,0:T(8,128)(2,1)S(1)} %copy-done.34), channel_id=1, source_target_pairs={{0,2},{2,4},{4,6},{6,0},{1,3},{3,5},{5,7},{7,1},{8,10},{10,12},{12... | collective-permute-start | bytes 1966088 | tf_op jit(solution)/shard_map/ppermute | solution.py:131
  47.0 73.3 %collective-permute-start.7 = (bf16[2,2,64,1280]{3,2,1,0:T(8,128)(2,1)S(1)}, bf16[2,2,64,1280]{3,2,1,0:T(8,128)(2,1)}, u32[]{:S(2)}, u32[]{:S(2)}) collective-permute-start(bf16[2,2,64,1280]{3,2,1,0:T(8,128)(2,1)S(1)} %copy-done.33), channel_id=1, source_target_pairs={{0,4},{2,6},{4,0},{6,2},{1,5},{3,7},{5,1},{7,3},{8,12},{10,14},{12... | collective-permute-start | bytes 1966088 | tf_op jit(solution)/shard_map/ppermute | solution.py:131
  48.4 72.0 %collective-permute-start.8 = (bf16[2,2,64,1280]{3,2,1,0:T(8,128)(2,1)S(1)}, bf16[2,2,64,1280]{3,2,1,0:T(8,128)(2,1)}, u32[]{:S(2)}, u32[]{:S(2)}) collective-permute-start(bf16[2,2,64,1280]{3,2,1,0:T(8,128)(2,1)S(1)} %copy-done.32), channel_id=1, source_target_pairs={{0,6},{2,0},{4,2},{6,4},{1,7},{3,1},{5,3},{7,5},{8,14},{10,8},{12,... | collective-permute-start | bytes 1966088 | tf_op jit(solution)/shard_map/ppermute | solution.py:131
  49.6 62.5 %collective-permute-start.4 = (bf16[64,1280]{1,0:T(8,128)(2,1)S(1)}, bf16[64,1280]{1,0:T(8,128)(2,1)S(1)}, u32[]{:S(2)}, u32[]{:S(2)}) collective-permute-start(bf16[64,1280]{1,0:T(8,128)(2,1)S(1)} %get-tuple-element.41), channel_id=1, source_target_pairs={{0,4},{2,6},{4,0},{6,2},{1,5},{3,7},{5,1},{7,3},{8,12},{10,14},{12... | collective-permute-start | bytes 491528 | tf_op jit(solution)/shard_map/ppermute | solution.py:131
  112.1 8.2 %copy-start.18 = (bf16[64,1280]{1,0:T(8,128)(2,1)}, bf16[64,1280]{1,0:T(8,128)(2,1)S(1)}, u32[]{:S(2)}) copy-start(bf16[64,1280]{1,0:T(8,128)(2,1)S(1)} %collective-permute-done.4.refs_7_) | copy-start | bytes 491524
  112.1 7.5 %collective-permute-start.5 = (bf16[64,1280]{1,0:T(8,128)(2,1)S(1)}, bf16[64,1280]{1,0:T(8,128)(2,1)S(1)}, u32[]{:S(2)}, u32[]{:S(2)}) collective-permute-start(bf16[64,1280]{1,0:T(8,128)(2,1)S(1)} %get-tuple-element.42), channel_id=1, source_target_pairs={{0,6},{2,0},{4,2},{6,4},{1,7},{3,1},{5,3},{7,5},{8,14},{10,8},{12,... | collective-permute-start | bytes 491528 | tf_op jit(solution)/shard_map/ppermute | solution.py:131
  120.3 130.0 %all-gather.5.cloned.1.call-start = ((), (), s32[]{:S(2)}) async-start(), calls=%async_computation.3 | async-start | bytes 3276800 | tf_op jit(solution)/shard_map/all_gather | solution.py:280
  122.0 3.8 %copy-start.31 = (bf16[1,64,1280]{2,1,0:T(8,128)(2,1)S(1)}, bf16[1,64,1280]{2,1,0:T(8,128)(2,1)}, u32[]{:S(2)}) copy-start(bf16[1,64,1280]{2,1,0:T(8,128)(2,1)} %get-tuple-element.83) | copy-start | bytes 491524
  122.0 57.1 %collective-permute-start.15 = (bf16[2,512,1280]{2,1,0:T(8,128)(2,1)S(1)}, bf16[2,512,1280]{2,1,0:T(8,128)(2,1)S(1)}, u32[]{:S(2)}, u32[]{:S(2)}) collective-permute-start(bf16[2,512,1280]{2,1,0:T(8,128)(2,1)S(1)} %pad_maximum_fusion.1), channel_id=1, source_target_pairs={{0,16},{8,24},{16,0},{24,8},{1,17},{9,25},{17,1},{25,9},{2,18},{10... | collective-permute-start | bytes 7864328 | tf_op jit(solution)/shard_map/ppermute | solution.py:139
  126.0 3.9 %copy-start.29 = (bf16[1,64,1280]{2,1,0:T(8,128)(2,1)S(1)}, bf16[1,64,1280]{2,1,0:T(8,128)(2,1)}, u32[]{:S(2)}) copy-start(bf16[1,64,1280]{2,1,0:T(8,128)(2,1)} %get-tuple-element.139) | copy-start | bytes 491524
  126.1 3.9 %copy-start.28 = (bf16[1,64,1280]{2,1,0:T(8,128)(2,1)S(1)}, bf16[1,64,1280]{2,1,0:T(8,128)(2,1)}, u32[]{:S(2)}) copy-start(bf16[1,64,1280]{2,1,0:T(8,128)(2,1)} %get-tuple-element.82) | copy-start | bytes 491524
  126.1 67.9 %collective-permute-start.9 = (bf16[2,4,64,1280]{3,2,1,0:T(8,128)(2,1)S(1)}, bf16[2,4,64,1280]{3,2,1,0:T(8,128)(2,1)S(1)}, u32[]{:S(2)}, u32[]{:S(2)}) collective-permute-start(bf16[2,4,64,1280]{3,2,1,0:T(8,128)(2,1)S(1)} %pad_maximum_fusion.2), channel_id=1, source_target_pairs={{0,8},{8,16},{16,24},{1,9},{9,17},{17,25},{2,10},{10,18},{18,26},{... | collective-permute-start | bytes 3932168 | tf_op jit(solution)/shard_map/ppermute | solution.py:126
  130.2 64.9 %collective-permute-start.10 = (bf16[2,4,64,1280]{3,2,1,0:T(8,128)(2,1)S(1)}, bf16[2,4,64,1280]{3,2,1,0:T(8,128)(2,1)S(1)}, u32[]{:S(2)}, u32[]{:S(2)}) collective-permute-start(bf16[2,4,64,1280]{3,2,1,0:T(8,128)(2,1)S(1)} %pad_maximum_fusion.3), channel_id=1, source_target_pairs={{8,0},{16,8},{24,16},{9,1},{17,9},{25,17},{10,2},{18,10},{26,18},{... | collective-permute-start | bytes 3932168 | tf_op jit(solution)/shard_map/ppermute | solution.py:126
  183.3 88.9 %collective-permute-start.16 = (bf16[4,512,1280]{2,1,0:T(8,128)(2,1)}, bf16[4,512,1280]{2,1,0:T(8,128)(2,1)}, u32[]{:S(2)}, u32[]{:S(2)}) collective-permute-start(bf16[4,512,1280]{2,1,0:T(8,128)(2,1)} %pad_maximum_fusion.near_ref), channel_id=1, source_target_pairs={{0,8},{8,0},{16,24},{24,16},{1,9},{9,1},{17,25},{25,17},{2,10},{10... | collective-permute-start | bytes 15728648 | tf_op jit(solution)/shard_map/ppermute | solution.py:139
  196.2 5.3 %copy-start.36 = (s32[8,2]{0,1:T(2,128)S(1)}, s32[8,2]{0,1:T(2,128)}, u32[]{:S(2)}) copy-start(s32[8,2]{0,1:T(2,128)} %param.17) | copy-start | bytes 196
  196.2 54.2 %all-to-all-start = ((bf16[8,256,640]{2,1,0:T(8,128)(2,1)}), bf16[8,256,640]{2,1,0:T(8,128)(2,1)}, u32[]{:S(2)}, u32[]{:S(2)}) async-start(bf16[8,256,640]{2,1,0:T(8,128)(2,1)} %all-gather.3.cloned.1.call-done.g_ref), calls=%async_computation | async-start | bytes 5242880 | tf_op jit(solution)/shard_map/all_to_all | solution.py:317
  203.6 11.4 %copy-start.4 = (bf16[1,2,64,5120]{3,2,1,0:T(8,128)(2,1)S(1)}, bf16[1,2,64,5120]{3,2,1,0:T(8,128)(2,1)}, u32[]{:S(2)}) copy-start(bf16[1,2,64,5120]{3,2,1,0:T(8,128)(2,1)} %refs_2_.3) | copy-start | bytes 3932164
  203.6 11.4 %copy-start.8 = (bf16[1,2,64,5120]{3,2,1,0:T(8,128)(2,1)S(1)}, bf16[1,2,64,5120]{3,2,1,0:T(8,128)(2,1)}, u32[]{:S(2)}) copy-start(bf16[1,2,64,5120]{3,2,1,0:T(8,128)(2,1)} %refs_0_.3) | copy-start | bytes 3932164
  203.6 11.4 %copy-start.11 = (bf16[2,4,64,1280]{3,2,1,0:T(8,128)(2,1)S(1)}, bf16[2,4,64,1280]{3,2,1,0:T(8,128)(2,1)}, u32[]{:S(2)}) copy-start(bf16[2,4,64,1280]{3,2,1,0:T(8,128)(2,1)} %copy-done.10) | copy-start | bytes 3932164
  203.6 11.4 %copy-start.14 = (bf16[2,4,64,1280]{3,2,1,0:T(8,128)(2,1)S(1)}, bf16[2,4,64,1280]{3,2,1,0:T(8,128)(2,1)}, u32[]{:S(2)}) copy-start(bf16[2,4,64,1280]{3,2,1,0:T(8,128)(2,1)} %copy-done.13) | copy-start | bytes 3932164
  203.6 11.4 %copy-start.19 = (bf16[64,1280]{1,0:T(8,128)(2,1)S(1)}, bf16[64,1280]{1,0:T(8,128)(2,1)}, u32[]{:S(2)}) copy-start(bf16[64,1280]{1,0:T(8,128)(2,1)} %copy-done.18) | copy-start | bytes 491524
  203.6 11.4 %copy-start.21 = (bf16[64,1280]{1,0:T(8,128)(2,1)S(1)}, bf16[64,1280]{1,0:T(8,128)(2,1)}, u32[]{:S(2)}) copy-start(bf16[64,1280]{1,0:T(8,128)(2,1)} %copy-done.20) | copy-start | bytes 491524
  233.7 48.2 %collective-permute-start.17 = (bf16[2,256,1280]{2,1,0:T(8,128)(2,1)}, bf16[2,256,1280]{2,1,0:T(8,128)(2,1)}, u32[]{:S(2)}, u32[]{:S(2)}) collective-permute-start(bf16[2,256,1280]{2,1,0:T(8,128)(2,1)} %get-tuple-element.68), channel_id=1, source_target_pairs={{8,0},{16,8},{24,16},{9,1},{17,9},{25,17},{10,2},{18,10},{26,18},{... | collective-permute-start | bytes 3932168 | tf_op jit(solution)/shard_map/ppermute | solution.py:126
  250.4 56.6 %all-to-all-start.1 = ((bf16[8,256,640]{2,1,0:T(8,128)(2,1)}), bf16[8,256,640]{2,1,0:T(8,128)(2,1)}, u32[]{:S(2)}, u32[]{:S(2)}) async-start(bf16[8,256,640]{2,1,0:T(8,128)(2,1)} %all-gather.5.cloned.1.call-done.g_ref), calls=%async_computation.1 | async-start | bytes 5242880 | tf_op jit(solution)/shard_map/all_to_all | solution.py:317
  255.8 26.0 %collective-permute-start.11 = (bf16[64,1280]{1,0:T(8,128)(2,1)}, bf16[64,1280]{1,0:T(8,128)(2,1)S(1)}, u32[]{:S(2)}, u32[]{:S(2)}) collective-permute-start(bf16[64,1280]{1,0:T(8,128)(2,1)} %get-tuple-element.61), channel_id=1, source_target_pairs={{0,2},{2,4},{4,6},{6,0},{1,3},{3,5},{5,7},{7,1},{8,10},{10,12},{12... | collective-permute-start | bytes 491528 | tf_op jit(solution)/shard_map/ppermute | solution.py:131
  257.7 24.1 %collective-permute-start.12 = (bf16[64,1280]{1,0:T(8,128)(2,1)}, bf16[64,1280]{1,0:T(8,128)(2,1)S(1)}, u32[]{:S(2)}, u32[]{:S(2)}) collective-permute-start(bf16[64,1280]{1,0:T(8,128)(2,1)} %get-tuple-element.62), channel_id=1, source_target_pairs={{0,4},{2,6},{4,0},{6,2},{1,5},{3,7},{5,1},{7,3},{8,12},{10,14},{12... | collective-permute-start | bytes 491528 | tf_op jit(solution)/shard_map/ppermute | solution.py:131
  260.0 21.8 %collective-permute-start.13 = (bf16[64,1280]{1,0:T(8,128)(2,1)}, bf16[64,1280]{1,0:T(8,128)(2,1)S(1)}, u32[]{:S(2)}, u32[]{:S(2)}) collective-permute-start(bf16[64,1280]{1,0:T(8,128)(2,1)} %get-tuple-element.63), channel_id=1, source_target_pairs={{0,6},{2,0},{4,2},{6,4},{1,7},{3,1},{5,3},{7,5},{8,14},{10,8},{12,... | collective-permute-start | bytes 491528 | tf_op jit(solution)/shard_map/ppermute | solution.py:131
  272.1 9.8 %copy-start.5 = (bf16[1,2,64,5120]{3,2,1,0:T(8,128)(2,1)S(1)}, bf16[1,2,64,5120]{3,2,1,0:T(8,128)(2,1)}, u32[]{:S(2)}) copy-start(bf16[1,2,64,5120]{3,2,1,0:T(8,128)(2,1)} %refs_2_.3) | copy-start | bytes 3932164
  272.1 9.8 %copy-start.9 = (bf16[1,2,64,5120]{3,2,1,0:T(8,128)(2,1)S(1)}, bf16[1,2,64,5120]{3,2,1,0:T(8,128)(2,1)}, u32[]{:S(2)}) copy-start(bf16[1,2,64,5120]{3,2,1,0:T(8,128)(2,1)} %refs_0_.3) | copy-start | bytes 3932164
  272.1 9.8 %copy-start.12 = (bf16[2,4,64,1280]{3,2,1,0:T(8,128)(2,1)S(1)}, bf16[2,4,64,1280]{3,2,1,0:T(8,128)(2,1)}, u32[]{:S(2)}) copy-start(bf16[2,4,64,1280]{3,2,1,0:T(8,128)(2,1)} %copy-done.10) | copy-start | bytes 3932164
  272.1 9.8 %copy-start.15 = (bf16[2,4,64,1280]{3,2,1,0:T(8,128)(2,1)S(1)}, bf16[2,4,64,1280]{3,2,1,0:T(8,128)(2,1)}, u32[]{:S(2)}) copy-start(bf16[2,4,64,1280]{3,2,1,0:T(8,128)(2,1)} %copy-done.13) | copy-start | bytes 3932164
  281.9 22.7 %copy-start.17 = (bf16[256,1280]{1,0:T(8,128)(2,1)S(1)}, bf16[256,1280]{1,0:T(8,128)(2,1)}, u32[]{:S(2)}) copy-start(bf16[256,1280]{1,0:T(8,128)(2,1)} %copy-done.16) | copy-start | bytes 1966084
  300.7 18.8 %collective-permute-start.18 = (bf16[2,256,1280]{2,1,0:T(8,128)(2,1)}, bf16[2,256,1280]{2,1,0:T(8,128)(2,1)}, u32[]{:S(2)}, u32[]{:S(2)}) collective-permute-start(bf16[2,256,1280]{2,1,0:T(8,128)(2,1)} %get-tuple-element.72), channel_id=1, source_target_pairs={{0,8},{8,16},{16,24},{1,9},{9,17},{17,25},{2,10},{10,18},{18,26},{... | collective-permute-start | bytes 3932168 | tf_op jit(solution)/shard_map/ppermute | solution.py:126
  304.7 2.9 copy-start.1
  307.5 12.0 %copy-start.26 = (f32[2,256,1280]{2,1,0:T(8,128)S(1)}, f32[2,256,1280]{2,1,0:T(8,128)}, u32[]{:S(2)}) copy-start(f32[2,256,1280]{2,1,0:T(8,128)} %get-tuple-element.70) | copy-start | bytes 7864324
  (12 other events, 14.4 us)
Sparse Core Ops, SparseCore 0:
  120.5 56.1 all-gather.2
  196.3 54.0 all-gather.4

commit v7 on v4

--- a/solution.py
+++ b/solution.py
@@ -268,11 +268,24 @@
 
     levels_xy = [("fsdp", 1 << i) for i in range(lax.axis_size("fsdp").bit_length() - 1)]
     levels_xy += [("frame", 1 << i) for i in range(lax.axis_size("frame").bit_length() - 2, 0, -1)]
-    near = o.reshape(1, parts * frames * rows, width)
-    flips = [(0, 0)]
-    for axis, bit in levels_xy:
-        near = jnp.concatenate([near, flipped(near, axis, bit)], axis=0)
-        flips += [(a ^ bit, b) if axis == "frame" else (a, b ^ bit) for a, b in flips]
+
+    def doubled(part, order):
+        flips = [(0, 0)]
+        for axis, bit in order:
+            part = jnp.concatenate([part, flipped(part, axis, bit)], axis=0)
+            flips += [(a ^ bit, b) if axis == "frame" else (a, b ^ bit) for a, b in flips]
+        return part, flips
+
+    o_rows = o.reshape(1, parts * frames * rows, width)
+    half = o_rows.shape[1] // 2
+    upper, flips = doubled(o_rows[:, :half], levels_xy)
+    lower, lower_flips = doubled(o_rows[:, half:], levels_xy[::-1])
+    near = jnp.stack(
+        [
+            jnp.concatenate([upper[i], lower[lower_flips.index(flip)]], axis=0)
+            for i, flip in enumerate(flips)
+        ]
+    )
     far = flipped(near, "frame", 1)
     my_frame, my_video = lax.axis_index("frame"), lax.axis_index("fsdp")
     videos = lax.axis_size("fsdp")
@@ -287,7 +300,7 @@
         gathered, ("frame", "fsdp"), split_axis=0, concat_axis=0, tiled=True
     )
     d_weight = weight_grad(table, near, far, gated_in, 1.0 / tokens_all)
-    d = project(gathered, out_weight)
+    kv, d_weight = after(kv, d_weight)
 
     first = (heads + 1) // 2
     groups = [(0, first), (first, heads - first)]
@@ -295,9 +308,8 @@
         [columns_for(queries, s, head0 * HD, count * HD) for s in shifts]
         for head0, count in groups
     ]
-    q_send, d = after(q_send, d)
-    kv, d = after(kv, d)
-    d = d.reshape(parts, frames, rows, width)
+    q_send, gathered, kv = lax.optimization_barrier((q_send, gathered, kv))
+    d = project(gathered, out_weight).reshape(parts, frames, rows, width)
     q_pieces = [[rotated(a, "head", s) for s, a in zip(shifts, sends)] for sends in q_send]
 
     ids = first_frame + jnp.arange(frames, dtype=jnp.int32)
@@ -316,7 +328,6 @@
     from_prev = shifted(boundary(frames - 1), "frame", 1)
     from_next = shifted(boundary(0), "frame", -1)
     local = (queries, key_rows, value_rows)
-    scal, d_weight = after(scal, d_weight)
     results = []
     for (head0, count), q_group in zip(groups, q_pieces):
         if results:

time: 345 us -> 306 us (0.89)
  starting transfers between devices: 70.6 us -> 47.5 us
  waiting for transfers between devices: 165 us -> 146 us
    all_to_all x1, waiting for transfers between devices: 0.01 us -> 49.5 us  [per_device(): lax.all_to_all(gathered, ('frame', 'fsdp'), split_axis=0, concat_axis=0,...]
    ppermute x12, waiting for transfers between devices: 84.8 us -> 46.1 us  [rotated(): lax.ppermute(array, axis, [(i, (i + step) % count) for i in range(count)])]
    ppermute x3 -> x5, waiting for transfers between devices: 70.5 us -> 38.1 us  [flipped(): lax.ppermute(array, axis, [(i, i ^ bit) for i in range(lax.axis_size(axis...]
    ppermute x12, starting transfers between devices: 36.5 us -> 16.4 us  [rotated(): lax.ppermute(array, axis, [(i, (i + step) % count) for i in range(count)])]
    all_gather x1, waiting for transfers between devices: 0.01 us -> 3.72 us  [per_device(): gathered = lax.all_gather(gated, 'head', axis=1, tiled=True)]
    ppermute x3 -> x5, starting transfers between devices: 10.9 us -> 9.03 us  [flipped(): lax.ppermute(array, axis, [(i, i ^ bit) for i in range(lax.axis_size(axis...]
  transfers between devices with their start and end apart: 23 -> 25, of which waited for: 9 -> 9; matrix products, arithmetic and copies ran while one was open for 5% -> 6% of each run, Pallas kernels for 13% -> 20%
where the time goes in v7:
time: 306 us; the launch traced here: 302 us
  waiting for transfers between devices  146 us (48%)
  Pallas kernels  59 us (19%)
  starting transfers between devices  47.5 us (16%)
  between operations  18.5 us (6%)
  local copies, waits for them, and re-layouts  15.8 us (5%)
  other arithmetic  14.9 us (5%)
    all_to_all x1, waiting for transfers between devices, per_device(): lax.all_to_all(gathered, ('frame', 'fsdp'), split_axis=0, concat_axis=0,...  49.5 us
    ppermute x12, waiting for transfers between devices, rotated(): lax.ppermute(array, axis, [(i, (i + step) % count) for i in range(count)])  46.1 us
    ppermute x5, waiting for transfers between devices, flipped(): lax.ppermute(array, axis, [(i, i ^ bit) for i in range(lax.axis_size(axis...  38.1 us
    pallas_call x2, Pallas kernels, attention(): pl.pallas_call(partial(attention_kernel, parts), grid_spec=pltpu.Prefetch...  31.9 us
    ppermute x6, starting transfers between devices, shifted(): return lax.ppermute(array, axis, pairs)  16.9 us
    ppermute x12, starting transfers between devices, rotated(): lax.ppermute(array, axis, [(i, (i + step) % count) for i in range(count)])  16.4 us
    pallas_call x1, Pallas kernels, weight_grad(): pl.pallas_call(partial(weight_kernel, scale), grid_spec=pltpu.PrefetchSca...  13.6 us
    pallas_call x1, Pallas kernels, project(): pl.pallas_call(project_kernel, grid=(blocks,), in_specs=[pl.BlockSpec((1,...  13.4 us
  transfers between devices with their start and end apart: 25, of which 9 were waited for; matrix products, arithmetic and copies ran while one was open for 6% of the time, Pallas kernels for 20%

profile of v7, /device:TPU:11, one launch (start us, length us, event | category | flops | bytes accessed | tf_op | source)
XLA Modules:
  0.0 301.6 jit_solution(16111299900789912874)
XLA Ops:
  7.4 1.1 copy-done.6
  9.3 1.3 collective-permute-start.3
  15.1 1.0 constant_dynamic-slice_fusion.2
  16.2 1.6 fusion
  18.0 1.0 copy-done.5
  19.1 1.1 collective-permute-start.4
  20.2 1.5 collective-permute-start.5
  21.6 1.0 bitcast_dynamic-update-slice_fusion.2
  22.6 32.8 %collective-permute-done.4 = bf16[2,64,1280]{2,1,0:T(8,128)(2,1)S(1)} collective-permute-done((bf16[2,64,1280]{2,1,0:T(8,128)(2,1)S(1)}, bf16[2,64,1280]{2,1,0:T(8,128)(2,1)S(1)}, u32[]{:S(2)}, u32[]{:S(2)}) %collective-permute-start.4) | collective-permute-done | bytes 327712 | tf_op jit(solution)/shard_map/ppermute | solution.py:136
  55.4 13.4 %collective-permute-done.5 = bf16[2,64,1280]{2,1,0:T(8,128)(2,1)S(1)} collective-permute-done((bf16[2,64,1280]{2,1,0:T(8,128)(2,1)S(1)}, bf16[2,64,1280]{2,1,0:T(8,128)(2,1)S(1)}, u32[]{:S(2)}, u32[]{:S(2)}) %collective-permute-start.5) | collective-permute-done | bytes 327712 | tf_op jit(solution)/shard_map/ppermute | solution.py:136
  69.0 1.4 collective-permute-start.7
  70.5 8.3 %collective-permute-done.7 = bf16[1,256,1280]{2,1,0:T(8,128)(2,1)S(1)} collective-permute-done((bf16[1,256,1280]{2,1,0:T(8,128)(2,1)S(1)}, bf16[1,256,1280]{2,1,0:T(8,128)(2,1)S(1)}, u32[]{:S(2)}, u32[]{:S(2)}) %collective-permute-start.7) | collective-permute-done | bytes 655392 | tf_op jit(solution)/shard_map/ppermute | solution.py:144
  79.4 0.9 collective-permute-done.6
  81.1 28.9 %collective-permute-done.8 = bf16[2,256,1280]{2,1,0:T(8,128)(2,1)S(1)} collective-permute-done((bf16[2,256,1280]{2,1,0:T(8,128)(2,1)S(1)}, bf16[2,256,1280]{2,1,0:T(8,128)(2,1)S(1)}, u32[]{:S(2)}, u32[]{:S(2)}) %collective-permute-start.8) | collective-permute-done | bytes 1310752 | tf_op jit(solution)/shard_map/ppermute | solution.py:144
  110.4 2.9 pad_maximum_fusion.near_ref
  113.4 6.7 %collective-permute-start.10 = (bf16[4,512,1280]{2,1,0:T(8,128)(2,1)}, bf16[4,512,1280]{2,1,0:T(8,128)(2,1)}, u32[]{:S(2)}, u32[]{:S(2)}) collective-permute-start(bf16[4,512,1280]{2,1,0:T(8,128)(2,1)} %pad_maximum_fusion.near_ref), channel_id=1, source_target_pairs={{0,8},{8,0},{16,24},{24,16},{1,9},{9,1},{17,25},{25,17},{2,10},{10... | collective-permute-start | bytes 15728648 | tf_op jit(solution)/shard_map/ppermute | solution.py:144
  120.1 0.9 pad_maximum_fusion.7
  121.0 0.9 pad_maximum_fusion.6
  121.9 0.9 pad_maximum_fusion.5
  122.8 3.7 %all-gather.2.cloned.1.call-done.g_ref = bf16[8,512,640]{2,1,0:T(8,128)(2,1)} async-done(((bf16[8,128,640]{2,1,0:T(8,128)(2,1)}), bf16[8,512,640]{2,1,0:T(8,128)(2,1)}) %all-gather.2.cloned.1.call-update) | async-done | bytes 5242896 | tf_op jit(solution)/shard_map/all_gather | solution.py:257
  126.5 5.1 %all-to-all-start = ((bf16[8,512,640]{2,1,0:T(8,128)(2,1)}), bf16[8,512,640]{2,1,0:T(8,128)(2,1)}, u32[]{:S(2)}, u32[]{:S(2)}) async-start(bf16[8,512,640]{2,1,0:T(8,128)(2,1)} %all-gather.2.cloned.1.call-done.g_ref), calls=%async_computation | async-start | bytes 10485760 | tf_op jit(solution)/shard_map/all_to_all | solution.py:299
  131.7 2.3 dynamic-slice_bitcast_fusion.7
  134.0 1.8 dynamic-slice_bitcast_fusion.3
  135.9 4.3 %collective-permute-start.1 = (bf16[2,2,64,1280]{3,2,1,0:T(8,128)(2,1)}, bf16[2,2,64,1280]{3,2,1,0:T(8,128)(2,1)}, u32[]{:S(2)}, u32[]{:S(2)}) collective-permute-start(bf16[2,2,64,1280]{3,2,1,0:T(8,128)(2,1)} %pad_maximum_fusion.6), channel_id=1, source_target_pairs={{0,4},{2,6},{4,0},{6,2},{1,5},{3,7},{5,1},{7,3},{8,12},{10,14},{12... | collective-permute-start | bytes 1966088 | tf_op jit(solution)/shard_map/ppermute | solution.py:136
  140.6 49.5 %all-to-all-done.g_near.g_far = bf16[8,512,640]{2,1,0:T(8,128)(2,1)} async-done(((bf16[8,512,640]{2,1,0:T(8,128)(2,1)}), bf16[8,512,640]{2,1,0:T(8,128)(2,1)}, u32[]{:S(2)}, u32[]{:S(2)}) %all-to-all-start) | async-done | bytes 5242912 | tf_op jit(solution)/shard_map/all_to_all | solution.py:299
  190.1 13.6 %weight_gradient.1 = f32[1280,640]{1,0:T(8,128)} custom-call(s32[2,4]{1,0:T(2,128)S(1)} %pad_add_fusion.table, bf16[4,512,1280]{2,1,0:T(8,128)(2,1)} %pad_maximum_fusion.near_ref, bf16[4,512,1280]{2,1,0:T(8,128)(2,1)} %collective-permute-done.10.far_ref, bf16[8,512,640]{2,1,0:T(8,128)(2,1)} %all-to-all-done.g_near.g_far, ...), custom_call_target="tpu_custom_call" | custom-call | flops 6710886400 | bytes 19005440 | tf_op jit(solution)/shard_map/weight_gradient/pallas_call | solution.py:162
  203.8 1.2 slice_bitcast_fusion.16
  205.1 1.2 slice_bitcast_fusion.15
  206.6 1.2 pad_maximum_fusion.4
  207.7 2.8 collective-permute-start.18
  210.7 1.2 pad_maximum_fusion.3
  211.9 2.8 collective-permute-start.17
  215.2 4.3 %collective-permute-start.15 = (bf16[2,64,640]{2,1,0:T(8,128)(2,1)}, bf16[2,64,640]{2,1,0:T(8,128)(2,1)S(1)}, u32[]{:S(2)}, u32[]{:S(2)}) collective-permute-start(bf16[2,64,640]{2,1,0:T(8,128)(2,1)} %get-tuple-element.50), channel_id=1, source_target_pairs={{0,4},{2,6},{4,0},{6,2},{1,5},{3,7},{5,1},{7,3},{8,12},{10,14},{12... | collective-permute-start | bytes 491528 | tf_op jit(solution)/shard_map/ppermute | solution.py:136
  219.8 2.5 copy-done.4
  222.3 13.4 %project_gated.1 = bf16[512,1280]{1,0:T(8,128)(2,1)S(1)} custom-call(bf16[8,512,640]{2,1,0:T(8,128)(2,1)S(1)} %copy-done.4, bf16[1280,5120]{1,0:T(8,128)(2,1)} %w_ref.1), custom_call_target="tpu_custom_call" | custom-call | flops 6710886400 | bytes 19660800 | tf_op jit(solution)/shard_map/project_gated/pallas_call | solution.py:209
  235.8 1.1 collective-permute-start.11
  236.9 1.8 collective-permute-start.12
  238.8 15.9 %attention_backward.2 = (bf16[2,256,640]{2,1,0:T(8,128)(2,1)S(1)}, f32[2,256,640]{2,1,0:T(8,128)S(1)}, f32[2,256,640]{2,1,0:T(8,128)S(1)}, bf16[2,256,640]{2,1,0:T(8,128)(2,1)S(1)}, bf16[2,256,640]{2,1,0:T(8,128)(2,1)S(1)}) custom-call(s32[6]{0:T(128)S(1)} %pad_add_fusion.1.scal, bf16[1,2,64,5120]{3,2,1,0:T(8,128)(2,1)S(1)} %copy-done.3, ...), custom_call_target="tpu_custom_call" | custom-call | flops 2516582400 | bytes 10485760 | tf_op jit(solution)/shard_map/attention_backward/pallas_call | solution.py:99
  254.7 3.9 %collective-permute-start.19 = (bf16[2,256,640]{2,1,0:T(8,128)(2,1)S(1)}, bf16[2,256,640]{2,1,0:T(8,128)(2,1)S(1)}, u32[]{:S(2)}, u32[]{:S(2)}) collective-permute-start(bf16[2,256,640]{2,1,0:T(8,128)(2,1)S(1)} %get-tuple-element.60), channel_id=1, source_target_pairs={{0,8},{8,16},{16,24},{1,9},{9,17},{17,25},{2,10},{10,18},{18,26},{... | collective-permute-start | bytes 1966088 | tf_op jit(solution)/shard_map/ppermute | solution.py:131
  258.6 1.9 collective-permute-start.20
  260.6 16.0 %attention_backward.3 = (bf16[2,256,640]{2,1,0:T(8,128)(2,1)S(1)}, f32[2,256,640]{2,1,0:T(8,128)S(1)}, f32[2,256,640]{2,1,0:T(8,128)S(1)}, bf16[2,256,640]{2,1,0:T(8,128)(2,1)S(1)}, bf16[2,256,640]{2,1,0:T(8,128)(2,1)S(1)}) custom-call(s32[6]{0:T(128)S(1)} %pad_add_fusion.1.scal, bf16[1,2,64,5120]{3,2,1,0:T(8,128)(2,1)S(1)} %copy-done.3, ...), custom_call_target="tpu_custom_call" | custom-call | flops 2516582400 | bytes 10485760 | tf_op jit(solution)/shard_map/attention_backward/pallas_call | solution.py:99
  276.5 3.6 %collective-permute-start.21 = (bf16[2,256,640]{2,1,0:T(8,128)(2,1)S(1)}, bf16[2,256,640]{2,1,0:T(8,128)(2,1)S(1)}, u32[]{:S(2)}, u32[]{:S(2)}) collective-permute-start(bf16[2,256,640]{2,1,0:T(8,128)(2,1)S(1)} %get-tuple-element.63), channel_id=1, source_target_pairs={{0,8},{8,16},{16,24},{1,9},{9,17},{17,25},{2,10},{10,18},{18,26},{... | collective-permute-start | bytes 1966088 | tf_op jit(solution)/shard_map/ppermute | solution.py:131
  280.2 1.9 collective-permute-start.22
  282.1 1.2 maximum_bitcast_fusion.4
  283.6 4.1 %collective-permute-done.21 = bf16[2,256,640]{2,1,0:T(8,128)(2,1)S(1)} collective-permute-done((bf16[2,256,640]{2,1,0:T(8,128)(2,1)S(1)}, bf16[2,256,640]{2,1,0:T(8,128)(2,1)S(1)}, u32[]{:S(2)}, u32[]{:S(2)}) %collective-permute-start.21) | collective-permute-done | bytes 655392 | tf_op jit(solution)/shard_map/ppermute | solution.py:131
  287.7 4.4 %collective-permute-done.22 = bf16[2,256,640]{2,1,0:T(8,128)(2,1)S(1)} collective-permute-done((bf16[2,256,640]{2,1,0:T(8,128)(2,1)S(1)}, bf16[2,256,640]{2,1,0:T(8,128)(2,1)S(1)}, u32[]{:S(2)}, u32[]{:S(2)}) %collective-permute-start.22) | collective-permute-done | bytes 655392 | tf_op jit(solution)/shard_map/ppermute | solution.py:131
  292.5 1.2 maximum_bitcast_fusion.6
  293.6 1.2 maximum_bitcast_fusion.5
  (93 shorter events, 6.5 us)
Async XLA Ops:
  7.2 1.3 copy-start.6
  7.2 119.3 %all-gather.2.cloned.1.call-start = ((), (), s32[]{:S(2)}) async-start(), calls=%async_computation.1 | async-start | bytes 6553600 | tf_op jit(solution)/shard_map/all_gather | solution.py:257
  8.5 2.1 copy-start.14
  9.3 12.3 %collective-permute-start.3 = (bf16[2,64,1280]{2,1,0:T(8,128)(2,1)}, bf16[2,64,1280]{2,1,0:T(8,128)(2,1)}, u32[]{:S(2)}, u32[]{:S(2)}) collective-permute-start(bf16[2,64,1280]{2,1,0:T(8,128)(2,1)} %get-tuple-element.93), channel_id=1, source_target_pairs={{0,2},{2,4},{4,6},{6,0},{1,3},{3,5},{5,7},{7,1},{8,10},{10,12},{12... | collective-permute-start | bytes 983048 | tf_op jit(solution)/shard_map/ppermute | solution.py:136
  18.0 1.1 copy-start.5
  19.1 36.3 %collective-permute-start.4 = (bf16[2,64,1280]{2,1,0:T(8,128)(2,1)S(1)}, bf16[2,64,1280]{2,1,0:T(8,128)(2,1)S(1)}, u32[]{:S(2)}, u32[]{:S(2)}) collective-permute-start(bf16[2,64,1280]{2,1,0:T(8,128)(2,1)S(1)} %get-tuple-element.95), channel_id=1, source_target_pairs={{0,4},{2,6},{4,0},{6,2},{1,5},{3,7},{5,1},{7,3},{8,12},{10,14},{12... | collective-permute-start | bytes 983048 | tf_op jit(solution)/shard_map/ppermute | solution.py:136
  20.2 48.6 %collective-permute-start.5 = (bf16[2,64,1280]{2,1,0:T(8,128)(2,1)S(1)}, bf16[2,64,1280]{2,1,0:T(8,128)(2,1)S(1)}, u32[]{:S(2)}, u32[]{:S(2)}) collective-permute-start(bf16[2,64,1280]{2,1,0:T(8,128)(2,1)S(1)} %get-tuple-element.92), channel_id=1, source_target_pairs={{0,6},{2,0},{4,2},{6,4},{1,7},{3,1},{5,3},{7,5},{8,14},{10,8},{12,... | collective-permute-start | bytes 983048 | tf_op jit(solution)/shard_map/ppermute | solution.py:136
  69.0 9.9 %collective-permute-start.7 = (bf16[1,256,1280]{2,1,0:T(8,128)(2,1)S(1)}, bf16[1,256,1280]{2,1,0:T(8,128)(2,1)S(1)}, u32[]{:S(2)}, u32[]{:S(2)}) collective-permute-start(bf16[1,256,1280]{2,1,0:T(8,128)(2,1)S(1)} %get-tuple-element.86), channel_id=1, source_target_pairs={{0,16},{8,24},{16,0},{24,8},{1,17},{9,25},{17,1},{25,9},{2,18},{10... | collective-permute-start | bytes 1966088 | tf_op jit(solution)/shard_map/ppermute | solution.py:144
  70.4 9.8 %collective-permute-start.6 = (bf16[1,256,1280]{2,1,0:T(8,128)(2,1)S(1)}, bf16[1,256,1280]{2,1,0:T(8,128)(2,1)S(1)}, u32[]{:S(2)}, u32[]{:S(2)}) collective-permute-start(bf16[1,256,1280]{2,1,0:T(8,128)(2,1)S(1)} %get-tuple-element.87), channel_id=1, source_target_pairs={{0,1},{1,0},{2,3},{3,2},{4,5},{5,4},{6,7},{7,6},{8,9},{9,8},{10,11... | collective-permute-start | bytes 1966088 | tf_op jit(solution)/shard_map/ppermute | solution.py:144
  79.0 1.8 copy-start
  79.0 1.8 copy-start.1
  79.0 30.9 %collective-permute-start.8 = (bf16[2,256,1280]{2,1,0:T(8,128)(2,1)S(1)}, bf16[2,256,1280]{2,1,0:T(8,128)(2,1)S(1)}, u32[]{:S(2)}, u32[]{:S(2)}) collective-permute-start(bf16[2,256,1280]{2,1,0:T(8,128)(2,1)S(1)} %pad_maximum_fusion.1), channel_id=1, source_target_pairs={{0,1},{1,0},{2,3},{3,2},{4,5},{5,4},{6,7},{7,6},{8,9},{9,8},{10,11... | collective-permute-start | bytes 3932168 | tf_op jit(solution)/shard_map/ppermute | solution.py:144
  80.4 29.8 %collective-permute-start.9 = (bf16[2,256,1280]{2,1,0:T(8,128)(2,1)S(1)}, bf16[2,256,1280]{2,1,0:T(8,128)(2,1)S(1)}, u32[]{:S(2)}, u32[]{:S(2)}) collective-permute-start(bf16[2,256,1280]{2,1,0:T(8,128)(2,1)S(1)} %pad_maximum_fusion.2), channel_id=1, source_target_pairs={{0,16},{8,24},{16,0},{24,8},{1,17},{9,25},{17,1},{25,9},{2,18},{10... | collective-permute-start | bytes 3932168 | tf_op jit(solution)/shard_map/ppermute | solution.py:144
  113.4 27.2 %collective-permute-start.10 = (bf16[4,512,1280]{2,1,0:T(8,128)(2,1)}, bf16[4,512,1280]{2,1,0:T(8,128)(2,1)}, u32[]{:S(2)}, u32[]{:S(2)}) collective-permute-start(bf16[4,512,1280]{2,1,0:T(8,128)(2,1)} %pad_maximum_fusion.near_ref), channel_id=1, source_target_pairs={{0,8},{8,0},{16,24},{24,16},{1,9},{9,1},{17,25},{25,17},{2,10},{10... | collective-permute-start | bytes 15728648 | tf_op jit(solution)/shard_map/ppermute | solution.py:144
  126.5 63.6 %all-to-all-start = ((bf16[8,512,640]{2,1,0:T(8,128)(2,1)}), bf16[8,512,640]{2,1,0:T(8,128)(2,1)}, u32[]{:S(2)}, u32[]{:S(2)}) async-start(bf16[8,512,640]{2,1,0:T(8,128)(2,1)} %all-gather.2.cloned.1.call-done.g_ref), calls=%async_computation | async-start | bytes 10485760 | tf_op jit(solution)/shard_map/all_to_all | solution.py:299
  135.8 68.0 %collective-permute-start = (bf16[2,2,64,1280]{3,2,1,0:T(8,128)(2,1)}, bf16[2,2,64,1280]{3,2,1,0:T(8,128)(2,1)S(1)}, u32[]{:S(2)}, u32[]{:S(2)}) collective-permute-start(bf16[2,2,64,1280]{3,2,1,0:T(8,128)(2,1)} %pad_maximum_fusion.5), channel_id=1, source_target_pairs={{0,2},{2,4},{4,6},{6,0},{1,3},{3,5},{5,7},{7,1},{8,10},{10,12},{12... | collective-permute-start | bytes 1966088 | tf_op jit(solution)/shard_map/ppermute | solution.py:136
  135.9 67.8 %collective-permute-start.1 = (bf16[2,2,64,1280]{3,2,1,0:T(8,128)(2,1)}, bf16[2,2,64,1280]{3,2,1,0:T(8,128)(2,1)}, u32[]{:S(2)}, u32[]{:S(2)}) collective-permute-start(bf16[2,2,64,1280]{3,2,1,0:T(8,128)(2,1)} %pad_maximum_fusion.6), channel_id=1, source_target_pairs={{0,4},{2,6},{4,0},{6,2},{1,5},{3,7},{5,1},{7,3},{8,12},{10,14},{12... | collective-permute-start | bytes 1966088 | tf_op jit(solution)/shard_map/ppermute | solution.py:136
  140.2 63.6 %collective-permute-start.2 = (bf16[2,2,64,1280]{3,2,1,0:T(8,128)(2,1)}, bf16[2,2,64,1280]{3,2,1,0:T(8,128)(2,1)}, u32[]{:S(2)}, u32[]{:S(2)}) collective-permute-start(bf16[2,2,64,1280]{3,2,1,0:T(8,128)(2,1)} %pad_maximum_fusion.7), channel_id=1, source_target_pairs={{0,6},{2,0},{4,2},{6,4},{1,7},{3,1},{5,3},{7,5},{8,14},{10,8},{12,... | collective-permute-start | bytes 1966088 | tf_op jit(solution)/shard_map/ppermute | solution.py:136
  203.8 2.5 copy-start.9
  205.1 1.4 copy-start.8
  206.5 4.0 %copy-start.7 = (bf16[1,64,1280]{2,1,0:T(8,128)(2,1)S(1)}, bf16[1,64,1280]{2,1,0:T(8,128)(2,1)}, u32[]{:S(2)}) copy-start(bf16[1,64,1280]{2,1,0:T(8,128)(2,1)} %get-tuple-element.131) | copy-start | bytes 491524
  207.7 31.0 %collective-permute-start.18 = (bf16[2,4,64,1280]{3,2,1,0:T(8,128)(2,1)}, bf16[2,4,64,1280]{3,2,1,0:T(8,128)(2,1)}, u32[]{:S(2)}, u32[]{:S(2)}) collective-permute-start(bf16[2,4,64,1280]{3,2,1,0:T(8,128)(2,1)} %pad_maximum_fusion.4), channel_id=1, source_target_pairs={{8,0},{16,8},{24,16},{9,1},{17,9},{25,17},{10,2},{18,10},{26,18},{... | collective-permute-start | bytes 3932168 | tf_op jit(solution)/shard_map/ppermute | solution.py:131
  210.7 4.0 %copy-start.15 = (s32[8,2]{0,1:T(2,128)S(1)}, s32[8,2]{0,1:T(2,128)}, u32[]{:S(2)}) copy-start(s32[8,2]{0,1:T(2,128)} %param.17) | copy-start | bytes 196
  210.7 8.7 %copy-start.13 = (bf16[2,64,640]{2,1,0:T(8,128)(2,1)S(1)}, bf16[2,64,640]{2,1,0:T(8,128)(2,1)}, u32[]{:S(2)}) copy-start(bf16[2,64,640]{2,1,0:T(8,128)(2,1)} %get-tuple-element.51) | copy-start | bytes 491524
  211.9 26.9 %collective-permute-start.17 = (bf16[2,4,64,1280]{3,2,1,0:T(8,128)(2,1)}, bf16[2,4,64,1280]{3,2,1,0:T(8,128)(2,1)}, u32[]{:S(2)}, u32[]{:S(2)}) collective-permute-start(bf16[2,4,64,1280]{3,2,1,0:T(8,128)(2,1)} %pad_maximum_fusion.3), channel_id=1, source_target_pairs={{0,8},{8,16},{16,24},{1,9},{9,17},{17,25},{2,10},{10,18},{18,26},{... | collective-permute-start | bytes 3932168 | tf_op jit(solution)/shard_map/ppermute | solution.py:131
  215.0 23.7 %copy-start.2 = (bf16[1,2,64,5120]{3,2,1,0:T(8,128)(2,1)S(1)}, bf16[1,2,64,5120]{3,2,1,0:T(8,128)(2,1)}, u32[]{:S(2)}) copy-start(bf16[1,2,64,5120]{3,2,1,0:T(8,128)(2,1)} %refs_2_.3) | copy-start | bytes 3932164
  215.0 23.7 %copy-start.3 = (bf16[1,2,64,5120]{3,2,1,0:T(8,128)(2,1)S(1)}, bf16[1,2,64,5120]{3,2,1,0:T(8,128)(2,1)}, u32[]{:S(2)}) copy-start(bf16[1,2,64,5120]{3,2,1,0:T(8,128)(2,1)} %refs_0_.3) | copy-start | bytes 3932164
  215.0 20.7 %collective-permute-start.14 = (bf16[2,64,640]{2,1,0:T(8,128)(2,1)}, bf16[2,64,640]{2,1,0:T(8,128)(2,1)S(1)}, u32[]{:S(2)}, u32[]{:S(2)}) collective-permute-start(bf16[2,64,640]{2,1,0:T(8,128)(2,1)} %get-tuple-element.49), channel_id=1, source_target_pairs={{0,2},{2,4},{4,6},{6,0},{1,3},{3,5},{5,7},{7,1},{8,10},{10,12},{12... | collective-permute-start | bytes 491528 | tf_op jit(solution)/shard_map/ppermute | solution.py:136
  215.2 21.7 %collective-permute-start.15 = (bf16[2,64,640]{2,1,0:T(8,128)(2,1)}, bf16[2,64,640]{2,1,0:T(8,128)(2,1)S(1)}, u32[]{:S(2)}, u32[]{:S(2)}) collective-permute-start(bf16[2,64,640]{2,1,0:T(8,128)(2,1)} %get-tuple-element.50), channel_id=1, source_target_pairs={{0,4},{2,6},{4,0},{6,2},{1,5},{3,7},{5,1},{7,3},{8,12},{10,14},{12... | collective-permute-start | bytes 491528 | tf_op jit(solution)/shard_map/ppermute | solution.py:136
  219.5 19.3 %collective-permute-start.16 = (bf16[2,64,640]{2,1,0:T(8,128)(2,1)S(1)}, bf16[2,64,640]{2,1,0:T(8,128)(2,1)S(1)}, u32[]{:S(2)}, u32[]{:S(2)}) collective-permute-start(bf16[2,64,640]{2,1,0:T(8,128)(2,1)S(1)} %copy-done.13), channel_id=1, source_target_pairs={{0,6},{2,0},{4,2},{6,4},{1,7},{3,1},{5,3},{7,5},{8,14},{10,8},{12,... | collective-permute-start | bytes 491528 | tf_op jit(solution)/shard_map/ppermute | solution.py:136
  219.8 2.5 copy-start.4
  222.3 13.4 %copy-start.12 = (bf16[2,64,640]{2,1,0:T(8,128)(2,1)S(1)}, bf16[2,64,640]{2,1,0:T(8,128)(2,1)}, u32[]{:S(2)}) copy-start(bf16[2,64,640]{2,1,0:T(8,128)(2,1)} %get-tuple-element.43) | copy-start | bytes 491524
  222.3 14.6 %copy-start.11 = (bf16[2,64,640]{2,1,0:T(8,128)(2,1)S(1)}, bf16[2,64,640]{2,1,0:T(8,128)(2,1)}, u32[]{:S(2)}) copy-start(bf16[2,64,640]{2,1,0:T(8,128)(2,1)} %get-tuple-element.44) | copy-start | bytes 491524
  222.3 16.4 %copy-start.10 = (bf16[2,64,640]{2,1,0:T(8,128)(2,1)S(1)}, bf16[2,64,640]{2,1,0:T(8,128)(2,1)}, u32[]{:S(2)}) copy-start(bf16[2,64,640]{2,1,0:T(8,128)(2,1)} %get-tuple-element.45) | copy-start | bytes 491524
  235.8 24.8 %collective-permute-start.11 = (bf16[2,64,640]{2,1,0:T(8,128)(2,1)S(1)}, bf16[2,64,640]{2,1,0:T(8,128)(2,1)S(1)}, u32[]{:S(2)}, u32[]{:S(2)}) collective-permute-start(bf16[2,64,640]{2,1,0:T(8,128)(2,1)S(1)} %copy-done.12), channel_id=1, source_target_pairs={{0,2},{2,4},{4,6},{6,0},{1,3},{3,5},{5,7},{7,1},{8,10},{10,12},{12... | collective-permute-start | bytes 491528 | tf_op jit(solution)/shard_map/ppermute | solution.py:136
  236.9 23.6 %collective-permute-start.12 = (bf16[2,64,640]{2,1,0:T(8,128)(2,1)S(1)}, bf16[2,64,640]{2,1,0:T(8,128)(2,1)S(1)}, u32[]{:S(2)}, u32[]{:S(2)}) collective-permute-start(bf16[2,64,640]{2,1,0:T(8,128)(2,1)S(1)} %copy-done.11), channel_id=1, source_target_pairs={{0,4},{2,6},{4,0},{6,2},{1,5},{3,7},{5,1},{7,3},{8,12},{10,14},{12... | collective-permute-start | bytes 491528 | tf_op jit(solution)/shard_map/ppermute | solution.py:136
  238.7 21.8 %collective-permute-start.13 = (bf16[2,64,640]{2,1,0:T(8,128)(2,1)S(1)}, bf16[2,64,640]{2,1,0:T(8,128)(2,1)S(1)}, u32[]{:S(2)}, u32[]{:S(2)}) collective-permute-start(bf16[2,64,640]{2,1,0:T(8,128)(2,1)S(1)} %copy-done.10), channel_id=1, source_target_pairs={{0,6},{2,0},{4,2},{6,4},{1,7},{3,1},{5,3},{7,5},{8,14},{10,8},{12,... | collective-permute-start | bytes 491528 | tf_op jit(solution)/shard_map/ppermute | solution.py:136
  254.7 28.6 %collective-permute-start.19 = (bf16[2,256,640]{2,1,0:T(8,128)(2,1)S(1)}, bf16[2,256,640]{2,1,0:T(8,128)(2,1)S(1)}, u32[]{:S(2)}, u32[]{:S(2)}) collective-permute-start(bf16[2,256,640]{2,1,0:T(8,128)(2,1)S(1)} %get-tuple-element.60), channel_id=1, source_target_pairs={{0,8},{8,16},{16,24},{1,9},{9,17},{17,25},{2,10},{10,18},{18,26},{... | collective-permute-start | bytes 1966088 | tf_op jit(solution)/shard_map/ppermute | solution.py:131
  258.6 24.7 %collective-permute-start.20 = (bf16[2,256,640]{2,1,0:T(8,128)(2,1)S(1)}, bf16[2,256,640]{2,1,0:T(8,128)(2,1)S(1)}, u32[]{:S(2)}, u32[]{:S(2)}) collective-permute-start(bf16[2,256,640]{2,1,0:T(8,128)(2,1)S(1)} %get-tuple-element.61), channel_id=1, source_target_pairs={{8,0},{16,8},{24,16},{9,1},{17,9},{25,17},{10,2},{18,10},{26,18},{... | collective-permute-start | bytes 1966088 | tf_op jit(solution)/shard_map/ppermute | solution.py:131
  276.5 11.2 %collective-permute-start.21 = (bf16[2,256,640]{2,1,0:T(8,128)(2,1)S(1)}, bf16[2,256,640]{2,1,0:T(8,128)(2,1)S(1)}, u32[]{:S(2)}, u32[]{:S(2)}) collective-permute-start(bf16[2,256,640]{2,1,0:T(8,128)(2,1)S(1)} %get-tuple-element.63), channel_id=1, source_target_pairs={{0,8},{8,16},{16,24},{1,9},{9,17},{17,25},{2,10},{10,18},{18,26},{... | collective-permute-start | bytes 1966088 | tf_op jit(solution)/shard_map/ppermute | solution.py:131
  280.2 11.9 %collective-permute-start.22 = (bf16[2,256,640]{2,1,0:T(8,128)(2,1)S(1)}, bf16[2,256,640]{2,1,0:T(8,128)(2,1)S(1)}, u32[]{:S(2)}, u32[]{:S(2)}) collective-permute-start(bf16[2,256,640]{2,1,0:T(8,128)(2,1)S(1)} %get-tuple-element.64), channel_id=1, source_target_pairs={{8,0},{16,8},{24,16},{9,1},{17,9},{25,17},{10,2},{18,10},{26,18},{... | collective-permute-start | bytes 1966088 | tf_op jit(solution)/shard_map/ppermute | solution.py:131
Sparse Core Ops, SparseCore 0:
  19.2 107.2 all-gather.1

commit v8 on v7

--- a/solution.py
+++ b/solution.py
@@ -300,7 +300,7 @@
         gathered, ("frame", "fsdp"), split_axis=0, concat_axis=0, tiled=True
     )
     d_weight = weight_grad(table, near, far, gated_in, 1.0 / tokens_all)
-    kv, d_weight = after(kv, d_weight)
+    d = project(gathered, out_weight)
 
     first = (heads + 1) // 2
     groups = [(0, first), (first, heads - first)]
@@ -308,8 +308,9 @@
         [columns_for(queries, s, head0 * HD, count * HD) for s in shifts]
         for head0, count in groups
     ]
-    q_send, gathered, kv = lax.optimization_barrier((q_send, gathered, kv))
-    d = project(gathered, out_weight).reshape(parts, frames, rows, width)
+    q_send, d = after(q_send, d)
+    kv, d = after(kv, d)
+    d = d.reshape(parts, frames, rows, width)
     q_pieces = [[rotated(a, "head", s) for s, a in zip(shifts, sends)] for sends in q_send]
 
     ids = first_frame + jnp.arange(frames, dtype=jnp.int32)
@@ -328,6 +329,7 @@
     from_prev = shifted(boundary(frames - 1), "frame", 1)
     from_next = shifted(boundary(0), "frame", -1)
     local = (queries, key_rows, value_rows)
+    scal, d_weight = after(scal, d_weight)
     results = []
     for (head0, count), q_group in zip(groups, q_pieces):
         if results:

time: 306 us -> 293 us (0.958)
  waiting for transfers between devices: 146 us -> 140 us
  starting transfers between devices: 47.5 us -> 43.3 us
    all_to_all x1, waiting for transfers between devices: 49.5 us -> 0.01 us  [per_device(): lax.all_to_all(gathered, ('frame', 'fsdp'), split_axis=0, concat_axis=0,...]
    ppermute x12, waiting for transfers between devices: 46.1 us -> 80.4 us  [rotated(): lax.ppermute(array, axis, [(i, (i + step) % count) for i in range(count)])]
    all_gather x1, waiting for transfers between devices: 3.72 us -> 7.99 us  [per_device(): gathered = lax.all_gather(gated, 'head', axis=1, tiled=True)]
    ppermute x5, starting transfers between devices: 9.03 us -> 5.73 us  [flipped(): lax.ppermute(array, axis, [(i, i ^ bit) for i in range(lax.axis_size(axis...]
    ppermute x5, waiting for transfers between devices: 38.1 us -> 41.3 us  [flipped(): lax.ppermute(array, axis, [(i, i ^ bit) for i in range(lax.axis_size(axis...]
  transfers between devices with their start and end apart: 25 -> 25, of which waited for: 9 -> 10; matrix products, arithmetic and copies ran while one was open for 6% -> 7% of each run, Pallas kernels for 20% -> 15%
where the time goes in v8:
time: 293 us; the launch traced here: 290 us
  waiting for transfers between devices  140 us (48%)
  Pallas kernels  59.4 us (20%)
  starting transfers between devices  43.3 us (15%)
  between operations  18.5 us (6%)
  other arithmetic  16 us (5%)
  local copies, waits for them, and re-layouts  13.1 us (4%)
    ppermute x12, waiting for transfers between devices, rotated(): lax.ppermute(array, axis, [(i, (i + step) % count) for i in range(count)])  80.4 us
    ppermute x5, waiting for transfers between devices, flipped(): lax.ppermute(array, axis, [(i, i ^ bit) for i in range(lax.axis_size(axis...  41.3 us
    pallas_call x2, Pallas kernels, attention(): pl.pallas_call(partial(attention_kernel, parts), grid_spec=pltpu.Prefetch...  32 us
    ppermute x6, starting transfers between devices, shifted(): return lax.ppermute(array, axis, pairs)  17.9 us
    ppermute x12, starting transfers between devices, rotated(): lax.ppermute(array, axis, [(i, (i + step) % count) for i in range(count)])  14.5 us
    pallas_call x1, Pallas kernels, weight_grad(): pl.pallas_call(partial(weight_kernel, scale), grid_spec=pltpu.PrefetchSca...  14 us
    pallas_call x1, Pallas kernels, project(): pl.pallas_call(project_kernel, grid=(blocks,), in_specs=[pl.BlockSpec((1,...  13.3 us
    ppermute x6, waiting for transfers between devices, shifted(): return lax.ppermute(array, axis, pairs)  9.97 us
  transfers between devices with their start and end apart: 25, of which 10 were waited for; matrix products, arithmetic and copies ran while one was open for 7% of the time, Pallas kernels for 15%

profile of v8, /device:TPU:11, one launch (start us, length us, event | category | flops | bytes accessed | tf_op | source)
XLA Modules:
  0.0 289.9 jit_solution(4971419708077780076)
XLA Ops:
  7.4 1.1 copy-done.13
  9.3 1.3 collective-permute-start.3
  15.1 1.0 constant_dynamic-slice_fusion.2
  16.2 1.6 fusion
  18.0 1.0 copy-done.12
  19.3 2.3 collective-permute-start.4
  21.6 1.0 bitcast_dynamic-update-slice_fusion.2
  22.6 40.9 %collective-permute-done.4 = bf16[2,64,1280]{2,1,0:T(8,128)(2,1)S(1)} collective-permute-done((bf16[2,64,1280]{2,1,0:T(8,128)(2,1)S(1)}, bf16[2,64,1280]{2,1,0:T(8,128)(2,1)S(1)}, u32[]{:S(2)}, u32[]{:S(2)}) %collective-permute-start.4) | collective-permute-done | bytes 327712 | tf_op jit(solution)/shard_map/ppermute | solution.py:136
  64.1 1.2 collective-permute-start.7
  65.3 14.2 %collective-permute-done.6 = bf16[1,256,1280]{2,1,0:T(8,128)(2,1)S(1)} collective-permute-done((bf16[1,256,1280]{2,1,0:T(8,128)(2,1)S(1)}, bf16[1,256,1280]{2,1,0:T(8,128)(2,1)S(1)}, u32[]{:S(2)}, u32[]{:S(2)}) %collective-permute-start.6) | collective-permute-done | bytes 655392 | tf_op jit(solution)/shard_map/ppermute | solution.py:144
  79.7 1.3 collective-permute-start.9
  81.5 1.0 constant_dynamic-slice_fusion.3
  82.6 26.1 %collective-permute-done.9 = bf16[2,256,1280]{2,1,0:T(8,128)(2,1)S(1)} collective-permute-done((bf16[2,256,1280]{2,1,0:T(8,128)(2,1)S(1)}, bf16[2,256,1280]{2,1,0:T(8,128)(2,1)S(1)}, u32[]{:S(2)}, u32[]{:S(2)}) %collective-permute-start.9) | collective-permute-done | bytes 1310752 | tf_op jit(solution)/shard_map/ppermute | solution.py:144
  108.9 1.0 collective-permute-done.8
  110.1 3.0 %pad_maximum_fusion.near_ref = bf16[4,512,1280]{2,1,0:T(8,128)(2,1)} fusion(bf16[1,512,1280]{2,1,0:T(8,128)(2,1)S(1)} %maximum_bitcast_fusion.3, bf16[1,512,1280]{2,1,0:T(8,128)(2,1)S(1)} %maximum_bitcast_fusion.2, bf16[1,512,1280]{2,1,0:T(8,128)(2,1)S(1)} %maximum_bitcast_fusion.1, bf16[1,512,1280]{2,1,0:T(8,128)(2,1)S(1)} %maximum_bitcast_fusion), kind=kLoop, calls=%fused_computation | loop fusion | flops 7864320 | bytes 10485760 | tf_op jit(solution)/shard_map/stack | solution.py:283
  113.1 2.5 collective-permute-start.10
  115.6 0.9 pad_maximum_fusion.7
  116.5 2.0 pad_maximum_fusion.6
  119.4 8.0 %all-gather.2.cloned.1.call-done.g_ref = bf16[8,512,640]{2,1,0:T(8,128)(2,1)} async-done(((bf16[8,128,640]{2,1,0:T(8,128)(2,1)}), bf16[8,512,640]{2,1,0:T(8,128)(2,1)}) %all-gather.2.cloned.1.call-update) | async-done | bytes 5242896 | tf_op jit(solution)/shard_map/all_gather | solution.py:257
  127.4 5.1 %all-to-all-start = ((bf16[8,512,640]{2,1,0:T(8,128)(2,1)}), bf16[8,512,640]{2,1,0:T(8,128)(2,1)}, u32[]{:S(2)}, u32[]{:S(2)}) async-start(bf16[8,512,640]{2,1,0:T(8,128)(2,1)} %all-gather.2.cloned.1.call-done.g_ref), calls=%async_computation | async-start | bytes 10485760 | tf_op jit(solution)/shard_map/all_to_all | solution.py:299
  132.5 1.2 dynamic-slice_bitcast_fusion.3
  133.7 3.7 %collective-permute-start.12 = (bf16[2,2,64,1280]{3,2,1,0:T(8,128)(2,1)}, bf16[2,2,64,1280]{3,2,1,0:T(8,128)(2,1)S(1)}, u32[]{:S(2)}, u32[]{:S(2)}) collective-permute-start(bf16[2,2,64,1280]{3,2,1,0:T(8,128)(2,1)} %pad_maximum_fusion.6), channel_id=1, source_target_pairs={{0,4},{2,6},{4,0},{6,2},{1,5},{3,7},{5,1},{7,3},{8,12},{10,14},{12... | collective-permute-start | bytes 1966088 | tf_op jit(solution)/shard_map/ppermute | solution.py:136
  137.5 1.0 collective-permute-start.13
  138.5 1.0 dynamic-slice_bitcast_fusion.7
  139.5 2.5 copy-done.11
  142.0 13.3 %project_gated.1 = bf16[512,1280]{1,0:T(8,128)(2,1)S(1)} custom-call(bf16[8,512,640]{2,1,0:T(8,128)(2,1)S(1)} %copy-done.11, bf16[1280,5120]{1,0:T(8,128)(2,1)} %w_ref.1), custom_call_target="tpu_custom_call" | custom-call | flops 6710886400 | bytes 19660800 | tf_op jit(solution)/shard_map/project_gated/pallas_call | solution.py:209
  155.3 34.9 %collective-permute-done.12.refs_4_ = bf16[2,2,64,1280]{3,2,1,0:T(8,128)(2,1)S(1)} collective-permute-done((bf16[2,2,64,1280]{3,2,1,0:T(8,128)(2,1)}, bf16[2,2,64,1280]{3,2,1,0:T(8,128)(2,1)S(1)}, u32[]{:S(2)}, u32[]{:S(2)}) %collective-permute-start.12) | collective-permute-done | bytes 655392 | tf_op jit(solution)/shard_map/ppermute | solution.py:136
  190.2 4.5 %collective-permute-done.13.refs_5_ = bf16[2,2,64,1280]{3,2,1,0:T(8,128)(2,1)S(1)} collective-permute-done((bf16[2,2,64,1280]{3,2,1,0:T(8,128)(2,1)}, bf16[2,2,64,1280]{3,2,1,0:T(8,128)(2,1)S(1)}, u32[]{:S(2)}, u32[]{:S(2)}) %collective-permute-start.13) | collective-permute-done | bytes 655392 | tf_op jit(solution)/shard_map/ppermute | solution.py:136
  195.9 1.2 pad_maximum_fusion.3
  197.0 3.6 %collective-permute-start.17 = (bf16[2,4,64,1280]{3,2,1,0:T(8,128)(2,1)}, bf16[2,4,64,1280]{3,2,1,0:T(8,128)(2,1)}, u32[]{:S(2)}, u32[]{:S(2)}) collective-permute-start(bf16[2,4,64,1280]{3,2,1,0:T(8,128)(2,1)} %pad_maximum_fusion.3), channel_id=1, source_target_pairs={{0,8},{8,16},{16,24},{1,9},{9,17},{17,25},{2,10},{10,18},{18,26},{... | collective-permute-start | bytes 3932168 | tf_op jit(solution)/shard_map/ppermute | solution.py:131
  200.9 1.2 pad_maximum_fusion.4
  202.0 1.9 collective-permute-start.18
  204.6 1.4 collective-permute-start.16
  206.0 14.0 %weight_gradient.1 = f32[1280,640]{1,0:T(8,128)} custom-call(s32[2,4]{1,0:T(2,128)S(1)} %pad_add_fusion.table, bf16[4,512,1280]{2,1,0:T(8,128)(2,1)} %pad_maximum_fusion.near_ref, bf16[4,512,1280]{2,1,0:T(8,128)(2,1)} %collective-permute-done.10.far_ref, bf16[8,512,640]{2,1,0:T(8,128)(2,1)} %all-to-all-done.g_near.g_far, ...), custom_call_target="tpu_custom_call" | custom-call | flops 6710886400 | bytes 19005440 | tf_op jit(solution)/shard_map/weight_gradient/pallas_call | solution.py:162
  220.1 1.3 collective-permute-start
  221.4 3.0 %collective-permute-start.1 = (bf16[2,64,640]{2,1,0:T(8,128)(2,1)S(1)}, bf16[2,64,640]{2,1,0:T(8,128)(2,1)S(1)}, u32[]{:S(2)}, u32[]{:S(2)}) collective-permute-start(bf16[2,64,640]{2,1,0:T(8,128)(2,1)S(1)} %copy-done.15), channel_id=1, source_target_pairs={{0,4},{2,6},{4,0},{6,2},{1,5},{3,7},{5,1},{7,3},{8,12},{10,14},{12... | collective-permute-start | bytes 491528 | tf_op jit(solution)/shard_map/ppermute | solution.py:136
  224.5 16.0 %attention_backward.2 = (bf16[2,256,640]{2,1,0:T(8,128)(2,1)S(1)}, f32[2,256,640]{2,1,0:T(8,128)S(1)}, f32[2,256,640]{2,1,0:T(8,128)S(1)}, bf16[2,256,640]{2,1,0:T(8,128)(2,1)S(1)}, bf16[2,256,640]{2,1,0:T(8,128)(2,1)S(1)}) custom-call(s32[6]{0:T(128)S(1)} %pad_add_fusion.1.scal, bf16[1,2,64,5120]{3,2,1,0:T(8,128)(2,1)S(1)} %copy-done.4, ...), custom_call_target="tpu_custom_call" | custom-call | flops 2516582400 | bytes 10485760 | tf_op jit(solution)/shard_map/attention_backward/pallas_call | solution.py:99
  240.5 16.1 %attention_backward.3 = (bf16[2,256,640]{2,1,0:T(8,128)(2,1)S(1)}, f32[2,256,640]{2,1,0:T(8,128)S(1)}, f32[2,256,640]{2,1,0:T(8,128)S(1)}, bf16[2,256,640]{2,1,0:T(8,128)(2,1)S(1)}, bf16[2,256,640]{2,1,0:T(8,128)(2,1)S(1)}) custom-call(s32[6]{0:T(128)S(1)} %pad_add_fusion.1.scal, bf16[1,2,64,5120]{3,2,1,0:T(8,128)(2,1)S(1)} %copy-done.4, ...), custom_call_target="tpu_custom_call" | custom-call | flops 2516582400 | bytes 10485760 | tf_op jit(solution)/shard_map/attention_backward/pallas_call | solution.py:99
  256.5 4.9 %collective-permute-start.21 = (bf16[2,256,640]{2,1,0:T(8,128)(2,1)S(1)}, bf16[2,256,640]{2,1,0:T(8,128)(2,1)S(1)}, u32[]{:S(2)}, u32[]{:S(2)}) collective-permute-start(bf16[2,256,640]{2,1,0:T(8,128)(2,1)S(1)} %get-tuple-element.61), channel_id=1, source_target_pairs={{0,8},{8,16},{16,24},{1,9},{9,17},{17,25},{2,10},{10,18},{18,26},{... | collective-permute-start | bytes 1966088 | tf_op jit(solution)/shard_map/ppermute | solution.py:131
  261.4 1.9 collective-permute-start.22
  263.4 3.6 %collective-permute-start.19 = (bf16[2,256,640]{2,1,0:T(8,128)(2,1)S(1)}, bf16[2,256,640]{2,1,0:T(8,128)(2,1)S(1)}, u32[]{:S(2)}, u32[]{:S(2)}) collective-permute-start(bf16[2,256,640]{2,1,0:T(8,128)(2,1)S(1)} %get-tuple-element.58), channel_id=1, source_target_pairs={{0,8},{8,16},{16,24},{1,9},{9,17},{17,25},{2,10},{10,18},{18,26},{... | collective-permute-start | bytes 1966088 | tf_op jit(solution)/shard_map/ppermute | solution.py:131
  267.0 1.9 collective-permute-start.20
  268.9 1.2 maximum_bitcast_fusion.4
  270.1 3.2 %collective-permute-done.22 = bf16[2,256,640]{2,1,0:T(8,128)(2,1)S(1)} collective-permute-done((bf16[2,256,640]{2,1,0:T(8,128)(2,1)S(1)}, bf16[2,256,640]{2,1,0:T(8,128)(2,1)S(1)}, u32[]{:S(2)}, u32[]{:S(2)}) %collective-permute-start.22) | collective-permute-done | bytes 655392 | tf_op jit(solution)/shard_map/ppermute | solution.py:131
  273.6 2.3 collective-permute-done.19
  276.0 4.4 %collective-permute-done.20 = bf16[2,256,640]{2,1,0:T(8,128)(2,1)S(1)} collective-permute-done((bf16[2,256,640]{2,1,0:T(8,128)(2,1)S(1)}, bf16[2,256,640]{2,1,0:T(8,128)(2,1)S(1)}, u32[]{:S(2)}, u32[]{:S(2)}) %collective-permute-start.20) | collective-permute-done | bytes 655392 | tf_op jit(solution)/shard_map/ppermute | solution.py:131
  280.8 1.2 maximum_bitcast_fusion.5
  281.9 1.2 maximum_bitcast_fusion.6
  (99 shorter events, 7.2 us)
Async XLA Ops:
  7.2 1.3 copy-start.13
  7.2 120.2 %all-gather.2.cloned.1.call-start = ((), (), s32[]{:S(2)}) async-start(), calls=%async_computation.1 | async-start | bytes 6553600 | tf_op jit(solution)/shard_map/all_gather | solution.py:257
  8.5 2.1 copy-start.17
  9.3 12.3 %collective-permute-start.3 = (bf16[2,64,1280]{2,1,0:T(8,128)(2,1)}, bf16[2,64,1280]{2,1,0:T(8,128)(2,1)}, u32[]{:S(2)}, u32[]{:S(2)}) collective-permute-start(bf16[2,64,1280]{2,1,0:T(8,128)(2,1)} %get-tuple-element.105), channel_id=1, source_target_pairs={{0,2},{2,4},{4,6},{6,0},{1,3},{3,5},{5,7},{7,1},{8,10},{10,12},{12... | collective-permute-start | bytes 983048 | tf_op jit(solution)/shard_map/ppermute | solution.py:136
  18.0 1.1 copy-start.12
  19.1 44.5 %collective-permute-start.5 = (bf16[2,64,1280]{2,1,0:T(8,128)(2,1)S(1)}, bf16[2,64,1280]{2,1,0:T(8,128)(2,1)S(1)}, u32[]{:S(2)}, u32[]{:S(2)}) collective-permute-start(bf16[2,64,1280]{2,1,0:T(8,128)(2,1)S(1)} %get-tuple-element.104), channel_id=1, source_target_pairs={{0,6},{2,0},{4,2},{6,4},{1,7},{3,1},{5,3},{7,5},{8,14},{10,8},{12,... | collective-permute-start | bytes 983048 | tf_op jit(solution)/shard_map/ppermute | solution.py:136
  19.3 44.2 %collective-permute-start.4 = (bf16[2,64,1280]{2,1,0:T(8,128)(2,1)S(1)}, bf16[2,64,1280]{2,1,0:T(8,128)(2,1)S(1)}, u32[]{:S(2)}, u32[]{:S(2)}) collective-permute-start(bf16[2,64,1280]{2,1,0:T(8,128)(2,1)S(1)} %get-tuple-element.107), channel_id=1, source_target_pairs={{0,4},{2,6},{4,0},{6,2},{1,5},{3,7},{5,1},{7,3},{8,12},{10,14},{12... | collective-permute-start | bytes 983048 | tf_op jit(solution)/shard_map/ppermute | solution.py:136
  63.8 15.8 %collective-permute-start.6 = (bf16[1,256,1280]{2,1,0:T(8,128)(2,1)S(1)}, bf16[1,256,1280]{2,1,0:T(8,128)(2,1)S(1)}, u32[]{:S(2)}, u32[]{:S(2)}) collective-permute-start(bf16[1,256,1280]{2,1,0:T(8,128)(2,1)S(1)} %get-tuple-element.99), channel_id=1, source_target_pairs={{0,1},{1,0},{2,3},{3,2},{4,5},{5,4},{6,7},{7,6},{8,9},{9,8},{10,11... | collective-permute-start | bytes 1966088 | tf_op jit(solution)/shard_map/ppermute | solution.py:144
  64.1 16.9 %collective-permute-start.7 = (bf16[1,256,1280]{2,1,0:T(8,128)(2,1)S(1)}, bf16[1,256,1280]{2,1,0:T(8,128)(2,1)S(1)}, u32[]{:S(2)}, u32[]{:S(2)}) collective-permute-start(bf16[1,256,1280]{2,1,0:T(8,128)(2,1)S(1)} %get-tuple-element.98), channel_id=1, source_target_pairs={{0,16},{8,24},{16,0},{24,8},{1,17},{9,25},{17,1},{25,9},{2,18},{10... | collective-permute-start | bytes 1966088 | tf_op jit(solution)/shard_map/ppermute | solution.py:144
  79.7 1.8 copy-start
  79.7 1.8 copy-start.1
  79.7 29.0 %collective-permute-start.9 = (bf16[2,256,1280]{2,1,0:T(8,128)(2,1)S(1)}, bf16[2,256,1280]{2,1,0:T(8,128)(2,1)S(1)}, u32[]{:S(2)}, u32[]{:S(2)}) collective-permute-start(bf16[2,256,1280]{2,1,0:T(8,128)(2,1)S(1)} %pad_maximum_fusion.2), channel_id=1, source_target_pairs={{0,16},{8,24},{16,0},{24,8},{1,17},{9,25},{17,1},{25,9},{2,18},{10... | collective-permute-start | bytes 3932168 | tf_op jit(solution)/shard_map/ppermute | solution.py:144
  81.1 28.7 %collective-permute-start.8 = (bf16[2,256,1280]{2,1,0:T(8,128)(2,1)S(1)}, bf16[2,256,1280]{2,1,0:T(8,128)(2,1)S(1)}, u32[]{:S(2)}, u32[]{:S(2)}) collective-permute-start(bf16[2,256,1280]{2,1,0:T(8,128)(2,1)S(1)} %pad_maximum_fusion.1), channel_id=1, source_target_pairs={{0,1},{1,0},{2,3},{3,2},{4,5},{5,4},{6,7},{7,6},{8,9},{9,8},{10,11... | collective-permute-start | bytes 3932168 | tf_op jit(solution)/shard_map/ppermute | solution.py:144
  113.1 91.5 %collective-permute-start.10 = (bf16[4,512,1280]{2,1,0:T(8,128)(2,1)}, bf16[4,512,1280]{2,1,0:T(8,128)(2,1)}, u32[]{:S(2)}, u32[]{:S(2)}) collective-permute-start(bf16[4,512,1280]{2,1,0:T(8,128)(2,1)} %pad_maximum_fusion.near_ref), channel_id=1, source_target_pairs={{0,8},{8,0},{16,24},{24,16},{1,9},{9,1},{17,25},{25,17},{2,10},{10... | collective-permute-start | bytes 15728648 | tf_op jit(solution)/shard_map/ppermute | solution.py:144
  127.4 78.6 %all-to-all-start = ((bf16[8,512,640]{2,1,0:T(8,128)(2,1)}), bf16[8,512,640]{2,1,0:T(8,128)(2,1)}, u32[]{:S(2)}, u32[]{:S(2)}) async-start(bf16[8,512,640]{2,1,0:T(8,128)(2,1)} %all-gather.2.cloned.1.call-done.g_ref), calls=%async_computation | async-start | bytes 10485760 | tf_op jit(solution)/shard_map/all_to_all | solution.py:299
  132.5 6.0 %copy-start.3 = (bf16[1,2,64,5120]{3,2,1,0:T(8,128)(2,1)S(1)}, bf16[1,2,64,5120]{3,2,1,0:T(8,128)(2,1)}, u32[]{:S(2)}) copy-start(bf16[1,2,64,5120]{3,2,1,0:T(8,128)(2,1)} %refs_0_.3) | copy-start | bytes 3932164
  133.7 21.6 %collective-permute-start.11 = (bf16[2,2,64,1280]{3,2,1,0:T(8,128)(2,1)}, bf16[2,2,64,1280]{3,2,1,0:T(8,128)(2,1)S(1)}, u32[]{:S(2)}, u32[]{:S(2)}) collective-permute-start(bf16[2,2,64,1280]{3,2,1,0:T(8,128)(2,1)} %pad_maximum_fusion.5), channel_id=1, source_target_pairs={{0,2},{2,4},{4,6},{6,0},{1,3},{3,5},{5,7},{7,1},{8,10},{10,12},{12... | collective-permute-start | bytes 1966088 | tf_op jit(solution)/shard_map/ppermute | solution.py:136
  133.7 56.5 %collective-permute-start.12 = (bf16[2,2,64,1280]{3,2,1,0:T(8,128)(2,1)}, bf16[2,2,64,1280]{3,2,1,0:T(8,128)(2,1)S(1)}, u32[]{:S(2)}, u32[]{:S(2)}) collective-permute-start(bf16[2,2,64,1280]{3,2,1,0:T(8,128)(2,1)} %pad_maximum_fusion.6), channel_id=1, source_target_pairs={{0,4},{2,6},{4,0},{6,2},{1,5},{3,7},{5,1},{7,3},{8,12},{10,14},{12... | collective-permute-start | bytes 1966088 | tf_op jit(solution)/shard_map/ppermute | solution.py:136
  137.5 57.3 %collective-permute-start.13 = (bf16[2,2,64,1280]{3,2,1,0:T(8,128)(2,1)}, bf16[2,2,64,1280]{3,2,1,0:T(8,128)(2,1)S(1)}, u32[]{:S(2)}, u32[]{:S(2)}) collective-permute-start(bf16[2,2,64,1280]{3,2,1,0:T(8,128)(2,1)} %pad_maximum_fusion.7), channel_id=1, source_target_pairs={{0,6},{2,0},{4,2},{6,4},{1,7},{3,1},{5,3},{7,5},{8,14},{10,8},{12,... | collective-permute-start | bytes 1966088 | tf_op jit(solution)/shard_map/ppermute | solution.py:136
  139.5 2.5 copy-start.11
  155.3 39.6 %copy-start.9 = (bf16[512,1280]{1,0:T(8,128)(2,1)}, bf16[512,1280]{1,0:T(8,128)(2,1)S(1)}, u32[]{:S(2)}) copy-start(bf16[512,1280]{1,0:T(8,128)(2,1)S(1)} %project_gated.1) | copy-start | bytes 3932164
  190.2 4.6 %copy-start.5 = (bf16[2,2,64,1280]{3,2,1,0:T(8,128)(2,1)}, bf16[2,2,64,1280]{3,2,1,0:T(8,128)(2,1)S(1)}, u32[]{:S(2)}) copy-start(bf16[2,2,64,1280]{3,2,1,0:T(8,128)(2,1)S(1)} %collective-permute-done.12.refs_4_) | copy-start | bytes 1966084
  194.7 0.9 copy-start.7
  197.0 27.4 %collective-permute-start.17 = (bf16[2,4,64,1280]{3,2,1,0:T(8,128)(2,1)}, bf16[2,4,64,1280]{3,2,1,0:T(8,128)(2,1)}, u32[]{:S(2)}, u32[]{:S(2)}) collective-permute-start(bf16[2,4,64,1280]{3,2,1,0:T(8,128)(2,1)} %pad_maximum_fusion.3), channel_id=1, source_target_pairs={{0,8},{8,16},{16,24},{1,9},{9,17},{17,25},{2,10},{10,18},{18,26},{... | collective-permute-start | bytes 3932168 | tf_op jit(solution)/shard_map/ppermute | solution.py:131
  200.9 3.1 %copy-start.18 = (s32[8,2]{0,1:T(2,128)S(1)}, s32[8,2]{0,1:T(2,128)}, u32[]{:S(2)}) copy-start(s32[8,2]{0,1:T(2,128)} %param.17) | copy-start | bytes 196
  202.0 22.4 %collective-permute-start.18 = (bf16[2,4,64,1280]{3,2,1,0:T(8,128)(2,1)}, bf16[2,4,64,1280]{3,2,1,0:T(8,128)(2,1)}, u32[]{:S(2)}, u32[]{:S(2)}) collective-permute-start(bf16[2,4,64,1280]{3,2,1,0:T(8,128)(2,1)} %pad_maximum_fusion.4), channel_id=1, source_target_pairs={{8,0},{16,8},{24,16},{9,1},{17,9},{25,17},{10,2},{18,10},{26,18},{... | collective-permute-start | bytes 3932168 | tf_op jit(solution)/shard_map/ppermute | solution.py:131
  204.4 15.6 %collective-permute-start.14 = (bf16[2,64,640]{2,1,0:T(8,128)(2,1)}, bf16[2,64,640]{2,1,0:T(8,128)(2,1)S(1)}, u32[]{:S(2)}, u32[]{:S(2)}) collective-permute-start(bf16[2,64,640]{2,1,0:T(8,128)(2,1)} %get-tuple-element.47), channel_id=1, source_target_pairs={{0,2},{2,4},{4,6},{6,0},{1,3},{3,5},{5,7},{7,1},{8,10},{10,12},{12... | collective-permute-start | bytes 491528 | tf_op jit(solution)/shard_map/ppermute | solution.py:136
  204.5 16.9 %collective-permute-start.15 = (bf16[2,64,640]{2,1,0:T(8,128)(2,1)}, bf16[2,64,640]{2,1,0:T(8,128)(2,1)}, u32[]{:S(2)}, u32[]{:S(2)}) collective-permute-start(bf16[2,64,640]{2,1,0:T(8,128)(2,1)} %get-tuple-element.48), channel_id=1, source_target_pairs={{0,4},{2,6},{4,0},{6,2},{1,5},{3,7},{5,1},{7,3},{8,12},{10,14},{12... | collective-permute-start | bytes 491528 | tf_op jit(solution)/shard_map/ppermute | solution.py:136
  204.6 19.8 %collective-permute-start.16 = (bf16[2,64,640]{2,1,0:T(8,128)(2,1)}, bf16[2,64,640]{2,1,0:T(8,128)(2,1)}, u32[]{:S(2)}, u32[]{:S(2)}) collective-permute-start(bf16[2,64,640]{2,1,0:T(8,128)(2,1)} %get-tuple-element.49), channel_id=1, source_target_pairs={{0,6},{2,0},{4,2},{6,4},{1,7},{3,1},{5,3},{7,5},{8,14},{10,8},{12,... | collective-permute-start | bytes 491528 | tf_op jit(solution)/shard_map/ppermute | solution.py:136
  206.0 14.1 %copy-start.16 = (bf16[2,64,640]{2,1,0:T(8,128)(2,1)S(1)}, bf16[2,64,640]{2,1,0:T(8,128)(2,1)}, u32[]{:S(2)}) copy-start(bf16[2,64,640]{2,1,0:T(8,128)(2,1)} %get-tuple-element.36) | copy-start | bytes 491524
  206.0 15.4 %copy-start.15 = (bf16[2,64,640]{2,1,0:T(8,128)(2,1)S(1)}, bf16[2,64,640]{2,1,0:T(8,128)(2,1)}, u32[]{:S(2)}) copy-start(bf16[2,64,640]{2,1,0:T(8,128)(2,1)} %get-tuple-element.37) | copy-start | bytes 491524
  206.0 18.4 %copy-start.14 = (bf16[2,64,640]{2,1,0:T(8,128)(2,1)S(1)}, bf16[2,64,640]{2,1,0:T(8,128)(2,1)}, u32[]{:S(2)}) copy-start(bf16[2,64,640]{2,1,0:T(8,128)(2,1)} %get-tuple-element.38) | copy-start | bytes 491524
  206.0 18.4 %copy-start.2 = (bf16[1,2,64,5120]{3,2,1,0:T(8,128)(2,1)S(1)}, bf16[1,2,64,5120]{3,2,1,0:T(8,128)(2,1)}, u32[]{:S(2)}) copy-start(bf16[1,2,64,5120]{3,2,1,0:T(8,128)(2,1)} %refs_2_.3) | copy-start | bytes 3932164
  206.0 18.4 %copy-start.4 = (bf16[1,2,64,5120]{3,2,1,0:T(8,128)(2,1)S(1)}, bf16[1,2,64,5120]{3,2,1,0:T(8,128)(2,1)}, u32[]{:S(2)}) copy-start(bf16[1,2,64,5120]{3,2,1,0:T(8,128)(2,1)} %refs_0_.3) | copy-start | bytes 3932164
  206.0 18.4 %copy-start.6 = (bf16[2,2,64,1280]{3,2,1,0:T(8,128)(2,1)S(1)}, bf16[2,2,64,1280]{3,2,1,0:T(8,128)(2,1)}, u32[]{:S(2)}) copy-start(bf16[2,2,64,1280]{3,2,1,0:T(8,128)(2,1)} %copy-done.5) | copy-start | bytes 1966084
  206.0 18.4 %copy-start.8 = (bf16[2,2,64,1280]{3,2,1,0:T(8,128)(2,1)S(1)}, bf16[2,2,64,1280]{3,2,1,0:T(8,128)(2,1)}, u32[]{:S(2)}) copy-start(bf16[2,2,64,1280]{3,2,1,0:T(8,128)(2,1)} %copy-done.7) | copy-start | bytes 1966084
  206.0 18.4 %copy-start.10 = (bf16[512,1280]{1,0:T(8,128)(2,1)S(1)}, bf16[512,1280]{1,0:T(8,128)(2,1)}, u32[]{:S(2)}) copy-start(bf16[512,1280]{1,0:T(8,128)(2,1)} %copy-done.9) | copy-start | bytes 3932164
  220.1 20.4 %collective-permute-start = (bf16[2,64,640]{2,1,0:T(8,128)(2,1)S(1)}, bf16[2,64,640]{2,1,0:T(8,128)(2,1)S(1)}, u32[]{:S(2)}, u32[]{:S(2)}) collective-permute-start(bf16[2,64,640]{2,1,0:T(8,128)(2,1)S(1)} %copy-done.16), channel_id=1, source_target_pairs={{0,2},{2,4},{4,6},{6,0},{1,3},{3,5},{5,7},{7,1},{8,10},{10,12},{12... | collective-permute-start | bytes 491528 | tf_op jit(solution)/shard_map/ppermute | solution.py:136
  221.4 19.1 %collective-permute-start.1 = (bf16[2,64,640]{2,1,0:T(8,128)(2,1)S(1)}, bf16[2,64,640]{2,1,0:T(8,128)(2,1)S(1)}, u32[]{:S(2)}, u32[]{:S(2)}) collective-permute-start(bf16[2,64,640]{2,1,0:T(8,128)(2,1)S(1)} %copy-done.15), channel_id=1, source_target_pairs={{0,4},{2,6},{4,0},{6,2},{1,5},{3,7},{5,1},{7,3},{8,12},{10,14},{12... | collective-permute-start | bytes 491528 | tf_op jit(solution)/shard_map/ppermute | solution.py:136
  224.4 16.1 %collective-permute-start.2 = (bf16[2,64,640]{2,1,0:T(8,128)(2,1)S(1)}, bf16[2,64,640]{2,1,0:T(8,128)(2,1)S(1)}, u32[]{:S(2)}, u32[]{:S(2)}) collective-permute-start(bf16[2,64,640]{2,1,0:T(8,128)(2,1)S(1)} %copy-done.14), channel_id=1, source_target_pairs={{0,6},{2,0},{4,2},{6,4},{1,7},{3,1},{5,3},{7,5},{8,14},{10,8},{12,... | collective-permute-start | bytes 491528 | tf_op jit(solution)/shard_map/ppermute | solution.py:136
  256.5 13.6 %collective-permute-start.21 = (bf16[2,256,640]{2,1,0:T(8,128)(2,1)S(1)}, bf16[2,256,640]{2,1,0:T(8,128)(2,1)S(1)}, u32[]{:S(2)}, u32[]{:S(2)}) collective-permute-start(bf16[2,256,640]{2,1,0:T(8,128)(2,1)S(1)} %get-tuple-element.61), channel_id=1, source_target_pairs={{0,8},{8,16},{16,24},{1,9},{9,17},{17,25},{2,10},{10,18},{18,26},{... | collective-permute-start | bytes 1966088 | tf_op jit(solution)/shard_map/ppermute | solution.py:131
  261.4 11.9 %collective-permute-start.22 = (bf16[2,256,640]{2,1,0:T(8,128)(2,1)S(1)}, bf16[2,256,640]{2,1,0:T(8,128)(2,1)S(1)}, u32[]{:S(2)}, u32[]{:S(2)}) collective-permute-start(bf16[2,256,640]{2,1,0:T(8,128)(2,1)S(1)} %get-tuple-element.62), channel_id=1, source_target_pairs={{8,0},{16,8},{24,16},{9,1},{17,9},{25,17},{10,2},{18,10},{26,18},{... | collective-permute-start | bytes 1966088 | tf_op jit(solution)/shard_map/ppermute | solution.py:131
  263.4 12.6 %collective-permute-start.19 = (bf16[2,256,640]{2,1,0:T(8,128)(2,1)S(1)}, bf16[2,256,640]{2,1,0:T(8,128)(2,1)S(1)}, u32[]{:S(2)}, u32[]{:S(2)}) collective-permute-start(bf16[2,256,640]{2,1,0:T(8,128)(2,1)S(1)} %get-tuple-element.58), channel_id=1, source_target_pairs={{0,8},{8,16},{16,24},{1,9},{9,17},{17,25},{2,10},{10,18},{18,26},{... | collective-permute-start | bytes 1966088 | tf_op jit(solution)/shard_map/ppermute | solution.py:131
  267.0 13.3 %collective-permute-start.20 = (bf16[2,256,640]{2,1,0:T(8,128)(2,1)S(1)}, bf16[2,256,640]{2,1,0:T(8,128)(2,1)S(1)}, u32[]{:S(2)}, u32[]{:S(2)}) collective-permute-start(bf16[2,256,640]{2,1,0:T(8,128)(2,1)S(1)} %get-tuple-element.59), channel_id=1, source_target_pairs={{8,0},{16,8},{24,16},{9,1},{17,9},{25,17},{10,2},{18,10},{26,18},{... | collective-permute-start | bytes 1966088 | tf_op jit(solution)/shard_map/ppermute | solution.py:131
Sparse Core Ops, SparseCore 0:
  19.2 108.1 all-gather.1

commit v9 on v8

--- a/solution.py
+++ b/solution.py
@@ -9,6 +9,7 @@
 
 HD = 128
 NEG = -1e30
+LOG2E = 1.4426950408889634
 NT = (((1,), (1,)), ((), ()))
 NN = (((1,), (0,)), ((), ()))
 TN = (((0,), (0,)), ((), ()))
@@ -55,12 +56,12 @@
         )[0:1]
         scores = []
         for w in range(3):
-            s = dot(k_all[f + w], q, NT) * inv_root
+            s = dot(k_all[f + w], q, NT) * (inv_root * LOG2E)
             if w != 1:
                 s = jnp.where(row < scal[2 + 2 * f + w // 2], s, NEG)
             scores.append(s)
         top = jnp.max(jnp.maximum(jnp.maximum(scores[0], scores[1]), scores[2]), axis=0, keepdims=True)
-        exps = [jnp.exp(s - top) for s in scores]
+        exps = [jnp.exp2(s - top) for s in scores]
         total = jnp.sum(exps[0] + exps[1] + exps[2], axis=0, keepdims=True)
         inv_total = 1.0 / total
         dq = None
@@ -70,9 +71,9 @@
             d_prob = dot(v_all[f + w], d, NT)
             d_score = (prob * (d_prob - delta)).astype(jnp.bfloat16)
             put(key_grads, f + w, dot(d_score, q, NN))
-            term = dot(d_score, k_all[f + w], TN)
+            term = dot(k_all[f + w], d_score, TN)
             dq = term if dq is None else dq + term
-        dq_ref[f] = (dq * inv_root).astype(jnp.bfloat16)
+        dq_ref[f] = (dq.T * inv_root).astype(jnp.bfloat16)
     for f in range(frames):
         dk_ref[f] = key_grads[f + 1] * inv_root
         dv_ref[f] = value_grads[f + 1]
@@ -183,6 +184,41 @@
     )(table, near, far, gated, gated)
 
 
+def gate_kernel(levels, cot_ref, table_ref, out_ref):
+    _, frames, rows, _ = cot_ref.shape
+    for f in range(frames):
+        gain = table_ref[pl.ds(levels[f], 1), :]
+        rounded = (cot_ref[0, f].astype(jnp.float32) * gain).astype(jnp.bfloat16)
+        out_ref[0, f * rows : (f + 1) * rows] = rounded
+
+
+def gate(cotangent, table, levels, blocks):
+    _, frames, rows, model = cotangent.shape
+    block = model // blocks
+    if block % 128:
+        gain = jnp.concatenate(
+            [lax.dynamic_slice_in_dim(table, levels[f], 1, axis=0) for f in range(frames)], axis=0
+        )
+        gated = (cotangent[0].astype(jnp.float32) * gain[:, None, :]).astype(jnp.bfloat16)
+        gated = gated.reshape(frames * rows, model)
+        return jnp.stack([gated[:, b * block : (b + 1) * block] for b in range(blocks)])
+    return pl.pallas_call(
+        gate_kernel,
+        grid_spec=pltpu.PrefetchScalarGridSpec(
+            num_scalar_prefetch=1,
+            grid=(blocks,),
+            in_specs=[
+                pl.BlockSpec((1, frames, rows, block), lambda b, lev: (0, 0, 0, b)),
+                pl.BlockSpec((table.shape[0], block), lambda b, lev: (0, b)),
+            ],
+            out_specs=pl.BlockSpec((1, frames * rows, block), lambda b, lev: (b, 0, 0)),
+        ),
+        out_shape=jax.ShapeDtypeStruct((blocks, frames * rows, block), jnp.bfloat16),
+        compiler_params=pltpu.CompilerParams(vmem_limit_bytes=40 * 2**20),
+        name="gate_cotangent",
+    )(levels, cotangent, table)
+
+
 def project_kernel(g_ref, w_ref, out_ref, acc_ref):
     step = pl.program_id(0)
     term = dot(g_ref[0], w_ref[...], NT)
@@ -248,12 +284,7 @@
     shifts = range(1, parts)
     o_pieces = [rotated(columns_for(saved_out, s, 0, width), "head", s) for s in shifts]
 
-    gain = jnp.concatenate(
-        [lax.dynamic_slice_in_dim(gate_table, levels[f], 1, axis=0) for f in range(frames)], axis=0
-    )
-    gated = (cotangent[0].astype(jnp.float32) * gain[:, None, :]).astype(jnp.bfloat16)
-    gated = gated.reshape(frames * rows, model)
-    gated = jnp.stack([gated[:, b * block : (b + 1) * block] for b in range(blocks)])
+    gated = gate(cotangent, gate_table, levels, blocks)
     gathered = lax.all_gather(gated, "head", axis=1, tiled=True)
 
     kv_send = [

time: 293 us -> 287 us (0.980)
  starting transfers between devices: 43.3 us -> 49.8 us
  between operations: 18.5 us -> 14.6 us
  waiting for transfers between devices: 140 us -> 137 us
    ppermute x5, waiting for transfers between devices: 41.3 us -> 34.6 us  [flipped(): lax.ppermute(array, axis, [(i, i ^ bit) for i in range(lax.axis_size(axis...]
    ppermute x5, starting transfers between devices: 5.73 us -> 11.3 us  [flipped(): lax.ppermute(array, axis, [(i, i ^ bit) for i in range(lax.axis_size(axis...]
    all_gather x1, waiting for transfers between devices: 7.99 us -> 11.8 us  [per_device(): gathered = lax.all_gather(gated, 'head', axis=1, tiled=True)]
    pallas_call x2, Pallas kernels: 32 us -> 28.6 us  [attention(): pl.pallas_call(partial(attention_kernel, parts), grid_spec=pltpu.Prefetch...]
  transfers between devices with their start and end apart: 25 -> 25, of which waited for: 10 -> 10; matrix products, arithmetic and copies ran while one was open for 7% -> 6% of each run, Pallas kernels for 15% -> 15%
where the time goes in v9:
time: 287 us; the launch traced here: 284 us
  waiting for transfers between devices  137 us (48%)
  Pallas kernels  57.1 us (20%)
  starting transfers between devices  49.8 us (17%)
  between operations  14.6 us (5%)
  other arithmetic  14.3 us (5%)
  local copies, waits for them, and re-layouts  11.4 us (4%)
    ppermute x12, waiting for transfers between devices, rotated(): lax.ppermute(array, axis, [(i, (i + step) % count) for i in range(count)])  80.5 us
    ppermute x5, waiting for transfers between devices, flipped(): lax.ppermute(array, axis, [(i, i ^ bit) for i in range(lax.axis_size(axis...  34.6 us
    pallas_call x2, Pallas kernels, attention(): pl.pallas_call(partial(attention_kernel, parts), grid_spec=pltpu.Prefetch...  28.6 us
    ppermute x6, starting transfers between devices, shifted(): return lax.ppermute(array, axis, pairs)  18.5 us
    ppermute x12, starting transfers between devices, rotated(): lax.ppermute(array, axis, [(i, (i + step) % count) for i in range(count)])  14.9 us
    pallas_call x1, Pallas kernels, weight_grad(): pl.pallas_call(partial(weight_kernel, scale), grid_spec=pltpu.PrefetchSca...  14 us
    pallas_call x1, Pallas kernels, project(): pl.pallas_call(project_kernel, grid=(blocks,), in_specs=[pl.BlockSpec((1,...  13.3 us
    all_gather x1, waiting for transfers between devices, per_device(): gathered = lax.all_gather(gated, 'head', axis=1, tiled=True)  11.8 us
  transfers between devices with their start and end apart: 25, of which 10 were waited for; matrix products, arithmetic and copies ran while one was open for 6% of the time, Pallas kernels for 15%

profile of v9, /device:TPU:11, one launch (start us, length us, event | category | flops | bytes accessed | tf_op | source)
XLA Modules:
  0.0 284.1 jit_solution(13066732049348495925)
XLA Ops:
  7.4 1.2 copy-done.16
  9.4 1.3 collective-permute-start.3
  10.7 1.2 gate_cotangent.1
  11.9 1.0 copy-done.12
  13.2 2.3 collective-permute-start.4
  15.5 2.8 collective-permute-done.3
  18.3 1.0 bitcast_dynamic-update-slice_fusion.2
  19.3 38.4 %collective-permute-done.4 = bf16[2,64,1280]{2,1,0:T(8,128)(2,1)S(1)} collective-permute-done((bf16[2,64,1280]{2,1,0:T(8,128)(2,1)S(1)}, bf16[2,64,1280]{2,1,0:T(8,128)(2,1)S(1)}, u32[]{:S(2)}, u32[]{:S(2)}) %collective-permute-start.4) | collective-permute-done | bytes 327712 | tf_op jit(solution)/shard_map/ppermute | solution.py:137
  58.3 1.2 collective-permute-start.7
  59.6 8.3 %collective-permute-done.6 = bf16[1,256,1280]{2,1,0:T(8,128)(2,1)S(1)} collective-permute-done((bf16[1,256,1280]{2,1,0:T(8,128)(2,1)S(1)}, bf16[1,256,1280]{2,1,0:T(8,128)(2,1)S(1)}, u32[]{:S(2)}, u32[]{:S(2)}) %collective-permute-start.6) | collective-permute-done | bytes 655392 | tf_op jit(solution)/shard_map/ppermute | solution.py:145
  68.1 1.3 collective-permute-start.9
  69.8 1.0 constant_dynamic-slice_fusion.1
  70.9 26.2 %collective-permute-done.9 = bf16[2,256,1280]{2,1,0:T(8,128)(2,1)S(1)} collective-permute-done((bf16[2,256,1280]{2,1,0:T(8,128)(2,1)S(1)}, bf16[2,256,1280]{2,1,0:T(8,128)(2,1)S(1)}, u32[]{:S(2)}, u32[]{:S(2)}) %collective-permute-start.9) | collective-permute-done | bytes 1310752 | tf_op jit(solution)/shard_map/ppermute | solution.py:145
  97.6 3.0 %pad_maximum_fusion.near_ref = bf16[4,512,1280]{2,1,0:T(8,128)(2,1)} fusion(bf16[1,512,1280]{2,1,0:T(8,128)(2,1)S(1)} %maximum_bitcast_fusion.3, bf16[1,512,1280]{2,1,0:T(8,128)(2,1)S(1)} %maximum_bitcast_fusion.2, bf16[1,512,1280]{2,1,0:T(8,128)(2,1)S(1)} %maximum_bitcast_fusion.1, bf16[1,512,1280]{2,1,0:T(8,128)(2,1)S(1)} %maximum_bitcast_fusion), kind=kLoop, calls=%fused_computation | loop fusion | flops 7864320 | bytes 10485760 | tf_op jit(solution)/shard_map/stack | solution.py:314
  100.6 8.1 %collective-permute-start.10 = (bf16[4,512,1280]{2,1,0:T(8,128)(2,1)}, bf16[4,512,1280]{2,1,0:T(8,128)(2,1)}, u32[]{:S(2)}, u32[]{:S(2)}) collective-permute-start(bf16[4,512,1280]{2,1,0:T(8,128)(2,1)} %pad_maximum_fusion.near_ref), channel_id=1, source_target_pairs={{0,8},{8,0},{16,24},{24,16},{1,9},{9,1},{17,25},{25,17},{2,10},{10... | collective-permute-start | bytes 15728648 | tf_op jit(solution)/shard_map/ppermute | solution.py:145
  108.7 0.9 pad_maximum_fusion.7
  109.6 2.0 pad_maximum_fusion.6
  111.6 0.9 pad_maximum_fusion.5
  112.4 11.8 %all-gather.2.cloned.1.call-done.g_ref = bf16[8,512,640]{2,1,0:T(8,128)(2,1)} async-done(((bf16[8,128,640]{2,1,0:T(8,128)(2,1)}), bf16[8,512,640]{2,1,0:T(8,128)(2,1)}) %all-gather.2.cloned.1.call-update) | async-done | bytes 5242896 | tf_op jit(solution)/shard_map/all_gather | solution.py:288
  124.2 5.1 %all-to-all-start = ((bf16[8,512,640]{2,1,0:T(8,128)(2,1)}), bf16[8,512,640]{2,1,0:T(8,128)(2,1)}, u32[]{:S(2)}, u32[]{:S(2)}) async-start(bf16[8,512,640]{2,1,0:T(8,128)(2,1)} %all-gather.2.cloned.1.call-done.g_ref), calls=%async_computation | async-start | bytes 10485760 | tf_op jit(solution)/shard_map/all_to_all | solution.py:330
  129.4 1.2 dynamic-slice_bitcast_fusion.3
  130.5 1.1 collective-permute-start.11
  131.6 4.2 %collective-permute-start.12 = (bf16[2,2,64,1280]{3,2,1,0:T(8,128)(2,1)}, bf16[2,2,64,1280]{3,2,1,0:T(8,128)(2,1)S(1)}, u32[]{:S(2)}, u32[]{:S(2)}) collective-permute-start(bf16[2,2,64,1280]{3,2,1,0:T(8,128)(2,1)} %pad_maximum_fusion.6), channel_id=1, source_target_pairs={{0,4},{2,6},{4,0},{6,2},{1,5},{3,7},{5,1},{7,3},{8,12},{10,14},{12... | collective-permute-start | bytes 1966088 | tf_op jit(solution)/shard_map/ppermute | solution.py:137
  135.8 1.0 dynamic-slice_bitcast_fusion.7
  136.8 2.5 copy-done.11
  139.3 13.3 %project_gated.1 = bf16[512,1280]{1,0:T(8,128)(2,1)S(1)} custom-call(bf16[8,512,640]{2,1,0:T(8,128)(2,1)S(1)} %copy-done.11, bf16[1280,5120]{1,0:T(8,128)(2,1)} %w_ref.1), custom_call_target="tpu_custom_call" | custom-call | flops 6710886400 | bytes 19660800 | tf_op jit(solution)/shard_map/project_gated/pallas_call | solution.py:245
  152.6 35.2 %collective-permute-done.12.refs_4_ = bf16[2,2,64,1280]{3,2,1,0:T(8,128)(2,1)S(1)} collective-permute-done((bf16[2,2,64,1280]{3,2,1,0:T(8,128)(2,1)}, bf16[2,2,64,1280]{3,2,1,0:T(8,128)(2,1)S(1)}, u32[]{:S(2)}, u32[]{:S(2)}) %collective-permute-start.12) | collective-permute-done | bytes 655392 | tf_op jit(solution)/shard_map/ppermute | solution.py:137
  187.8 4.1 %collective-permute-done.13.refs_5_ = bf16[2,2,64,1280]{3,2,1,0:T(8,128)(2,1)S(1)} collective-permute-done((bf16[2,2,64,1280]{3,2,1,0:T(8,128)(2,1)}, bf16[2,2,64,1280]{3,2,1,0:T(8,128)(2,1)S(1)}, u32[]{:S(2)}, u32[]{:S(2)}) %collective-permute-start.13) | collective-permute-done | bytes 655392 | tf_op jit(solution)/shard_map/ppermute | solution.py:137
  193.0 1.2 pad_maximum_fusion.3
  194.1 4.2 %collective-permute-start.17 = (bf16[2,4,64,1280]{3,2,1,0:T(8,128)(2,1)}, bf16[2,4,64,1280]{3,2,1,0:T(8,128)(2,1)}, u32[]{:S(2)}, u32[]{:S(2)}) collective-permute-start(bf16[2,4,64,1280]{3,2,1,0:T(8,128)(2,1)} %pad_maximum_fusion.3), channel_id=1, source_target_pairs={{0,8},{8,16},{16,24},{1,9},{9,17},{17,25},{2,10},{10,18},{18,26},{... | collective-permute-start | bytes 3932168 | tf_op jit(solution)/shard_map/ppermute | solution.py:132
  198.5 1.2 pad_maximum_fusion.4
  199.7 1.9 collective-permute-start.18
  202.2 1.4 collective-permute-start.16
  203.7 14.0 %weight_gradient.1 = f32[1280,640]{1,0:T(8,128)} custom-call(s32[2,4]{1,0:T(2,128)S(1)} %pad_add_fusion.table, bf16[4,512,1280]{2,1,0:T(8,128)(2,1)} %pad_maximum_fusion.near_ref, bf16[4,512,1280]{2,1,0:T(8,128)(2,1)} %collective-permute-done.10.far_ref, bf16[8,512,640]{2,1,0:T(8,128)(2,1)} %all-to-all-done.g_near.g_far, ...), custom_call_target="tpu_custom_call" | custom-call | flops 6710886400 | bytes 19005440 | tf_op jit(solution)/shard_map/weight_gradient/pallas_call | solution.py:163
  217.7 1.3 collective-permute-start
  219.0 3.0 %collective-permute-start.1 = (bf16[2,64,640]{2,1,0:T(8,128)(2,1)S(1)}, bf16[2,64,640]{2,1,0:T(8,128)(2,1)S(1)}, u32[]{:S(2)}, u32[]{:S(2)}) collective-permute-start(bf16[2,64,640]{2,1,0:T(8,128)(2,1)S(1)} %copy-done.18), channel_id=1, source_target_pairs={{0,4},{2,6},{4,0},{6,2},{1,5},{3,7},{5,1},{7,3},{8,12},{10,14},{12... | collective-permute-start | bytes 491528 | tf_op jit(solution)/shard_map/ppermute | solution.py:137
  222.1 14.3 %attention_backward.2 = (bf16[2,256,640]{2,1,0:T(8,128)(2,1)S(1)}, f32[2,256,640]{2,1,0:T(8,128)S(1)}, f32[2,256,640]{2,1,0:T(8,128)S(1)}, bf16[2,256,640]{2,1,0:T(8,128)(2,1)S(1)}, bf16[2,256,640]{2,1,0:T(8,128)(2,1)S(1)}) custom-call(s32[6]{0:T(128)S(1)} %pad_add_fusion.1.scal, bf16[1,2,64,5120]{3,2,1,0:T(8,128)(2,1)S(1)} %copy-done.4, ...), custom_call_target="tpu_custom_call" | custom-call | flops 2516582400 | bytes 10485760 | tf_op jit(solution)/shard_map/attention_backward/pallas_call | solution.py:100
  236.4 14.3 %attention_backward.3 = (bf16[2,256,640]{2,1,0:T(8,128)(2,1)S(1)}, f32[2,256,640]{2,1,0:T(8,128)S(1)}, f32[2,256,640]{2,1,0:T(8,128)S(1)}, bf16[2,256,640]{2,1,0:T(8,128)(2,1)S(1)}, bf16[2,256,640]{2,1,0:T(8,128)(2,1)S(1)}) custom-call(s32[6]{0:T(128)S(1)} %pad_add_fusion.1.scal, bf16[1,2,64,5120]{3,2,1,0:T(8,128)(2,1)S(1)} %copy-done.4, ...), custom_call_target="tpu_custom_call" | custom-call | flops 2516582400 | bytes 10485760 | tf_op jit(solution)/shard_map/attention_backward/pallas_call | solution.py:100
  250.8 4.9 %collective-permute-start.21 = (bf16[2,256,640]{2,1,0:T(8,128)(2,1)S(1)}, bf16[2,256,640]{2,1,0:T(8,128)(2,1)S(1)}, u32[]{:S(2)}, u32[]{:S(2)}) collective-permute-start(bf16[2,256,640]{2,1,0:T(8,128)(2,1)S(1)} %get-tuple-element.61), channel_id=1, source_target_pairs={{0,8},{8,16},{16,24},{1,9},{9,17},{17,25},{2,10},{10,18},{18,26},{... | collective-permute-start | bytes 1966088 | tf_op jit(solution)/shard_map/ppermute | solution.py:132
  255.7 1.9 collective-permute-start.22
  257.6 3.6 %collective-permute-start.19 = (bf16[2,256,640]{2,1,0:T(8,128)(2,1)S(1)}, bf16[2,256,640]{2,1,0:T(8,128)(2,1)S(1)}, u32[]{:S(2)}, u32[]{:S(2)}) collective-permute-start(bf16[2,256,640]{2,1,0:T(8,128)(2,1)S(1)} %get-tuple-element.58), channel_id=1, source_target_pairs={{0,8},{8,16},{16,24},{1,9},{9,17},{17,25},{2,10},{10,18},{18,26},{... | collective-permute-start | bytes 1966088 | tf_op jit(solution)/shard_map/ppermute | solution.py:132
  261.2 1.9 collective-permute-start.20
  263.2 1.2 maximum_bitcast_fusion.4
  264.3 3.2 %collective-permute-done.22 = bf16[2,256,640]{2,1,0:T(8,128)(2,1)S(1)} collective-permute-done((bf16[2,256,640]{2,1,0:T(8,128)(2,1)S(1)}, bf16[2,256,640]{2,1,0:T(8,128)(2,1)S(1)}, u32[]{:S(2)}, u32[]{:S(2)}) %collective-permute-start.22) | collective-permute-done | bytes 655392 | tf_op jit(solution)/shard_map/ppermute | solution.py:132
  267.8 2.4 collective-permute-done.19
  270.2 4.4 %collective-permute-done.20 = bf16[2,256,640]{2,1,0:T(8,128)(2,1)S(1)} collective-permute-done((bf16[2,256,640]{2,1,0:T(8,128)(2,1)S(1)}, bf16[2,256,640]{2,1,0:T(8,128)(2,1)S(1)}, u32[]{:S(2)}, u32[]{:S(2)}) %collective-permute-start.20) | collective-permute-done | bytes 655392 | tf_op jit(solution)/shard_map/ppermute | solution.py:132
  275.0 1.2 maximum_bitcast_fusion.5
  276.1 1.2 maximum_bitcast_fusion.6
  (92 shorter events, 5.4 us)
Async XLA Ops:
  7.2 117.1 %all-gather.2.cloned.1.call-start = ((), (), s32[]{:S(2)}) async-start(), calls=%async_computation.1 | async-start | bytes 6553600 | tf_op jit(solution)/shard_map/all_gather | solution.py:288
  7.3 1.3 copy-start.16
  8.6 2.1 copy-start.13
  8.6 2.1 copy-start.14
  8.6 2.1 copy-start.15
  9.4 8.9 %collective-permute-start.3 = (bf16[2,64,1280]{2,1,0:T(8,128)(2,1)}, bf16[2,64,1280]{2,1,0:T(8,128)(2,1)}, u32[]{:S(2)}, u32[]{:S(2)}) collective-permute-start(bf16[2,64,1280]{2,1,0:T(8,128)(2,1)} %get-tuple-element.103), channel_id=1, source_target_pairs={{0,2},{2,4},{4,6},{6,0},{1,3},{3,5},{5,7},{7,1},{8,10},{10,12},{12... | collective-permute-start | bytes 983048 | tf_op jit(solution)/shard_map/ppermute | solution.py:137
  11.9 1.1 copy-start.12
  13.0 44.8 %collective-permute-start.5 = (bf16[2,64,1280]{2,1,0:T(8,128)(2,1)S(1)}, bf16[2,64,1280]{2,1,0:T(8,128)(2,1)S(1)}, u32[]{:S(2)}, u32[]{:S(2)}) collective-permute-start(bf16[2,64,1280]{2,1,0:T(8,128)(2,1)S(1)} %get-tuple-element.102), channel_id=1, source_target_pairs={{0,6},{2,0},{4,2},{6,4},{1,7},{3,1},{5,3},{7,5},{8,14},{10,8},{12,... | collective-permute-start | bytes 983048 | tf_op jit(solution)/shard_map/ppermute | solution.py:137
  13.2 44.5 %collective-permute-start.4 = (bf16[2,64,1280]{2,1,0:T(8,128)(2,1)S(1)}, bf16[2,64,1280]{2,1,0:T(8,128)(2,1)S(1)}, u32[]{:S(2)}, u32[]{:S(2)}) collective-permute-start(bf16[2,64,1280]{2,1,0:T(8,128)(2,1)S(1)} %get-tuple-element.105), channel_id=1, source_target_pairs={{0,4},{2,6},{4,0},{6,2},{1,5},{3,7},{5,1},{7,3},{8,12},{10,14},{12... | collective-permute-start | bytes 983048 | tf_op jit(solution)/shard_map/ppermute | solution.py:137
  58.0 9.9 %collective-permute-start.6 = (bf16[1,256,1280]{2,1,0:T(8,128)(2,1)S(1)}, bf16[1,256,1280]{2,1,0:T(8,128)(2,1)S(1)}, u32[]{:S(2)}, u32[]{:S(2)}) collective-permute-start(bf16[1,256,1280]{2,1,0:T(8,128)(2,1)S(1)} %get-tuple-element.97), channel_id=1, source_target_pairs={{0,1},{1,0},{2,3},{3,2},{4,5},{5,4},{6,7},{7,6},{8,9},{9,8},{10,11... | collective-permute-start | bytes 1966088 | tf_op jit(solution)/shard_map/ppermute | solution.py:145
  58.3 11.0 %collective-permute-start.7 = (bf16[1,256,1280]{2,1,0:T(8,128)(2,1)S(1)}, bf16[1,256,1280]{2,1,0:T(8,128)(2,1)S(1)}, u32[]{:S(2)}, u32[]{:S(2)}) collective-permute-start(bf16[1,256,1280]{2,1,0:T(8,128)(2,1)S(1)} %get-tuple-element.96), channel_id=1, source_target_pairs={{0,16},{8,24},{16,0},{24,8},{1,17},{9,25},{17,1},{25,9},{2,18},{10... | collective-permute-start | bytes 1966088 | tf_op jit(solution)/shard_map/ppermute | solution.py:145
  68.0 1.8 copy-start
  68.1 1.8 copy-start.1
  68.1 29.1 %collective-permute-start.9 = (bf16[2,256,1280]{2,1,0:T(8,128)(2,1)S(1)}, bf16[2,256,1280]{2,1,0:T(8,128)(2,1)S(1)}, u32[]{:S(2)}, u32[]{:S(2)}) collective-permute-start(bf16[2,256,1280]{2,1,0:T(8,128)(2,1)S(1)} %pad_maximum_fusion.2), channel_id=1, source_target_pairs={{0,16},{8,24},{16,0},{24,8},{1,17},{9,25},{17,1},{25,9},{2,18},{10... | collective-permute-start | bytes 3932168 | tf_op jit(solution)/shard_map/ppermute | solution.py:145
  69.5 27.8 %collective-permute-start.8 = (bf16[2,256,1280]{2,1,0:T(8,128)(2,1)S(1)}, bf16[2,256,1280]{2,1,0:T(8,128)(2,1)S(1)}, u32[]{:S(2)}, u32[]{:S(2)}) collective-permute-start(bf16[2,256,1280]{2,1,0:T(8,128)(2,1)S(1)} %pad_maximum_fusion.1), channel_id=1, source_target_pairs={{0,1},{1,0},{2,3},{3,2},{4,5},{5,4},{6,7},{7,6},{8,9},{9,8},{10,11... | collective-permute-start | bytes 3932168 | tf_op jit(solution)/shard_map/ppermute | solution.py:145
  100.6 101.7 %collective-permute-start.10 = (bf16[4,512,1280]{2,1,0:T(8,128)(2,1)}, bf16[4,512,1280]{2,1,0:T(8,128)(2,1)}, u32[]{:S(2)}, u32[]{:S(2)}) collective-permute-start(bf16[4,512,1280]{2,1,0:T(8,128)(2,1)} %pad_maximum_fusion.near_ref), channel_id=1, source_target_pairs={{0,8},{8,0},{16,24},{24,16},{1,9},{9,1},{17,25},{25,17},{2,10},{10... | collective-permute-start | bytes 15728648 | tf_op jit(solution)/shard_map/ppermute | solution.py:145
  124.2 79.4 %all-to-all-start = ((bf16[8,512,640]{2,1,0:T(8,128)(2,1)}), bf16[8,512,640]{2,1,0:T(8,128)(2,1)}, u32[]{:S(2)}, u32[]{:S(2)}) async-start(bf16[8,512,640]{2,1,0:T(8,128)(2,1)} %all-gather.2.cloned.1.call-done.g_ref), calls=%async_computation | async-start | bytes 10485760 | tf_op jit(solution)/shard_map/all_to_all | solution.py:330
  129.4 6.4 %copy-start.3 = (bf16[1,2,64,5120]{3,2,1,0:T(8,128)(2,1)S(1)}, bf16[1,2,64,5120]{3,2,1,0:T(8,128)(2,1)}, u32[]{:S(2)}) copy-start(bf16[1,2,64,5120]{3,2,1,0:T(8,128)(2,1)} %refs_0_.3) | copy-start | bytes 3932164
  130.5 22.1 %collective-permute-start.11 = (bf16[2,2,64,1280]{3,2,1,0:T(8,128)(2,1)}, bf16[2,2,64,1280]{3,2,1,0:T(8,128)(2,1)S(1)}, u32[]{:S(2)}, u32[]{:S(2)}) collective-permute-start(bf16[2,2,64,1280]{3,2,1,0:T(8,128)(2,1)} %pad_maximum_fusion.5), channel_id=1, source_target_pairs={{0,2},{2,4},{4,6},{6,0},{1,3},{3,5},{5,7},{7,1},{8,10},{10,12},{12... | collective-permute-start | bytes 1966088 | tf_op jit(solution)/shard_map/ppermute | solution.py:137
  131.6 56.2 %collective-permute-start.12 = (bf16[2,2,64,1280]{3,2,1,0:T(8,128)(2,1)}, bf16[2,2,64,1280]{3,2,1,0:T(8,128)(2,1)S(1)}, u32[]{:S(2)}, u32[]{:S(2)}) collective-permute-start(bf16[2,2,64,1280]{3,2,1,0:T(8,128)(2,1)} %pad_maximum_fusion.6), channel_id=1, source_target_pairs={{0,4},{2,6},{4,0},{6,2},{1,5},{3,7},{5,1},{7,3},{8,12},{10,14},{12... | collective-permute-start | bytes 1966088 | tf_op jit(solution)/shard_map/ppermute | solution.py:137
  135.8 56.1 %collective-permute-start.13 = (bf16[2,2,64,1280]{3,2,1,0:T(8,128)(2,1)}, bf16[2,2,64,1280]{3,2,1,0:T(8,128)(2,1)S(1)}, u32[]{:S(2)}, u32[]{:S(2)}) collective-permute-start(bf16[2,2,64,1280]{3,2,1,0:T(8,128)(2,1)} %pad_maximum_fusion.7), channel_id=1, source_target_pairs={{0,6},{2,0},{4,2},{6,4},{1,7},{3,1},{5,3},{7,5},{8,14},{10,8},{12,... | collective-permute-start | bytes 1966088 | tf_op jit(solution)/shard_map/ppermute | solution.py:137
  136.8 2.5 copy-start.11
  152.6 39.4 %copy-start.9 = (bf16[512,1280]{1,0:T(8,128)(2,1)}, bf16[512,1280]{1,0:T(8,128)(2,1)S(1)}, u32[]{:S(2)}) copy-start(bf16[512,1280]{1,0:T(8,128)(2,1)S(1)} %project_gated.1) | copy-start | bytes 3932164
  187.8 4.2 %copy-start.5 = (bf16[2,2,64,1280]{3,2,1,0:T(8,128)(2,1)}, bf16[2,2,64,1280]{3,2,1,0:T(8,128)(2,1)S(1)}, u32[]{:S(2)}) copy-start(bf16[2,2,64,1280]{3,2,1,0:T(8,128)(2,1)S(1)} %collective-permute-done.12.refs_4_) | copy-start | bytes 1966084
  191.9 0.9 copy-start.7
  194.1 27.9 %collective-permute-start.17 = (bf16[2,4,64,1280]{3,2,1,0:T(8,128)(2,1)}, bf16[2,4,64,1280]{3,2,1,0:T(8,128)(2,1)}, u32[]{:S(2)}, u32[]{:S(2)}) collective-permute-start(bf16[2,4,64,1280]{3,2,1,0:T(8,128)(2,1)} %pad_maximum_fusion.3), channel_id=1, source_target_pairs={{0,8},{8,16},{16,24},{1,9},{9,17},{17,25},{2,10},{10,18},{18,26},{... | collective-permute-start | bytes 3932168 | tf_op jit(solution)/shard_map/ppermute | solution.py:132
  198.5 3.1 %copy-start.20 = (s32[8,2]{0,1:T(2,128)S(1)}, s32[8,2]{0,1:T(2,128)}, u32[]{:S(2)}) copy-start(s32[8,2]{0,1:T(2,128)} %param.17) | copy-start | bytes 196
  199.7 22.4 %collective-permute-start.18 = (bf16[2,4,64,1280]{3,2,1,0:T(8,128)(2,1)}, bf16[2,4,64,1280]{3,2,1,0:T(8,128)(2,1)}, u32[]{:S(2)}, u32[]{:S(2)}) collective-permute-start(bf16[2,4,64,1280]{3,2,1,0:T(8,128)(2,1)} %pad_maximum_fusion.4), channel_id=1, source_target_pairs={{8,0},{16,8},{24,16},{9,1},{17,9},{25,17},{10,2},{18,10},{26,18},{... | collective-permute-start | bytes 3932168 | tf_op jit(solution)/shard_map/ppermute | solution.py:132
  202.1 15.6 %collective-permute-start.14 = (bf16[2,64,640]{2,1,0:T(8,128)(2,1)}, bf16[2,64,640]{2,1,0:T(8,128)(2,1)S(1)}, u32[]{:S(2)}, u32[]{:S(2)}) collective-permute-start(bf16[2,64,640]{2,1,0:T(8,128)(2,1)} %get-tuple-element.47), channel_id=1, source_target_pairs={{0,2},{2,4},{4,6},{6,0},{1,3},{3,5},{5,7},{7,1},{8,10},{10,12},{12... | collective-permute-start | bytes 491528 | tf_op jit(solution)/shard_map/ppermute | solution.py:137
  202.2 16.9 %collective-permute-start.15 = (bf16[2,64,640]{2,1,0:T(8,128)(2,1)}, bf16[2,64,640]{2,1,0:T(8,128)(2,1)}, u32[]{:S(2)}, u32[]{:S(2)}) collective-permute-start(bf16[2,64,640]{2,1,0:T(8,128)(2,1)} %get-tuple-element.48), channel_id=1, source_target_pairs={{0,4},{2,6},{4,0},{6,2},{1,5},{3,7},{5,1},{7,3},{8,12},{10,14},{12... | collective-permute-start | bytes 491528 | tf_op jit(solution)/shard_map/ppermute | solution.py:137
  202.2 19.8 %collective-permute-start.16 = (bf16[2,64,640]{2,1,0:T(8,128)(2,1)}, bf16[2,64,640]{2,1,0:T(8,128)(2,1)}, u32[]{:S(2)}, u32[]{:S(2)}) collective-permute-start(bf16[2,64,640]{2,1,0:T(8,128)(2,1)} %get-tuple-element.49), channel_id=1, source_target_pairs={{0,6},{2,0},{4,2},{6,4},{1,7},{3,1},{5,3},{7,5},{8,14},{10,8},{12,... | collective-permute-start | bytes 491528 | tf_op jit(solution)/shard_map/ppermute | solution.py:137
  203.6 14.1 %copy-start.19 = (bf16[2,64,640]{2,1,0:T(8,128)(2,1)S(1)}, bf16[2,64,640]{2,1,0:T(8,128)(2,1)}, u32[]{:S(2)}) copy-start(bf16[2,64,640]{2,1,0:T(8,128)(2,1)} %get-tuple-element.36) | copy-start | bytes 491524
  203.6 15.4 %copy-start.18 = (bf16[2,64,640]{2,1,0:T(8,128)(2,1)S(1)}, bf16[2,64,640]{2,1,0:T(8,128)(2,1)}, u32[]{:S(2)}) copy-start(bf16[2,64,640]{2,1,0:T(8,128)(2,1)} %get-tuple-element.37) | copy-start | bytes 491524
  203.6 18.4 %copy-start.17 = (bf16[2,64,640]{2,1,0:T(8,128)(2,1)S(1)}, bf16[2,64,640]{2,1,0:T(8,128)(2,1)}, u32[]{:S(2)}) copy-start(bf16[2,64,640]{2,1,0:T(8,128)(2,1)} %get-tuple-element.38) | copy-start | bytes 491524
  203.6 18.4 %copy-start.2 = (bf16[1,2,64,5120]{3,2,1,0:T(8,128)(2,1)S(1)}, bf16[1,2,64,5120]{3,2,1,0:T(8,128)(2,1)}, u32[]{:S(2)}) copy-start(bf16[1,2,64,5120]{3,2,1,0:T(8,128)(2,1)} %refs_2_.3) | copy-start | bytes 3932164
  203.6 18.4 %copy-start.4 = (bf16[1,2,64,5120]{3,2,1,0:T(8,128)(2,1)S(1)}, bf16[1,2,64,5120]{3,2,1,0:T(8,128)(2,1)}, u32[]{:S(2)}) copy-start(bf16[1,2,64,5120]{3,2,1,0:T(8,128)(2,1)} %refs_0_.3) | copy-start | bytes 3932164
  203.7 18.4 %copy-start.6 = (bf16[2,2,64,1280]{3,2,1,0:T(8,128)(2,1)S(1)}, bf16[2,2,64,1280]{3,2,1,0:T(8,128)(2,1)}, u32[]{:S(2)}) copy-start(bf16[2,2,64,1280]{3,2,1,0:T(8,128)(2,1)} %copy-done.5) | copy-start | bytes 1966084
  203.7 18.4 %copy-start.8 = (bf16[2,2,64,1280]{3,2,1,0:T(8,128)(2,1)S(1)}, bf16[2,2,64,1280]{3,2,1,0:T(8,128)(2,1)}, u32[]{:S(2)}) copy-start(bf16[2,2,64,1280]{3,2,1,0:T(8,128)(2,1)} %copy-done.7) | copy-start | bytes 1966084
  203.7 18.4 %copy-start.10 = (bf16[512,1280]{1,0:T(8,128)(2,1)S(1)}, bf16[512,1280]{1,0:T(8,128)(2,1)}, u32[]{:S(2)}) copy-start(bf16[512,1280]{1,0:T(8,128)(2,1)} %copy-done.9) | copy-start | bytes 3932164
  217.7 18.7 %collective-permute-start = (bf16[2,64,640]{2,1,0:T(8,128)(2,1)S(1)}, bf16[2,64,640]{2,1,0:T(8,128)(2,1)S(1)}, u32[]{:S(2)}, u32[]{:S(2)}) collective-permute-start(bf16[2,64,640]{2,1,0:T(8,128)(2,1)S(1)} %copy-done.19), channel_id=1, source_target_pairs={{0,2},{2,4},{4,6},{6,0},{1,3},{3,5},{5,7},{7,1},{8,10},{10,12},{12... | collective-permute-start | bytes 491528 | tf_op jit(solution)/shard_map/ppermute | solution.py:137
  219.0 17.4 %collective-permute-start.1 = (bf16[2,64,640]{2,1,0:T(8,128)(2,1)S(1)}, bf16[2,64,640]{2,1,0:T(8,128)(2,1)S(1)}, u32[]{:S(2)}, u32[]{:S(2)}) collective-permute-start(bf16[2,64,640]{2,1,0:T(8,128)(2,1)S(1)} %copy-done.18), channel_id=1, source_target_pairs={{0,4},{2,6},{4,0},{6,2},{1,5},{3,7},{5,1},{7,3},{8,12},{10,14},{12... | collective-permute-start | bytes 491528 | tf_op jit(solution)/shard_map/ppermute | solution.py:137
  222.0 14.4 %collective-permute-start.2 = (bf16[2,64,640]{2,1,0:T(8,128)(2,1)S(1)}, bf16[2,64,640]{2,1,0:T(8,128)(2,1)S(1)}, u32[]{:S(2)}, u32[]{:S(2)}) collective-permute-start(bf16[2,64,640]{2,1,0:T(8,128)(2,1)S(1)} %copy-done.17), channel_id=1, source_target_pairs={{0,6},{2,0},{4,2},{6,4},{1,7},{3,1},{5,3},{7,5},{8,14},{10,8},{12,... | collective-permute-start | bytes 491528 | tf_op jit(solution)/shard_map/ppermute | solution.py:137
  250.8 13.6 %collective-permute-start.21 = (bf16[2,256,640]{2,1,0:T(8,128)(2,1)S(1)}, bf16[2,256,640]{2,1,0:T(8,128)(2,1)S(1)}, u32[]{:S(2)}, u32[]{:S(2)}) collective-permute-start(bf16[2,256,640]{2,1,0:T(8,128)(2,1)S(1)} %get-tuple-element.61), channel_id=1, source_target_pairs={{0,8},{8,16},{16,24},{1,9},{9,17},{17,25},{2,10},{10,18},{18,26},{... | collective-permute-start | bytes 1966088 | tf_op jit(solution)/shard_map/ppermute | solution.py:132
  255.7 11.9 %collective-permute-start.22 = (bf16[2,256,640]{2,1,0:T(8,128)(2,1)S(1)}, bf16[2,256,640]{2,1,0:T(8,128)(2,1)S(1)}, u32[]{:S(2)}, u32[]{:S(2)}) collective-permute-start(bf16[2,256,640]{2,1,0:T(8,128)(2,1)S(1)} %get-tuple-element.62), channel_id=1, source_target_pairs={{8,0},{16,8},{24,16},{9,1},{17,9},{25,17},{10,2},{18,10},{26,18},{... | collective-permute-start | bytes 1966088 | tf_op jit(solution)/shard_map/ppermute | solution.py:132
  257.6 12.6 %collective-permute-start.19 = (bf16[2,256,640]{2,1,0:T(8,128)(2,1)S(1)}, bf16[2,256,640]{2,1,0:T(8,128)(2,1)S(1)}, u32[]{:S(2)}, u32[]{:S(2)}) collective-permute-start(bf16[2,256,640]{2,1,0:T(8,128)(2,1)S(1)} %get-tuple-element.58), channel_id=1, source_target_pairs={{0,8},{8,16},{16,24},{1,9},{9,17},{17,25},{2,10},{10,18},{18,26},{... | collective-permute-start | bytes 1966088 | tf_op jit(solution)/shard_map/ppermute | solution.py:132
  261.2 13.3 %collective-permute-start.20 = (bf16[2,256,640]{2,1,0:T(8,128)(2,1)S(1)}, bf16[2,256,640]{2,1,0:T(8,128)(2,1)S(1)}, u32[]{:S(2)}, u32[]{:S(2)}) collective-permute-start(bf16[2,256,640]{2,1,0:T(8,128)(2,1)S(1)} %get-tuple-element.59), channel_id=1, source_target_pairs={{8,0},{16,8},{24,16},{9,1},{17,9},{25,17},{10,2},{18,10},{26,18},{... | collective-permute-start | bytes 1966088 | tf_op jit(solution)/shard_map/ppermute | solution.py:132
Sparse Core Ops, SparseCore 0:
  13.1 111.0 all-gather.1

commit v10 on v9

--- a/solution.py
+++ b/solution.py
@@ -40,7 +40,7 @@
         k_all[frames + 1, at] = next_ref[0, s]
         v_all[frames + 1, at] = next_ref[1, s]
     tokens = rows * parts
-    row = lax.broadcasted_iota(jnp.int32, (tokens, tokens), 0)
+    half = tokens // 2
     key_grads = [None] * (frames + 2)
     value_grads = [None] * (frames + 2)
 
@@ -58,7 +58,14 @@
         for w in range(3):
             s = dot(k_all[f + w], q, NT) * (inv_root * LOG2E)
             if w != 1:
-                s = jnp.where(row < scal[2 + 2 * f + w // 2], s, NEG)
+                limit = scal[2 + 2 * f + w // 2]
+                s = jnp.concatenate(
+                    [
+                        s[:half] + jnp.where(limit > 0, 0.0, NEG),
+                        s[half:] + jnp.where(limit > half, 0.0, NEG),
+                    ],
+                    axis=0,
+                )
             scores.append(s)
         top = jnp.max(jnp.maximum(jnp.maximum(scores[0], scores[1]), scores[2]), axis=0, keepdims=True)
         exps = [jnp.exp2(s - top) for s in scores]

time: 287 us -> 287 us (level)
  no operation moved by 1% of the time
where the time goes in v10:
time: 287 us; the launch traced here: 284 us
  waiting for transfers between devices  137 us (48%)
  Pallas kernels  57.1 us (20%)
  starting transfers between devices  49.8 us (17%)
  between operations  14.6 us (5%)
  other arithmetic  14.3 us (5%)
  local copies, waits for them, and re-layouts  11.4 us (4%)
    ppermute x12, waiting for transfers between devices, rotated(): lax.ppermute(array, axis, [(i, (i + step) % count) for i in range(count)])  80.5 us
    ppermute x5, waiting for transfers between devices, flipped(): lax.ppermute(array, axis, [(i, i ^ bit) for i in range(lax.axis_size(axis...  34.6 us
    pallas_call x2, Pallas kernels, attention(): pl.pallas_call(partial(attention_kernel, parts), grid_spec=pltpu.Prefetch...  28.5 us
    ppermute x6, starting transfers between devices, shifted(): return lax.ppermute(array, axis, pairs)  18.5 us
    ppermute x12, starting transfers between devices, rotated(): lax.ppermute(array, axis, [(i, (i + step) % count) for i in range(count)])  14.9 us
    pallas_call x1, Pallas kernels, weight_grad(): pl.pallas_call(partial(weight_kernel, scale), grid_spec=pltpu.PrefetchSca...  14 us
    pallas_call x1, Pallas kernels, project(): pl.pallas_call(project_kernel, grid=(blocks,), in_specs=[pl.BlockSpec((1,...  13.3 us
    all_gather x1, waiting for transfers between devices, per_device(): gathered = lax.all_gather(gated, 'head', axis=1, tiled=True)  11.8 us
  transfers between devices with their start and end apart: 25, of which 10 were waited for; matrix products, arithmetic and copies ran while one was open for 6% of the time, Pallas kernels for 15%

profile of v10, /device:TPU:11, one launch (start us, length us, event | category | flops | bytes accessed | tf_op | source)
XLA Modules:
  0.0 284.1 jit_solution(12596578073980441428)
XLA Ops:
  7.4 1.2 copy-done.16
  9.4 1.3 collective-permute-start.3
  10.7 1.2 gate_cotangent.1
  11.9 1.0 copy-done.12
  13.2 2.3 collective-permute-start.4
  15.5 2.8 collective-permute-done.3
  18.3 1.0 bitcast_dynamic-update-slice_fusion.2
  19.3 38.4 %collective-permute-done.4 = bf16[2,64,1280]{2,1,0:T(8,128)(2,1)S(1)} collective-permute-done((bf16[2,64,1280]{2,1,0:T(8,128)(2,1)S(1)}, bf16[2,64,1280]{2,1,0:T(8,128)(2,1)S(1)}, u32[]{:S(2)}, u32[]{:S(2)}) %collective-permute-start.4) | collective-permute-done | bytes 327712 | tf_op jit(solution)/shard_map/ppermute | solution.py:144
  58.3 1.2 collective-permute-start.7
  59.6 8.3 %collective-permute-done.6 = bf16[1,256,1280]{2,1,0:T(8,128)(2,1)S(1)} collective-permute-done((bf16[1,256,1280]{2,1,0:T(8,128)(2,1)S(1)}, bf16[1,256,1280]{2,1,0:T(8,128)(2,1)S(1)}, u32[]{:S(2)}, u32[]{:S(2)}) %collective-permute-start.6) | collective-permute-done | bytes 655392 | tf_op jit(solution)/shard_map/ppermute | solution.py:152
  68.1 1.3 collective-permute-start.9
  69.8 1.0 constant_dynamic-slice_fusion.1
  70.9 26.2 %collective-permute-done.9 = bf16[2,256,1280]{2,1,0:T(8,128)(2,1)S(1)} collective-permute-done((bf16[2,256,1280]{2,1,0:T(8,128)(2,1)S(1)}, bf16[2,256,1280]{2,1,0:T(8,128)(2,1)S(1)}, u32[]{:S(2)}, u32[]{:S(2)}) %collective-permute-start.9) | collective-permute-done | bytes 1310752 | tf_op jit(solution)/shard_map/ppermute | solution.py:152
  97.6 3.0 %pad_maximum_fusion.near_ref = bf16[4,512,1280]{2,1,0:T(8,128)(2,1)} fusion(bf16[1,512,1280]{2,1,0:T(8,128)(2,1)S(1)} %maximum_bitcast_fusion.3, bf16[1,512,1280]{2,1,0:T(8,128)(2,1)S(1)} %maximum_bitcast_fusion.2, bf16[1,512,1280]{2,1,0:T(8,128)(2,1)S(1)} %maximum_bitcast_fusion.1, bf16[1,512,1280]{2,1,0:T(8,128)(2,1)S(1)} %maximum_bitcast_fusion), kind=kLoop, calls=%fused_computation | loop fusion | flops 7864320 | bytes 10485760 | tf_op jit(solution)/shard_map/stack | solution.py:321
  100.6 8.1 %collective-permute-start.10 = (bf16[4,512,1280]{2,1,0:T(8,128)(2,1)}, bf16[4,512,1280]{2,1,0:T(8,128)(2,1)}, u32[]{:S(2)}, u32[]{:S(2)}) collective-permute-start(bf16[4,512,1280]{2,1,0:T(8,128)(2,1)} %pad_maximum_fusion.near_ref), channel_id=1, source_target_pairs={{0,8},{8,0},{16,24},{24,16},{1,9},{9,1},{17,25},{25,17},{2,10},{10... | collective-permute-start | bytes 15728648 | tf_op jit(solution)/shard_map/ppermute | solution.py:152
  108.7 0.9 pad_maximum_fusion.7
  109.6 2.0 pad_maximum_fusion.6
  111.6 0.9 pad_maximum_fusion.5
  112.4 11.8 %all-gather.2.cloned.1.call-done.g_ref = bf16[8,512,640]{2,1,0:T(8,128)(2,1)} async-done(((bf16[8,128,640]{2,1,0:T(8,128)(2,1)}), bf16[8,512,640]{2,1,0:T(8,128)(2,1)}) %all-gather.2.cloned.1.call-update) | async-done | bytes 5242896 | tf_op jit(solution)/shard_map/all_gather | solution.py:295
  124.2 5.1 %all-to-all-start = ((bf16[8,512,640]{2,1,0:T(8,128)(2,1)}), bf16[8,512,640]{2,1,0:T(8,128)(2,1)}, u32[]{:S(2)}, u32[]{:S(2)}) async-start(bf16[8,512,640]{2,1,0:T(8,128)(2,1)} %all-gather.2.cloned.1.call-done.g_ref), calls=%async_computation | async-start | bytes 10485760 | tf_op jit(solution)/shard_map/all_to_all | solution.py:337
  129.4 1.2 dynamic-slice_bitcast_fusion.3
  130.5 1.1 collective-permute-start.11
  131.6 4.2 %collective-permute-start.12 = (bf16[2,2,64,1280]{3,2,1,0:T(8,128)(2,1)}, bf16[2,2,64,1280]{3,2,1,0:T(8,128)(2,1)S(1)}, u32[]{:S(2)}, u32[]{:S(2)}) collective-permute-start(bf16[2,2,64,1280]{3,2,1,0:T(8,128)(2,1)} %pad_maximum_fusion.6), channel_id=1, source_target_pairs={{0,4},{2,6},{4,0},{6,2},{1,5},{3,7},{5,1},{7,3},{8,12},{10,14},{12... | collective-permute-start | bytes 1966088 | tf_op jit(solution)/shard_map/ppermute | solution.py:144
  135.8 1.0 dynamic-slice_bitcast_fusion.7
  136.8 2.5 copy-done.11
  139.3 13.3 %project_gated.1 = bf16[512,1280]{1,0:T(8,128)(2,1)S(1)} custom-call(bf16[8,512,640]{2,1,0:T(8,128)(2,1)S(1)} %copy-done.11, bf16[1280,5120]{1,0:T(8,128)(2,1)} %w_ref.1), custom_call_target="tpu_custom_call" | custom-call | flops 6710886400 | bytes 19660800 | tf_op jit(solution)/shard_map/project_gated/pallas_call | solution.py:252
  152.6 35.2 %collective-permute-done.12.refs_4_ = bf16[2,2,64,1280]{3,2,1,0:T(8,128)(2,1)S(1)} collective-permute-done((bf16[2,2,64,1280]{3,2,1,0:T(8,128)(2,1)}, bf16[2,2,64,1280]{3,2,1,0:T(8,128)(2,1)S(1)}, u32[]{:S(2)}, u32[]{:S(2)}) %collective-permute-start.12) | collective-permute-done | bytes 655392 | tf_op jit(solution)/shard_map/ppermute | solution.py:144
  187.8 4.1 %collective-permute-done.13.refs_5_ = bf16[2,2,64,1280]{3,2,1,0:T(8,128)(2,1)S(1)} collective-permute-done((bf16[2,2,64,1280]{3,2,1,0:T(8,128)(2,1)}, bf16[2,2,64,1280]{3,2,1,0:T(8,128)(2,1)S(1)}, u32[]{:S(2)}, u32[]{:S(2)}) %collective-permute-start.13) | collective-permute-done | bytes 655392 | tf_op jit(solution)/shard_map/ppermute | solution.py:144
  193.0 1.2 pad_maximum_fusion.3
  194.1 4.2 %collective-permute-start.17 = (bf16[2,4,64,1280]{3,2,1,0:T(8,128)(2,1)}, bf16[2,4,64,1280]{3,2,1,0:T(8,128)(2,1)}, u32[]{:S(2)}, u32[]{:S(2)}) collective-permute-start(bf16[2,4,64,1280]{3,2,1,0:T(8,128)(2,1)} %pad_maximum_fusion.3), channel_id=1, source_target_pairs={{0,8},{8,16},{16,24},{1,9},{9,17},{17,25},{2,10},{10,18},{18,26},{... | collective-permute-start | bytes 3932168 | tf_op jit(solution)/shard_map/ppermute | solution.py:139
  198.5 1.2 pad_maximum_fusion.4
  199.7 1.9 collective-permute-start.18
  202.2 1.4 collective-permute-start.16
  203.7 14.0 %weight_gradient.1 = f32[1280,640]{1,0:T(8,128)} custom-call(s32[2,4]{1,0:T(2,128)S(1)} %pad_add_fusion.table, bf16[4,512,1280]{2,1,0:T(8,128)(2,1)} %pad_maximum_fusion.near_ref, bf16[4,512,1280]{2,1,0:T(8,128)(2,1)} %collective-permute-done.10.far_ref, bf16[8,512,640]{2,1,0:T(8,128)(2,1)} %all-to-all-done.g_near.g_far, ...), custom_call_target="tpu_custom_call" | custom-call | flops 6710886400 | bytes 19005440 | tf_op jit(solution)/shard_map/weight_gradient/pallas_call | solution.py:170
  217.7 1.3 collective-permute-start
  219.0 3.0 %collective-permute-start.1 = (bf16[2,64,640]{2,1,0:T(8,128)(2,1)S(1)}, bf16[2,64,640]{2,1,0:T(8,128)(2,1)S(1)}, u32[]{:S(2)}, u32[]{:S(2)}) collective-permute-start(bf16[2,64,640]{2,1,0:T(8,128)(2,1)S(1)} %copy-done.18), channel_id=1, source_target_pairs={{0,4},{2,6},{4,0},{6,2},{1,5},{3,7},{5,1},{7,3},{8,12},{10,14},{12... | collective-permute-start | bytes 491528 | tf_op jit(solution)/shard_map/ppermute | solution.py:144
  222.1 14.2 %attention_backward.2 = (bf16[2,256,640]{2,1,0:T(8,128)(2,1)S(1)}, f32[2,256,640]{2,1,0:T(8,128)S(1)}, f32[2,256,640]{2,1,0:T(8,128)S(1)}, bf16[2,256,640]{2,1,0:T(8,128)(2,1)S(1)}, bf16[2,256,640]{2,1,0:T(8,128)(2,1)S(1)}) custom-call(s32[6]{0:T(128)S(1)} %pad_add_fusion.1.scal, bf16[1,2,64,5120]{3,2,1,0:T(8,128)(2,1)S(1)} %copy-done.4, ...), custom_call_target="tpu_custom_call" | custom-call | flops 2516582400 | bytes 10485760 | tf_op jit(solution)/shard_map/attention_backward/pallas_call | solution.py:107
  236.4 14.3 %attention_backward.3 = (bf16[2,256,640]{2,1,0:T(8,128)(2,1)S(1)}, f32[2,256,640]{2,1,0:T(8,128)S(1)}, f32[2,256,640]{2,1,0:T(8,128)S(1)}, bf16[2,256,640]{2,1,0:T(8,128)(2,1)S(1)}, bf16[2,256,640]{2,1,0:T(8,128)(2,1)S(1)}) custom-call(s32[6]{0:T(128)S(1)} %pad_add_fusion.1.scal, bf16[1,2,64,5120]{3,2,1,0:T(8,128)(2,1)S(1)} %copy-done.4, ...), custom_call_target="tpu_custom_call" | custom-call | flops 2516582400 | bytes 10485760 | tf_op jit(solution)/shard_map/attention_backward/pallas_call | solution.py:107
  250.7 4.9 %collective-permute-start.21 = (bf16[2,256,640]{2,1,0:T(8,128)(2,1)S(1)}, bf16[2,256,640]{2,1,0:T(8,128)(2,1)S(1)}, u32[]{:S(2)}, u32[]{:S(2)}) collective-permute-start(bf16[2,256,640]{2,1,0:T(8,128)(2,1)S(1)} %get-tuple-element.61), channel_id=1, source_target_pairs={{0,8},{8,16},{16,24},{1,9},{9,17},{17,25},{2,10},{10,18},{18,26},{... | collective-permute-start | bytes 1966088 | tf_op jit(solution)/shard_map/ppermute | solution.py:139
  255.6 1.9 collective-permute-start.22
  257.5 3.6 %collective-permute-start.19 = (bf16[2,256,640]{2,1,0:T(8,128)(2,1)S(1)}, bf16[2,256,640]{2,1,0:T(8,128)(2,1)S(1)}, u32[]{:S(2)}, u32[]{:S(2)}) collective-permute-start(bf16[2,256,640]{2,1,0:T(8,128)(2,1)S(1)} %get-tuple-element.58), channel_id=1, source_target_pairs={{0,8},{8,16},{16,24},{1,9},{9,17},{17,25},{2,10},{10,18},{18,26},{... | collective-permute-start | bytes 1966088 | tf_op jit(solution)/shard_map/ppermute | solution.py:139
  261.2 1.9 collective-permute-start.20
  263.1 1.2 maximum_bitcast_fusion.4
  264.3 3.2 %collective-permute-done.22 = bf16[2,256,640]{2,1,0:T(8,128)(2,1)S(1)} collective-permute-done((bf16[2,256,640]{2,1,0:T(8,128)(2,1)S(1)}, bf16[2,256,640]{2,1,0:T(8,128)(2,1)S(1)}, u32[]{:S(2)}, u32[]{:S(2)}) %collective-permute-start.22) | collective-permute-done | bytes 655392 | tf_op jit(solution)/shard_map/ppermute | solution.py:139
  267.8 2.4 collective-permute-done.19
  270.1 4.4 %collective-permute-done.20 = bf16[2,256,640]{2,1,0:T(8,128)(2,1)S(1)} collective-permute-done((bf16[2,256,640]{2,1,0:T(8,128)(2,1)S(1)}, bf16[2,256,640]{2,1,0:T(8,128)(2,1)S(1)}, u32[]{:S(2)}, u32[]{:S(2)}) %collective-permute-start.20) | collective-permute-done | bytes 655392 | tf_op jit(solution)/shard_map/ppermute | solution.py:139
  274.9 1.2 maximum_bitcast_fusion.5
  276.1 1.2 maximum_bitcast_fusion.6
  (92 shorter events, 5.4 us)
Async XLA Ops:
  7.2 117.1 %all-gather.2.cloned.1.call-start = ((), (), s32[]{:S(2)}) async-start(), calls=%async_computation.1 | async-start | bytes 6553600 | tf_op jit(solution)/shard_map/all_gather | solution.py:295
  7.3 1.3 copy-start.16
  8.6 2.1 copy-start.13
  8.6 2.1 copy-start.14
  8.6 2.1 copy-start.15
  9.4 8.9 %collective-permute-start.3 = (bf16[2,64,1280]{2,1,0:T(8,128)(2,1)}, bf16[2,64,1280]{2,1,0:T(8,128)(2,1)}, u32[]{:S(2)}, u32[]{:S(2)}) collective-permute-start(bf16[2,64,1280]{2,1,0:T(8,128)(2,1)} %get-tuple-element.103), channel_id=1, source_target_pairs={{0,2},{2,4},{4,6},{6,0},{1,3},{3,5},{5,7},{7,1},{8,10},{10,12},{12... | collective-permute-start | bytes 983048 | tf_op jit(solution)/shard_map/ppermute | solution.py:144
  11.9 1.1 copy-start.12
  13.0 44.8 %collective-permute-start.5 = (bf16[2,64,1280]{2,1,0:T(8,128)(2,1)S(1)}, bf16[2,64,1280]{2,1,0:T(8,128)(2,1)S(1)}, u32[]{:S(2)}, u32[]{:S(2)}) collective-permute-start(bf16[2,64,1280]{2,1,0:T(8,128)(2,1)S(1)} %get-tuple-element.102), channel_id=1, source_target_pairs={{0,6},{2,0},{4,2},{6,4},{1,7},{3,1},{5,3},{7,5},{8,14},{10,8},{12,... | collective-permute-start | bytes 983048 | tf_op jit(solution)/shard_map/ppermute | solution.py:144
  13.2 44.5 %collective-permute-start.4 = (bf16[2,64,1280]{2,1,0:T(8,128)(2,1)S(1)}, bf16[2,64,1280]{2,1,0:T(8,128)(2,1)S(1)}, u32[]{:S(2)}, u32[]{:S(2)}) collective-permute-start(bf16[2,64,1280]{2,1,0:T(8,128)(2,1)S(1)} %get-tuple-element.105), channel_id=1, source_target_pairs={{0,4},{2,6},{4,0},{6,2},{1,5},{3,7},{5,1},{7,3},{8,12},{10,14},{12... | collective-permute-start | bytes 983048 | tf_op jit(solution)/shard_map/ppermute | solution.py:144
  58.0 9.9 %collective-permute-start.6 = (bf16[1,256,1280]{2,1,0:T(8,128)(2,1)S(1)}, bf16[1,256,1280]{2,1,0:T(8,128)(2,1)S(1)}, u32[]{:S(2)}, u32[]{:S(2)}) collective-permute-start(bf16[1,256,1280]{2,1,0:T(8,128)(2,1)S(1)} %get-tuple-element.97), channel_id=1, source_target_pairs={{0,1},{1,0},{2,3},{3,2},{4,5},{5,4},{6,7},{7,6},{8,9},{9,8},{10,11... | collective-permute-start | bytes 1966088 | tf_op jit(solution)/shard_map/ppermute | solution.py:152
  58.3 11.0 %collective-permute-start.7 = (bf16[1,256,1280]{2,1,0:T(8,128)(2,1)S(1)}, bf16[1,256,1280]{2,1,0:T(8,128)(2,1)S(1)}, u32[]{:S(2)}, u32[]{:S(2)}) collective-permute-start(bf16[1,256,1280]{2,1,0:T(8,128)(2,1)S(1)} %get-tuple-element.96), channel_id=1, source_target_pairs={{0,16},{8,24},{16,0},{24,8},{1,17},{9,25},{17,1},{25,9},{2,18},{10... | collective-permute-start | bytes 1966088 | tf_op jit(solution)/shard_map/ppermute | solution.py:152
  68.0 1.8 copy-start
  68.1 1.8 copy-start.1
  68.1 29.1 %collective-permute-start.9 = (bf16[2,256,1280]{2,1,0:T(8,128)(2,1)S(1)}, bf16[2,256,1280]{2,1,0:T(8,128)(2,1)S(1)}, u32[]{:S(2)}, u32[]{:S(2)}) collective-permute-start(bf16[2,256,1280]{2,1,0:T(8,128)(2,1)S(1)} %pad_maximum_fusion.2), channel_id=1, source_target_pairs={{0,16},{8,24},{16,0},{24,8},{1,17},{9,25},{17,1},{25,9},{2,18},{10... | collective-permute-start | bytes 3932168 | tf_op jit(solution)/shard_map/ppermute | solution.py:152
  69.5 27.8 %collective-permute-start.8 = (bf16[2,256,1280]{2,1,0:T(8,128)(2,1)S(1)}, bf16[2,256,1280]{2,1,0:T(8,128)(2,1)S(1)}, u32[]{:S(2)}, u32[]{:S(2)}) collective-permute-start(bf16[2,256,1280]{2,1,0:T(8,128)(2,1)S(1)} %pad_maximum_fusion.1), channel_id=1, source_target_pairs={{0,1},{1,0},{2,3},{3,2},{4,5},{5,4},{6,7},{7,6},{8,9},{9,8},{10,11... | collective-permute-start | bytes 3932168 | tf_op jit(solution)/shard_map/ppermute | solution.py:152
  100.6 101.7 %collective-permute-start.10 = (bf16[4,512,1280]{2,1,0:T(8,128)(2,1)}, bf16[4,512,1280]{2,1,0:T(8,128)(2,1)}, u32[]{:S(2)}, u32[]{:S(2)}) collective-permute-start(bf16[4,512,1280]{2,1,0:T(8,128)(2,1)} %pad_maximum_fusion.near_ref), channel_id=1, source_target_pairs={{0,8},{8,0},{16,24},{24,16},{1,9},{9,1},{17,25},{25,17},{2,10},{10... | collective-permute-start | bytes 15728648 | tf_op jit(solution)/shard_map/ppermute | solution.py:152
  124.2 79.4 %all-to-all-start = ((bf16[8,512,640]{2,1,0:T(8,128)(2,1)}), bf16[8,512,640]{2,1,0:T(8,128)(2,1)}, u32[]{:S(2)}, u32[]{:S(2)}) async-start(bf16[8,512,640]{2,1,0:T(8,128)(2,1)} %all-gather.2.cloned.1.call-done.g_ref), calls=%async_computation | async-start | bytes 10485760 | tf_op jit(solution)/shard_map/all_to_all | solution.py:337
  129.4 6.4 %copy-start.3 = (bf16[1,2,64,5120]{3,2,1,0:T(8,128)(2,1)S(1)}, bf16[1,2,64,5120]{3,2,1,0:T(8,128)(2,1)}, u32[]{:S(2)}) copy-start(bf16[1,2,64,5120]{3,2,1,0:T(8,128)(2,1)} %refs_0_.3) | copy-start | bytes 3932164
  130.5 22.1 %collective-permute-start.11 = (bf16[2,2,64,1280]{3,2,1,0:T(8,128)(2,1)}, bf16[2,2,64,1280]{3,2,1,0:T(8,128)(2,1)S(1)}, u32[]{:S(2)}, u32[]{:S(2)}) collective-permute-start(bf16[2,2,64,1280]{3,2,1,0:T(8,128)(2,1)} %pad_maximum_fusion.5), channel_id=1, source_target_pairs={{0,2},{2,4},{4,6},{6,0},{1,3},{3,5},{5,7},{7,1},{8,10},{10,12},{12... | collective-permute-start | bytes 1966088 | tf_op jit(solution)/shard_map/ppermute | solution.py:144
  131.6 56.2 %collective-permute-start.12 = (bf16[2,2,64,1280]{3,2,1,0:T(8,128)(2,1)}, bf16[2,2,64,1280]{3,2,1,0:T(8,128)(2,1)S(1)}, u32[]{:S(2)}, u32[]{:S(2)}) collective-permute-start(bf16[2,2,64,1280]{3,2,1,0:T(8,128)(2,1)} %pad_maximum_fusion.6), channel_id=1, source_target_pairs={{0,4},{2,6},{4,0},{6,2},{1,5},{3,7},{5,1},{7,3},{8,12},{10,14},{12... | collective-permute-start | bytes 1966088 | tf_op jit(solution)/shard_map/ppermute | solution.py:144
  135.8 56.1 %collective-permute-start.13 = (bf16[2,2,64,1280]{3,2,1,0:T(8,128)(2,1)}, bf16[2,2,64,1280]{3,2,1,0:T(8,128)(2,1)S(1)}, u32[]{:S(2)}, u32[]{:S(2)}) collective-permute-start(bf16[2,2,64,1280]{3,2,1,0:T(8,128)(2,1)} %pad_maximum_fusion.7), channel_id=1, source_target_pairs={{0,6},{2,0},{4,2},{6,4},{1,7},{3,1},{5,3},{7,5},{8,14},{10,8},{12,... | collective-permute-start | bytes 1966088 | tf_op jit(solution)/shard_map/ppermute | solution.py:144
  136.8 2.5 copy-start.11
  152.6 39.4 %copy-start.9 = (bf16[512,1280]{1,0:T(8,128)(2,1)}, bf16[512,1280]{1,0:T(8,128)(2,1)S(1)}, u32[]{:S(2)}) copy-start(bf16[512,1280]{1,0:T(8,128)(2,1)S(1)} %project_gated.1) | copy-start | bytes 3932164
  187.8 4.2 %copy-start.5 = (bf16[2,2,64,1280]{3,2,1,0:T(8,128)(2,1)}, bf16[2,2,64,1280]{3,2,1,0:T(8,128)(2,1)S(1)}, u32[]{:S(2)}) copy-start(bf16[2,2,64,1280]{3,2,1,0:T(8,128)(2,1)S(1)} %collective-permute-done.12.refs_4_) | copy-start | bytes 1966084
  191.9 0.9 copy-start.7
  194.1 27.9 %collective-permute-start.17 = (bf16[2,4,64,1280]{3,2,1,0:T(8,128)(2,1)}, bf16[2,4,64,1280]{3,2,1,0:T(8,128)(2,1)}, u32[]{:S(2)}, u32[]{:S(2)}) collective-permute-start(bf16[2,4,64,1280]{3,2,1,0:T(8,128)(2,1)} %pad_maximum_fusion.3), channel_id=1, source_target_pairs={{0,8},{8,16},{16,24},{1,9},{9,17},{17,25},{2,10},{10,18},{18,26},{... | collective-permute-start | bytes 3932168 | tf_op jit(solution)/shard_map/ppermute | solution.py:139
  198.5 3.1 %copy-start.20 = (s32[8,2]{0,1:T(2,128)S(1)}, s32[8,2]{0,1:T(2,128)}, u32[]{:S(2)}) copy-start(s32[8,2]{0,1:T(2,128)} %param.17) | copy-start | bytes 196
  199.7 22.4 %collective-permute-start.18 = (bf16[2,4,64,1280]{3,2,1,0:T(8,128)(2,1)}, bf16[2,4,64,1280]{3,2,1,0:T(8,128)(2,1)}, u32[]{:S(2)}, u32[]{:S(2)}) collective-permute-start(bf16[2,4,64,1280]{3,2,1,0:T(8,128)(2,1)} %pad_maximum_fusion.4), channel_id=1, source_target_pairs={{8,0},{16,8},{24,16},{9,1},{17,9},{25,17},{10,2},{18,10},{26,18},{... | collective-permute-start | bytes 3932168 | tf_op jit(solution)/shard_map/ppermute | solution.py:139
  202.1 15.6 %collective-permute-start.14 = (bf16[2,64,640]{2,1,0:T(8,128)(2,1)}, bf16[2,64,640]{2,1,0:T(8,128)(2,1)S(1)}, u32[]{:S(2)}, u32[]{:S(2)}) collective-permute-start(bf16[2,64,640]{2,1,0:T(8,128)(2,1)} %get-tuple-element.47), channel_id=1, source_target_pairs={{0,2},{2,4},{4,6},{6,0},{1,3},{3,5},{5,7},{7,1},{8,10},{10,12},{12... | collective-permute-start | bytes 491528 | tf_op jit(solution)/shard_map/ppermute | solution.py:144
  202.2 16.9 %collective-permute-start.15 = (bf16[2,64,640]{2,1,0:T(8,128)(2,1)}, bf16[2,64,640]{2,1,0:T(8,128)(2,1)}, u32[]{:S(2)}, u32[]{:S(2)}) collective-permute-start(bf16[2,64,640]{2,1,0:T(8,128)(2,1)} %get-tuple-element.48), channel_id=1, source_target_pairs={{0,4},{2,6},{4,0},{6,2},{1,5},{3,7},{5,1},{7,3},{8,12},{10,14},{12... | collective-permute-start | bytes 491528 | tf_op jit(solution)/shard_map/ppermute | solution.py:144
  202.2 19.8 %collective-permute-start.16 = (bf16[2,64,640]{2,1,0:T(8,128)(2,1)}, bf16[2,64,640]{2,1,0:T(8,128)(2,1)}, u32[]{:S(2)}, u32[]{:S(2)}) collective-permute-start(bf16[2,64,640]{2,1,0:T(8,128)(2,1)} %get-tuple-element.49), channel_id=1, source_target_pairs={{0,6},{2,0},{4,2},{6,4},{1,7},{3,1},{5,3},{7,5},{8,14},{10,8},{12,... | collective-permute-start | bytes 491528 | tf_op jit(solution)/shard_map/ppermute | solution.py:144
  203.6 14.1 %copy-start.19 = (bf16[2,64,640]{2,1,0:T(8,128)(2,1)S(1)}, bf16[2,64,640]{2,1,0:T(8,128)(2,1)}, u32[]{:S(2)}) copy-start(bf16[2,64,640]{2,1,0:T(8,128)(2,1)} %get-tuple-element.36) | copy-start | bytes 491524
  203.6 15.4 %copy-start.18 = (bf16[2,64,640]{2,1,0:T(8,128)(2,1)S(1)}, bf16[2,64,640]{2,1,0:T(8,128)(2,1)}, u32[]{:S(2)}) copy-start(bf16[2,64,640]{2,1,0:T(8,128)(2,1)} %get-tuple-element.37) | copy-start | bytes 491524
  203.6 18.4 %copy-start.17 = (bf16[2,64,640]{2,1,0:T(8,128)(2,1)S(1)}, bf16[2,64,640]{2,1,0:T(8,128)(2,1)}, u32[]{:S(2)}) copy-start(bf16[2,64,640]{2,1,0:T(8,128)(2,1)} %get-tuple-element.38) | copy-start | bytes 491524
  203.6 18.4 %copy-start.2 = (bf16[1,2,64,5120]{3,2,1,0:T(8,128)(2,1)S(1)}, bf16[1,2,64,5120]{3,2,1,0:T(8,128)(2,1)}, u32[]{:S(2)}) copy-start(bf16[1,2,64,5120]{3,2,1,0:T(8,128)(2,1)} %refs_2_.3) | copy-start | bytes 3932164
  203.6 18.4 %copy-start.4 = (bf16[1,2,64,5120]{3,2,1,0:T(8,128)(2,1)S(1)}, bf16[1,2,64,5120]{3,2,1,0:T(8,128)(2,1)}, u32[]{:S(2)}) copy-start(bf16[1,2,64,5120]{3,2,1,0:T(8,128)(2,1)} %refs_0_.3) | copy-start | bytes 3932164
  203.7 18.4 %copy-start.6 = (bf16[2,2,64,1280]{3,2,1,0:T(8,128)(2,1)S(1)}, bf16[2,2,64,1280]{3,2,1,0:T(8,128)(2,1)}, u32[]{:S(2)}) copy-start(bf16[2,2,64,1280]{3,2,1,0:T(8,128)(2,1)} %copy-done.5) | copy-start | bytes 1966084
  203.7 18.4 %copy-start.8 = (bf16[2,2,64,1280]{3,2,1,0:T(8,128)(2,1)S(1)}, bf16[2,2,64,1280]{3,2,1,0:T(8,128)(2,1)}, u32[]{:S(2)}) copy-start(bf16[2,2,64,1280]{3,2,1,0:T(8,128)(2,1)} %copy-done.7) | copy-start | bytes 1966084
  203.7 18.4 %copy-start.10 = (bf16[512,1280]{1,0:T(8,128)(2,1)S(1)}, bf16[512,1280]{1,0:T(8,128)(2,1)}, u32[]{:S(2)}) copy-start(bf16[512,1280]{1,0:T(8,128)(2,1)} %copy-done.9) | copy-start | bytes 3932164
  217.7 18.6 %collective-permute-start = (bf16[2,64,640]{2,1,0:T(8,128)(2,1)S(1)}, bf16[2,64,640]{2,1,0:T(8,128)(2,1)S(1)}, u32[]{:S(2)}, u32[]{:S(2)}) collective-permute-start(bf16[2,64,640]{2,1,0:T(8,128)(2,1)S(1)} %copy-done.19), channel_id=1, source_target_pairs={{0,2},{2,4},{4,6},{6,0},{1,3},{3,5},{5,7},{7,1},{8,10},{10,12},{12... | collective-permute-start | bytes 491528 | tf_op jit(solution)/shard_map/ppermute | solution.py:144
  219.0 17.4 %collective-permute-start.1 = (bf16[2,64,640]{2,1,0:T(8,128)(2,1)S(1)}, bf16[2,64,640]{2,1,0:T(8,128)(2,1)S(1)}, u32[]{:S(2)}, u32[]{:S(2)}) collective-permute-start(bf16[2,64,640]{2,1,0:T(8,128)(2,1)S(1)} %copy-done.18), channel_id=1, source_target_pairs={{0,4},{2,6},{4,0},{6,2},{1,5},{3,7},{5,1},{7,3},{8,12},{10,14},{12... | collective-permute-start | bytes 491528 | tf_op jit(solution)/shard_map/ppermute | solution.py:144
  222.0 14.3 %collective-permute-start.2 = (bf16[2,64,640]{2,1,0:T(8,128)(2,1)S(1)}, bf16[2,64,640]{2,1,0:T(8,128)(2,1)S(1)}, u32[]{:S(2)}, u32[]{:S(2)}) collective-permute-start(bf16[2,64,640]{2,1,0:T(8,128)(2,1)S(1)} %copy-done.17), channel_id=1, source_target_pairs={{0,6},{2,0},{4,2},{6,4},{1,7},{3,1},{5,3},{7,5},{8,14},{10,8},{12,... | collective-permute-start | bytes 491528 | tf_op jit(solution)/shard_map/ppermute | solution.py:144
  250.7 13.6 %collective-permute-start.21 = (bf16[2,256,640]{2,1,0:T(8,128)(2,1)S(1)}, bf16[2,256,640]{2,1,0:T(8,128)(2,1)S(1)}, u32[]{:S(2)}, u32[]{:S(2)}) collective-permute-start(bf16[2,256,640]{2,1,0:T(8,128)(2,1)S(1)} %get-tuple-element.61), channel_id=1, source_target_pairs={{0,8},{8,16},{16,24},{1,9},{9,17},{17,25},{2,10},{10,18},{18,26},{... | collective-permute-start | bytes 1966088 | tf_op jit(solution)/shard_map/ppermute | solution.py:139
  255.6 11.9 %collective-permute-start.22 = (bf16[2,256,640]{2,1,0:T(8,128)(2,1)S(1)}, bf16[2,256,640]{2,1,0:T(8,128)(2,1)S(1)}, u32[]{:S(2)}, u32[]{:S(2)}) collective-permute-start(bf16[2,256,640]{2,1,0:T(8,128)(2,1)S(1)} %get-tuple-element.62), channel_id=1, source_target_pairs={{8,0},{16,8},{24,16},{9,1},{17,9},{25,17},{10,2},{18,10},{26,18},{... | collective-permute-start | bytes 1966088 | tf_op jit(solution)/shard_map/ppermute | solution.py:139
  257.5 12.6 %collective-permute-start.19 = (bf16[2,256,640]{2,1,0:T(8,128)(2,1)S(1)}, bf16[2,256,640]{2,1,0:T(8,128)(2,1)S(1)}, u32[]{:S(2)}, u32[]{:S(2)}) collective-permute-start(bf16[2,256,640]{2,1,0:T(8,128)(2,1)S(1)} %get-tuple-element.58), channel_id=1, source_target_pairs={{0,8},{8,16},{16,24},{1,9},{9,17},{17,25},{2,10},{10,18},{18,26},{... | collective-permute-start | bytes 1966088 | tf_op jit(solution)/shard_map/ppermute | solution.py:139
  261.2 13.3 %collective-permute-start.20 = (bf16[2,256,640]{2,1,0:T(8,128)(2,1)S(1)}, bf16[2,256,640]{2,1,0:T(8,128)(2,1)S(1)}, u32[]{:S(2)}, u32[]{:S(2)}) collective-permute-start(bf16[2,256,640]{2,1,0:T(8,128)(2,1)S(1)} %get-tuple-element.59), channel_id=1, source_target_pairs={{8,0},{16,8},{24,16},{9,1},{17,9},{25,17},{10,2},{18,10},{26,18},{... | collective-permute-start | bytes 1966088 | tf_op jit(solution)/shard_map/ppermute | solution.py:139
Sparse Core Ops, SparseCore 0:
  13.1 111.0 all-gather.1

commit v11 on v10

--- a/solution.py
+++ b/solution.py
@@ -152,15 +152,21 @@
     return lax.ppermute(array, axis, [(i, i ^ bit) for i in range(lax.axis_size(axis))])
 
 
-def weight_kernel(scale, table, near_ref, far_ref, g_near, g_far, out_ref):
+def weight_kernel(scale, table, near_ref, far_ref, g_near, g_far, out_ref, acc_ref):
     step = pl.program_id(0)
+    total = dot(g_near[0], near_ref[0], TN) + dot(g_far[0], far_ref[0], TN)
 
     @pl.when(step == 0)
     def _():
-        out_ref[...] = jnp.zeros_like(out_ref)
-
-    total = dot(near_ref[0], g_near[0], TN) + dot(far_ref[0], g_far[0], TN)
-    out_ref[...] += total * scale
+        acc_ref[...] = total
+
+    @pl.when(step > 0)
+    def _():
+        acc_ref[...] += total
+
+    @pl.when(step == pl.num_programs(0) - 1)
+    def _():
+        out_ref[...] = acc_ref[...].T * scale
 
 
 def weight_grad(table, near, far, gated, scale):
@@ -179,6 +185,7 @@
                 pl.BlockSpec((1, rows, columns), lambda j, tab: (tab[1, j], 0, 0)),
             ],
             out_specs=pl.BlockSpec((width, columns), lambda j, tab: (0, 0)),
+            scratch_shapes=[pltpu.VMEM((columns, width), jnp.float32)],
         ),
         out_shape=jax.ShapeDtypeStruct((width, columns), jnp.float32),
         compiler_params=pltpu.CompilerParams(vmem_limit_bytes=40 * 2**20),

time: 287 us -> 287 us (level)
  no operation moved by 1% of the time
where the time goes in v11:
time: 287 us; the launch traced here: 285 us
  waiting for transfers between devices  137 us (48%)
  Pallas kernels  57.6 us (20%)
  starting transfers between devices  49.8 us (17%)
  between operations  14.6 us (5%)
  other arithmetic  14.3 us (5%)
  local copies, waits for them, and re-layouts  11.4 us (4%)
    ppermute x12, waiting for transfers between devices, rotated(): lax.ppermute(array, axis, [(i, (i + step) % count) for i in range(count)])  80.5 us
    ppermute x5, waiting for transfers between devices, flipped(): lax.ppermute(array, axis, [(i, i ^ bit) for i in range(lax.axis_size(axis...  34.6 us
    pallas_call x2, Pallas kernels, attention(): pl.pallas_call(partial(attention_kernel, parts), grid_spec=pltpu.Prefetch...  28.5 us
    ppermute x6, starting transfers between devices, shifted(): return lax.ppermute(array, axis, pairs)  18.5 us
    ppermute x12, starting transfers between devices, rotated(): lax.ppermute(array, axis, [(i, (i + step) % count) for i in range(count)])  14.9 us
    pallas_call x1, Pallas kernels, weight_grad(): pl.pallas_call(partial(weight_kernel, scale), grid_spec=pltpu.PrefetchSca...  14.5 us
    pallas_call x1, Pallas kernels, project(): pl.pallas_call(project_kernel, grid=(blocks,), in_specs=[pl.BlockSpec((1,...  13.3 us
    all_gather x1, waiting for transfers between devices, per_device(): gathered = lax.all_gather(gated, 'head', axis=1, tiled=True)  11.8 us
  transfers between devices with their start and end apart: 25, of which 10 were waited for; matrix products, arithmetic and copies ran while one was open for 6% of the time, Pallas kernels for 15%

profile of v11, /device:TPU:11, one launch (start us, length us, event | category | flops | bytes accessed | tf_op | source)
XLA Modules:
  0.0 284.5 jit_solution(6209455909615316665)
XLA Ops:
  7.4 1.2 copy-done.16
  9.4 1.3 collective-permute-start.3
  10.7 1.2 gate_cotangent.1
  11.9 1.0 copy-done.12
  13.2 2.3 collective-permute-start.4
  15.5 2.8 collective-permute-done.3
  18.3 1.0 bitcast_dynamic-update-slice_fusion.2
  19.3 38.4 %collective-permute-done.4 = bf16[2,64,1280]{2,1,0:T(8,128)(2,1)S(1)} collective-permute-done((bf16[2,64,1280]{2,1,0:T(8,128)(2,1)S(1)}, bf16[2,64,1280]{2,1,0:T(8,128)(2,1)S(1)}, u32[]{:S(2)}, u32[]{:S(2)}) %collective-permute-start.4) | collective-permute-done | bytes 327712 | tf_op jit(solution)/shard_map/ppermute | solution.py:144
  58.3 1.2 collective-permute-start.7
  59.6 8.3 %collective-permute-done.6 = bf16[1,256,1280]{2,1,0:T(8,128)(2,1)S(1)} collective-permute-done((bf16[1,256,1280]{2,1,0:T(8,128)(2,1)S(1)}, bf16[1,256,1280]{2,1,0:T(8,128)(2,1)S(1)}, u32[]{:S(2)}, u32[]{:S(2)}) %collective-permute-start.6) | collective-permute-done | bytes 655392 | tf_op jit(solution)/shard_map/ppermute | solution.py:152
  68.1 1.3 collective-permute-start.9
  69.8 1.0 constant_dynamic-slice_fusion.1
  70.9 26.2 %collective-permute-done.9 = bf16[2,256,1280]{2,1,0:T(8,128)(2,1)S(1)} collective-permute-done((bf16[2,256,1280]{2,1,0:T(8,128)(2,1)S(1)}, bf16[2,256,1280]{2,1,0:T(8,128)(2,1)S(1)}, u32[]{:S(2)}, u32[]{:S(2)}) %collective-permute-start.9) | collective-permute-done | bytes 1310752 | tf_op jit(solution)/shard_map/ppermute | solution.py:152
  97.6 3.0 %pad_maximum_fusion.near_ref = bf16[4,512,1280]{2,1,0:T(8,128)(2,1)} fusion(bf16[1,512,1280]{2,1,0:T(8,128)(2,1)S(1)} %maximum_bitcast_fusion.3, bf16[1,512,1280]{2,1,0:T(8,128)(2,1)S(1)} %maximum_bitcast_fusion.2, bf16[1,512,1280]{2,1,0:T(8,128)(2,1)S(1)} %maximum_bitcast_fusion.1, bf16[1,512,1280]{2,1,0:T(8,128)(2,1)S(1)} %maximum_bitcast_fusion), kind=kLoop, calls=%fused_computation | loop fusion | flops 7864320 | bytes 10485760 | tf_op jit(solution)/shard_map/stack | solution.py:328
  100.6 8.1 %collective-permute-start.10 = (bf16[4,512,1280]{2,1,0:T(8,128)(2,1)}, bf16[4,512,1280]{2,1,0:T(8,128)(2,1)}, u32[]{:S(2)}, u32[]{:S(2)}) collective-permute-start(bf16[4,512,1280]{2,1,0:T(8,128)(2,1)} %pad_maximum_fusion.near_ref), channel_id=1, source_target_pairs={{0,8},{8,0},{16,24},{24,16},{1,9},{9,1},{17,25},{25,17},{2,10},{10... | collective-permute-start | bytes 15728648 | tf_op jit(solution)/shard_map/ppermute | solution.py:152
  108.7 0.9 pad_maximum_fusion.7
  109.6 2.0 pad_maximum_fusion.6
  111.6 0.9 pad_maximum_fusion.5
  112.4 11.8 %all-gather.2.cloned.1.call-done.g_ref = bf16[8,512,640]{2,1,0:T(8,128)(2,1)} async-done(((bf16[8,128,640]{2,1,0:T(8,128)(2,1)}), bf16[8,512,640]{2,1,0:T(8,128)(2,1)}) %all-gather.2.cloned.1.call-update) | async-done | bytes 5242896 | tf_op jit(solution)/shard_map/all_gather | solution.py:302
  124.2 5.1 %all-to-all-start = ((bf16[8,512,640]{2,1,0:T(8,128)(2,1)}), bf16[8,512,640]{2,1,0:T(8,128)(2,1)}, u32[]{:S(2)}, u32[]{:S(2)}) async-start(bf16[8,512,640]{2,1,0:T(8,128)(2,1)} %all-gather.2.cloned.1.call-done.g_ref), calls=%async_computation | async-start | bytes 10485760 | tf_op jit(solution)/shard_map/all_to_all | solution.py:344
  129.4 1.2 dynamic-slice_bitcast_fusion.3
  130.5 1.1 collective-permute-start.11
  131.6 4.2 %collective-permute-start.12 = (bf16[2,2,64,1280]{3,2,1,0:T(8,128)(2,1)}, bf16[2,2,64,1280]{3,2,1,0:T(8,128)(2,1)S(1)}, u32[]{:S(2)}, u32[]{:S(2)}) collective-permute-start(bf16[2,2,64,1280]{3,2,1,0:T(8,128)(2,1)} %pad_maximum_fusion.6), channel_id=1, source_target_pairs={{0,4},{2,6},{4,0},{6,2},{1,5},{3,7},{5,1},{7,3},{8,12},{10,14},{12... | collective-permute-start | bytes 1966088 | tf_op jit(solution)/shard_map/ppermute | solution.py:144
  135.8 1.0 dynamic-slice_bitcast_fusion.7
  136.8 2.5 copy-done.11
  139.3 13.3 %project_gated.1 = bf16[512,1280]{1,0:T(8,128)(2,1)S(1)} custom-call(bf16[8,512,640]{2,1,0:T(8,128)(2,1)S(1)} %copy-done.11, bf16[1280,5120]{1,0:T(8,128)(2,1)} %w_ref.1), custom_call_target="tpu_custom_call" | custom-call | flops 6710886400 | bytes 19660800 | tf_op jit(solution)/shard_map/project_gated/pallas_call | solution.py:259
  152.6 35.2 %collective-permute-done.12.refs_4_ = bf16[2,2,64,1280]{3,2,1,0:T(8,128)(2,1)S(1)} collective-permute-done((bf16[2,2,64,1280]{3,2,1,0:T(8,128)(2,1)}, bf16[2,2,64,1280]{3,2,1,0:T(8,128)(2,1)S(1)}, u32[]{:S(2)}, u32[]{:S(2)}) %collective-permute-start.12) | collective-permute-done | bytes 655392 | tf_op jit(solution)/shard_map/ppermute | solution.py:144
  187.8 4.1 %collective-permute-done.13.refs_5_ = bf16[2,2,64,1280]{3,2,1,0:T(8,128)(2,1)S(1)} collective-permute-done((bf16[2,2,64,1280]{3,2,1,0:T(8,128)(2,1)}, bf16[2,2,64,1280]{3,2,1,0:T(8,128)(2,1)S(1)}, u32[]{:S(2)}, u32[]{:S(2)}) %collective-permute-start.13) | collective-permute-done | bytes 655392 | tf_op jit(solution)/shard_map/ppermute | solution.py:144
  193.0 1.2 pad_maximum_fusion.3
  194.1 4.2 %collective-permute-start.17 = (bf16[2,4,64,1280]{3,2,1,0:T(8,128)(2,1)}, bf16[2,4,64,1280]{3,2,1,0:T(8,128)(2,1)}, u32[]{:S(2)}, u32[]{:S(2)}) collective-permute-start(bf16[2,4,64,1280]{3,2,1,0:T(8,128)(2,1)} %pad_maximum_fusion.3), channel_id=1, source_target_pairs={{0,8},{8,16},{16,24},{1,9},{9,17},{17,25},{2,10},{10,18},{18,26},{... | collective-permute-start | bytes 3932168 | tf_op jit(solution)/shard_map/ppermute | solution.py:139
  198.5 1.2 pad_maximum_fusion.4
  199.7 1.9 collective-permute-start.18
  202.2 1.4 collective-permute-start.16
  203.7 14.5 %weight_gradient.1 = f32[1280,640]{1,0:T(8,128)} custom-call(s32[2,4]{1,0:T(2,128)S(1)} %pad_add_fusion.table, bf16[4,512,1280]{2,1,0:T(8,128)(2,1)} %pad_maximum_fusion.near_ref, bf16[4,512,1280]{2,1,0:T(8,128)(2,1)} %collective-permute-done.10.far_ref, bf16[8,512,640]{2,1,0:T(8,128)(2,1)} %all-to-all-done.g_near.g_far, ...), custom_call_target="tpu_custom_call" | custom-call | flops 6710886400 | bytes 19005440 | tf_op jit(solution)/shard_map/weight_gradient/pallas_call | solution.py:176
  218.2 1.3 collective-permute-start
  219.5 3.0 %collective-permute-start.1 = (bf16[2,64,640]{2,1,0:T(8,128)(2,1)S(1)}, bf16[2,64,640]{2,1,0:T(8,128)(2,1)S(1)}, u32[]{:S(2)}, u32[]{:S(2)}) collective-permute-start(bf16[2,64,640]{2,1,0:T(8,128)(2,1)S(1)} %copy-done.18), channel_id=1, source_target_pairs={{0,4},{2,6},{4,0},{6,2},{1,5},{3,7},{5,1},{7,3},{8,12},{10,14},{12... | collective-permute-start | bytes 491528 | tf_op jit(solution)/shard_map/ppermute | solution.py:144
  222.6 14.2 %attention_backward.2 = (bf16[2,256,640]{2,1,0:T(8,128)(2,1)S(1)}, f32[2,256,640]{2,1,0:T(8,128)S(1)}, f32[2,256,640]{2,1,0:T(8,128)S(1)}, bf16[2,256,640]{2,1,0:T(8,128)(2,1)S(1)}, bf16[2,256,640]{2,1,0:T(8,128)(2,1)S(1)}) custom-call(s32[6]{0:T(128)S(1)} %pad_add_fusion.1.scal, bf16[1,2,64,5120]{3,2,1,0:T(8,128)(2,1)S(1)} %copy-done.4, ...), custom_call_target="tpu_custom_call" | custom-call | flops 2516582400 | bytes 10485760 | tf_op jit(solution)/shard_map/attention_backward/pallas_call | solution.py:107
  236.9 14.3 %attention_backward.3 = (bf16[2,256,640]{2,1,0:T(8,128)(2,1)S(1)}, f32[2,256,640]{2,1,0:T(8,128)S(1)}, f32[2,256,640]{2,1,0:T(8,128)S(1)}, bf16[2,256,640]{2,1,0:T(8,128)(2,1)S(1)}, bf16[2,256,640]{2,1,0:T(8,128)(2,1)S(1)}) custom-call(s32[6]{0:T(128)S(1)} %pad_add_fusion.1.scal, bf16[1,2,64,5120]{3,2,1,0:T(8,128)(2,1)S(1)} %copy-done.4, ...), custom_call_target="tpu_custom_call" | custom-call | flops 2516582400 | bytes 10485760 | tf_op jit(solution)/shard_map/attention_backward/pallas_call | solution.py:107
  251.2 4.9 %collective-permute-start.21 = (bf16[2,256,640]{2,1,0:T(8,128)(2,1)S(1)}, bf16[2,256,640]{2,1,0:T(8,128)(2,1)S(1)}, u32[]{:S(2)}, u32[]{:S(2)}) collective-permute-start(bf16[2,256,640]{2,1,0:T(8,128)(2,1)S(1)} %get-tuple-element.61), channel_id=1, source_target_pairs={{0,8},{8,16},{16,24},{1,9},{9,17},{17,25},{2,10},{10,18},{18,26},{... | collective-permute-start | bytes 1966088 | tf_op jit(solution)/shard_map/ppermute | solution.py:139
  256.1 1.9 collective-permute-start.22
  258.0 3.6 %collective-permute-start.19 = (bf16[2,256,640]{2,1,0:T(8,128)(2,1)S(1)}, bf16[2,256,640]{2,1,0:T(8,128)(2,1)S(1)}, u32[]{:S(2)}, u32[]{:S(2)}) collective-permute-start(bf16[2,256,640]{2,1,0:T(8,128)(2,1)S(1)} %get-tuple-element.58), channel_id=1, source_target_pairs={{0,8},{8,16},{16,24},{1,9},{9,17},{17,25},{2,10},{10,18},{18,26},{... | collective-permute-start | bytes 1966088 | tf_op jit(solution)/shard_map/ppermute | solution.py:139
  261.7 1.9 collective-permute-start.20
  263.6 1.2 maximum_bitcast_fusion.4
  264.7 3.2 %collective-permute-done.22 = bf16[2,256,640]{2,1,0:T(8,128)(2,1)S(1)} collective-permute-done((bf16[2,256,640]{2,1,0:T(8,128)(2,1)S(1)}, bf16[2,256,640]{2,1,0:T(8,128)(2,1)S(1)}, u32[]{:S(2)}, u32[]{:S(2)}) %collective-permute-start.22) | collective-permute-done | bytes 655392 | tf_op jit(solution)/shard_map/ppermute | solution.py:139
  268.3 2.4 collective-permute-done.19
  270.6 4.4 %collective-permute-done.20 = bf16[2,256,640]{2,1,0:T(8,128)(2,1)S(1)} collective-permute-done((bf16[2,256,640]{2,1,0:T(8,128)(2,1)S(1)}, bf16[2,256,640]{2,1,0:T(8,128)(2,1)S(1)}, u32[]{:S(2)}, u32[]{:S(2)}) %collective-permute-start.20) | collective-permute-done | bytes 655392 | tf_op jit(solution)/shard_map/ppermute | solution.py:139
  275.4 1.2 maximum_bitcast_fusion.5
  276.5 1.2 maximum_bitcast_fusion.6
  (92 shorter events, 5.4 us)
Async XLA Ops:
  7.2 117.1 %all-gather.2.cloned.1.call-start = ((), (), s32[]{:S(2)}) async-start(), calls=%async_computation.1 | async-start | bytes 6553600 | tf_op jit(solution)/shard_map/all_gather | solution.py:302
  7.3 1.3 copy-start.16
  8.6 2.1 copy-start.13
  8.6 2.1 copy-start.14
  8.6 2.1 copy-start.15
  9.4 8.9 %collective-permute-start.3 = (bf16[2,64,1280]{2,1,0:T(8,128)(2,1)}, bf16[2,64,1280]{2,1,0:T(8,128)(2,1)}, u32[]{:S(2)}, u32[]{:S(2)}) collective-permute-start(bf16[2,64,1280]{2,1,0:T(8,128)(2,1)} %get-tuple-element.103), channel_id=1, source_target_pairs={{0,2},{2,4},{4,6},{6,0},{1,3},{3,5},{5,7},{7,1},{8,10},{10,12},{12... | collective-permute-start | bytes 983048 | tf_op jit(solution)/shard_map/ppermute | solution.py:144
  11.9 1.1 copy-start.12
  13.0 44.8 %collective-permute-start.5 = (bf16[2,64,1280]{2,1,0:T(8,128)(2,1)S(1)}, bf16[2,64,1280]{2,1,0:T(8,128)(2,1)S(1)}, u32[]{:S(2)}, u32[]{:S(2)}) collective-permute-start(bf16[2,64,1280]{2,1,0:T(8,128)(2,1)S(1)} %get-tuple-element.102), channel_id=1, source_target_pairs={{0,6},{2,0},{4,2},{6,4},{1,7},{3,1},{5,3},{7,5},{8,14},{10,8},{12,... | collective-permute-start | bytes 983048 | tf_op jit(solution)/shard_map/ppermute | solution.py:144
  13.2 44.5 %collective-permute-start.4 = (bf16[2,64,1280]{2,1,0:T(8,128)(2,1)S(1)}, bf16[2,64,1280]{2,1,0:T(8,128)(2,1)S(1)}, u32[]{:S(2)}, u32[]{:S(2)}) collective-permute-start(bf16[2,64,1280]{2,1,0:T(8,128)(2,1)S(1)} %get-tuple-element.105), channel_id=1, source_target_pairs={{0,4},{2,6},{4,0},{6,2},{1,5},{3,7},{5,1},{7,3},{8,12},{10,14},{12... | collective-permute-start | bytes 983048 | tf_op jit(solution)/shard_map/ppermute | solution.py:144
  58.0 9.9 %collective-permute-start.6 = (bf16[1,256,1280]{2,1,0:T(8,128)(2,1)S(1)}, bf16[1,256,1280]{2,1,0:T(8,128)(2,1)S(1)}, u32[]{:S(2)}, u32[]{:S(2)}) collective-permute-start(bf16[1,256,1280]{2,1,0:T(8,128)(2,1)S(1)} %get-tuple-element.97), channel_id=1, source_target_pairs={{0,1},{1,0},{2,3},{3,2},{4,5},{5,4},{6,7},{7,6},{8,9},{9,8},{10,11... | collective-permute-start | bytes 1966088 | tf_op jit(solution)/shard_map/ppermute | solution.py:152
  58.3 11.0 %collective-permute-start.7 = (bf16[1,256,1280]{2,1,0:T(8,128)(2,1)S(1)}, bf16[1,256,1280]{2,1,0:T(8,128)(2,1)S(1)}, u32[]{:S(2)}, u32[]{:S(2)}) collective-permute-start(bf16[1,256,1280]{2,1,0:T(8,128)(2,1)S(1)} %get-tuple-element.96), channel_id=1, source_target_pairs={{0,16},{8,24},{16,0},{24,8},{1,17},{9,25},{17,1},{25,9},{2,18},{10... | collective-permute-start | bytes 1966088 | tf_op jit(solution)/shard_map/ppermute | solution.py:152
  68.0 1.8 copy-start
  68.1 1.8 copy-start.1
  68.1 29.1 %collective-permute-start.9 = (bf16[2,256,1280]{2,1,0:T(8,128)(2,1)S(1)}, bf16[2,256,1280]{2,1,0:T(8,128)(2,1)S(1)}, u32[]{:S(2)}, u32[]{:S(2)}) collective-permute-start(bf16[2,256,1280]{2,1,0:T(8,128)(2,1)S(1)} %pad_maximum_fusion.2), channel_id=1, source_target_pairs={{0,16},{8,24},{16,0},{24,8},{1,17},{9,25},{17,1},{25,9},{2,18},{10... | collective-permute-start | bytes 3932168 | tf_op jit(solution)/shard_map/ppermute | solution.py:152
  69.5 27.8 %collective-permute-start.8 = (bf16[2,256,1280]{2,1,0:T(8,128)(2,1)S(1)}, bf16[2,256,1280]{2,1,0:T(8,128)(2,1)S(1)}, u32[]{:S(2)}, u32[]{:S(2)}) collective-permute-start(bf16[2,256,1280]{2,1,0:T(8,128)(2,1)S(1)} %pad_maximum_fusion.1), channel_id=1, source_target_pairs={{0,1},{1,0},{2,3},{3,2},{4,5},{5,4},{6,7},{7,6},{8,9},{9,8},{10,11... | collective-permute-start | bytes 3932168 | tf_op jit(solution)/shard_map/ppermute | solution.py:152
  100.6 101.7 %collective-permute-start.10 = (bf16[4,512,1280]{2,1,0:T(8,128)(2,1)}, bf16[4,512,1280]{2,1,0:T(8,128)(2,1)}, u32[]{:S(2)}, u32[]{:S(2)}) collective-permute-start(bf16[4,512,1280]{2,1,0:T(8,128)(2,1)} %pad_maximum_fusion.near_ref), channel_id=1, source_target_pairs={{0,8},{8,0},{16,24},{24,16},{1,9},{9,1},{17,25},{25,17},{2,10},{10... | collective-permute-start | bytes 15728648 | tf_op jit(solution)/shard_map/ppermute | solution.py:152
  124.2 79.4 %all-to-all-start = ((bf16[8,512,640]{2,1,0:T(8,128)(2,1)}), bf16[8,512,640]{2,1,0:T(8,128)(2,1)}, u32[]{:S(2)}, u32[]{:S(2)}) async-start(bf16[8,512,640]{2,1,0:T(8,128)(2,1)} %all-gather.2.cloned.1.call-done.g_ref), calls=%async_computation | async-start | bytes 10485760 | tf_op jit(solution)/shard_map/all_to_all | solution.py:344
  129.4 6.4 %copy-start.3 = (bf16[1,2,64,5120]{3,2,1,0:T(8,128)(2,1)S(1)}, bf16[1,2,64,5120]{3,2,1,0:T(8,128)(2,1)}, u32[]{:S(2)}) copy-start(bf16[1,2,64,5120]{3,2,1,0:T(8,128)(2,1)} %refs_0_.3) | copy-start | bytes 3932164
  130.5 22.1 %collective-permute-start.11 = (bf16[2,2,64,1280]{3,2,1,0:T(8,128)(2,1)}, bf16[2,2,64,1280]{3,2,1,0:T(8,128)(2,1)S(1)}, u32[]{:S(2)}, u32[]{:S(2)}) collective-permute-start(bf16[2,2,64,1280]{3,2,1,0:T(8,128)(2,1)} %pad_maximum_fusion.5), channel_id=1, source_target_pairs={{0,2},{2,4},{4,6},{6,0},{1,3},{3,5},{5,7},{7,1},{8,10},{10,12},{12... | collective-permute-start | bytes 1966088 | tf_op jit(solution)/shard_map/ppermute | solution.py:144
  131.6 56.2 %collective-permute-start.12 = (bf16[2,2,64,1280]{3,2,1,0:T(8,128)(2,1)}, bf16[2,2,64,1280]{3,2,1,0:T(8,128)(2,1)S(1)}, u32[]{:S(2)}, u32[]{:S(2)}) collective-permute-start(bf16[2,2,64,1280]{3,2,1,0:T(8,128)(2,1)} %pad_maximum_fusion.6), channel_id=1, source_target_pairs={{0,4},{2,6},{4,0},{6,2},{1,5},{3,7},{5,1},{7,3},{8,12},{10,14},{12... | collective-permute-start | bytes 1966088 | tf_op jit(solution)/shard_map/ppermute | solution.py:144
  135.8 56.1 %collective-permute-start.13 = (bf16[2,2,64,1280]{3,2,1,0:T(8,128)(2,1)}, bf16[2,2,64,1280]{3,2,1,0:T(8,128)(2,1)S(1)}, u32[]{:S(2)}, u32[]{:S(2)}) collective-permute-start(bf16[2,2,64,1280]{3,2,1,0:T(8,128)(2,1)} %pad_maximum_fusion.7), channel_id=1, source_target_pairs={{0,6},{2,0},{4,2},{6,4},{1,7},{3,1},{5,3},{7,5},{8,14},{10,8},{12,... | collective-permute-start | bytes 1966088 | tf_op jit(solution)/shard_map/ppermute | solution.py:144
  136.8 2.5 copy-start.11
  152.6 39.4 %copy-start.9 = (bf16[512,1280]{1,0:T(8,128)(2,1)}, bf16[512,1280]{1,0:T(8,128)(2,1)S(1)}, u32[]{:S(2)}) copy-start(bf16[512,1280]{1,0:T(8,128)(2,1)S(1)} %project_gated.1) | copy-start | bytes 3932164
  187.8 4.2 %copy-start.5 = (bf16[2,2,64,1280]{3,2,1,0:T(8,128)(2,1)}, bf16[2,2,64,1280]{3,2,1,0:T(8,128)(2,1)S(1)}, u32[]{:S(2)}) copy-start(bf16[2,2,64,1280]{3,2,1,0:T(8,128)(2,1)S(1)} %collective-permute-done.12.refs_4_) | copy-start | bytes 1966084
  191.9 0.9 copy-start.7
  194.1 28.4 %collective-permute-start.17 = (bf16[2,4,64,1280]{3,2,1,0:T(8,128)(2,1)}, bf16[2,4,64,1280]{3,2,1,0:T(8,128)(2,1)}, u32[]{:S(2)}, u32[]{:S(2)}) collective-permute-start(bf16[2,4,64,1280]{3,2,1,0:T(8,128)(2,1)} %pad_maximum_fusion.3), channel_id=1, source_target_pairs={{0,8},{8,16},{16,24},{1,9},{9,17},{17,25},{2,10},{10,18},{18,26},{... | collective-permute-start | bytes 3932168 | tf_op jit(solution)/shard_map/ppermute | solution.py:139
  198.5 3.1 %copy-start.20 = (s32[8,2]{0,1:T(2,128)S(1)}, s32[8,2]{0,1:T(2,128)}, u32[]{:S(2)}) copy-start(s32[8,2]{0,1:T(2,128)} %param.17) | copy-start | bytes 196
  199.7 22.8 %collective-permute-start.18 = (bf16[2,4,64,1280]{3,2,1,0:T(8,128)(2,1)}, bf16[2,4,64,1280]{3,2,1,0:T(8,128)(2,1)}, u32[]{:S(2)}, u32[]{:S(2)}) collective-permute-start(bf16[2,4,64,1280]{3,2,1,0:T(8,128)(2,1)} %pad_maximum_fusion.4), channel_id=1, source_target_pairs={{8,0},{16,8},{24,16},{9,1},{17,9},{25,17},{10,2},{18,10},{26,18},{... | collective-permute-start | bytes 3932168 | tf_op jit(solution)/shard_map/ppermute | solution.py:139
  202.1 16.1 %collective-permute-start.14 = (bf16[2,64,640]{2,1,0:T(8,128)(2,1)}, bf16[2,64,640]{2,1,0:T(8,128)(2,1)S(1)}, u32[]{:S(2)}, u32[]{:S(2)}) collective-permute-start(bf16[2,64,640]{2,1,0:T(8,128)(2,1)} %get-tuple-element.47), channel_id=1, source_target_pairs={{0,2},{2,4},{4,6},{6,0},{1,3},{3,5},{5,7},{7,1},{8,10},{10,12},{12... | collective-permute-start | bytes 491528 | tf_op jit(solution)/shard_map/ppermute | solution.py:144
  202.2 17.3 %collective-permute-start.15 = (bf16[2,64,640]{2,1,0:T(8,128)(2,1)}, bf16[2,64,640]{2,1,0:T(8,128)(2,1)}, u32[]{:S(2)}, u32[]{:S(2)}) collective-permute-start(bf16[2,64,640]{2,1,0:T(8,128)(2,1)} %get-tuple-element.48), channel_id=1, source_target_pairs={{0,4},{2,6},{4,0},{6,2},{1,5},{3,7},{5,1},{7,3},{8,12},{10,14},{12... | collective-permute-start | bytes 491528 | tf_op jit(solution)/shard_map/ppermute | solution.py:144
  202.2 20.3 %collective-permute-start.16 = (bf16[2,64,640]{2,1,0:T(8,128)(2,1)}, bf16[2,64,640]{2,1,0:T(8,128)(2,1)}, u32[]{:S(2)}, u32[]{:S(2)}) collective-permute-start(bf16[2,64,640]{2,1,0:T(8,128)(2,1)} %get-tuple-element.49), channel_id=1, source_target_pairs={{0,6},{2,0},{4,2},{6,4},{1,7},{3,1},{5,3},{7,5},{8,14},{10,8},{12,... | collective-permute-start | bytes 491528 | tf_op jit(solution)/shard_map/ppermute | solution.py:144
  203.6 14.6 %copy-start.19 = (bf16[2,64,640]{2,1,0:T(8,128)(2,1)S(1)}, bf16[2,64,640]{2,1,0:T(8,128)(2,1)}, u32[]{:S(2)}) copy-start(bf16[2,64,640]{2,1,0:T(8,128)(2,1)} %get-tuple-element.36) | copy-start | bytes 491524
  203.6 15.9 %copy-start.18 = (bf16[2,64,640]{2,1,0:T(8,128)(2,1)S(1)}, bf16[2,64,640]{2,1,0:T(8,128)(2,1)}, u32[]{:S(2)}) copy-start(bf16[2,64,640]{2,1,0:T(8,128)(2,1)} %get-tuple-element.37) | copy-start | bytes 491524
  203.6 18.9 %copy-start.17 = (bf16[2,64,640]{2,1,0:T(8,128)(2,1)S(1)}, bf16[2,64,640]{2,1,0:T(8,128)(2,1)}, u32[]{:S(2)}) copy-start(bf16[2,64,640]{2,1,0:T(8,128)(2,1)} %get-tuple-element.38) | copy-start | bytes 491524
  203.6 18.9 %copy-start.2 = (bf16[1,2,64,5120]{3,2,1,0:T(8,128)(2,1)S(1)}, bf16[1,2,64,5120]{3,2,1,0:T(8,128)(2,1)}, u32[]{:S(2)}) copy-start(bf16[1,2,64,5120]{3,2,1,0:T(8,128)(2,1)} %refs_2_.3) | copy-start | bytes 3932164
  203.6 18.9 %copy-start.4 = (bf16[1,2,64,5120]{3,2,1,0:T(8,128)(2,1)S(1)}, bf16[1,2,64,5120]{3,2,1,0:T(8,128)(2,1)}, u32[]{:S(2)}) copy-start(bf16[1,2,64,5120]{3,2,1,0:T(8,128)(2,1)} %refs_0_.3) | copy-start | bytes 3932164
  203.7 18.9 %copy-start.6 = (bf16[2,2,64,1280]{3,2,1,0:T(8,128)(2,1)S(1)}, bf16[2,2,64,1280]{3,2,1,0:T(8,128)(2,1)}, u32[]{:S(2)}) copy-start(bf16[2,2,64,1280]{3,2,1,0:T(8,128)(2,1)} %copy-done.5) | copy-start | bytes 1966084
  203.7 18.9 %copy-start.8 = (bf16[2,2,64,1280]{3,2,1,0:T(8,128)(2,1)S(1)}, bf16[2,2,64,1280]{3,2,1,0:T(8,128)(2,1)}, u32[]{:S(2)}) copy-start(bf16[2,2,64,1280]{3,2,1,0:T(8,128)(2,1)} %copy-done.7) | copy-start | bytes 1966084
  203.7 18.9 %copy-start.10 = (bf16[512,1280]{1,0:T(8,128)(2,1)S(1)}, bf16[512,1280]{1,0:T(8,128)(2,1)}, u32[]{:S(2)}) copy-start(bf16[512,1280]{1,0:T(8,128)(2,1)} %copy-done.9) | copy-start | bytes 3932164
  218.2 18.6 %collective-permute-start = (bf16[2,64,640]{2,1,0:T(8,128)(2,1)S(1)}, bf16[2,64,640]{2,1,0:T(8,128)(2,1)S(1)}, u32[]{:S(2)}, u32[]{:S(2)}) collective-permute-start(bf16[2,64,640]{2,1,0:T(8,128)(2,1)S(1)} %copy-done.19), channel_id=1, source_target_pairs={{0,2},{2,4},{4,6},{6,0},{1,3},{3,5},{5,7},{7,1},{8,10},{10,12},{12... | collective-permute-start | bytes 491528 | tf_op jit(solution)/shard_map/ppermute | solution.py:144
  219.5 17.4 %collective-permute-start.1 = (bf16[2,64,640]{2,1,0:T(8,128)(2,1)S(1)}, bf16[2,64,640]{2,1,0:T(8,128)(2,1)S(1)}, u32[]{:S(2)}, u32[]{:S(2)}) collective-permute-start(bf16[2,64,640]{2,1,0:T(8,128)(2,1)S(1)} %copy-done.18), channel_id=1, source_target_pairs={{0,4},{2,6},{4,0},{6,2},{1,5},{3,7},{5,1},{7,3},{8,12},{10,14},{12... | collective-permute-start | bytes 491528 | tf_op jit(solution)/shard_map/ppermute | solution.py:144
  222.5 14.3 %collective-permute-start.2 = (bf16[2,64,640]{2,1,0:T(8,128)(2,1)S(1)}, bf16[2,64,640]{2,1,0:T(8,128)(2,1)S(1)}, u32[]{:S(2)}, u32[]{:S(2)}) collective-permute-start(bf16[2,64,640]{2,1,0:T(8,128)(2,1)S(1)} %copy-done.17), channel_id=1, source_target_pairs={{0,6},{2,0},{4,2},{6,4},{1,7},{3,1},{5,3},{7,5},{8,14},{10,8},{12,... | collective-permute-start | bytes 491528 | tf_op jit(solution)/shard_map/ppermute | solution.py:144
  251.2 13.5 %collective-permute-start.21 = (bf16[2,256,640]{2,1,0:T(8,128)(2,1)S(1)}, bf16[2,256,640]{2,1,0:T(8,128)(2,1)S(1)}, u32[]{:S(2)}, u32[]{:S(2)}) collective-permute-start(bf16[2,256,640]{2,1,0:T(8,128)(2,1)S(1)} %get-tuple-element.61), channel_id=1, source_target_pairs={{0,8},{8,16},{16,24},{1,9},{9,17},{17,25},{2,10},{10,18},{18,26},{... | collective-permute-start | bytes 1966088 | tf_op jit(solution)/shard_map/ppermute | solution.py:139
  256.1 11.9 %collective-permute-start.22 = (bf16[2,256,640]{2,1,0:T(8,128)(2,1)S(1)}, bf16[2,256,640]{2,1,0:T(8,128)(2,1)S(1)}, u32[]{:S(2)}, u32[]{:S(2)}) collective-permute-start(bf16[2,256,640]{2,1,0:T(8,128)(2,1)S(1)} %get-tuple-element.62), channel_id=1, source_target_pairs={{8,0},{16,8},{24,16},{9,1},{17,9},{25,17},{10,2},{18,10},{26,18},{... | collective-permute-start | bytes 1966088 | tf_op jit(solution)/shard_map/ppermute | solution.py:139
  258.0 12.6 %collective-permute-start.19 = (bf16[2,256,640]{2,1,0:T(8,128)(2,1)S(1)}, bf16[2,256,640]{2,1,0:T(8,128)(2,1)S(1)}, u32[]{:S(2)}, u32[]{:S(2)}) collective-permute-start(bf16[2,256,640]{2,1,0:T(8,128)(2,1)S(1)} %get-tuple-element.58), channel_id=1, source_target_pairs={{0,8},{8,16},{16,24},{1,9},{9,17},{17,25},{2,10},{10,18},{18,26},{... | collective-permute-start | bytes 1966088 | tf_op jit(solution)/shard_map/ppermute | solution.py:139
  261.7 13.3 %collective-permute-start.20 = (bf16[2,256,640]{2,1,0:T(8,128)(2,1)S(1)}, bf16[2,256,640]{2,1,0:T(8,128)(2,1)S(1)}, u32[]{:S(2)}, u32[]{:S(2)}) collective-permute-start(bf16[2,256,640]{2,1,0:T(8,128)(2,1)S(1)} %get-tuple-element.59), channel_id=1, source_target_pairs={{8,0},{16,8},{24,16},{9,1},{17,9},{25,17},{10,2},{18,10},{26,18},{... | collective-permute-start | bytes 1966088 | tf_op jit(solution)/shard_map/ppermute | solution.py:139
Sparse Core Ops, SparseCore 0:
  13.1 111.0 all-gather.1
